TPU v7x, 32 devices: a whole 2x2x4 slice. The times are simulated.
32 devices in a mesh: groups: 2 (over x), row: 16 (over z, y, core).
Axes of the slice: x: 2, y: 2, z: 4, core: 2. Of those that a mesh axis runs over, the one named last changes fastest.
Arguments:
- velocity: float32 [3, 8, 1024, 1024], P(None, 'groups', 'row'), parts along dimension 1, may hold values from -8 to 8
- slope_matrix: float32 [1024, 1024], replicated, may hold values from -0.1875 to 0.1875
- curve_matrix: float32 [1024, 1024], replicated, may hold values from -0.1875 to 0.1875
Outputs:
- advanced: float32 [3, 8, 1024, 1024], P(None, 'groups', 'row'), parts along dimension 1
There are 2 independent parts, one for each index of `groups`. A program takes and returns all parts, laid end to end along the dimension named above; an argument that names none is the same for every part. Nothing has to cross between parts.
All inputs are finite; a program needn't handle non-finite values.
Results may differ from a plain program's by a relative error of at most 0.00005.
Values sent between devices are 32-bit elements; how exact they have to be, the bound alone decides.
No kernel may reach another device: no remote copies, remote signals or barrier semaphores. Data moves between devices by JAX's collectives and lax.ppermute only.
A program may use at most 192 MiB of HBM per device.

v0:
```python
import jax
import jax.numpy as jnp
from jax import lax
from jax.sharding import PartitionSpec as P

viscosity = 0.2
power_input = 2.0
time_step = 0.5


def column_terms(columns, slope_matrix, stacked):
    length = columns.shape[2]
    flux = columns[1:2] * columns
    both = jnp.einsum("czkx,kj->czjx", columns, stacked, precision=lax.Precision.HIGHEST)
    slope_vel = both[:, :, :length]
    curve_vel = both[:, :, length:]
    slope_flux = jnp.einsum("czkx,ky->czyx", flux, slope_matrix, precision=lax.Precision.HIGHEST)
    return -0.5 * (columns[1:2] * slope_vel + slope_flux) + viscosity * curve_vel


def tendency(field, slope_matrix, stacked):
    length = field.shape[3]
    cells = 3 * field.shape[1] * field.shape[2] * lax.axis_size("row") * length
    total = lax.psum(jnp.sum(field * field), "row")
    columns = lax.all_to_all(field, "row", split_axis=3, concat_axis=2, tiled=True)
    returned = lax.all_to_all(
        column_terms(columns, slope_matrix, stacked), "row", split_axis=2, concat_axis=3, tiled=True
    )
    flat = field.reshape(-1, length)
    both = jnp.dot(flat, stacked, precision=lax.Precision.HIGHEST).reshape(
        field.shape[:3] + (2 * length,)
    )
    slope_vel = both[..., :length]
    curve_vel = both[..., length:]
    flux = (field[0:1] * field).reshape(-1, length)
    slope_flux = jnp.dot(flux, slope_matrix, precision=lax.Precision.HIGHEST).reshape(field.shape)
    x_part = -0.5 * (field[0:1] * slope_vel + slope_flux) + viscosity * curve_vel
    forcing = power_input / (total / cells)
    return x_part + returned + forcing * field


def on_device(velocity, slope_matrix, curve_matrix):
    stacked = jnp.concatenate([slope_matrix, curve_matrix], axis=1)
    first = tendency(velocity, slope_matrix, stacked)
    middle = velocity + time_step * (8.0 / 15.0) * first
    second = tendency(middle, slope_matrix, stacked)
    return middle + time_step * (5.0 / 12.0 * second - 17.0 / 60.0 * first)


def solution(mesh):
    placed = (P(None, "groups", "row", None), P(), P())
    return jax.shard_map(
        on_device,
        mesh=mesh,
        in_specs=placed,
        out_specs=P(None, "groups", "row", None),
        check_vma=False,
    )
```

profile of v0, /device:TPU:18, one launch (start us, length us, event | category | flops | bytes accessed | tf_op | source)
XLA Modules:
  0.0 708.4 jit_solution(13406671682096772345)
XLA Ops:
  0.0 6.7 copy.12
  6.7 9.6 %reshape.26 = f32[16,1,49152]{2,1,0:T(1,128)} reshape(f32[1024,3,4,64]{3,2,1,0:T(4,128)} %bitcast.112) | data formatting | bytes 6291456
  29.6 62.9 %all-to-all-done = f32[16,1,49152]{2,1,0:T(1,128)S(1)} async-done(((f32[16,1,49152]{2,1,0:T(1,128)}), f32[16,1,49152]{2,1,0:T(1,128)S(1)}, u32[]{:S(2)}, u32[]{:S(2)}) %all-to-all-start) | async-done | bytes 3145760 | tf_op jit(solution)/shard_map/all_to_all | solution.py:25
  93.2 10.8 %reduce = f32[16,49152]{1,0:T(8,128)} reduce(f32[16,1,49152]{2,1,0:T(1,128)S(1)} %all-to-all-done, f32[]{:T(128)} %broadcast.24), dimensions={1}, to_apply=%all_to_all.52.reduce_sub_computation | reduce | bytes 6291460 | tf_op jit(solution)/shard_map/all_to_all | solution.py:25
  104.0 7.8 %reshape.27 = f32[1024,3,4,64]{3,2,1,0:T(4,128)} reshape(f32[16,49152]{1,0:T(8,128)} %reduce) | data formatting | bytes 6291456
  111.7 6.4 copy.29
  121.0 6.3 all_to_all.55
  127.9 25.0 %fusion.14 = f32[3,4,2048,64]{2,3,1,0:T(8,128)S(1)} fusion(f32[3,4,1024,64]{2,3,1,0:T(8,128)} %all_to_all.55, f32[1024,2048]{1,0:T(8,128)} %constant_dynamic-update-slice_fusion), kind=kOutput, calls=%fused_computation.18 | convolution fusion | flops 19327352832 | bytes 17825792 | tf_op jit(solution)/shard_map/czkx,kj->czjx/dot_general | solution.py:14
  152.9 12.5 %fusion.32 = f32[3,4,1024,64]{2,3,1,0:T(8,128)} fusion(f32[3,4,2048,64]{2,3,1,0:T(8,128)S(1)} %fusion.14, f32[1024,1024]{1,0:T(8,128)S(1)} %copy-done, f32[3,4,1024,64]{2,3,1,0:T(8,128)S(1)} %copy-done.6, f32[4,1024,64]{1,2,0:T(8,128)S(1)} %mul.136), kind=kOutput, calls=%fused_computation.37 | convolution fusion | flops 9668395008 | bytes 18874368 | tf_op jit(solution)/shard_map/czkx,ky->czyx/dot_general | solution.py:17
  165.5 6.8 copy.14
  172.3 9.6 %reshape.28 = f32[16,1,49152]{2,1,0:T(1,128)} reshape(f32[1024,3,4,64]{3,2,1,0:T(4,128)} %bitcast.105) | data formatting | bytes 6291456
  188.2 87.4 %psum.14 = f32[]{:T(128)} all-reduce(f32[]{:T(128)} %multiply_reduce_fusion.1), channel_id=1, replica_groups=mesh['groups'=2,'row'=16] {'row'}, use_global_device_ids=true, to_apply=%region_1.0 | all-reduce | flops 1 | bytes 8 | tf_op jit(solution)/shard_map/psum | solution.py:24
  277.3 24.6 %fusion.64 = f32[2048,768]{0,1:T(8,128)} fusion(f32[1024,2048]{1,0:T(8,128)} %constant_dynamic-update-slice_fusion, f32[768,1024]{1,0:T(8,128)S(1)} %bitcast.99), kind=kOutput, calls=%fused_computation.63 | convolution fusion | flops 19327352832 | bytes 17825792 | tf_op jit(solution)/shard_map/dot_general | solution.py:30
  301.9 10.1 %reduce.1 = f32[16,49152]{1,0:T(8,128)S(1)} reduce(f32[16,1,49152]{2,1,0:T(1,128)} %all-to-all-done.1, f32[]{:T(128)} %broadcast.24), dimensions={1}, to_apply=%all_to_all.56.reduce_sub_computation | reduce | bytes 6291460 | tf_op jit(solution)/shard_map/all_to_all | solution.py:26
  318.1 9.1 %copy.28 = f32[3,4,16,64,64]{4,2,3,1,0:T(8,128)} copy(f32[3,4,16,64,64]{4,1,0,3,2:T(4,128)} %bitcast.106) | data formatting | bytes 6291456 | tf_op jit(solution)/shard_map/all_to_all | solution.py:26
  333.5 20.7 %multiply_reduce_fusion = (f32[]{:T(128)}, f32[3,4,64,1024]{3,2,1,0:T(8,128)S(1)}, f32[3,4,64,1024]{3,2,1,0:T(8,128)}) fusion(f32[3,4,64,1024]{3,2,1,0:T(8,128)} %param.3, f32[]{:T(128)S(6)} %div.13, f32[3,4,64,1024]{3,2,1,0:T(8,128)} %all_to_all.59, f32[3,4,64,2048]{3,2,1,0:T(8,128)} %bitcast.114, f32[1024,1024]{1,0:T(8,128)} %param.4, ...), kind=kOutput, calls=%fused_computation.48 | convolution fusion | flops 9673900032 | bytes 28311560 | tf_op jit(solution)/shard_map/dot_general | solution.py:36
  359.0 9.6 %reshape.30 = f32[16,1,49152]{2,1,0:T(1,128)} reshape(f32[1024,3,4,64]{3,2,1,0:T(4,128)} %bitcast.113) | data formatting | bytes 6291456
  368.7 74.8 %all_to_all.72 = f32[16,1,49152]{2,1,0:T(1,128)} all-to-all(f32[16,1,49152]{2,1,0:T(1,128)} %reshape.30), channel_id=1, replica_groups=mesh['groups'=2,'row'=16] {'row'}, dimensions={0} | all-to-all | bytes 6291456 | tf_op jit(solution)/shard_map/all_to_all | solution.py:25
  443.5 11.8 %reduce.2 = f32[16,49152]{1,0:T(8,128)} reduce(f32[16,1,49152]{2,1,0:T(1,128)} %all_to_all.72, f32[]{:T(128)} %broadcast.24), dimensions={1}, to_apply=%all_to_all.60.reduce_sub_computation | reduce | bytes 6291460 | tf_op jit(solution)/shard_map/all_to_all | solution.py:25
  455.2 7.5 %reshape.31 = f32[1024,3,4,64]{3,2,1,0:T(4,128)} reshape(f32[16,49152]{1,0:T(8,128)} %reduce.2) | data formatting | bytes 6291456
  462.7 6.4 copy.27
  482.5 25.2 %fusion.17 = f32[3,4,2048,64]{2,3,1,0:T(8,128)S(1)} fusion(f32[3,4,1024,64]{2,3,1,0:T(8,128)} %all_to_all.63, f32[1024,2048]{1,0:T(8,128)} %constant_dynamic-update-slice_fusion), kind=kOutput, calls=%fused_computation.19 | convolution fusion | flops 19327352832 | bytes 17825792 | tf_op jit(solution)/shard_map/czkx,kj->czjx/dot_general | solution.py:14
  507.7 12.4 %fusion.20 = f32[3,4,1024,64]{2,3,1,0:T(8,128)} fusion(f32[3,4,2048,64]{2,3,1,0:T(8,128)S(1)} %fusion.17, f32[1024,1024]{1,0:T(8,128)S(1)} %copy-done.1, f32[3,4,1024,64]{2,3,1,0:T(8,128)S(1)} %copy-done.7, f32[4,1024,64]{1,2,0:T(8,128)S(1)} %copy-done.5), kind=kOutput, calls=%fused_computation.21 | convolution fusion | flops 9668395008 | bytes 18874368 | tf_op jit(solution)/shard_map/czkx,ky->czyx/dot_general | solution.py:17
  520.1 6.8 copy.18
  526.9 9.6 %reshape.32 = f32[16,1,49152]{2,1,0:T(1,128)} reshape(f32[1024,3,4,64]{3,2,1,0:T(4,128)} %bitcast.109) | data formatting | bytes 6291456
  541.4 88.8 %psum.15 = f32[]{:T(128)} all-reduce(f32[]{:T(128)} %get-tuple-element.5), channel_id=1, replica_groups=mesh['groups'=2,'row'=16] {'row'}, use_global_device_ids=true, to_apply=%region_3.0 | all-reduce | flops 1 | bytes 8 | tf_op jit(solution)/shard_map/psum | solution.py:24
  631.9 24.3 %fusion.2 = f32[3,4,64,2048]{3,2,1,0:T(8,128)} fusion(f32[3,4,64,1024]{3,2,1,0:T(8,128)S(1)} %get-tuple-element.6, f32[1024,2048]{1,0:T(8,128)} %constant_dynamic-update-slice_fusion), kind=kOutput, calls=%fused_computation.2 | convolution fusion | flops 19327352832 | bytes 17825792 | tf_op jit(solution)/shard_map/dot_general | solution.py:30
  656.2 11.8 %reduce.3 = f32[16,49152]{1,0:T(8,128)} reduce(f32[16,1,49152]{2,1,0:T(1,128)} %all-to-all-done.3, f32[]{:T(128)} %broadcast.24), dimensions={1}, to_apply=%all_to_all.64.reduce_sub_computation | reduce | bytes 6291460 | tf_op jit(solution)/shard_map/all_to_all | solution.py:26
  667.9 7.6 %reshape.33 = f32[1024,3,4,64]{3,2,1,0:T(4,128)} reshape(f32[16,49152]{1,0:T(8,128)} %reduce.3) | data formatting | bytes 6291456
  675.5 9.0 %copy.26 = f32[3,4,16,64,64]{4,2,3,1,0:T(8,128)} copy(f32[3,4,16,64,64]{4,1,0,3,2:T(4,128)} %bitcast.110) | data formatting | bytes 6291456 | tf_op jit(solution)/shard_map/all_to_all | solution.py:26
  684.5 6.3 all_to_all.67
  690.8 17.3 %fusion.29 = f32[3,4,64,1024]{3,2,1,0:T(8,128)} fusion(f32[3,4,64,1024]{3,2,1,0:T(8,128)S(1)} %get-tuple-element.6, f32[3,4,64,1024]{3,2,1,0:T(8,128)} %all_to_all.67, f32[3,4,64,2048]{3,2,1,0:T(8,128)} %fusion.2, f32[3,4,64,1024]{3,2,1,0:T(8,128)} %get-tuple-element.7, f32[1024,1024]{1,0:T(8,128)} %param.4, f32[]{:T(128)S(6)} %div.15, ...), kind=kOutput, calls=%fused_computation.32 | convolution fusion | flops 9674686464 | bytes 28311556 | tf_op jit(solution)/shard_map/dot_general | solution.py:36
  (37 shorter events, 61.3 us)
Async XLA Ops:
  16.3 76.3 %all-to-all-start = ((f32[16,1,49152]{2,1,0:T(1,128)}), f32[16,1,49152]{2,1,0:T(1,128)S(1)}, u32[]{:S(2)}, u32[]{:S(2)}) async-start(f32[16,1,49152]{2,1,0:T(1,128)} %reshape.26), calls=%async_computation | async-start | bytes 6291456 | tf_op jit(solution)/shard_map/all_to_all | solution.py:25
  22.5 4.9 copy-start.8
  118.2 2.7 copy-start.3
  127.9 25.0 %copy-start = (f32[1024,1024]{1,0:T(8,128)S(1)}, f32[1024,1024]{1,0:T(8,128)}, u32[]{:S(2)}) copy-start(f32[1024,1024]{1,0:T(8,128)} %param.4) | copy-start | bytes 12582916
  127.9 25.0 %copy-start.6 = (f32[3,4,1024,64]{2,3,1,0:T(8,128)S(1)}, f32[3,4,1024,64]{2,3,1,0:T(8,128)}, u32[]{:S(2)}) copy-start(f32[3,4,1024,64]{2,3,1,0:T(8,128)} %all_to_all.55) | copy-start | bytes 9437188
  181.9 4.9 copy-start.2
  181.9 120.0 %all-to-all-start.1 = ((f32[16,1,49152]{2,1,0:T(1,128)}), f32[16,1,49152]{2,1,0:T(1,128)}, u32[]{:S(2)}, u32[]{:S(2)}) async-start(f32[16,1,49152]{2,1,0:T(1,128)} %reshape.28), calls=%async_computation.1 | async-start | bytes 6291456 | tf_op jit(solution)/shard_map/all_to_all | solution.py:26
  469.1 2.7 copy-start.4
  482.5 25.2 %copy-start.1 = (f32[1024,1024]{1,0:T(8,128)S(1)}, f32[1024,1024]{1,0:T(8,128)}, u32[]{:S(2)}) copy-start(f32[1024,1024]{1,0:T(8,128)} %param.4) | copy-start | bytes 12582916
  482.5 25.2 %copy-start.5 = (f32[4,1024,64]{1,2,0:T(8,128)S(1)}, f32[4,1024,64]{1,2,0:T(8,128)}, u32[]{:S(2)}) copy-start(f32[4,1024,64]{1,2,0:T(8,128)} %mul.153) | copy-start | bytes 3145732
  482.5 25.2 %copy-start.7 = (f32[3,4,1024,64]{2,3,1,0:T(8,128)S(1)}, f32[3,4,1024,64]{2,3,1,0:T(8,128)}, u32[]{:S(2)}) copy-start(f32[3,4,1024,64]{2,3,1,0:T(8,128)} %all_to_all.63) | copy-start | bytes 9437188
  536.6 119.6 %all-to-all-start.3 = ((f32[16,1,49152]{2,1,0:T(1,128)}), f32[16,1,49152]{2,1,0:T(1,128)}, u32[]{:S(2)}, u32[]{:S(2)}) async-start(f32[16,1,49152]{2,1,0:T(1,128)} %reshape.32), calls=%async_computation.3 | async-start | bytes 6291456 | tf_op jit(solution)/shard_map/all_to_all | solution.py:26
where the time goes:
time: 720 us; the launch traced here: 708 us
  blocking collectives  251 us (35%)
  local copies, waits for them, and re-layouts  169 us (23%)
  matrix products  162 us (22%)
  waiting for transfers between devices  62.9 us (9%)
  other arithmetic  45.9 us (6%)
  starting transfers between devices  16 us (2%)
    psum x2, blocking collectives, tendency(): total = lax.psum(jnp.sum(field * field), 'row')  176 us
    unnamed x28, local copies, waits for them, and re-layouts  84.3 us
    all_to_all x1, blocking collectives, tendency(): lax.all_to_all(field, 'row', split_axis=3, concat_axis=2, tiled=True)  74.8 us
    all_to_all x1, waiting for transfers between devices, tendency(): lax.all_to_all(field, 'row', split_axis=3, concat_axis=2, tiled=True)  62.9 us
    dot_general x2, matrix products, column_terms(): jnp.einsum('czkx,kj->czjx', columns, stacked, precision=lax.Precision.HIG...  50.2 us
    dot_general x2, matrix products, tendency(): jnp.dot(flat, stacked, precision=lax.Precision.HIGHEST)  48.9 us
    dot_general x2, matrix products, tendency(): jnp.dot(flux, slope_matrix, precision=lax.Precision.HIGHEST)  38 us
    all_to_all x4, local copies, waits for them, and re-layouts, tendency(): lax.all_to_all(column_terms(columns, slope_matrix, stacked), 'row', split...  30.7 us
  transfers between devices with their start and end apart: 3, of which 1 were waited for; matrix products, arithmetic and copies ran while one was open for 8% of the time, Pallas kernels for 0%

commit v1 on v0

v1 whole, which is shorter than its diff:
```python
import functools

import jax
import jax.numpy as jnp
from jax import lax
from jax.experimental import pallas as pl
from jax.experimental.pallas import tpu as pltpu
from jax.sharding import PartitionSpec as P

viscosity = 0.2
power_input = 2.0
time_step = 0.5
first_weight = 8.0 / 15.0
second_weight = 5.0 / 12.0
back_weight = 17.0 / 60.0

BF16 = jnp.bfloat16
F32 = jnp.float32
VMEM_BYTES = 50 * 1024 * 1024


def halves(x):
    high = x.astype(BF16)
    return high, (x - high.astype(F32)).astype(BF16)


def product(a, b):
    return jnp.dot(a, b, preferred_element_type=F32)


def params():
    return pltpu.CompilerParams(vmem_limit_bytes=VMEM_BYTES)


def matrices_kernel(count, order_ref, *refs):
    slope_parts, curve_parts = refs[:count], refs[count:2 * count]
    slope_ref, curve_ref, along_x_ref, along_y_ref, turned = refs[2 * count:]
    size = slope_parts[0].shape[0]
    for place, ref, scale in ((0, slope_ref, -0.5), (2, curve_ref, viscosity)):
        high, low = halves(ref[...] * scale)
        along_x_ref[place] = high
        along_x_ref[place + 1] = low
    for high_place, low_place, parts, scale in ((1, 0, slope_parts, -0.5), (2, 3, curve_parts, viscosity)):
        turned[...] = jnp.concatenate([part[...] for part in parts], axis=0).T
        for block in range(along_y_ref.shape[1] // size):
            source = pl.ds(pl.multiple_of(order_ref[block] * size, size), size)
            high, low = halves(turned[source, :] * scale)
            along_y_ref[high_place, block * size:(block + 1) * size, :] = high
            along_y_ref[low_place, block * size:(block + 1) * size, :] = low


def prepare_matrices(order, slope_matrix, curve_matrix, size):
    length = slope_matrix.shape[0]
    width = min(128, length)
    count = width // size

    def part(place):
        return pl.BlockSpec((size, length), lambda j, order_ref: (order_ref[count * j + place], 0))

    parts = [part(place) for place in range(count)]
    straight = pl.BlockSpec((width, length), lambda j, order_ref: (j, 0))
    return pl.pallas_call(
        functools.partial(matrices_kernel, count),
        grid_spec=pltpu.PrefetchScalarGridSpec(
            num_scalar_prefetch=1,
            grid=(length // width,),
            in_specs=parts + parts + [straight, straight],
            out_specs=[
                pl.BlockSpec((4, width, length), lambda j, order_ref: (0, j, 0)),
                pl.BlockSpec((4, length // 2, width), lambda j, order_ref: (0, 0, j)),
            ],
            scratch_shapes=[pltpu.VMEM((length, width), F32)],
        ),
        out_shape=[
            jax.ShapeDtypeStruct((4, length, length), BF16),
            jax.ShapeDtypeStruct((4, length // 2, length), BF16),
        ],
        compiler_params=params(),
    )(order, *([slope_matrix] * count), *([curve_matrix] * count), slope_matrix, curve_matrix)


def along_x_kernel(carrier_ref, field_ref, matrix_ref, out_ref, stack):
    rows = field_ref.shape[0]

    @pl.when(pl.program_id(0) == 0)
    def _():
        field = field_ref[...]
        high, low = halves(field)
        stack[0:rows] = low
        stack[rows:2 * rows] = high
        high, low = halves(carrier_ref[...] * field)
        stack[2 * rows:3 * rows] = high
        stack[3 * rows:4 * rows] = low

    tile = out_ref.shape[1]
    columns = pl.ds(pl.multiple_of(pl.program_id(0) * tile, tile), tile)
    a = product(stack[...], matrix_ref[0])
    b = product(stack[rows:3 * rows], matrix_ref[1])
    c = product(stack[0:2 * rows], matrix_ref[2])
    d = product(stack[rows:2 * rows], matrix_ref[3])
    slope = a[0:rows] + a[rows:2 * rows] + b[0:rows]
    rest = a[2 * rows:3 * rows] + a[3 * rows:] + b[rows:] + c[0:rows] + c[rows:] + d
    out_ref[...] = carrier_ref[:, columns] * slope + rest


def along_x(carrier, field, matrix, name):
    rows, length = field.shape
    tile = min(256, length)
    whole = pl.BlockSpec((rows, length), lambda n: (0, 0))
    return pl.pallas_call(
        along_x_kernel,
        grid=(length // tile,),
        in_specs=[whole, whole, pl.BlockSpec((4, length, tile), lambda n: (0, 0, n))],
        out_specs=pl.BlockSpec((rows, tile), lambda n: (0, n)),
        out_shape=jax.ShapeDtypeStruct((rows, length), F32),
        scratch_shapes=[pltpu.VMEM((4 * rows, length), BF16)],
        compiler_params=params(),
        cost_estimate=pl.CostEstimate(
            flops=18 * rows * length * length, bytes_accessed=8 * length * length + 12 * rows * length, transcendentals=0
        ),
        name=name,
    )(carrier, field, matrix)


def y_products(matrix_ref, near_ref, far_ref, carrier_near_ref, carrier_far_ref):
    rows, length = matrix_ref.shape[1:]
    field = jnp.concatenate([near_ref[...], far_ref[...]], axis=0)
    carrier = jnp.concatenate([carrier_near_ref[...], carrier_far_ref[...]], axis=0)
    field_high, field_low = halves(field)
    flux_high, flux_low = halves(field * carrier)
    matrix = matrix_ref[...].reshape(4 * rows, length)
    a = product(matrix, field_high)
    b = product(matrix[rows:3 * rows], field_low)
    c = product(matrix[0:2 * rows], flux_high)
    d = product(matrix[rows:2 * rows], flux_low)
    slope = a[0:rows] + a[rows:2 * rows] + b[0:rows]
    rest = a[2 * rows:3 * rows] + a[3 * rows:] + b[rows:] + c[0:rows] + c[rows:] + d
    return carrier[0:rows] * slope + rest


def first_kernel(forcing_ref, matrix_ref, near, far, carrier_near, carrier_far, x_ref, middle_ref, base_ref, square_ref):
    rows = matrix_ref.shape[1]
    kept = base_ref.shape[0]
    terms = x_ref[...] + y_products(matrix_ref, near, far, carrier_near, carrier_far)
    field = near[0:rows, :]
    first = terms + forcing_ref[0, 0] * field
    middle = field + (time_step * first_weight) * first
    middle_ref[...] = middle
    base_ref[...] = middle[0:kept] - (time_step * back_weight) * first[0:kept]
    square_ref[...] = jnp.sum((middle * middle).reshape(rows // 8, 8, middle.shape[1]), axis=0)


def second_kernel(matrix_ref, near, far, carrier_near, carrier_far, x_ref, base_ref, out_ref):
    terms = x_ref[...] + y_products(matrix_ref, near, far, carrier_near, carrier_far)
    out_ref[...] = base_ref[...] + (time_step * second_weight) * terms


def y_call(kernel, rows, matrix, fields, rest, out_rows, scalars, name):
    half, length = fields[0].shape
    tile = min(256, length)
    columns = lambda count: pl.BlockSpec((count, tile), lambda n: (0, n))
    return pl.pallas_call(
        kernel,
        grid=(length // tile,),
        in_specs=[pl.BlockSpec(memory_space=pltpu.SMEM)] * len(scalars)
        + [pl.BlockSpec((4, rows, length), lambda n: (0, 0, 0))]
        + [columns(x.shape[0]) for x in fields + rest],
        out_specs=[columns(count) for count in out_rows],
        out_shape=[jax.ShapeDtypeStruct((count, length), F32) for count in out_rows],
        compiler_params=params(),
        cost_estimate=pl.CostEstimate(
            flops=18 * rows * length * length,
            bytes_accessed=8 * rows * length + 16 * length * length + 12 * rows * length,
            transcendentals=0,
        ),
        name=name,
    )(*scalars, matrix, *fields, *rest)


def on_device(velocity, slope_matrix, curve_matrix):
    planes, size, length = velocity.shape[1:]
    devices = lax.axis_size("row")
    group = devices // planes
    chips = group // 2
    place = lax.axis_index("row")
    plane, member = place // group, place % group

    def swap(x, distance):
        return lax.ppermute(x, "row", [(r, r ^ distance) for r in range(devices)])

    def order_of(index):
        core, rest = index // (chips * planes), index % (chips * planes)
        chip, far = rest // planes, rest % planes
        return (plane ^ far) * group + (member ^ (2 * chip + core))

    order = jnp.stack([order_of(index) for index in range(devices)]).astype(jnp.int32)
    cells = 3 * planes * size * devices * length

    own = [[lax.dynamic_index_in_dim(velocity[i], plane ^ d, axis=0, keepdims=False) for d in range(planes)] for i in range(3)]
    near, far = [], []
    for i in range(3):
        mine = jnp.concatenate([own[i][0]] + [swap(own[i][d], d * group) for d in range(1, planes)], axis=0)
        others = [swap(mine, 2 * h) for h in range(1, chips)]
        near.append(jnp.concatenate([mine] + others, axis=0))
        far.append(swap(near[i], 1))

    along_x_matrix, along_y_matrix = prepare_matrices(order, slope_matrix, curve_matrix, size)
    total = lax.psum(jnp.sum(velocity * velocity), "row")
    forcing = (power_input / (total / cells)).reshape(1, 1)

    half, kept = length // 2, length // group
    middle_near, middle_far, base, squares = [], [], [], 0.0
    for i in range(3):
        x_terms = along_x(near[0], near[i], along_x_matrix, f"x_first_{i}")
        middle, back, square = y_call(
            first_kernel, half, along_y_matrix, [near[i], far[i], near[1], far[1]], [x_terms],
            [half, kept, 8], [forcing], f"y_first_{i}",
        )
        middle_near.append(middle)
        middle_far.append(swap(middle, 1))
        base.append(back)
        squares = squares + jnp.sum(square)
    total = lax.psum(squares, "row") / chips
    forcing = power_input / (total / cells)

    ends = []
    for i in range(3):
        x_terms = along_x(middle_near[0][:kept], middle_near[i][:kept], along_x_matrix, f"x_second_{i}")
        (end,) = y_call(
            second_kernel, kept, along_y_matrix, [middle_near[i], middle_far[i], middle_near[1], middle_far[1]],
            [x_terms, base[i]], [kept], [], f"y_second_{i}",
        )
        ends.append(end)

    out = jnp.zeros(velocity.shape, F32)
    for i in range(3):
        final = ends[i] + (time_step * second_weight) * forcing * middle_near[i][:kept]
        for d in range(planes):
            block = final[d * size:(d + 1) * size]
            block = swap(block, d * group) if d else block
            out = lax.dynamic_update_slice(out, block[None, None], (i, plane ^ d, 0, 0))
    return out


def solution(mesh):
    placed = (P(None, "groups", "row", None), P(), P())
    return jax.shard_map(
        on_device,
        mesh=mesh,
        in_specs=placed,
        out_specs=P(None, "groups", "row", None),
        check_vma=False,
    )
```

time: 720 us -> 422 us (0.59); the launches traced: 708 us -> 420 us
  blocking collectives: 251 us -> 70.5 us
  matrix products: 162 us -> 0 us
  Pallas kernels: 0 us -> 152 us
  local copies, waits for them, and re-layouts: 169 us -> 35.4 us
  waiting for transfers between devices: 62.9 us -> 109 us
  other arithmetic: 45.9 us -> 8.74 us
  starting transfers between devices: 16 us -> 41.1 us
    dot_general x8 -> x0, matrix products: 162 us -> none  [the longest x2 50.2 us: column_terms(): jnp.einsum('czkx,kj->czjx', columns, stacked, precision=lax.Precision.HIG...]
    pallas_call x0 -> x13, Pallas kernels: none -> 152 us  [the longest x6 70.2 us: y_call(): pl.pallas_call(kernel, grid=(length // tile,), in_specs=[pl.BlockSpec(mem...]
    ppermute x0 -> x27, waiting for transfers between devices: none -> 109 us  [swap(): return lax.ppermute(x, 'row', [(r, r ^ distance) for r in range(devices)])]
    psum x2, blocking collectives: 176 us -> 70.5 us  [the longest x1 46.6 us: on_device(): total = lax.psum(jnp.sum(velocity * velocity), 'row')]
    all_to_all x1 -> x0, blocking collectives: 74.8 us -> none  [tendency(): lax.all_to_all(field, 'row', split_axis=3, concat_axis=2, tiled=True)]
    unnamed x28 -> x65, local copies, waits for them, and re-layouts: 84.3 us -> 20.5 us
    all_to_all x3 -> x0, waiting for transfers between devices: 62.9 us -> none  [the longest x1 62.9 us: tendency(): lax.all_to_all(field, 'row', split_axis=3, concat_axis=2, tiled=True)]
    all_to_all x9 -> x0, local copies, waits for them, and re-layouts: 56.7 us -> none  [the longest x4 30.7 us: tendency(): lax.all_to_all(column_terms(columns, slope_matrix, stacked), 'row', split...]
  transfers between devices with their start and end apart: 3 -> 27, of which waited for: 1 -> 10; matrix products, arithmetic and copies ran while one was open for 8% -> 5% of each run, Pallas kernels for 0% -> 34%
where the time goes in v1:
time: 422 us; the launch traced here: 420 us
  Pallas kernels  152 us (36%)
  waiting for transfers between devices  109 us (26%)
  blocking collectives  70.5 us (17%)
  starting transfers between devices  41.1 us (10%)
  local copies, waits for them, and re-layouts  35.4 us (8%)
  other arithmetic  8.74 us (2%)
    ppermute x27, waiting for transfers between devices, swap(): return lax.ppermute(x, 'row', [(r, r ^ distance) for r in range(devices)])  109 us
    pallas_call x6, Pallas kernels, y_call(): pl.pallas_call(kernel, grid=(length // tile,), in_specs=[pl.BlockSpec(mem...  70.2 us
    pallas_call x6, Pallas kernels, along_x(): pl.pallas_call(along_x_kernel, grid=(length // tile,), in_specs=[whole, w...  66.7 us
    psum x1, blocking collectives, on_device(): total = lax.psum(jnp.sum(velocity * velocity), 'row')  46.6 us
    ppermute x27, starting transfers between devices, swap(): return lax.ppermute(x, 'row', [(r, r ^ distance) for r in range(devices)])  41.1 us
    psum x1, blocking collectives, on_device(): total = lax.psum(squares, 'row') / chips  23.9 us
    unnamed x65, local copies, waits for them, and re-layouts  20.5 us
    pallas_call x1, Pallas kernels, prepare_matrices(): pl.pallas_call(functools.partial(matrices_kernel, count), grid_spec=pltpu...  14.9 us
  transfers between devices with their start and end apart: 27, of which 10 were waited for; matrix products, arithmetic and copies ran while one was open for 5% of the time, Pallas kernels for 34%

profile of v1, /device:TPU:18, one launch (start us, length us, event | category | flops | bytes accessed | tf_op | source)
XLA Modules:
  0.0 420.0 jit_solution(8778211340780710595)
XLA Ops:
  0.0 3.6 fusion.3
  11.4 2.5 collective-permute-start
  15.3 46.6 %psum.14 = f32[]{:T(128)} all-reduce(f32[]{:T(128)} %multiply_reduce_fusion), channel_id=1, replica_groups=mesh['groups'=2,'row'=16] {'row'}, use_global_device_ids=true, to_apply=%region_1.2 | all-reduce | flops 1 | bytes 8 | tf_op jit(solution)/shard_map/psum | solution.py:208
  62.7 14.9 %shard_map.37 = (bf16[4,1024,1024]{2,1,0:T(8,128)(2,1)}, bf16[4,512,1024]{2,1,0:T(8,128)(2,1)}) custom-call(s32[16]{0:T(128)S(1)} %stack.67.order_ref, f32[1024,1024]{1,0:T(8,128)} %refs_4_.1, f32[1024,1024]{1,0:T(8,128)} %refs_4_.1, f32[1024,1024]{1,0:T(8,128)} %refs_5_.1, f32[1024,1024]{1,0:T(8,128)} %refs_5_.1, f32[1024,1024]{1,0:T(8,128)} %refs_4_.1, ...), custom_call_target="tpu_custom_call" | custom-call | tf_op jit(solution)/shard_map/pallas_call | solution.py:62
  79.8 4.2 collective-permute-start.5
  86.7 15.3 %collective-permute-done.2 = f32[64,1024]{1,0:T(8,128)S(1)} collective-permute-done((f32[64,1024]{1,0:T(8,128)S(1)}, f32[64,1024]{1,0:T(8,128)S(1)}, u32[]{:S(2)}, u32[]{:S(2)}) %collective-permute-start.2) | collective-permute-done | bytes 262176 | tf_op jit(solution)/shard_map/ppermute | solution.py:189
  103.3 4.6 %collective-permute-done.6 = f32[64,1024]{1,0:T(8,128)S(1)} collective-permute-done((f32[64,1024]{1,0:T(8,128)S(1)}, f32[64,1024]{1,0:T(8,128)S(1)}, u32[]{:S(2)}, u32[]{:S(2)}) %collective-permute-start.6) | collective-permute-done | bytes 262176 | tf_op jit(solution)/shard_map/ppermute | solution.py:189
  107.9 5.3 %collective-permute-done.7 = f32[64,1024]{1,0:T(8,128)S(1)} collective-permute-done((f32[64,1024]{1,0:T(8,128)S(1)}, f32[64,1024]{1,0:T(8,128)S(1)}, u32[]{:S(2)}, u32[]{:S(2)}) %collective-permute-start.7) | collective-permute-done | bytes 262176 | tf_op jit(solution)/shard_map/ppermute | solution.py:189
  117.9 35.2 %collective-permute-done.8 = f32[256,1024]{1,0:T(8,128)S(1)} collective-permute-done((f32[256,1024]{1,0:T(8,128)S(1)}, f32[256,1024]{1,0:T(8,128)S(1)}, u32[]{:S(2)}, u32[]{:S(2)}) %collective-permute-start.8) | collective-permute-done | bytes 1048608 | tf_op jit(solution)/shard_map/ppermute | solution.py:189
  154.8 14.2 %x_first_2.1.x_ref = f32[512,1024]{1,0:T(8,128)S(1)} custom-call(f32[512,1024]{1,0:T(8,128)} %copy-done.23, f32[512,1024]{1,0:T(8,128)} %copy-done.24, bf16[4,1024,1024]{2,1,0:T(8,128)(2,1)} %get-tuple-element.17.matrix_ref), custom_call_target="tpu_custom_call" | custom-call | flops 9663676416 | bytes 14680064 | tf_op jit(solution)/shard_map/x_first_2/pallas_call | solution.py:110
  170.4 14.6 %x_first_0.1.x_ref = f32[512,1024]{1,0:T(8,128)S(1)} custom-call(f32[512,1024]{1,0:T(8,128)} %copy-done.23, f32[512,1024]{1,0:T(8,128)} %copy-done.23, bf16[4,1024,1024]{2,1,0:T(8,128)(2,1)} %get-tuple-element.17.matrix_ref), custom_call_target="tpu_custom_call" | custom-call | flops 9663676416 | bytes 14680064 | tf_op jit(solution)/shard_map/x_first_0/pallas_call | solution.py:110
  186.4 14.2 %x_first_1.1.x_ref = f32[512,1024]{1,0:T(8,128)S(1)} custom-call(f32[512,1024]{1,0:T(8,128)} %copy-done.23, f32[512,1024]{1,0:T(8,128)} %copy-done.22, bf16[4,1024,1024]{2,1,0:T(8,128)(2,1)} %get-tuple-element.17.matrix_ref), custom_call_target="tpu_custom_call" | custom-call | flops 9663676416 | bytes 14680064 | tf_op jit(solution)/shard_map/x_first_1/pallas_call | solution.py:110
  203.9 15.2 %y_first_2.1 = (f32[512,1024]{1,0:T(8,128)}, f32[256,1024]{1,0:T(8,128)S(1)}, f32[8,1024]{1,0:T(8,128)S(1)}) custom-call(f32[1,1]{1,0:T(1,128)} %bitcast.16.forcing_ref, bf16[4,512,1024]{2,1,0:T(8,128)(2,1)} %get-tuple-element.16.matrix_ref, f32[512,1024]{1,0:T(8,128)} %copy-done.24, f32[512,1024]{1,0:T(8,128)} %copy-done.26, f32[512,1024]{1,0:T(8,128)} %copy-done.22, ...), custom_call_target="tpu_custom_call" | custom-call | flops 9663676416 | bytes 27262976 | tf_op jit(solution)/shard_map/y_first_2/pallas_call | solution.py:162
  221.3 14.4 %y_first_1.1 = (f32[512,1024]{1,0:T(8,128)S(1)}, f32[256,1024]{1,0:T(8,128)S(1)}, f32[8,1024]{1,0:T(8,128)S(1)}) custom-call(f32[1,1]{1,0:T(1,128)} %bitcast.16.forcing_ref, bf16[4,512,1024]{2,1,0:T(8,128)(2,1)} %get-tuple-element.16.matrix_ref, f32[512,1024]{1,0:T(8,128)} %copy-done.22, f32[512,1024]{1,0:T(8,128)} %copy-done.25, f32[512,1024]{1,0:T(8,128)} %copy-done.22, ...), custom_call_target="tpu_custom_call" | custom-call | flops 9663676416 | bytes 27262976 | tf_op jit(solution)/shard_map/y_first_1/pallas_call | solution.py:162
  236.8 15.9 %y_first_0.1 = (f32[512,1024]{1,0:T(8,128)}, f32[256,1024]{1,0:T(8,128)S(1)}, f32[8,1024]{1,0:T(8,128)S(1)}) custom-call(f32[1,1]{1,0:T(1,128)} %bitcast.16.forcing_ref, bf16[4,512,1024]{2,1,0:T(8,128)(2,1)} %get-tuple-element.16.matrix_ref, f32[512,1024]{1,0:T(8,128)} %copy-done.23, f32[512,1024]{1,0:T(8,128)} %collective-permute-done.4.far, ...), custom_call_target="tpu_custom_call" | custom-call | flops 9663676416 | bytes 27262976 | tf_op jit(solution)/shard_map/y_first_0/pallas_call | solution.py:162
  260.9 7.8 %x_second_0.1.x_ref = f32[256,1024]{1,0:T(8,128)S(1)} custom-call(f32[256,1024]{1,0:T(8,128)S(1)} %copy-done.2, f32[256,1024]{1,0:T(8,128)S(1)} %copy-done.2, bf16[4,1024,1024]{2,1,0:T(8,128)(2,1)} %get-tuple-element.17.matrix_ref), custom_call_target="tpu_custom_call" | custom-call | flops 4831838208 | bytes 11534336 | tf_op jit(solution)/shard_map/x_second_0/pallas_call | solution.py:110
  269.7 7.8 %x_second_2.1.x_ref = f32[256,1024]{1,0:T(8,128)S(1)} custom-call(f32[256,1024]{1,0:T(8,128)S(1)} %copy-done.2, f32[256,1024]{1,0:T(8,128)S(1)} %slice.82.field_ref, bf16[4,1024,1024]{2,1,0:T(8,128)(2,1)} %get-tuple-element.17.matrix_ref), custom_call_target="tpu_custom_call" | custom-call | flops 4831838208 | bytes 11534336 | tf_op jit(solution)/shard_map/x_second_2/pallas_call | solution.py:110
  278.5 23.9 %psum.15 = f32[]{:T(128)} all-reduce(f32[]{:T(128)S(6)} %add.127), channel_id=1, replica_groups=mesh['groups'=2,'row'=16] {'row'}, use_global_device_ids=true, to_apply=%region_5.6 | all-reduce | flops 1 | bytes 8 | tf_op jit(solution)/shard_map/psum | solution.py:223
  305.4 8.0 %x_second_1.1.x_ref = f32[256,1024]{1,0:T(8,128)S(1)} custom-call(f32[256,1024]{1,0:T(8,128)S(1)} %copy-done.3, f32[256,1024]{1,0:T(8,128)S(1)} %copy-done.4, bf16[4,1024,1024]{2,1,0:T(8,128)(2,1)} %get-tuple-element.17.matrix_ref), custom_call_target="tpu_custom_call" | custom-call | flops 4831838208 | bytes 11534336 | tf_op jit(solution)/shard_map/x_second_1/pallas_call | solution.py:110
  313.5 8.2 %y_second_2.1 = f32[256,1024]{1,0:T(8,128)S(1)} custom-call(bf16[4,512,1024]{2,1,0:T(8,128)(2,1)} %get-tuple-element.16.matrix_ref, f32[512,1024]{1,0:T(8,128)} %get-tuple-element.25.near, f32[512,1024]{1,0:T(8,128)} %collective-permute-done.23.far, f32[512,1024]{1,0:T(8,128)} %copy-done, f32[512,1024]{1,0:T(8,128)} %collective-permute-done.11.carrier_far.far, ...), custom_call_target="tpu_custom_call" | custom-call | flops 4831838208 | bytes 22020096 | tf_op jit(solution)/shard_map/y_second_2/pallas_call | solution.py:162
  323.2 8.3 %y_second_1.1 = f32[256,1024]{1,0:T(8,128)S(1)} custom-call(bf16[4,512,1024]{2,1,0:T(8,128)(2,1)} %get-tuple-element.16.matrix_ref, f32[512,1024]{1,0:T(8,128)} %copy-done, f32[512,1024]{1,0:T(8,128)} %collective-permute-done.11.carrier_far.far, f32[512,1024]{1,0:T(8,128)} %copy-done, f32[512,1024]{1,0:T(8,128)} %collective-permute-done.11.carrier_far.far, ...), custom_call_target="tpu_custom_call" | custom-call | flops 4831838208 | bytes 22020096 | tf_op jit(solution)/shard_map/y_second_1/pallas_call | solution.py:162
  333.1 8.2 %y_second_0.1 = f32[256,1024]{1,0:T(8,128)S(1)} custom-call(bf16[4,512,1024]{2,1,0:T(8,128)(2,1)} %get-tuple-element.16.matrix_ref, f32[512,1024]{1,0:T(8,128)} %get-tuple-element.18.near, f32[512,1024]{1,0:T(8,128)} %collective-permute-done.10.far, f32[512,1024]{1,0:T(8,128)} %copy-done, f32[512,1024]{1,0:T(8,128)} %collective-permute-done.11.carrier_far.far, ...), custom_call_target="tpu_custom_call" | custom-call | flops 4831838208 | bytes 22020096 | tf_op jit(solution)/shard_map/y_second_0/pallas_call | solution.py:162
  342.7 2.5 collective-permute-start.17
  345.2 8.6 %collective-permute-start.18 = (f32[64,1024]{1,0:T(8,128)S(1)}, f32[64,1024]{1,0:T(8,128)S(1)}, u32[]{:S(2)}, u32[]{:S(2)}) collective-permute-start(f32[64,1024]{1,0:T(8,128)S(1)} %get-tuple-element.43), channel_id=1, source_target_pairs={{0,8},{1,9},{2,10},{3,11},{4,12},{5,13},{6,14},{7,15},{8,0},{9,1},... | collective-permute-start | bytes 786440 | tf_op jit(solution)/shard_map/ppermute | solution.py:189
  356.4 2.4 collective-permute-start.21
  358.8 10.6 %collective-permute-start.22 = (f32[64,1024]{1,0:T(8,128)S(1)}, f32[64,1024]{1,0:T(8,128)S(1)}, u32[]{:S(2)}, u32[]{:S(2)}) collective-permute-start(f32[64,1024]{1,0:T(8,128)S(1)} %get-tuple-element.39), channel_id=1, source_target_pairs={{0,12},{1,13},{2,14},{3,15},{4,8},{5,9},{6,10},{7,11},{8,4},{9,5},... | collective-permute-start | bytes 786440 | tf_op jit(solution)/shard_map/ppermute | solution.py:189
  369.4 3.6 collective-permute-done.18
  374.3 15.4 %collective-permute-done.19 = f32[64,1024]{1,0:T(8,128)S(1)} collective-permute-done((f32[64,1024]{1,0:T(8,128)S(1)}, f32[64,1024]{1,0:T(8,128)S(1)}, u32[]{:S(2)}, u32[]{:S(2)}) %collective-permute-start.19) | collective-permute-done | bytes 262176 | tf_op jit(solution)/shard_map/ppermute | solution.py:189
  389.9 12.9 %collective-permute-done.21 = f32[64,1024]{1,0:T(8,128)S(1)} collective-permute-done((f32[64,1024]{1,0:T(8,128)S(1)}, f32[64,1024]{1,0:T(8,128)S(1)}, u32[]{:S(2)}, u32[]{:S(2)}) %collective-permute-start.21) | collective-permute-done | bytes 262176 | tf_op jit(solution)/shard_map/ppermute | solution.py:189
  402.8 8.1 %collective-permute-done.22 = f32[64,1024]{1,0:T(8,128)S(1)} collective-permute-done((f32[64,1024]{1,0:T(8,128)S(1)}, f32[64,1024]{1,0:T(8,128)S(1)}, u32[]{:S(2)}, u32[]{:S(2)}) %collective-permute-start.22) | collective-permute-done | bytes 262176 | tf_op jit(solution)/shard_map/ppermute | solution.py:189
  411.0 3.0 collective-permute-done.25
  414.0 5.3 %collective-permute-done.26 = f32[64,1024]{1,0:T(8,128)S(1)} collective-permute-done((f32[64,1024]{1,0:T(8,128)S(1)}, f32[64,1024]{1,0:T(8,128)S(1)}, u32[]{:S(2)}, u32[]{:S(2)}) %collective-permute-start.26) | collective-permute-done | bytes 262176 | tf_op jit(solution)/shard_map/ppermute | solution.py:189
  (139 shorter events, 50.9 us)
Async XLA Ops:
  5.9 72.8 %collective-permute-start.12 = (f32[64,1024]{1,0:T(8,128)}, f32[64,1024]{1,0:T(8,128)S(1)}, u32[]{:S(2)}, u32[]{:S(2)}) collective-permute-start(f32[64,1024]{1,0:T(8,128)} %get-tuple-element.47), channel_id=1, source_target_pairs={{0,4},{1,5},{2,6},{3,7},{4,0},{5,1},{6,2},{7,3},{8,12},{9,13},{10,... | collective-permute-start | bytes 786440 | tf_op jit(solution)/shard_map/ppermute | solution.py:189
  7.4 72.3 %collective-permute-start.13 = (f32[64,1024]{1,0:T(8,128)}, f32[64,1024]{1,0:T(8,128)}, u32[]{:S(2)}, u32[]{:S(2)}) collective-permute-start(f32[64,1024]{1,0:T(8,128)} %get-tuple-element.46), channel_id=1, source_target_pairs={{0,8},{1,9},{2,10},{3,11},{4,12},{5,13},{6,14},{7,15},{8,0},{9,1},... | collective-permute-start | bytes 786440 | tf_op jit(solution)/shard_map/ppermute | solution.py:189
  7.8 76.2 %collective-permute-start.14 = (f32[64,1024]{1,0:T(8,128)}, f32[64,1024]{1,0:T(8,128)}, u32[]{:S(2)}, u32[]{:S(2)}) collective-permute-start(f32[64,1024]{1,0:T(8,128)} %get-tuple-element.45), channel_id=1, source_target_pairs={{0,12},{1,13},{2,14},{3,15},{4,8},{5,9},{6,10},{7,11},{8,4},{9,5},... | collective-permute-start | bytes 786440 | tf_op jit(solution)/shard_map/ppermute | solution.py:189
  11.4 72.6 %collective-permute-start = (f32[64,1024]{1,0:T(8,128)}, f32[64,1024]{1,0:T(8,128)}, u32[]{:S(2)}, u32[]{:S(2)}) collective-permute-start(f32[64,1024]{1,0:T(8,128)} %get-tuple-element.53), channel_id=1, source_target_pairs={{0,4},{1,5},{2,6},{3,7},{4,0},{5,1},{6,2},{7,3},{8,12},{9,13},{10,... | collective-permute-start | bytes 786440 | tf_op jit(solution)/shard_map/ppermute | solution.py:189
  13.9 72.8 %collective-permute-start.1 = (f32[64,1024]{1,0:T(8,128)}, f32[64,1024]{1,0:T(8,128)}, u32[]{:S(2)}, u32[]{:S(2)}) collective-permute-start(f32[64,1024]{1,0:T(8,128)} %get-tuple-element.52), channel_id=1, source_target_pairs={{0,8},{1,9},{2,10},{3,11},{4,12},{5,13},{6,14},{7,15},{8,0},{9,1},... | collective-permute-start | bytes 786440 | tf_op jit(solution)/shard_map/ppermute | solution.py:189
  62.7 14.9 %copy-start.19 = (f32[1,4,64,1024]{3,2,1,0:T(8,128)S(1)}, f32[1,4,64,1024]{3,2,1,0:T(8,128)}, u32[]{:S(2)}) copy-start(f32[1,4,64,1024]{3,2,1,0:T(8,128)} %get-tuple-element.35) | copy-start | bytes 3145732
  78.7 23.4 %collective-permute-start.2 = (f32[64,1024]{1,0:T(8,128)S(1)}, f32[64,1024]{1,0:T(8,128)S(1)}, u32[]{:S(2)}, u32[]{:S(2)}) collective-permute-start(f32[64,1024]{1,0:T(8,128)S(1)} %copy-done.21), channel_id=1, source_target_pairs={{0,12},{1,13},{2,14},{3,15},{4,8},{5,9},{6,10},{7,11},{8,4},{9,5},... | collective-permute-start | bytes 786440 | tf_op jit(solution)/shard_map/ppermute | solution.py:189
  79.8 23.5 %collective-permute-start.5 = (f32[64,1024]{1,0:T(8,128)S(1)}, f32[64,1024]{1,0:T(8,128)S(1)}, u32[]{:S(2)}, u32[]{:S(2)}) collective-permute-start(f32[64,1024]{1,0:T(8,128)S(1)} %get-tuple-element.50), channel_id=1, source_target_pairs={{0,4},{1,5},{2,6},{3,7},{4,0},{5,1},{6,2},{7,3},{8,12},{9,13},{10,... | collective-permute-start | bytes 786440 | tf_op jit(solution)/shard_map/ppermute | solution.py:189
  83.9 24.0 %collective-permute-start.6 = (f32[64,1024]{1,0:T(8,128)S(1)}, f32[64,1024]{1,0:T(8,128)S(1)}, u32[]{:S(2)}, u32[]{:S(2)}) collective-permute-start(f32[64,1024]{1,0:T(8,128)S(1)} %get-tuple-element.49), channel_id=1, source_target_pairs={{0,8},{1,9},{2,10},{3,11},{4,12},{5,13},{6,14},{7,15},{8,0},{9,1},... | collective-permute-start | bytes 786440 | tf_op jit(solution)/shard_map/ppermute | solution.py:189
  83.9 29.2 %collective-permute-start.7 = (f32[64,1024]{1,0:T(8,128)S(1)}, f32[64,1024]{1,0:T(8,128)S(1)}, u32[]{:S(2)}, u32[]{:S(2)}) collective-permute-start(f32[64,1024]{1,0:T(8,128)S(1)} %get-tuple-element.48), channel_id=1, source_target_pairs={{0,12},{1,13},{2,14},{3,15},{4,8},{5,9},{6,10},{7,11},{8,4},{9,5},... | collective-permute-start | bytes 786440 | tf_op jit(solution)/shard_map/ppermute | solution.py:189
  86.6 31.1 %collective-permute-start.15 = (f32[256,1024]{1,0:T(8,128)S(1)}, f32[256,1024]{1,0:T(8,128)S(1)}, u32[]{:S(2)}, u32[]{:S(2)}) collective-permute-start(f32[256,1024]{1,0:T(8,128)S(1)} %pad_maximum_fusion.2), channel_id=1, source_target_pairs={{0,2},{1,3},{2,0},{3,1},{4,6},{5,7},{6,4},{7,5},{8,10},{9,11},{10,... | collective-permute-start | bytes 3145736 | tf_op jit(solution)/shard_map/ppermute | solution.py:189
  103.2 50.1 %collective-permute-start.3 = (f32[256,1024]{1,0:T(8,128)S(1)}, f32[256,1024]{1,0:T(8,128)S(1)}, u32[]{:S(2)}, u32[]{:S(2)}) collective-permute-start(f32[256,1024]{1,0:T(8,128)S(1)} %pad_maximum_fusion), channel_id=1, source_target_pairs={{0,2},{1,3},{2,0},{3,1},{4,6},{5,7},{6,4},{7,5},{8,10},{9,11},{10,... | collective-permute-start | bytes 3145736 | tf_op jit(solution)/shard_map/ppermute | solution.py:189
  113.3 39.8 %collective-permute-start.8 = (f32[256,1024]{1,0:T(8,128)S(1)}, f32[256,1024]{1,0:T(8,128)S(1)}, u32[]{:S(2)}, u32[]{:S(2)}) collective-permute-start(f32[256,1024]{1,0:T(8,128)S(1)} %pad_maximum_fusion.1), channel_id=1, source_target_pairs={{0,2},{1,3},{2,0},{3,1},{4,6},{5,7},{6,4},{7,5},{8,10},{9,11},{10,... | collective-permute-start | bytes 3145736 | tf_op jit(solution)/shard_map/ppermute | solution.py:189
  117.8 36.1 %copy-start.24 = (f32[512,1024]{1,0:T(8,128)}, f32[512,1024]{1,0:T(8,128)S(1)}, u32[]{:S(2)}) copy-start(f32[512,1024]{1,0:T(8,128)S(1)} %constant_dynamic-update-slice_fusion.10.field_ref.near) | copy-start | bytes 6291460
  117.8 84.1 %collective-permute-start.16 = (f32[512,1024]{1,0:T(8,128)S(1)}, f32[512,1024]{1,0:T(8,128)S(1)}, u32[]{:S(2)}, u32[]{:S(2)}) collective-permute-start(f32[512,1024]{1,0:T(8,128)S(1)} %constant_dynamic-update-slice_fusion.10.field_ref.near), channel_id=1, source_target_pairs={{0,1},{1,0},{2,3},{3,2},{4,5},{5,4},{6,7},{7,6},{8,9},{9,8},{10,11... | collective-permute-start | bytes 6291464 | tf_op jit(solution)/shard_map/ppermute | solution.py:189
  153.2 15.9 %copy-start.22 = (f32[512,1024]{1,0:T(8,128)}, f32[512,1024]{1,0:T(8,128)S(1)}, u32[]{:S(2)}) copy-start(f32[512,1024]{1,0:T(8,128)S(1)} %constant_dynamic-update-slice_fusion.5.carrier_near.field_ref.near) | copy-start | bytes 6291460
  153.2 48.7 %collective-permute-start.9 = (f32[512,1024]{1,0:T(8,128)S(1)}, f32[512,1024]{1,0:T(8,128)S(1)}, u32[]{:S(2)}, u32[]{:S(2)}) collective-permute-start(f32[512,1024]{1,0:T(8,128)S(1)} %constant_dynamic-update-slice_fusion.5.carrier_near.field_ref.near), channel_id=1, source_target_pairs={{0,1},{1,0},{2,3},{3,2},{4,5},{5,4},{6,7},{7,6},{8,9},{9,8},{10,11... | collective-permute-start | bytes 6291464 | tf_op jit(solution)/shard_map/ppermute | solution.py:189
  153.4 83.4 %collective-permute-start.4 = (f32[512,1024]{1,0:T(8,128)S(1)}, f32[512,1024]{1,0:T(8,128)}, u32[]{:S(2)}, u32[]{:S(2)}) collective-permute-start(f32[512,1024]{1,0:T(8,128)S(1)} %constant_dynamic-update-slice_fusion.carrier_ref.field_ref.near), channel_id=1, source_target_pairs={{0,1},{1,0},{2,3},{3,2},{4,5},{5,4},{6,7},{7,6},{8,9},{9,8},{10,11... | collective-permute-start | bytes 6291464 | tf_op jit(solution)/shard_map/ppermute | solution.py:189
  220.8 92.6 %collective-permute-start.23 = (f32[512,1024]{1,0:T(8,128)}, f32[512,1024]{1,0:T(8,128)}, u32[]{:S(2)}, u32[]{:S(2)}) collective-permute-start(f32[512,1024]{1,0:T(8,128)} %get-tuple-element.25.near), channel_id=1, source_target_pairs={{0,1},{1,0},{2,3},{3,2},{4,5},{5,4},{6,7},{7,6},{8,9},{9,8},{10,11... | collective-permute-start | bytes 6291464 | tf_op jit(solution)/shard_map/ppermute | solution.py:189
  236.7 65.7 %copy-start = (f32[512,1024]{1,0:T(8,128)}, f32[512,1024]{1,0:T(8,128)S(1)}, u32[]{:S(2)}) copy-start(f32[512,1024]{1,0:T(8,128)S(1)} %get-tuple-element.19.carrier_near.near) | copy-start | bytes 6291460
  236.7 76.7 %collective-permute-start.11 = (f32[512,1024]{1,0:T(8,128)S(1)}, f32[512,1024]{1,0:T(8,128)}, u32[]{:S(2)}, u32[]{:S(2)}) collective-permute-start(f32[512,1024]{1,0:T(8,128)S(1)} %get-tuple-element.19.carrier_near.near), channel_id=1, source_target_pairs={{0,1},{1,0},{2,3},{3,2},{4,5},{5,4},{6,7},{7,6},{8,9},{9,8},{10,11... | collective-permute-start | bytes 6291464 | tf_op jit(solution)/shard_map/ppermute | solution.py:189
  256.0 75.8 %collective-permute-start.10 = (f32[512,1024]{1,0:T(8,128)}, f32[512,1024]{1,0:T(8,128)}, u32[]{:S(2)}, u32[]{:S(2)}) collective-permute-start(f32[512,1024]{1,0:T(8,128)} %get-tuple-element.18.near), channel_id=1, source_target_pairs={{0,1},{1,0},{2,3},{3,2},{4,5},{5,4},{6,7},{7,6},{8,9},{9,8},{10,11... | collective-permute-start | bytes 6291464 | tf_op jit(solution)/shard_map/ppermute | solution.py:189
  278.5 25.7 %copy-start.3 = (f32[256,1024]{1,0:T(8,128)S(1)}, f32[256,1024]{1,0:T(8,128)}, u32[]{:S(2)}) copy-start(f32[256,1024]{1,0:T(8,128)} %slice.71.carrier_ref.field_ref) | copy-start | bytes 3145732
  342.7 16.1 %collective-permute-start.17 = (f32[64,1024]{1,0:T(8,128)S(1)}, f32[64,1024]{1,0:T(8,128)S(1)}, u32[]{:S(2)}, u32[]{:S(2)}) collective-permute-start(f32[64,1024]{1,0:T(8,128)S(1)} %get-tuple-element.44), channel_id=1, source_target_pairs={{0,4},{1,5},{2,6},{3,7},{4,0},{5,1},{6,2},{7,3},{8,12},{9,13},{10,... | collective-permute-start | bytes 786440 | tf_op jit(solution)/shard_map/ppermute | solution.py:189
  345.2 27.7 %collective-permute-start.18 = (f32[64,1024]{1,0:T(8,128)S(1)}, f32[64,1024]{1,0:T(8,128)S(1)}, u32[]{:S(2)}, u32[]{:S(2)}) collective-permute-start(f32[64,1024]{1,0:T(8,128)S(1)} %get-tuple-element.43), channel_id=1, source_target_pairs={{0,8},{1,9},{2,10},{3,11},{4,12},{5,13},{6,14},{7,15},{8,0},{9,1},... | collective-permute-start | bytes 786440 | tf_op jit(solution)/shard_map/ppermute | solution.py:189
  353.8 35.9 %collective-permute-start.19 = (f32[64,1024]{1,0:T(8,128)S(1)}, f32[64,1024]{1,0:T(8,128)S(1)}, u32[]{:S(2)}, u32[]{:S(2)}) collective-permute-start(f32[64,1024]{1,0:T(8,128)S(1)} %get-tuple-element.42), channel_id=1, source_target_pairs={{0,12},{1,13},{2,14},{3,15},{4,8},{5,9},{6,10},{7,11},{8,4},{9,5},... | collective-permute-start | bytes 786440 | tf_op jit(solution)/shard_map/ppermute | solution.py:189
  354.4 35.4 %collective-permute-start.20 = (f32[64,1024]{1,0:T(8,128)S(1)}, f32[64,1024]{1,0:T(8,128)S(1)}, u32[]{:S(2)}, u32[]{:S(2)}) collective-permute-start(f32[64,1024]{1,0:T(8,128)S(1)} %get-tuple-element.41), channel_id=1, source_target_pairs={{0,4},{1,5},{2,6},{3,7},{4,0},{5,1},{6,2},{7,3},{8,12},{9,13},{10,... | collective-permute-start | bytes 786440 | tf_op jit(solution)/shard_map/ppermute | solution.py:189
  356.4 46.4 %collective-permute-start.21 = (f32[64,1024]{1,0:T(8,128)S(1)}, f32[64,1024]{1,0:T(8,128)S(1)}, u32[]{:S(2)}, u32[]{:S(2)}) collective-permute-start(f32[64,1024]{1,0:T(8,128)S(1)} %get-tuple-element.40), channel_id=1, source_target_pairs={{0,8},{1,9},{2,10},{3,11},{4,12},{5,13},{6,14},{7,15},{8,0},{9,1},... | collective-permute-start | bytes 786440 | tf_op jit(solution)/shard_map/ppermute | solution.py:189
  358.8 52.1 %collective-permute-start.22 = (f32[64,1024]{1,0:T(8,128)S(1)}, f32[64,1024]{1,0:T(8,128)S(1)}, u32[]{:S(2)}, u32[]{:S(2)}) collective-permute-start(f32[64,1024]{1,0:T(8,128)S(1)} %get-tuple-element.39), channel_id=1, source_target_pairs={{0,12},{1,13},{2,14},{3,15},{4,8},{5,9},{6,10},{7,11},{8,4},{9,5},... | collective-permute-start | bytes 786440 | tf_op jit(solution)/shard_map/ppermute | solution.py:189
  373.0 37.9 %collective-permute-start.24 = (f32[64,1024]{1,0:T(8,128)S(1)}, f32[64,1024]{1,0:T(8,128)S(1)}, u32[]{:S(2)}, u32[]{:S(2)}) collective-permute-start(f32[64,1024]{1,0:T(8,128)S(1)} %get-tuple-element.38), channel_id=1, source_target_pairs={{0,4},{1,5},{2,6},{3,7},{4,0},{5,1},{6,2},{7,3},{8,12},{9,13},{10,... | collective-permute-start | bytes 786440 | tf_op jit(solution)/shard_map/ppermute | solution.py:189
  389.7 24.3 %collective-permute-start.25 = (f32[64,1024]{1,0:T(8,128)S(1)}, f32[64,1024]{1,0:T(8,128)S(1)}, u32[]{:S(2)}, u32[]{:S(2)}) collective-permute-start(f32[64,1024]{1,0:T(8,128)S(1)} %get-tuple-element.37), channel_id=1, source_target_pairs={{0,8},{1,9},{2,10},{3,11},{4,12},{5,13},{6,14},{7,15},{8,0},{9,1},... | collective-permute-start | bytes 786440 | tf_op jit(solution)/shard_map/ppermute | solution.py:189
  389.7 29.5 %collective-permute-start.26 = (f32[64,1024]{1,0:T(8,128)S(1)}, f32[64,1024]{1,0:T(8,128)S(1)}, u32[]{:S(2)}, u32[]{:S(2)}) collective-permute-start(f32[64,1024]{1,0:T(8,128)S(1)} %get-tuple-element.36), channel_id=1, source_target_pairs={{0,12},{1,13},{2,14},{3,15},{4,8},{5,9},{6,10},{7,11},{8,4},{9,5},... | collective-permute-start | bytes 786440 | tf_op jit(solution)/shard_map/ppermute | solution.py:189
  (22 other events, 62.1 us)

commit v2 on v1

--- a/solution.py
+++ b/solution.py
@@ -103,8 +103,8 @@
     out_ref[...] = carrier_ref[:, columns] * slope + rest
 
 
-def along_x(carrier, field, matrix, name):
-    rows, length = field.shape
+def along_x(carrier, field, matrix, rows, name):
+    length = field.shape[1]
     tile = min(256, length)
     whole = pl.BlockSpec((rows, length), lambda n: (0, 0))
     return pl.pallas_call(
@@ -116,16 +116,20 @@
         scratch_shapes=[pltpu.VMEM((4 * rows, length), BF16)],
         compiler_params=params(),
         cost_estimate=pl.CostEstimate(
-            flops=18 * rows * length * length, bytes_accessed=8 * length * length + 12 * rows * length, transcendentals=0
+            flops=2 * rows * length * length, bytes_accessed=4 * rows * length, transcendentals=0
         ),
         name=name,
     )(carrier, field, matrix)
 
 
-def y_products(matrix_ref, near_ref, far_ref, carrier_near_ref, carrier_far_ref):
+def joined(refs):
+    return jnp.concatenate([ref[...] for ref in refs], axis=0)
+
+
+def y_products(matrix_ref, fields, carriers):
     rows, length = matrix_ref.shape[1:]
-    field = jnp.concatenate([near_ref[...], far_ref[...]], axis=0)
-    carrier = jnp.concatenate([carrier_near_ref[...], carrier_far_ref[...]], axis=0)
+    field = joined(fields)
+    carrier = joined(carriers) if carriers else field
     field_high, field_low = halves(field)
     flux_high, flux_low = halves(field * carrier)
     matrix = matrix_ref[...].reshape(4 * rows, length)
@@ -135,46 +139,62 @@
     d = product(matrix[rows:2 * rows], flux_low)
     slope = a[0:rows] + a[rows:2 * rows] + b[0:rows]
     rest = a[2 * rows:3 * rows] + a[3 * rows:] + b[rows:] + c[0:rows] + c[rows:] + d
-    return carrier[0:rows] * slope + rest
-
-
-def first_kernel(forcing_ref, matrix_ref, near, far, carrier_near, carrier_far, x_ref, middle_ref, base_ref, square_ref):
+    return field[0:rows], carrier[0:rows] * slope + rest
+
+
+def first_kernel(counts, forcing_ref, matrix_ref, *refs):
+    fields, carriers, x_terms, (middle_ref, base_ref, square_ref) = cut(refs, counts)
     rows = matrix_ref.shape[1]
     kept = base_ref.shape[0]
-    terms = x_ref[...] + y_products(matrix_ref, near, far, carrier_near, carrier_far)
-    field = near[0:rows, :]
-    first = terms + forcing_ref[0, 0] * field
+    field, terms = y_products(matrix_ref, fields, carriers)
+    first = terms + joined(x_terms) + forcing_ref[0, 0] * field
     middle = field + (time_step * first_weight) * first
     middle_ref[...] = middle
     base_ref[...] = middle[0:kept] - (time_step * back_weight) * first[0:kept]
     square_ref[...] = jnp.sum((middle * middle).reshape(rows // 8, 8, middle.shape[1]), axis=0)
 
 
-def second_kernel(matrix_ref, near, far, carrier_near, carrier_far, x_ref, base_ref, out_ref):
-    terms = x_ref[...] + y_products(matrix_ref, near, far, carrier_near, carrier_far)
-    out_ref[...] = base_ref[...] + (time_step * second_weight) * terms
-
-
-def y_call(kernel, rows, matrix, fields, rest, out_rows, scalars, name):
-    half, length = fields[0].shape
+def second_kernel(counts, forcing_ref, matrix_ref, *refs):
+    fields, carriers, x_terms, (base_ref, *out_refs) = cut(refs, counts)
+    field, terms = y_products(matrix_ref, fields, carriers)
+    second = terms + joined(x_terms) + forcing_ref[0, 0] * field
+    out = base_ref[...] + (time_step * second_weight) * second
+    size = out_refs[0].shape[0]
+    for place, out_ref in enumerate(out_refs):
+        out_ref[...] = out[place * size:(place + 1) * size]
+
+
+def cut(refs, counts):
+    pieces, start = [], 0
+    for count in counts:
+        pieces.append(refs[start:start + count])
+        start += count
+    return *pieces, refs[start:]
+
+
+def y_call(kernel, rows, matrix, fields, carriers, x_terms, rest, out_rows, scalars, name):
+    length = fields[0].shape[1]
     tile = min(256, length)
     columns = lambda count: pl.BlockSpec((count, tile), lambda n: (0, n))
+    arrays = fields + carriers + x_terms + rest
     return pl.pallas_call(
-        kernel,
+        functools.partial(kernel, (len(fields), len(carriers), len(x_terms))),
         grid=(length // tile,),
         in_specs=[pl.BlockSpec(memory_space=pltpu.SMEM)] * len(scalars)
         + [pl.BlockSpec((4, rows, length), lambda n: (0, 0, 0))]
-        + [columns(x.shape[0]) for x in fields + rest],
+        + [columns(x.shape[0]) for x in arrays],
         out_specs=[columns(count) for count in out_rows],
         out_shape=[jax.ShapeDtypeStruct((count, length), F32) for count in out_rows],
         compiler_params=params(),
         cost_estimate=pl.CostEstimate(
-            flops=18 * rows * length * length,
-            bytes_accessed=8 * rows * length + 16 * length * length + 12 * rows * length,
-            transcendentals=0,
+            flops=2 * rows * length * length, bytes_accessed=4 * rows * length, transcendentals=0
         ),
         name=name,
-    )(*scalars, matrix, *fields, *rest)
+    )(*scalars, matrix, *arrays)
+
+
+def after(values, *earlier):
+    return lax.optimization_barrier((values, earlier))[0]
 
 
 def on_device(velocity, slope_matrix, curve_matrix):
@@ -182,6 +202,7 @@
     devices = lax.axis_size("row")
     group = devices // planes
     chips = group // 2
+    half, kept = length // 2, length // group
     place = lax.axis_index("row")
     plane, member = place // group, place % group
 
@@ -193,50 +214,92 @@
         chip, far = rest // planes, rest % planes
         return (plane ^ far) * group + (member ^ (2 * chip + core))
 
+    def exchanged_sum(x, distances, works=()):
+        for step, distance in enumerate(distances):
+            arrived = swap(x, distance)
+            x = x + (after(arrived, works[min(step, len(works) - 1)]) if works else arrived)
+        return jnp.sum(x)
+
+    def doubling(start, stop):
+        distances = []
+        while start < stop:
+            distances.append(start)
+            start *= 2
+        return distances
+
     order = jnp.stack([order_of(index) for index in range(devices)]).astype(jnp.int32)
     cells = 3 * planes * size * devices * length
-
-    own = [[lax.dynamic_index_in_dim(velocity[i], plane ^ d, axis=0, keepdims=False) for d in range(planes)] for i in range(3)]
-    near, far = [], []
-    for i in range(3):
-        mine = jnp.concatenate([own[i][0]] + [swap(own[i][d], d * group) for d in range(1, planes)], axis=0)
-        others = [swap(mine, 2 * h) for h in range(1, chips)]
-        near.append(jnp.concatenate([mine] + others, axis=0))
-        far.append(swap(near[i], 1))
-
     along_x_matrix, along_y_matrix = prepare_matrices(order, slope_matrix, curve_matrix, size)
-    total = lax.psum(jnp.sum(velocity * velocity), "row")
+
+    def blocks(i):
+        return [lax.dynamic_index_in_dim(velocity[i], plane ^ d, axis=0, keepdims=False) for d in range(planes)]
+
+    def send(own):
+        return [own[0]] + [swap(block, d * group) for d, block in enumerate(own) if d]
+
+    def x_first(i, pieces, name):
+        return [along_x(near[0][p], near[i][p], along_x_matrix, kept, f"{name}_{p}") for p in pieces]
+
+    rest = list(range(1, chips))
+    near, far = [None] * 3, [None] * 3
+    arriving = [send(blocks(0)), send(blocks(1)), None]
+    squares = jnp.sum((velocity * velocity).reshape(-1, 8, length // 128, 128), axis=(0, 2))
+
+    def pass_on(i):
+        mine = jnp.concatenate(arriving[i], axis=0)
+        near[i] = [mine] + [swap(mine, 2 * h) for h in rest]
+
+    def pass_across(i):
+        far[i] = [swap(piece, 1) for piece in near[i]]
+
+    arriving[0] = after(arriving[0], along_x_matrix, along_y_matrix)
+    pass_on(0)
+    x_terms = [x_first(0, [0], "x_first_0"), None, None]
+    arriving[1] = after(arriving[1], x_terms[0])
+    arriving[2] = send(after(blocks(2), x_terms[0]))
+    pass_on(1)
+    pass_across(0)
+    x_terms[1] = x_first(1, [0], "x_first_1")
+    x_terms[0] += x_first(0, rest, "x_first_0")
+    arriving[2] = after(arriving[2], x_terms[0], x_terms[1])
+    pass_on(2)
+    pass_across(1)
+    pass_across(2)
+    x_terms[1] += x_first(1, rest, "x_first_1")
+    total = exchanged_sum(
+        squares, doubling(1, devices), [along_x_matrix, x_terms[0][0], x_terms[1][0], x_terms[0][-1]]
+    )
     forcing = (power_input / (total / cells)).reshape(1, 1)
 
-    half, kept = length // 2, length // group
-    middle_near, middle_far, base, squares = [], [], [], 0.0
-    for i in range(3):
-        x_terms = along_x(near[0], near[i], along_x_matrix, f"x_first_{i}")
-        middle, back, square = y_call(
-            first_kernel, half, along_y_matrix, [near[i], far[i], near[1], far[1]], [x_terms],
+    def first_step(i):
+        return y_call(
+            first_kernel, half, along_y_matrix, near[i] + far[i], near[1] + far[1] if i != 1 else [], x_terms[i], [],
             [half, kept, 8], [forcing], f"y_first_{i}",
         )
-        middle_near.append(middle)
-        middle_far.append(swap(middle, 1))
-        base.append(back)
-        squares = squares + jnp.sum(square)
-    total = lax.psum(squares, "row") / chips
-    forcing = power_input / (total / cells)
-
-    ends = []
+
+    middle_near, middle_far, base, square = [None] * 3, [None] * 3, [None] * 3, [None] * 3
+    for i in (0, 1):
+        middle_near[i], base[i], square[i] = first_step(i)
+        middle_far[i] = swap(middle_near[i], 1)
+    x_terms[2] = x_first(2, [0] + rest, "x_first_2")
+    far[2] = after(far[2], middle_near[0], middle_near[1], x_terms[2])
+    middle_near[2], base[2], square[2] = first_step(2)
+    middle_far[2] = swap(middle_near[2], 1)
+    squares = jnp.sum((square[0] + square[1] + square[2]).reshape(8, length // 128, 128), axis=1)
+    total = exchanged_sum(squares, [1] + doubling(group, devices))
+    forcing = (power_input / (total / cells)).reshape(1, 1)
+
+    out = jnp.zeros(velocity.shape, F32)
+    previous = square[2]
     for i in range(3):
-        x_terms = along_x(middle_near[0][:kept], middle_near[i][:kept], along_x_matrix, f"x_second_{i}")
-        (end,) = y_call(
-            second_kernel, kept, along_y_matrix, [middle_near[i], middle_far[i], middle_near[1], middle_far[1]],
-            [x_terms, base[i]], [kept], [], f"y_second_{i}",
+        carrier, field = after((middle_near[0], middle_near[i]), previous)
+        x_second = along_x(carrier, field, along_x_matrix, kept, f"x_second_{i}")
+        ends = y_call(
+            second_kernel, kept, along_y_matrix, [middle_near[i], middle_far[i]],
+            [middle_near[1], middle_far[1]] if i != 1 else [], [x_second], [base[i]], [size] * planes, [forcing], f"y_second_{i}",
         )
-        ends.append(end)
-
-    out = jnp.zeros(velocity.shape, F32)
-    for i in range(3):
-        final = ends[i] + (time_step * second_weight) * forcing * middle_near[i][:kept]
-        for d in range(planes):
-            block = final[d * size:(d + 1) * size]
+        previous = ends
+        for d, block in enumerate(ends):
             block = swap(block, d * group) if d else block
             out = lax.dynamic_update_slice(out, block[None, None], (i, plane ^ d, 0, 0))
     return out

time: 422 us -> 323 us (0.77)
  blocking collectives: 70.5 us -> 0 us
  waiting for transfers between devices: 109 us -> 88.5 us
  starting transfers between devices: 41.1 us -> 32.8 us
  other arithmetic: 8.74 us -> 14.4 us
    psum x2 -> x0, blocking collectives: 70.5 us -> none  [the longest x1 46.6 us: on_device(): total = lax.psum(jnp.sum(velocity * velocity), 'row')]
    ppermute x27 -> x37, waiting for transfers between devices: 109 us -> 88.5 us  [swap(): return lax.ppermute(x, 'row', [(r, r ^ distance) for r in range(devices)])]
    dynamic_update_slice x12 -> x11, local copies, waits for them, and re-layouts: 0.97 us -> 11.7 us  [on_device(): out = lax.dynamic_update_slice(out, block[None, None], (i, plane ^ d, 0, 0))]
    pallas_call x6 -> x5, Pallas kernels: 70.2 us -> 60.8 us  [y_call(): pl.pallas_call(functools.partial(kernel, (len(fields), len(carriers), len...]
    ppermute x27 -> x37, starting transfers between devices: 41.1 us -> 32.8 us  [swap(): return lax.ppermute(x, 'row', [(r, r ^ distance) for r in range(devices)])]
    pallas_call x0 -> x1, other arithmetic: none -> 7.83 us  [y_call(): pl.pallas_call(functools.partial(kernel, (len(fields), len(carriers), len...]
    pallas_call x6 -> x9, Pallas kernels: 66.7 us -> 72.6 us  [along_x(): pl.pallas_call(along_x_kernel, grid=(length // tile,), in_specs=[whole, w...]
    slice x7 -> x1, local copies, waits for them, and re-layouts: 8.88 us -> 3.11 us  [blocks(): velocity[i]]
  transfers between devices with their start and end apart: 27 -> 37, of which waited for: 10 -> 11; matrix products, arithmetic and copies ran while one was open for 5% -> 9% of each run, Pallas kernels for 34% -> 46%
where the time goes in v2:
time: 323 us; the launch traced here: 321 us
  Pallas kernels  148 us (46%)
  waiting for transfers between devices  88.5 us (27%)
  local copies, waits for them, and re-layouts  35.5 us (11%)
  starting transfers between devices  32.8 us (10%)
  other arithmetic  14.4 us (4%)
    ppermute x37, waiting for transfers between devices, swap(): return lax.ppermute(x, 'row', [(r, r ^ distance) for r in range(devices)])  88.5 us
    pallas_call x9, Pallas kernels, along_x(): pl.pallas_call(along_x_kernel, grid=(length // tile,), in_specs=[whole, w...  72.6 us
    pallas_call x5, Pallas kernels, y_call(): pl.pallas_call(functools.partial(kernel, (len(fields), len(carriers), len...  60.8 us
    ppermute x37, starting transfers between devices, swap(): return lax.ppermute(x, 'row', [(r, r ^ distance) for r in range(devices)])  32.8 us
    unnamed x53, local copies, waits for them, and re-layouts  15.6 us
    pallas_call x1, Pallas kernels, prepare_matrices(): pl.pallas_call(functools.partial(matrices_kernel, count), grid_spec=pltpu...  14.9 us
    dynamic_update_slice x11, local copies, waits for them, and re-layouts, on_device(): out = lax.dynamic_update_slice(out, block[None, None], (i, plane ^ d, 0, 0))  11.7 us
    pallas_call x1, other arithmetic, y_call(): pl.pallas_call(functools.partial(kernel, (len(fields), len(carriers), len...  7.83 us
  transfers between devices with their start and end apart: 37, of which 11 were waited for; matrix products, arithmetic and copies ran while one was open for 9% of the time, Pallas kernels for 46%

profile of v2, /device:TPU:18, one launch (start us, length us, event | category | flops | bytes accessed | tf_op | source)
XLA Modules:
  0.0 321.3 jit_solution(6909263713867389559)
XLA Ops:
  0.0 3.1 fusion.5
  6.9 2.5 collective-permute-start.6
  9.5 14.9 %shard_map.37 = (bf16[4,1024,1024]{2,1,0:T(8,128)(2,1)}, bf16[4,512,1024]{2,1,0:T(8,128)(2,1)}) custom-call(s32[16]{0:T(128)S(1)} %stack.67.order_ref, f32[1024,1024]{1,0:T(8,128)} %refs_4_.1, f32[1024,1024]{1,0:T(8,128)} %refs_4_.1, f32[1024,1024]{1,0:T(8,128)} %refs_5_.1, f32[1024,1024]{1,0:T(8,128)} %refs_5_.1, f32[1024,1024]{1,0:T(8,128)} %refs_4_.1, ...), custom_call_target="tpu_custom_call" | custom-call | tf_op jit(solution)/shard_map/pallas_call | solution.py:62
  24.4 2.2 collective-permute-start.8
  26.6 15.6 %collective-permute-done.4 = f32[64,1024]{1,0:T(8,128)} collective-permute-done((f32[64,1024]{1,0:T(8,128)S(1)}, f32[64,1024]{1,0:T(8,128)}, u32[]{:S(2)}, u32[]{:S(2)}) %collective-permute-start.4) | collective-permute-done | bytes 262176 | tf_op jit(solution)/shard_map/ppermute | solution.py:210
  45.2 7.9 %x_first_0_0.1.refs_8_ = f32[256,1024]{1,0:T(8,128)S(1)} custom-call(f32[256,1024]{1,0:T(8,128)S(1)} %constant_dynamic-update-slice_fusion.carrier_ref.field_ref.refs_0_, f32[256,1024]{1,0:T(8,128)S(1)} %constant_dynamic-update-slice_fusion.carrier_ref.field_ref.refs_0_, bf16[4,1024,1024]{2,1,0:T(8,128)(2,1)} %get-tuple-element.56.matrix_ref), custom_call_target="tpu_custom_call" | custom-call | flops 536870912 | bytes 1048576 | tf_op jit(solution)/shard_map/x_first_0_0/pallas_call | solution.py:110
  59.6 2.6 mul.10
  62.2 2.7 reduce_sum.36
  67.7 31.7 %collective-permute-done.1 = f32[8,128]{1,0:T(8,128)S(1)} collective-permute-done((f32[8,128]{1,0:T(8,128)S(1)}, f32[8,128]{1,0:T(8,128)S(1)}, u32[]{:S(2)}, u32[]{:S(2)}) %collective-permute-start.1) | collective-permute-done | bytes 4128 | tf_op jit(solution)/shard_map/ppermute | solution.py:210
  99.4 3.6 %collective-permute-done.5 = f32[8,128]{1,0:T(8,128)S(1)} collective-permute-done((f32[8,128]{1,0:T(8,128)S(1)}, f32[8,128]{1,0:T(8,128)S(1)}, u32[]{:S(2)}, u32[]{:S(2)}) %collective-permute-start.5) | collective-permute-done | bytes 4128 | tf_op jit(solution)/shard_map/ppermute | solution.py:210
  104.5 7.8 %x_first_1_0.1.refs_4_ = f32[256,1024]{1,0:T(8,128)S(1)} custom-call(f32[256,1024]{1,0:T(8,128)S(1)} %constant_dynamic-update-slice_fusion.carrier_ref.field_ref.refs_0_, f32[256,1024]{1,0:T(8,128)S(1)} %constant_dynamic-update-slice_fusion.4.field_ref.refs_4_.refs_0_, bf16[4,1024,1024]{2,1,0:T(8,128)(2,1)} %get-tuple-element.56.matrix_ref), custom_call_target="tpu_custom_call" | custom-call | flops 536870912 | bytes 1048576 | tf_op jit(solution)/shard_map/x_first_1_0/pallas_call | solution.py:110
  113.3 7.8 %x_first_0_1.1.refs_9_ = f32[256,1024]{1,0:T(8,128)S(1)} custom-call(f32[256,1024]{1,0:T(8,128)S(1)} %collective-permute-done.10.carrier_ref.field_ref.refs_1_, f32[256,1024]{1,0:T(8,128)S(1)} %collective-permute-done.10.carrier_ref.field_ref.refs_1_, bf16[4,1024,1024]{2,1,0:T(8,128)(2,1)} %get-tuple-element.56.matrix_ref), custom_call_target="tpu_custom_call" | custom-call | flops 536870912 | bytes 1048576 | tf_op jit(solution)/shard_map/x_first_0_1/pallas_call | solution.py:110
  131.6 8.1 %x_first_1_1.1.refs_5_ = f32[256,1024]{1,0:T(8,128)S(1)} custom-call(f32[256,1024]{1,0:T(8,128)S(1)} %collective-permute-done.10.carrier_ref.field_ref.refs_1_, f32[256,1024]{1,0:T(8,128)} %collective-permute-done.13.refs_5_.field_ref.refs_1_, bf16[4,1024,1024]{2,1,0:T(8,128)(2,1)} %get-tuple-element.56.matrix_ref), custom_call_target="tpu_custom_call" | custom-call | flops 536870912 | bytes 1048576 | tf_op jit(solution)/shard_map/x_first_1_1/pallas_call | solution.py:110
  140.7 14.4 %y_first_1.1 = (f32[512,1024]{1,0:T(8,128)}, f32[256,1024]{1,0:T(8,128)S(1)}, f32[8,1024]{1,0:T(8,128)S(1)}) custom-call(f32[1,1]{1,0:T(1,128)} %bitcast.25.forcing_ref, bf16[4,512,1024]{2,1,0:T(8,128)(2,1)} %get-tuple-element.58.matrix_ref, f32[256,1024]{1,0:T(8,128)S(1)} %constant_dynamic-update-slice_fusion.4.field_ref.refs_4_.refs_0_, ...), custom_call_target="tpu_custom_call" | custom-call | flops 1073741824 | bytes 2097152 | tf_op jit(solution)/shard_map/y_first_1/pallas_call | solution.py:180
  155.1 15.0 %y_first_0.1 = (f32[512,1024]{1,0:T(8,128)}, f32[256,1024]{1,0:T(8,128)S(1)}, f32[8,1024]{1,0:T(8,128)S(1)}) custom-call(f32[1,1]{1,0:T(1,128)} %bitcast.25.forcing_ref, bf16[4,512,1024]{2,1,0:T(8,128)(2,1)} %get-tuple-element.58.matrix_ref, f32[256,1024]{1,0:T(8,128)S(1)} %constant_dynamic-update-slice_fusion.carrier_ref.field_ref.refs_0_, ...), custom_call_target="tpu_custom_call" | custom-call | flops 1073741824 | bytes 2097152 | tf_op jit(solution)/shard_map/y_first_0/pallas_call | solution.py:180
  172.0 8.1 %x_first_2_0.1.refs_8_ = f32[256,1024]{1,0:T(8,128)S(1)} custom-call(f32[256,1024]{1,0:T(8,128)S(1)} %constant_dynamic-update-slice_fusion.carrier_ref.field_ref.refs_0_, f32[256,1024]{1,0:T(8,128)} %constant_dynamic-update-slice_fusion.8.field_ref.refs_0_, bf16[4,1024,1024]{2,1,0:T(8,128)(2,1)} %get-tuple-element.56.matrix_ref), custom_call_target="tpu_custom_call" | custom-call | flops 536870912 | bytes 1048576 | tf_op jit(solution)/shard_map/x_first_2_0/pallas_call | solution.py:110
  180.1 8.5 %x_first_2_1.1.refs_9_ = f32[256,1024]{1,0:T(8,128)S(1)} custom-call(f32[256,1024]{1,0:T(8,128)S(1)} %collective-permute-done.10.carrier_ref.field_ref.refs_1_, f32[256,1024]{1,0:T(8,128)} %collective-permute-done.19.field_ref.refs_1_, bf16[4,1024,1024]{2,1,0:T(8,128)(2,1)} %get-tuple-element.56.matrix_ref), custom_call_target="tpu_custom_call" | custom-call | flops 536870912 | bytes 1048576 | tf_op jit(solution)/shard_map/x_first_2_1/pallas_call | solution.py:110
  191.7 15.3 %y_first_2.1 = (f32[512,1024]{1,0:T(8,128)}, f32[256,1024]{1,0:T(8,128)S(1)}, f32[8,1024]{1,0:T(8,128)S(1)}) custom-call(f32[1,1]{1,0:T(1,128)} %bitcast.25.forcing_ref, bf16[4,512,1024]{2,1,0:T(8,128)(2,1)} %get-tuple-element.58.matrix_ref, f32[256,1024]{1,0:T(8,128)} %constant_dynamic-update-slice_fusion.8.field_ref.refs_0_, ...), custom_call_target="tpu_custom_call" | custom-call | flops 1073741824 | bytes 2097152 | tf_op jit(solution)/shard_map/y_first_2/pallas_call | solution.py:180
  209.3 2.5 collective-permute-done.23
  212.8 7.8 %x_second_0.1.refs_4_ = f32[256,1024]{1,0:T(8,128)S(1)} custom-call(f32[512,1024]{1,0:T(8,128)S(1)} %copy-done, f32[512,1024]{1,0:T(8,128)S(1)} %copy-done, bf16[4,1024,1024]{2,1,0:T(8,128)(2,1)} %get-tuple-element.56.matrix_ref), custom_call_target="tpu_custom_call" | custom-call | flops 536870912 | bytes 1048576 | tf_op jit(solution)/shard_map/x_second_0/pallas_call | solution.py:110
  223.3 8.3 %y_second_0.1 = (f32[64,1024]{1,0:T(8,128)S(1)}, f32[64,1024]{1,0:T(8,128)S(1)}, f32[64,1024]{1,0:T(8,128)S(1)}, f32[64,1024]{1,0:T(8,128)S(1)}) custom-call(f32[1,1]{1,0:T(1,128)} %bitcast.31.forcing_ref, bf16[4,512,1024]{2,1,0:T(8,128)(2,1)} %get-tuple-element.58.matrix_ref, f32[512,1024]{1,0:T(8,128)} %get-tuple-element.100.carrier_ref.field_ref.refs_0_, ...), custom_call_target="tpu_custom_call" | custom-call | flops 536870912 | bytes 1048576 | tf_op jit(solution)/shard_map/y_second_0/pallas_call | solution.py:180
  232.6 2.1 collective-permute-start.28
  235.2 8.2 %x_second_1.1.refs_2_ = f32[256,1024]{1,0:T(8,128)S(1)} custom-call(f32[512,1024]{1,0:T(8,128)S(1)} %copy-done.1, f32[512,1024]{1,0:T(8,128)} %get-tuple-element.93.refs_2_.field_ref.refs_0_, bf16[4,1024,1024]{2,1,0:T(8,128)(2,1)} %get-tuple-element.56.matrix_ref), custom_call_target="tpu_custom_call" | custom-call | flops 536870912 | bytes 1048576 | tf_op jit(solution)/shard_map/x_second_1/pallas_call | solution.py:110
  243.4 7.9 %y_second_1.1 = (f32[64,1024]{1,0:T(8,128)S(1)}, f32[64,1024]{1,0:T(8,128)S(1)}, f32[64,1024]{1,0:T(8,128)S(1)}, f32[64,1024]{1,0:T(8,128)S(1)}) custom-call(f32[1,1]{1,0:T(1,128)} %bitcast.31.forcing_ref, bf16[4,512,1024]{2,1,0:T(8,128)(2,1)} %get-tuple-element.58.matrix_ref, f32[512,1024]{1,0:T(8,128)} %get-tuple-element.93.refs_2_.field_ref.refs_0_, ...), custom_call_target="tpu_custom_call" | custom-call | flops 536870912 | bytes 1048576 | tf_op jit(solution)/shard_map/y_second_1/pallas_call | solution.py:180
  255.9 8.3 %x_second_2.1 = f32[256,1024]{1,0:T(8,128)S(1)} custom-call(f32[512,1024]{1,0:T(8,128)S(1)} %copy-done.1, f32[512,1024]{1,0:T(8,128)} %get-tuple-element.101.field_ref, bf16[4,1024,1024]{2,1,0:T(8,128)(2,1)} %get-tuple-element.56.matrix_ref), custom_call_target="tpu_custom_call" | custom-call | flops 536870912 | bytes 1048576 | tf_op jit(solution)/shard_map/x_second_2/pallas_call | solution.py:110
  273.5 8.0 %collective-permute-done.31 = f32[64,1024]{1,0:T(8,128)S(1)} collective-permute-done((f32[64,1024]{1,0:T(8,128)S(1)}, f32[64,1024]{1,0:T(8,128)S(1)}, u32[]{:S(2)}, u32[]{:S(2)}) %collective-permute-start.31) | collective-permute-done | bytes 262176 | tf_op jit(solution)/shard_map/ppermute | solution.py:210
  282.2 4.6 %collective-permute-done.32 = f32[64,1024]{1,0:T(8,128)S(1)} collective-permute-done((f32[64,1024]{1,0:T(8,128)S(1)}, f32[64,1024]{1,0:T(8,128)S(1)}, u32[]{:S(2)}, u32[]{:S(2)}) %collective-permute-start.32) | collective-permute-done | bytes 262176 | tf_op jit(solution)/shard_map/ppermute | solution.py:210
  287.6 7.8 %y_second_2.1 = (f32[3,4,64,1024]{3,2,1,0:T(8,128)}, f32[64,1024]{1,0:T(8,128)S(1)}, f32[64,1024]{1,0:T(8,128)S(1)}, f32[64,1024]{1,0:T(8,128)S(1)}) fusion(f32[3,4,64,1024]{3,2,1,0:T(8,128)} %bitcast_dynamic-update-slice_fusion.4, s32[]{:T(128)S(6)} %select_n.46, f32[1,1]{1,0:T(1,128)} %bitcast.31.forcing_ref, bf16[4,512,1024]{2,1,0:T(8,128)(2,1)S(1)} %copy-done.15, ...), kind=kCustom, calls=%fused_computation.3 | custom fusion | flops 536870912 | bytes 15729156 | tf_op jit(solution)/shard_map/y_second_2/pallas_call | solution.py:180
  295.4 2.9 collective-permute-start.35
  298.9 5.8 %collective-permute-done.34 = f32[64,1024]{1,0:T(8,128)S(1)} collective-permute-done((f32[64,1024]{1,0:T(8,128)S(1)}, f32[64,1024]{1,0:T(8,128)S(1)}, u32[]{:S(2)}, u32[]{:S(2)}) %collective-permute-start.34) | collective-permute-done | bytes 262176 | tf_op jit(solution)/shard_map/ppermute | solution.py:210
  305.4 10.9 %collective-permute-done.35 = f32[64,1024]{1,0:T(8,128)S(1)} collective-permute-done((f32[64,1024]{1,0:T(8,128)S(1)}, f32[64,1024]{1,0:T(8,128)S(1)}, u32[]{:S(2)}, u32[]{:S(2)}) %collective-permute-start.35) | collective-permute-done | bytes 262176 | tf_op jit(solution)/shard_map/ppermute | solution.py:210
  317.0 3.6 %collective-permute-done.36 = f32[64,1024]{1,0:T(8,128)S(1)} collective-permute-done((f32[64,1024]{1,0:T(8,128)S(1)}, f32[64,1024]{1,0:T(8,128)S(1)}, u32[]{:S(2)}, u32[]{:S(2)}) %collective-permute-start.36) | collective-permute-done | bytes 262176 | tf_op jit(solution)/shard_map/ppermute | solution.py:210
  (141 shorter events, 58.9 us)
Async XLA Ops:
  3.2 21.2 %collective-permute-start.2 = (f32[64,1024]{1,0:T(8,128)S(1)}, f32[64,1024]{1,0:T(8,128)}, u32[]{:S(2)}, u32[]{:S(2)}) collective-permute-start(f32[64,1024]{1,0:T(8,128)S(1)} %get-tuple-element.128), channel_id=1, source_target_pairs={{0,4},{1,5},{2,6},{3,7},{4,0},{5,1},{6,2},{7,3},{8,12},{9,13},{10,... | collective-permute-start | bytes 786440 | tf_op jit(solution)/shard_map/ppermute | solution.py:210
  4.9 21.7 %collective-permute-start.3 = (f32[64,1024]{1,0:T(8,128)S(1)}, f32[64,1024]{1,0:T(8,128)}, u32[]{:S(2)}, u32[]{:S(2)}) collective-permute-start(f32[64,1024]{1,0:T(8,128)S(1)} %get-tuple-element.127), channel_id=1, source_target_pairs={{0,8},{1,9},{2,10},{3,11},{4,12},{5,13},{6,14},{7,15},{8,0},{9,1},... | collective-permute-start | bytes 786440 | tf_op jit(solution)/shard_map/ppermute | solution.py:210
  5.2 37.0 %collective-permute-start.4 = (f32[64,1024]{1,0:T(8,128)S(1)}, f32[64,1024]{1,0:T(8,128)}, u32[]{:S(2)}, u32[]{:S(2)}) collective-permute-start(f32[64,1024]{1,0:T(8,128)S(1)} %get-tuple-element.126), channel_id=1, source_target_pairs={{0,12},{1,13},{2,14},{3,15},{4,8},{5,9},{6,10},{7,11},{8,4},{9,5},... | collective-permute-start | bytes 786440 | tf_op jit(solution)/shard_map/ppermute | solution.py:210
  6.9 46.2 %collective-permute-start.6 = (f32[64,1024]{1,0:T(8,128)S(1)}, f32[64,1024]{1,0:T(8,128)S(1)}, u32[]{:S(2)}, u32[]{:S(2)}) collective-permute-start(f32[64,1024]{1,0:T(8,128)S(1)} %get-tuple-element.124), channel_id=1, source_target_pairs={{0,4},{1,5},{2,6},{3,7},{4,0},{5,1},{6,2},{7,3},{8,12},{9,13},{10,... | collective-permute-start | bytes 786440 | tf_op jit(solution)/shard_map/ppermute | solution.py:210
  9.4 43.7 %collective-permute-start.7 = (f32[64,1024]{1,0:T(8,128)S(1)}, f32[64,1024]{1,0:T(8,128)}, u32[]{:S(2)}, u32[]{:S(2)}) collective-permute-start(f32[64,1024]{1,0:T(8,128)S(1)} %get-tuple-element.123), channel_id=1, source_target_pairs={{0,8},{1,9},{2,10},{3,11},{4,12},{5,13},{6,14},{7,15},{8,0},{9,1},... | collective-permute-start | bytes 786440 | tf_op jit(solution)/shard_map/ppermute | solution.py:210
  24.4 28.7 %collective-permute-start.8 = (f32[64,1024]{1,0:T(8,128)S(1)}, f32[64,1024]{1,0:T(8,128)S(1)}, u32[]{:S(2)}, u32[]{:S(2)}) collective-permute-start(f32[64,1024]{1,0:T(8,128)S(1)} %get-tuple-element.122), channel_id=1, source_target_pairs={{0,12},{1,13},{2,14},{3,15},{4,8},{5,9},{6,10},{7,11},{8,4},{9,5},... | collective-permute-start | bytes 786440 | tf_op jit(solution)/shard_map/ppermute | solution.py:210
  54.7 48.3 %collective-permute-start.13 = (f32[256,1024]{1,0:T(8,128)S(1)}, f32[256,1024]{1,0:T(8,128)}, u32[]{:S(2)}, u32[]{:S(2)}) collective-permute-start(f32[256,1024]{1,0:T(8,128)S(1)} %constant_dynamic-update-slice_fusion.4.field_ref.refs_4_.refs_0_), channel_id=1, source_target_pairs={{0,2},{1,3},{2,0},{3,1},{4,6},{5,7},{6,4},{7,5},{8,10},{9,11},{10,... | collective-permute-start | bytes 3145736 | tf_op jit(solution)/shard_map/ppermute | solution.py:210
  56.2 47.3 %collective-permute-start.10 = (f32[256,1024]{1,0:T(8,128)S(1)}, f32[256,1024]{1,0:T(8,128)S(1)}, u32[]{:S(2)}, u32[]{:S(2)}) collective-permute-start(f32[256,1024]{1,0:T(8,128)S(1)} %constant_dynamic-update-slice_fusion.carrier_ref.field_ref.refs_0_), channel_id=1, source_target_pairs={{0,2},{1,3},{2,0},{3,1},{4,6},{5,7},{6,4},{7,5},{8,10},{9,11},{10,... | collective-permute-start | bytes 3145736 | tf_op jit(solution)/shard_map/ppermute | solution.py:210
  57.7 45.8 %collective-permute-start.16 = (f32[64,1024]{1,0:T(8,128)}, f32[64,1024]{1,0:T(8,128)}, u32[]{:S(2)}, u32[]{:S(2)}) collective-permute-start(f32[64,1024]{1,0:T(8,128)} %get-tuple-element.73), channel_id=1, source_target_pairs={{0,4},{1,5},{2,6},{3,7},{4,0},{5,1},{6,2},{7,3},{8,12},{9,13},{10,... | collective-permute-start | bytes 786440 | tf_op jit(solution)/shard_map/ppermute | solution.py:210
  57.7 46.3 %collective-permute-start.17 = (f32[64,1024]{1,0:T(8,128)}, f32[64,1024]{1,0:T(8,128)}, u32[]{:S(2)}, u32[]{:S(2)}) collective-permute-start(f32[64,1024]{1,0:T(8,128)} %get-tuple-element.74), channel_id=1, source_target_pairs={{0,8},{1,9},{2,10},{3,11},{4,12},{5,13},{6,14},{7,15},{8,0},{9,1},... | collective-permute-start | bytes 786440 | tf_op jit(solution)/shard_map/ppermute | solution.py:210
  66.1 33.2 %collective-permute-start.1 = (f32[8,128]{1,0:T(8,128)S(1)}, f32[8,128]{1,0:T(8,128)S(1)}, u32[]{:S(2)}, u32[]{:S(2)}) collective-permute-start(f32[8,128]{1,0:T(8,128)S(1)} %add.130), channel_id=1, source_target_pairs={{0,2},{1,3},{2,0},{3,1},{4,6},{5,7},{6,4},{7,5},{8,10},{9,11},{10,... | collective-permute-start | bytes 12296 | tf_op jit(solution)/shard_map/ppermute | solution.py:210
  103.0 37.7 %collective-permute-start.14 = (f32[256,1024]{1,0:T(8,128)S(1)}, f32[256,1024]{1,0:T(8,128)}, u32[]{:S(2)}, u32[]{:S(2)}) collective-permute-start(f32[256,1024]{1,0:T(8,128)S(1)} %constant_dynamic-update-slice_fusion.4.field_ref.refs_4_.refs_0_), channel_id=1, source_target_pairs={{0,1},{1,0},{2,3},{3,2},{4,5},{5,4},{6,7},{7,6},{8,9},{9,8},{10,11... | collective-permute-start | bytes 3145736 | tf_op jit(solution)/shard_map/ppermute | solution.py:210
  103.0 37.7 %collective-permute-start.15 = (f32[256,1024]{1,0:T(8,128)}, f32[256,1024]{1,0:T(8,128)}, u32[]{:S(2)}, u32[]{:S(2)}) collective-permute-start(f32[256,1024]{1,0:T(8,128)} %collective-permute-done.13.refs_5_.field_ref.refs_1_), channel_id=1, source_target_pairs={{0,1},{1,0},{2,3},{3,2},{4,5},{5,4},{6,7},{7,6},{8,9},{9,8},{10,11... | collective-permute-start | bytes 3145736 | tf_op jit(solution)/shard_map/ppermute | solution.py:210
  103.5 51.6 %collective-permute-start.11 = (f32[256,1024]{1,0:T(8,128)S(1)}, f32[256,1024]{1,0:T(8,128)}, u32[]{:S(2)}, u32[]{:S(2)}) collective-permute-start(f32[256,1024]{1,0:T(8,128)S(1)} %constant_dynamic-update-slice_fusion.carrier_ref.field_ref.refs_0_), channel_id=1, source_target_pairs={{0,1},{1,0},{2,3},{3,2},{4,5},{5,4},{6,7},{7,6},{8,9},{9,8},{10,11... | collective-permute-start | bytes 3145736 | tf_op jit(solution)/shard_map/ppermute | solution.py:210
  103.6 51.5 %collective-permute-start.12 = (f32[256,1024]{1,0:T(8,128)S(1)}, f32[256,1024]{1,0:T(8,128)}, u32[]{:S(2)}, u32[]{:S(2)}) collective-permute-start(f32[256,1024]{1,0:T(8,128)S(1)} %collective-permute-done.10.carrier_ref.field_ref.refs_1_), channel_id=1, source_target_pairs={{0,1},{1,0},{2,3},{3,2},{4,5},{5,4},{6,7},{7,6},{8,9},{9,8},{10,11... | collective-permute-start | bytes 3145736 | tf_op jit(solution)/shard_map/ppermute | solution.py:210
  104.0 18.1 %collective-permute-start.18 = (f32[64,1024]{1,0:T(8,128)}, f32[64,1024]{1,0:T(8,128)S(1)}, u32[]{:S(2)}, u32[]{:S(2)}) collective-permute-start(f32[64,1024]{1,0:T(8,128)} %get-tuple-element.75), channel_id=1, source_target_pairs={{0,12},{1,13},{2,14},{3,15},{4,8},{5,9},{6,10},{7,11},{8,4},{9,5},... | collective-permute-start | bytes 786440 | tf_op jit(solution)/shard_map/ppermute | solution.py:210
  128.9 42.7 %collective-permute-start.19 = (f32[256,1024]{1,0:T(8,128)}, f32[256,1024]{1,0:T(8,128)}, u32[]{:S(2)}, u32[]{:S(2)}) collective-permute-start(f32[256,1024]{1,0:T(8,128)} %constant_dynamic-update-slice_fusion.8.field_ref.refs_0_), channel_id=1, source_target_pairs={{0,2},{1,3},{2,0},{3,1},{4,6},{5,7},{6,4},{7,5},{8,10},{9,11},{10,... | collective-permute-start | bytes 3145736 | tf_op jit(solution)/shard_map/ppermute | solution.py:210
  155.1 66.9 %collective-permute-start.26 = (f32[512,1024]{1,0:T(8,128)}, f32[512,1024]{1,0:T(8,128)}, u32[]{:S(2)}, u32[]{:S(2)}) collective-permute-start(f32[512,1024]{1,0:T(8,128)} %get-tuple-element.93.refs_2_.field_ref.refs_0_), channel_id=1, source_target_pairs={{0,1},{1,0},{2,3},{3,2},{4,5},{5,4},{6,7},{7,6},{8,9},{9,8},{10,11... | collective-permute-start | bytes 6291464 | tf_op jit(solution)/shard_map/ppermute | solution.py:210
  171.0 51.0 %collective-permute-start.25 = (f32[512,1024]{1,0:T(8,128)}, f32[512,1024]{1,0:T(8,128)}, u32[]{:S(2)}, u32[]{:S(2)}) collective-permute-start(f32[512,1024]{1,0:T(8,128)} %get-tuple-element.100.carrier_ref.field_ref.refs_0_), channel_id=1, source_target_pairs={{0,1},{1,0},{2,3},{3,2},{4,5},{5,4},{6,7},{7,6},{8,9},{9,8},{10,11... | collective-permute-start | bytes 6291464 | tf_op jit(solution)/shard_map/ppermute | solution.py:210
  171.5 18.2 %collective-permute-start.20 = (f32[256,1024]{1,0:T(8,128)}, f32[256,1024]{1,0:T(8,128)S(1)}, u32[]{:S(2)}, u32[]{:S(2)}) collective-permute-start(f32[256,1024]{1,0:T(8,128)} %constant_dynamic-update-slice_fusion.8.field_ref.refs_0_), channel_id=1, source_target_pairs={{0,1},{1,0},{2,3},{3,2},{4,5},{5,4},{6,7},{7,6},{8,9},{9,8},{10,11... | collective-permute-start | bytes 3145736 | tf_op jit(solution)/shard_map/ppermute | solution.py:210
  171.6 18.1 %collective-permute-start.21 = (f32[256,1024]{1,0:T(8,128)}, f32[256,1024]{1,0:T(8,128)S(1)}, u32[]{:S(2)}, u32[]{:S(2)}) collective-permute-start(f32[256,1024]{1,0:T(8,128)} %collective-permute-done.19.field_ref.refs_1_), channel_id=1, source_target_pairs={{0,1},{1,0},{2,3},{3,2},{4,5},{5,4},{6,7},{7,6},{8,9},{9,8},{10,11... | collective-permute-start | bytes 3145736 | tf_op jit(solution)/shard_map/ppermute | solution.py:210
  209.3 78.2 %collective-permute-start.33 = (f32[512,1024]{1,0:T(8,128)}, f32[512,1024]{1,0:T(8,128)S(1)}, u32[]{:S(2)}, u32[]{:S(2)}) collective-permute-start(f32[512,1024]{1,0:T(8,128)} %get-tuple-element.101.field_ref), channel_id=1, source_target_pairs={{0,1},{1,0},{2,3},{3,2},{4,5},{5,4},{6,7},{7,6},{8,9},{9,8},{10,11... | collective-permute-start | bytes 6291464 | tf_op jit(solution)/shard_map/ppermute | solution.py:210
  211.8 8.9 %collective-permute-start.24 = (f32[8,128]{1,0:T(8,128)S(1)}, f32[8,128]{1,0:T(8,128)S(1)}, u32[]{:S(2)}, u32[]{:S(2)}) collective-permute-start(f32[8,128]{1,0:T(8,128)S(1)} %add.141), channel_id=1, source_target_pairs={{0,8},{1,9},{2,10},{3,11},{4,12},{5,13},{6,14},{7,15},{8,0},{9,1},... | collective-permute-start | bytes 12296 | tf_op jit(solution)/shard_map/ppermute | solution.py:210
  231.6 32.6 %collective-permute-start.27 = (f32[64,1024]{1,0:T(8,128)S(1)}, f32[64,1024]{1,0:T(8,128)}, u32[]{:S(2)}, u32[]{:S(2)}) collective-permute-start(f32[64,1024]{1,0:T(8,128)S(1)} %get-tuple-element.89), channel_id=1, source_target_pairs={{0,4},{1,5},{2,6},{3,7},{4,0},{5,1},{6,2},{7,3},{8,12},{9,13},{10,... | collective-permute-start | bytes 786440 | tf_op jit(solution)/shard_map/ppermute | solution.py:210
  232.6 34.6 %collective-permute-start.28 = (f32[64,1024]{1,0:T(8,128)S(1)}, f32[64,1024]{1,0:T(8,128)}, u32[]{:S(2)}, u32[]{:S(2)}) collective-permute-start(f32[64,1024]{1,0:T(8,128)S(1)} %get-tuple-element.90), channel_id=1, source_target_pairs={{0,8},{1,9},{2,10},{3,11},{4,12},{5,13},{6,14},{7,15},{8,0},{9,1},... | collective-permute-start | bytes 786440 | tf_op jit(solution)/shard_map/ppermute | solution.py:210
  234.7 34.8 %collective-permute-start.29 = (f32[64,1024]{1,0:T(8,128)S(1)}, f32[64,1024]{1,0:T(8,128)}, u32[]{:S(2)}, u32[]{:S(2)}) collective-permute-start(f32[64,1024]{1,0:T(8,128)S(1)} %get-tuple-element.91), channel_id=1, source_target_pairs={{0,12},{1,13},{2,14},{3,15},{4,8},{5,9},{6,10},{7,11},{8,4},{9,5},... | collective-permute-start | bytes 786440 | tf_op jit(solution)/shard_map/ppermute | solution.py:210
  251.3 20.6 %collective-permute-start.30 = (f32[64,1024]{1,0:T(8,128)S(1)}, f32[64,1024]{1,0:T(8,128)}, u32[]{:S(2)}, u32[]{:S(2)}) collective-permute-start(f32[64,1024]{1,0:T(8,128)S(1)} %get-tuple-element.96), channel_id=1, source_target_pairs={{0,4},{1,5},{2,6},{3,7},{4,0},{5,1},{6,2},{7,3},{8,12},{9,13},{10,... | collective-permute-start | bytes 786440 | tf_op jit(solution)/shard_map/ppermute | solution.py:210
  264.2 17.3 %collective-permute-start.31 = (f32[64,1024]{1,0:T(8,128)S(1)}, f32[64,1024]{1,0:T(8,128)S(1)}, u32[]{:S(2)}, u32[]{:S(2)}) collective-permute-start(f32[64,1024]{1,0:T(8,128)S(1)} %get-tuple-element.97), channel_id=1, source_target_pairs={{0,8},{1,9},{2,10},{3,11},{4,12},{5,13},{6,14},{7,15},{8,0},{9,1},... | collective-permute-start | bytes 786440 | tf_op jit(solution)/shard_map/ppermute | solution.py:210
  267.2 19.6 %collective-permute-start.32 = (f32[64,1024]{1,0:T(8,128)S(1)}, f32[64,1024]{1,0:T(8,128)S(1)}, u32[]{:S(2)}, u32[]{:S(2)}) collective-permute-start(f32[64,1024]{1,0:T(8,128)S(1)} %get-tuple-element.98), channel_id=1, source_target_pairs={{0,12},{1,13},{2,14},{3,15},{4,8},{5,9},{6,10},{7,11},{8,4},{9,5},... | collective-permute-start | bytes 786440 | tf_op jit(solution)/shard_map/ppermute | solution.py:210
  295.4 9.2 %collective-permute-start.34 = (f32[64,1024]{1,0:T(8,128)S(1)}, f32[64,1024]{1,0:T(8,128)S(1)}, u32[]{:S(2)}, u32[]{:S(2)}) collective-permute-start(f32[64,1024]{1,0:T(8,128)S(1)} %get-tuple-element.110), channel_id=1, source_target_pairs={{0,4},{1,5},{2,6},{3,7},{4,0},{5,1},{6,2},{7,3},{8,12},{9,13},{10,... | collective-permute-start | bytes 786440 | tf_op jit(solution)/shard_map/ppermute | solution.py:210
  295.4 20.9 %collective-permute-start.35 = (f32[64,1024]{1,0:T(8,128)S(1)}, f32[64,1024]{1,0:T(8,128)S(1)}, u32[]{:S(2)}, u32[]{:S(2)}) collective-permute-start(f32[64,1024]{1,0:T(8,128)S(1)} %get-tuple-element.112), channel_id=1, source_target_pairs={{0,8},{1,9},{2,10},{3,11},{4,12},{5,13},{6,14},{7,15},{8,0},{9,1},... | collective-permute-start | bytes 786440 | tf_op jit(solution)/shard_map/ppermute | solution.py:210
  298.3 22.2 %collective-permute-start.36 = (f32[64,1024]{1,0:T(8,128)S(1)}, f32[64,1024]{1,0:T(8,128)S(1)}, u32[]{:S(2)}, u32[]{:S(2)}) collective-permute-start(f32[64,1024]{1,0:T(8,128)S(1)} %get-tuple-element.114), channel_id=1, source_target_pairs={{0,12},{1,13},{2,14},{3,15},{4,8},{5,9},{6,10},{7,11},{8,4},{9,5},... | collective-permute-start | bytes 786440 | tf_op jit(solution)/shard_map/ppermute | solution.py:210
  (27 other events, 328.2 us)

commit v3 on v2

v3 whole, which is shorter than its diff:
```python
import functools

import jax
import jax.numpy as jnp
from jax import lax
from jax.experimental import pallas as pl
from jax.experimental.pallas import tpu as pltpu
from jax.sharding import PartitionSpec as P

viscosity = 0.2
power_input = 2.0
time_step = 0.5
first_weight = 8.0 / 15.0
second_weight = 5.0 / 12.0
back_weight = 17.0 / 60.0

BF16 = jnp.bfloat16
F32 = jnp.float32
VMEM_BYTES = 50 * 1024 * 1024


def halves(x):
    high = x.astype(BF16)
    return high, (x - high.astype(F32)).astype(BF16)


def product(a, b):
    return jnp.dot(a, b, preferred_element_type=F32)


def params():
    return pltpu.CompilerParams(vmem_limit_bytes=VMEM_BYTES)


def matrices_kernel(count, order_ref, *refs):
    slope_parts, curve_parts = refs[:count], refs[count:2 * count]
    slope_ref, curve_ref, along_x_ref, along_y_ref, turned = refs[2 * count:]
    size = slope_parts[0].shape[0]
    for place, ref, scale in ((0, slope_ref, -0.5), (2, curve_ref, viscosity)):
        high, low = halves(ref[...] * scale)
        along_x_ref[place] = high
        along_x_ref[place + 1] = low
    for high_place, low_place, parts, scale in ((1, 0, slope_parts, -0.5), (2, 3, curve_parts, viscosity)):
        turned[...] = jnp.concatenate([part[...] for part in parts], axis=0).T
        for block in range(along_y_ref.shape[1] // size):
            source = pl.ds(pl.multiple_of(order_ref[block] * size, size), size)
            high, low = halves(turned[source, :] * scale)
            along_y_ref[high_place, block * size:(block + 1) * size, :] = high
            along_y_ref[low_place, block * size:(block + 1) * size, :] = low


def prepare_matrices(order, slope_matrix, curve_matrix, size):
    length = slope_matrix.shape[0]
    width = min(128, length)
    count = width // size

    def part(place):
        return pl.BlockSpec((size, length), lambda j, order_ref: (order_ref[count * j + place], 0))

    parts = [part(place) for place in range(count)]
    straight = pl.BlockSpec((width, length), lambda j, order_ref: (j, 0))
    return pl.pallas_call(
        functools.partial(matrices_kernel, count),
        grid_spec=pltpu.PrefetchScalarGridSpec(
            num_scalar_prefetch=1,
            grid=(length // width,),
            in_specs=parts + parts + [straight, straight],
            out_specs=[
                pl.BlockSpec((4, width, length), lambda j, order_ref: (0, j, 0)),
                pl.BlockSpec((4, length // 2, width), lambda j, order_ref: (0, 0, j)),
            ],
            scratch_shapes=[pltpu.VMEM((length, width), F32)],
        ),
        out_shape=[
            jax.ShapeDtypeStruct((4, length, length), BF16),
            jax.ShapeDtypeStruct((4, length // 2, length), BF16),
        ],
        compiler_params=params(),
    )(order, *([slope_matrix] * count), *([curve_matrix] * count), slope_matrix, curve_matrix)


def piece_spec(piece, width, column):
    _, component, rows = piece
    if component is None:
        return pl.BlockSpec((rows, width), lambda n: (0, column(n)))
    return pl.BlockSpec((None, rows, width), lambda n: (component, 0, column(n)))


def joined(refs, columns=slice(None)):
    return jnp.concatenate([ref[:, columns] for ref in refs], axis=0)


def pack_kernel(holds_squares, plane_ref, velocity_ref, own_ref, squares_ref, *block_refs):
    components, planes, size, length = velocity_ref.shape
    plane = plane_ref[0]
    velocity = velocity_ref[...].reshape(components * planes * size // 8, 8, length)
    squares = jnp.sum(velocity * velocity, axis=0)
    squares_ref[...] = squares
    for i in range(components):
        own_ref[i] = velocity_ref[i, plane]
        for d in range(1, planes):
            ref = block_refs[i * (planes - 1) + d - 1]
            ref[0:size, :] = velocity_ref[i, plane ^ d]
            if i == holds_squares:
                ref[size:, :] = squares


def pack(plane, velocity, holds_squares):
    components, planes, size, length = velocity.shape
    whole = lambda *shape: pl.BlockSpec(shape, lambda n, plane_ref: (0,) * len(shape))
    shapes = [(components, size, length), (8, length)]
    for i in range(components):
        shapes += [(size + (8 if i == holds_squares else 0), length)] * (planes - 1)
    own, squares, *blocks = pl.pallas_call(
        functools.partial(pack_kernel, holds_squares),
        grid_spec=pltpu.PrefetchScalarGridSpec(
            num_scalar_prefetch=1,
            grid=(1,),
            in_specs=[whole(*velocity.shape)],
            out_specs=[whole(*shape) for shape in shapes],
        ),
        out_shape=[jax.ShapeDtypeStruct(shape, F32) for shape in shapes],
        compiler_params=params(),
        name="pack",
    )(plane.reshape(1).astype(jnp.int32), velocity)
    return own, squares, [blocks[i * (planes - 1):(i + 1) * (planes - 1)] for i in range(components)]


def join_kernel(size, extra, *refs):
    out_ref = refs[-1]
    blocks = refs[:-1]
    if extra:
        *blocks, squares_ref = blocks
        squares = squares_ref[...]
        for ref in blocks:
            squares = squares + ref[size:, :]
        out_ref[len(blocks) * size:, :] = squares
    for place, ref in enumerate(blocks):
        out_ref[place * size:(place + 1) * size, :] = ref[0:size, :]


def join(blocks, size, squares=None):
    extra = [] if squares is None else [squares]
    rows = len(blocks) * size + (8 if extra else 0)
    return pl.pallas_call(
        functools.partial(join_kernel, size, len(extra)),
        out_shape=jax.ShapeDtypeStruct((rows, blocks[0].shape[1]), F32),
        compiler_params=params(),
        name="join",
    )(*blocks, *extra)


def along_x_kernel(counts, *refs):
    fields, carriers, _, (matrix_ref, out_ref, stack) = cut(refs, counts)
    rows = out_ref.shape[0]
    carriers = carriers or fields

    @pl.when(pl.program_id(0) == 0)
    def _():
        field = joined(fields)
        high, low = halves(field)
        stack[0:rows] = low
        stack[rows:2 * rows] = high
        high, low = halves(joined(carriers) * field)
        stack[2 * rows:3 * rows] = high
        stack[3 * rows:4 * rows] = low

    tile = out_ref.shape[1]
    columns = pl.ds(pl.multiple_of(pl.program_id(0) * tile, tile), tile)
    a = product(stack[...], matrix_ref[0])
    b = product(stack[rows:3 * rows], matrix_ref[1])
    c = product(stack[0:2 * rows], matrix_ref[2])
    d = product(stack[rows:2 * rows], matrix_ref[3])
    slope = a[0:rows] + a[rows:2 * rows] + b[0:rows]
    rest = a[2 * rows:3 * rows] + a[3 * rows:] + b[rows:] + c[0:rows] + c[rows:] + d
    out_ref[...] = joined(carriers, columns) * slope + rest


def along_x(fields, carriers, matrix, name):
    rows, length = sum(piece[2] for piece in fields), fields[0][0].shape[-1]
    tile = min(256, length)
    pieces = fields + carriers
    return pl.pallas_call(
        functools.partial(along_x_kernel, (len(fields), len(carriers), 0)),
        grid=(length // tile,),
        in_specs=[piece_spec(piece, length, lambda n: 0) for piece in pieces]
        + [pl.BlockSpec((4, length, tile), lambda n: (0, 0, n))],
        out_specs=pl.BlockSpec((rows, tile), lambda n: (0, n)),
        out_shape=jax.ShapeDtypeStruct((rows, length), F32),
        scratch_shapes=[pltpu.VMEM((4 * rows, length), BF16)],
        compiler_params=params(),
        cost_estimate=pl.CostEstimate(
            flops=2 * rows * length * length, bytes_accessed=4 * rows * length, transcendentals=0
        ),
        name=name,
    )(*[piece[0] for piece in pieces], matrix)


def y_products(matrix_ref, fields, carriers):
    rows, length = matrix_ref.shape[1:]
    field = joined(fields)
    carrier = joined(carriers) if carriers else field
    field_high, field_low = halves(field)
    flux_high, flux_low = halves(field * carrier)
    matrix = matrix_ref[...].reshape(4 * rows, length)
    a = product(matrix, field_high)
    b = product(matrix[rows:3 * rows], field_low)
    c = product(matrix[0:2 * rows], flux_high)
    d = product(matrix[rows:2 * rows], flux_low)
    slope = a[0:rows] + a[rows:2 * rows] + b[0:rows]
    rest = a[2 * rows:3 * rows] + a[3 * rows:] + b[rows:] + c[0:rows] + c[rows:] + d
    return field[0:rows], carrier[0:rows] * slope + rest


def first_kernel(counts, forcing_ref, matrix_ref, *refs):
    fields, carriers, x_terms, (middle_ref, base_ref, square_ref) = cut(refs, counts)
    rows = matrix_ref.shape[1]
    field, terms = y_products(matrix_ref, fields, carriers)
    first = terms + joined(x_terms) + forcing_ref[0, 0] * field
    middle = field + (time_step * first_weight) * first
    middle_ref[...] = middle
    base_ref[...] = middle - (time_step * back_weight) * first
    square_ref[...] = jnp.sum((middle * middle).reshape(rows // 8, 8, middle.shape[1]), axis=0)


def second_kernel(counts, forcing_ref, matrix_ref, *refs):
    fields, carriers, x_terms, (base_ref, *out_refs) = cut(refs, counts)
    field, terms = y_products(matrix_ref, fields, carriers)
    second = terms + joined(x_terms) + forcing_ref[0, 0] * field
    out = base_ref[...] + (time_step * second_weight) * second
    size = out_refs[0].shape[0]
    for place, out_ref in enumerate(out_refs):
        out_ref[...] = out[place * size:(place + 1) * size]


def cut(refs, counts):
    pieces, start = [], 0
    for count in counts:
        pieces.append(refs[start:start + count])
        start += count
    return *pieces, refs[start:]


def y_call(kernel, rows, matrix, fields, carriers, x_terms, rest, out_rows, forcing, name):
    length = fields[0][0].shape[-1]
    tile = min(256, length)
    columns = lambda count: pl.BlockSpec((count, tile), lambda n: (0, n))
    pieces = fields + carriers + [(x, None, rows) for x in [x_terms] + rest]
    return pl.pallas_call(
        functools.partial(kernel, (len(fields), len(carriers), 1)),
        grid=(length // tile,),
        in_specs=[
            pl.BlockSpec(memory_space=pltpu.SMEM),
            pl.BlockSpec((4, rows, length), lambda n: (0, 0, 0)),
            *[piece_spec(piece, tile, lambda n: n) for piece in pieces],
        ],
        out_specs=[columns(count) for count in out_rows],
        out_shape=[jax.ShapeDtypeStruct((count, length), F32) for count in out_rows],
        compiler_params=params(),
        cost_estimate=pl.CostEstimate(
            flops=2 * rows * length * length, bytes_accessed=4 * rows * length, transcendentals=0
        ),
        name=name,
    )(forcing, matrix, *[piece[0] for piece in pieces])


def after(values, *earlier):
    return lax.optimization_barrier((values, earlier))[0]


def on_device(velocity, slope_matrix, curve_matrix):
    planes, size, length = velocity.shape[1:]
    devices = lax.axis_size("row")
    group = devices // planes
    chips = group // 2
    kept = length // group
    place = lax.axis_index("row")
    plane, member = place // group, place % group
    cells = 3 * planes * size * devices * length

    def swap(x, distance):
        return lax.ppermute(x, "row", [(r, r ^ distance) for r in range(devices)])

    def swap_sum(x, distances):
        for distance in distances:
            x = x + swap(x, distance)
        return x

    def doubling(start, stop):
        return [start << step for step in range((stop // start).bit_length() - 1)]

    def order_of(index):
        core, rest = index // (chips * planes), index % (chips * planes)
        chip, far = rest // planes, rest % planes
        return (plane ^ far) * group + (member ^ (2 * chip + core))

    def forcing_of(total):
        return (power_input / (jnp.sum(total) / cells)).reshape(1, 1)

    order = jnp.stack([order_of(index) for index in range(devices)]).astype(jnp.int32)

    def send(blocks):
        return [swap(block, d * group) for d, block in enumerate(blocks, 1)]

    def across_chips(mine):
        return [mine] + [swap(mine, 2 * h) for h in range(1, chips)]

    def across_cores(near):
        return near + [swap(piece, 1) for piece in near]

    def pieces_of(i, own, rest):
        return [x for a, b in zip(own, rest) for x in ((a, i, size), (b, None, kept - size))]

    def x_terms_of(i, field, carrier, name):
        return along_x(field, carrier if i else [], along_x_matrix, name)

    def whole_piece(x):
        return (x, None, kept)

    own, squares, blocks = pack(plane, velocity, 1)
    own_near = across_chips(own)
    arriving = [None] * 3
    arriving[1] = send(blocks[1])
    arriving[0] = send(blocks[0])
    arriving[2] = send(blocks[2])
    along_x_matrix, along_y_matrix = prepare_matrices(order, slope_matrix, curve_matrix, size)

    arriving[1] = after(arriving[1], along_x_matrix, along_y_matrix)
    rest = [None] * 3
    rest[1] = across_chips(join(arriving[1], size, squares))
    own_whole = across_cores(after(own_near, rest[1][0]))
    rest[0] = across_chips(join(arriving[0], size))
    rest[1] = after(rest[1], rest[0][0])
    whole_rest = [None] * 3
    whole_rest[1] = across_cores(rest[1])
    forcing = forcing_of(sum(piece[kept - size:] for piece in whole_rest[1]))

    x_terms, near, whole = [None] * 3, [None] * 3, [None] * 3
    near[1], near[0] = pieces_of(1, own_whole[:1], rest[1][:1]), pieces_of(0, own_whole[:1], rest[0][:1])
    x_terms[1] = x_terms_of(1, near[1], near[0], "x_first_1")
    whole[1] = pieces_of(1, own_whole, whole_rest[1])

    def first_step(i):
        return y_call(
            first_kernel, kept, along_y_matrix, whole[i], whole[1] if i != 1 else [], x_terms[i], [],
            [kept, kept, 8], forcing, f"y_first_{i}",
        )

    middle, base, square, middle_near, middle_whole = [None] * 3, [None] * 3, [None] * 3, [None] * 3, [None] * 3
    middle[1], base[1], square[1] = first_step(1)
    near[0] = [(after(array, middle[1]), *place) for array, *place in near[0]]
    x_terms[0] = x_terms_of(0, near[0], [], "x_first_0")
    arriving[2] = after(arriving[2], x_terms[0])
    rest[2] = across_chips(join(arriving[2], size))
    middle_near[1] = across_chips(after(middle[1], rest[2][0]))
    whole_rest[0] = across_cores(rest[0])
    whole[0] = pieces_of(0, own_whole, after(whole_rest[0], rest[2][0]))
    middle[0], base[0], square[0] = first_step(0)
    near[2] = pieces_of(2, own_whole[:1], [after(rest[2][0], middle[0])])
    x_terms[2] = x_terms_of(2, near[2], near[0], "x_first_2")
    whole_rest[2] = across_cores(after(rest[2], x_terms[2]))
    whole[2] = pieces_of(2, own_whole, whole_rest[2])
    middle[2], base[2], square[2] = first_step(2)

    total = jnp.sum((square[0] + square[1] + square[2]).reshape(8, length // 128, 128), axis=1)
    total = swap_sum(total, doubling(group, devices) + doubling(1, group))
    forcing = forcing_of(total)

    carrier = [whole_piece(middle[0])]
    x_terms[1] = x_terms_of(1, [whole_piece(after(middle[1], square[2]))], carrier, "x_second_1")
    middle_whole[1] = across_cores(after(middle_near[1], x_terms[1]))
    middle_near[0] = across_chips(after(middle[0], total))

    def second_step(i):
        return y_call(
            second_kernel, kept, along_y_matrix, [whole_piece(x) for x in middle_whole[i]],
            [whole_piece(x) for x in middle_whole[1]] if i != 1 else [], x_terms[i], [base[i]],
            [size] * planes, forcing, f"y_second_{i}",
        )

    ends = [None] * 3
    ends[1] = second_step(1)
    x_terms[0] = x_terms_of(0, [whole_piece(after(middle[0], ends[1]))], [], "x_second_0")
    middle_near[2] = across_chips(after(middle[2], x_terms[0]))
    middle_whole[0] = across_cores(after(middle_near[0], x_terms[0]))
    x_terms[2] = x_terms_of(2, [whole_piece(after(middle[2], x_terms[0]))], carrier, "x_second_2")
    middle_whole[0] = after(middle_whole[0], x_terms[2])
    ends[0] = second_step(0)
    middle_whole[2] = across_cores(after(middle_near[2], ends[0]))
    ends[2] = second_step(2)

    out = jnp.zeros(velocity.shape, F32)
    for i in (1, 0, 2):
        for d, block in enumerate(ends[i]):
            block = swap(block, d * group) if d else block
            out = lax.dynamic_update_slice(out, block[None, None], (i, plane ^ d, 0, 0))
    return out


def solution(mesh):
    placed = (P(None, "groups", "row", None), P(), P())
    return jax.shard_map(
        on_device,
        mesh=mesh,
        in_specs=placed,
        out_specs=P(None, "groups", "row", None),
        check_vma=False,
    )
```

time: 323 us -> 294 us (0.910)
  Pallas kernels: 148 us -> 110 us
  waiting for transfers between devices: 88.5 us -> 119 us
  local copies, waits for them, and re-layouts: 35.5 us -> 10.1 us
  starting transfers between devices: 32.8 us -> 42.7 us
  other arithmetic: 14.4 us -> 8.68 us
    pallas_call x14 -> x15, Pallas kernels: 133 us -> 95.7 us  [the longest x6 47.4 us: along_x(): pl.pallas_call(functools.partial(along_x_kernel, (len(fields), len(carrie...]
    ppermute x37 -> x43, waiting for transfers between devices: 88.5 us -> 119 us  [swap(): return lax.ppermute(x, 'row', [(r, r ^ distance) for r in range(devices)])]
    dynamic_update_slice x11, local copies, waits for them, and re-layouts: 11.7 us -> 0.93 us  [on_device(): out = lax.dynamic_update_slice(out, block[None, None], (i, plane ^ d, 0, 0))]
    ppermute x37 -> x43, starting transfers between devices: 32.8 us -> 42.7 us  [swap(): return lax.ppermute(x, 'row', [(r, r ^ distance) for r in range(devices)])]
    unnamed x53 -> x48, local copies, waits for them, and re-layouts: 15.6 us -> 8.75 us
  transfers between devices with their start and end apart: 37 -> 43, of which waited for: 11 -> 23; matrix products, arithmetic and copies ran while one was open for 9% -> 1% of each run, Pallas kernels for 46% -> 37%
where the time goes in v3:
time: 294 us; the launch traced here: 292 us
  waiting for transfers between devices  119 us (40%)
  Pallas kernels  110 us (37%)
  starting transfers between devices  42.7 us (15%)
  local copies, waits for them, and re-layouts  10.1 us (3%)
  other arithmetic  8.68 us (3%)
    ppermute x43, waiting for transfers between devices, swap(): return lax.ppermute(x, 'row', [(r, r ^ distance) for r in range(devices)])  119 us
    pallas_call x6, Pallas kernels, along_x(): pl.pallas_call(functools.partial(along_x_kernel, (len(fields), len(carrie...  47.4 us
    pallas_call x5, Pallas kernels, y_call(): pl.pallas_call(functools.partial(kernel, (len(fields), len(carriers), 1))...  43.9 us
    ppermute x43, starting transfers between devices, swap(): return lax.ppermute(x, 'row', [(r, r ^ distance) for r in range(devices)])  42.7 us
    pallas_call x1, Pallas kernels, prepare_matrices(): pl.pallas_call(functools.partial(matrices_kernel, count), grid_spec=pltpu...  14.8 us
    unnamed x48, local copies, waits for them, and re-layouts  8.75 us
    pallas_call x1, other arithmetic, y_call(): pl.pallas_call(functools.partial(kernel, (len(fields), len(carriers), 1))...  7.43 us
  transfers between devices with their start and end apart: 43, of which 23 were waited for; matrix products, arithmetic and copies ran while one was open for 1% of the time, Pallas kernels for 37%

profile of v3, /device:TPU:18, one launch (start us, length us, event | category | flops | bytes accessed | tf_op | source)
XLA Modules:
  0.0 292.4 jit_solution(9946182453471943124)
XLA Ops:
  0.0 3.0 %pack.1 = (f32[3,64,1024]{2,1,0:T(8,128)S(1)}, f32[8,1024]{1,0:T(8,128)S(1)}, f32[64,1024]{1,0:T(8,128)S(1)}, f32[64,1024]{1,0:T(8,128)S(1)}, f32[64,1024]{1,0:T...) custom-call(s32[1]{0:T(128)} %bitcast.plane_ref, ...), custom_call_target="tpu_custom_call" | custom-call | tf_op jit(solution)/shard_map/pack/pallas_call | solution.py:114
  7.3 14.8 %shard_map.37 = (bf16[4,1024,1024]{2,1,0:T(8,128)(2,1)}, bf16[4,512,1024]{2,1,0:T(8,128)(2,1)}) custom-call(s32[16]{0:T(128)S(1)} %stack.67.order_ref, f32[1024,1024]{1,0:T(8,128)} %refs_4_.1, f32[1024,1024]{1,0:T(8,128)} %refs_4_.1, f32[1024,1024]{1,0:T(8,128)} %refs_5_.1, f32[1024,1024]{1,0:T(8,128)} %refs_5_.1, f32[1024,1024]{1,0:T(8,128)} %refs_4_.1, ...), custom_call_target="tpu_custom_call" | custom-call | tf_op jit(solution)/shard_map/pallas_call | solution.py:62
  22.2 3.6 %collective-permute-done.1.refs_1_ = f32[72,1024]{1,0:T(8,128)S(1)} collective-permute-done((f32[72,1024]{1,0:T(8,128)S(1)}, f32[72,1024]{1,0:T(8,128)S(1)}, u32[]{:S(2)}, u32[]{:S(2)}) %collective-permute-start.1) | collective-permute-done | bytes 294944 | tf_op jit(solution)/shard_map/ppermute | solution.py:282
  25.7 6.9 %collective-permute-done.2.refs_2_ = f32[72,1024]{1,0:T(8,128)S(1)} collective-permute-done((f32[72,1024]{1,0:T(8,128)S(1)}, f32[72,1024]{1,0:T(8,128)S(1)}, u32[]{:S(2)}, u32[]{:S(2)}) %collective-permute-start.2) | collective-permute-done | bytes 294944 | tf_op jit(solution)/shard_map/ppermute | solution.py:282
  34.8 1.9 collective-permute-start.5
  38.3 5.8 %collective-permute-done.4.refs_0_ = f32[64,1024]{1,0:T(8,128)S(1)} collective-permute-done((f32[64,1024]{1,0:T(8,128)S(1)}, f32[64,1024]{1,0:T(8,128)S(1)}, u32[]{:S(2)}, u32[]{:S(2)}) %collective-permute-start.4) | collective-permute-done | bytes 262176 | tf_op jit(solution)/shard_map/ppermute | solution.py:282
  44.1 10.4 %collective-permute-done.5.refs_1_ = f32[64,1024]{1,0:T(8,128)S(1)} collective-permute-done((f32[64,1024]{1,0:T(8,128)S(1)}, f32[64,1024]{1,0:T(8,128)S(1)}, u32[]{:S(2)}, u32[]{:S(2)}) %collective-permute-start.5) | collective-permute-done | bytes 262176 | tf_op jit(solution)/shard_map/ppermute | solution.py:282
  54.4 4.8 %collective-permute-done.6.refs_2_ = f32[64,1024]{1,0:T(8,128)S(1)} collective-permute-done((f32[64,1024]{1,0:T(8,128)S(1)}, f32[64,1024]{1,0:T(8,128)S(1)}, u32[]{:S(2)}, u32[]{:S(2)}) %collective-permute-start.6) | collective-permute-done | bytes 262176 | tf_op jit(solution)/shard_map/ppermute | solution.py:282
  61.4 9.4 %collective-permute-done.9.refs_2_.refs_10_ = f32[3,64,1024]{2,1,0:T(8,128)S(1)} collective-permute-done((f32[3,64,1024]{2,1,0:T(8,128)S(1)}, f32[3,64,1024]{2,1,0:T(8,128)S(1)}, u32[]{:S(2)}, u32[]{:S(2)}) %collective-permute-start.9) | collective-permute-done | bytes 786464 | tf_op jit(solution)/shard_map/ppermute | solution.py:282
  71.3 14.0 %collective-permute-done.10.refs_3_ = f32[192,1024]{1,0:T(8,128)S(1)} collective-permute-done((f32[192,1024]{1,0:T(8,128)S(1)}, f32[192,1024]{1,0:T(8,128)S(1)}, u32[]{:S(2)}, u32[]{:S(2)}) %collective-permute-start.10) | collective-permute-done | bytes 786464 | tf_op jit(solution)/shard_map/ppermute | solution.py:282
  88.9 7.8 %x_first_1.1.refs_8_ = f32[256,1024]{1,0:T(8,128)S(1)} custom-call(f32[3,64,1024]{2,1,0:T(8,128)S(1)} %get-tuple-element.94.refs_0_.refs_2_.refs_8_, f32[200,1024]{1,0:T(8,128)S(1)} %join.3.refs_1_.refs_9_, f32[3,64,1024]{2,1,0:T(8,128)S(1)} %get-tuple-element.94.refs_0_.refs_2_.refs_8_, f32[192,1024]{1,0:T(8,128)S(1)} %join.4.refs_3_.refs_1_, ...), custom_call_target="tpu_custom_call" | custom-call | flops 536870912 | bytes 1048576 | tf_op jit(solution)/shard_map/x_first_1/pallas_call | solution.py:183
  99.6 8.9 %y_first_1.1 = (f32[256,1024]{1,0:T(8,128)}, f32[256,1024]{1,0:T(8,128)}, f32[8,1024]{1,0:T(8,128)S(1)}) custom-call(f32[1,1]{1,0:T(1,128)} %bitcast.17.forcing_ref, bf16[4,512,1024]{2,1,0:T(8,128)(2,1)} %get-tuple-element.77.matrix_ref, f32[3,64,1024]{2,1,0:T(8,128)S(1)} %get-tuple-element.94.refs_0_.refs_2_.refs_8_, f32[200,1024]{1,0:T(8,128)S(1)} %join.3.refs_1_.refs_9_, ...), custom_call_target="tpu_custom_call" | custom-call | flops 536870912 | bytes 1048576 | tf_op jit(solution)/shard_map/y_first_1/pallas_call | solution.py:249
  108.5 7.9 %x_first_0.1.refs_16_ = f32[256,1024]{1,0:T(8,128)S(1)} custom-call(f32[3,64,1024]{2,1,0:T(8,128)S(1)} %get-tuple-element.94.refs_0_.refs_2_.refs_8_, f32[192,1024]{1,0:T(8,128)S(1)} %join.4.refs_3_.refs_1_, bf16[4,1024,1024]{2,1,0:T(8,128)(2,1)} %get-tuple-element.76.refs_4_.refs_2_.refs_1_), custom_call_target="tpu_custom_call" | custom-call | flops 536870912 | bytes 1048576 | tf_op jit(solution)/shard_map/x_first_0/pallas_call | solution.py:183
  121.9 9.3 %y_first_0.1 = (f32[256,1024]{1,0:T(8,128)}, f32[256,1024]{1,0:T(8,128)}, f32[8,1024]{1,0:T(8,128)S(1)}) custom-call(f32[1,1]{1,0:T(1,128)} %bitcast.17.forcing_ref, bf16[4,512,1024]{2,1,0:T(8,128)(2,1)} %get-tuple-element.77.matrix_ref, f32[3,64,1024]{2,1,0:T(8,128)S(1)} %get-tuple-element.94.refs_0_.refs_2_.refs_8_, f32[192,1024]{1,0:T(8,128)S(1)} %join.4.refs_3_.refs_1_, ...), custom_call_target="tpu_custom_call" | custom-call | flops 536870912 | bytes 1048576 | tf_op jit(solution)/shard_map/y_first_0/pallas_call | solution.py:249
  131.8 7.8 %x_first_2.1.refs_16_ = f32[256,1024]{1,0:T(8,128)S(1)} custom-call(f32[3,64,1024]{2,1,0:T(8,128)S(1)} %get-tuple-element.94.refs_0_.refs_2_.refs_8_, f32[192,1024]{1,0:T(8,128)S(1)} %join.5.refs_1_, f32[3,64,1024]{2,1,0:T(8,128)S(1)} %get-tuple-element.94.refs_0_.refs_2_.refs_8_, f32[192,1024]{1,0:T(8,128)S(1)} %join.4.refs_3_.refs_1_, ...), custom_call_target="tpu_custom_call" | custom-call | flops 536870912 | bytes 1048576 | tf_op jit(solution)/shard_map/x_first_2/pallas_call | solution.py:183
  144.9 9.3 %y_first_2.1 = (f32[256,1024]{1,0:T(8,128)}, f32[256,1024]{1,0:T(8,128)}, f32[8,1024]{1,0:T(8,128)S(1)}) custom-call(f32[1,1]{1,0:T(1,128)} %bitcast.17.forcing_ref, bf16[4,512,1024]{2,1,0:T(8,128)(2,1)} %get-tuple-element.77.matrix_ref, f32[3,64,1024]{2,1,0:T(8,128)S(1)} %get-tuple-element.94.refs_0_.refs_2_.refs_8_, f32[192,1024]{1,0:T(8,128)S(1)} %join.5.refs_1_, ...), custom_call_target="tpu_custom_call" | custom-call | flops 536870912 | bytes 1048576 | tf_op jit(solution)/shard_map/y_first_2/pallas_call | solution.py:249
  155.2 2.6 collective-permute-done.21
  158.8 3.6 %collective-permute-done.22 = f32[8,128]{1,0:T(8,128)S(1)} collective-permute-done((f32[8,128]{1,0:T(8,128)S(1)}, f32[8,128]{1,0:T(8,128)S(1)}, u32[]{:S(2)}, u32[]{:S(2)}) %collective-permute-start.22) | collective-permute-done | bytes 4128 | tf_op jit(solution)/shard_map/ppermute | solution.py:282
  165.1 8.1 %x_second_1.1.refs_4_ = f32[256,1024]{1,0:T(8,128)S(1)} custom-call(f32[256,1024]{1,0:T(8,128)} %get-tuple-element.112.refs_0_.refs_4_, f32[256,1024]{1,0:T(8,128)S(1)} %copy-done.1, bf16[4,1024,1024]{2,1,0:T(8,128)(2,1)} %get-tuple-element.76.refs_4_.refs_2_.refs_1_), custom_call_target="tpu_custom_call" | custom-call | flops 536870912 | bytes 1048576 | tf_op jit(solution)/shard_map/x_second_1/pallas_call | solution.py:183
  179.2 7.9 %y_second_1.1 = (f32[64,1024]{1,0:T(8,128)S(1)}, f32[64,1024]{1,0:T(8,128)S(1)}, f32[64,1024]{1,0:T(8,128)S(1)}, f32[64,1024]{1,0:T(8,128)S(1)}) custom-call(f32[1,1]{1,0:T(1,128)} %bitcast.19.forcing_ref, bf16[4,512,1024]{2,1,0:T(8,128)(2,1)} %get-tuple-element.77.matrix_ref, f32[256,1024]{1,0:T(8,128)} %get-tuple-element.112.refs_0_.refs_4_, ...), custom_call_target="tpu_custom_call" | custom-call | flops 536870912 | bytes 1048576 | tf_op jit(solution)/shard_map/y_second_1/pallas_call | solution.py:249
  187.1 7.9 %x_second_0.1.refs_8_ = f32[256,1024]{1,0:T(8,128)S(1)} custom-call(f32[256,1024]{1,0:T(8,128)S(1)} %copy-done.1, bf16[4,1024,1024]{2,1,0:T(8,128)(2,1)} %get-tuple-element.76.refs_4_.refs_2_.refs_1_), custom_call_target="tpu_custom_call" | custom-call | flops 536870912 | bytes 1048576 | tf_op jit(solution)/shard_map/x_second_0/pallas_call | solution.py:183
  196.1 4.4 %collective-permute-done.31.refs_1_ = f32[256,1024]{1,0:T(8,128)} collective-permute-done((f32[256,1024]{1,0:T(8,128)S(1)}, f32[256,1024]{1,0:T(8,128)}, u32[]{:S(2)}, u32[]{:S(2)}) %collective-permute-start.31) | collective-permute-done | bytes 1048608 | tf_op jit(solution)/shard_map/ppermute | solution.py:282
  203.8 7.8 %x_second_2.1 = f32[256,1024]{1,0:T(8,128)S(1)} custom-call(f32[256,1024]{1,0:T(8,128)S(1)} %copy-done.4, f32[256,1024]{1,0:T(8,128)S(1)} %copy-done.1, bf16[4,1024,1024]{2,1,0:T(8,128)(2,1)} %get-tuple-element.76.refs_4_.refs_2_.refs_1_), custom_call_target="tpu_custom_call" | custom-call | flops 536870912 | bytes 1048576 | tf_op jit(solution)/shard_map/x_second_2/pallas_call | solution.py:183
  215.1 8.6 %y_second_0.1 = (f32[64,1024]{1,0:T(8,128)S(1)}, f32[64,1024]{1,0:T(8,128)S(1)}, f32[64,1024]{1,0:T(8,128)S(1)}, f32[64,1024]{1,0:T(8,128)S(1)}) custom-call(f32[1,1]{1,0:T(1,128)} %bitcast.19.forcing_ref, bf16[4,512,1024]{2,1,0:T(8,128)(2,1)} %get-tuple-element.77.matrix_ref, f32[256,1024]{1,0:T(8,128)S(1)} %copy-done.1, ...), custom_call_target="tpu_custom_call" | custom-call | flops 536870912 | bytes 1048576 | tf_op jit(solution)/shard_map/y_second_0/pallas_call | solution.py:249
  223.7 9.6 %collective-permute-start.34 = (f32[64,1024]{1,0:T(8,128)S(1)}, f32[64,1024]{1,0:T(8,128)S(1)}, u32[]{:S(2)}, u32[]{:S(2)}) collective-permute-start(f32[64,1024]{1,0:T(8,128)S(1)} %get-tuple-element.131), channel_id=1, source_target_pairs={{0,4},{1,5},{2,6},{3,7},{4,0},{5,1},{6,2},{7,3},{8,12},{9,13},{10,... | collective-permute-start | bytes 786440 | tf_op jit(solution)/shard_map/ppermute | solution.py:282
  235.5 4.9 %collective-permute-done.34 = f32[64,1024]{1,0:T(8,128)S(1)} collective-permute-done((f32[64,1024]{1,0:T(8,128)S(1)}, f32[64,1024]{1,0:T(8,128)S(1)}, u32[]{:S(2)}, u32[]{:S(2)}) %collective-permute-start.34) | collective-permute-done | bytes 262176 | tf_op jit(solution)/shard_map/ppermute | solution.py:282
  240.4 10.9 %collective-permute-done.35 = f32[64,1024]{1,0:T(8,128)S(1)} collective-permute-done((f32[64,1024]{1,0:T(8,128)S(1)}, f32[64,1024]{1,0:T(8,128)S(1)}, u32[]{:S(2)}, u32[]{:S(2)}) %collective-permute-start.35) | collective-permute-done | bytes 262176 | tf_op jit(solution)/shard_map/ppermute | solution.py:282
  251.3 7.3 %collective-permute-done.36 = f32[64,1024]{1,0:T(8,128)S(1)} collective-permute-done((f32[64,1024]{1,0:T(8,128)S(1)}, f32[64,1024]{1,0:T(8,128)S(1)}, u32[]{:S(2)}, u32[]{:S(2)}) %collective-permute-start.36) | collective-permute-done | bytes 262176 | tf_op jit(solution)/shard_map/ppermute | solution.py:282
  258.7 7.4 %y_second_2.1 = (f32[3,4,64,1024]{3,2,1,0:T(8,128)S(1)}, f32[64,1024]{1,0:T(8,128)S(1)}, f32[64,1024]{1,0:T(8,128)S(1)}, f32[64,1024]{1,0:T(8,128)S(1)}) fusion(f32[3,4,64,1024]{3,2,1,0:T(8,128)S(1)} %bitcast_dynamic-update-slice_fusion.4, s32[]{:T(128)S(6)} %select_n.33, f32[1,1]{1,0:T(1,128)} %bitcast.19.forcing_ref, ...), kind=kCustom, calls=%fused_computation.3 | custom fusion | flops 536870912 | bytes 15728648 | tf_op jit(solution)/shard_map/y_second_2/pallas_call | solution.py:249
  269.7 6.0 %collective-permute-done.40 = f32[64,1024]{1,0:T(8,128)S(1)} collective-permute-done((f32[64,1024]{1,0:T(8,128)S(1)}, f32[64,1024]{1,0:T(8,128)S(1)}, u32[]{:S(2)}, u32[]{:S(2)}) %collective-permute-start.40) | collective-permute-done | bytes 262176 | tf_op jit(solution)/shard_map/ppermute | solution.py:282
  275.7 10.4 %collective-permute-done.41 = f32[64,1024]{1,0:T(8,128)S(1)} collective-permute-done((f32[64,1024]{1,0:T(8,128)S(1)}, f32[64,1024]{1,0:T(8,128)S(1)}, u32[]{:S(2)}, u32[]{:S(2)}) %collective-permute-start.41) | collective-permute-done | bytes 262176 | tf_op jit(solution)/shard_map/ppermute | solution.py:282
  286.1 5.6 %collective-permute-done.42 = f32[64,1024]{1,0:T(8,128)S(1)} collective-permute-done((f32[64,1024]{1,0:T(8,128)S(1)}, f32[64,1024]{1,0:T(8,128)S(1)}, u32[]{:S(2)}, u32[]{:S(2)}) %collective-permute-start.42) | collective-permute-done | bytes 262176 | tf_op jit(solution)/shard_map/ppermute | solution.py:282
  (138 shorter events, 51.9 us)
Async XLA Ops:
  3.7 18.4 %collective-permute-start = (f32[72,1024]{1,0:T(8,128)S(1)}, f32[72,1024]{1,0:T(8,128)S(1)}, u32[]{:S(2)}, u32[]{:S(2)}) collective-permute-start(f32[72,1024]{1,0:T(8,128)S(1)} %get-tuple-element.73), channel_id=1, source_target_pairs={{0,4},{1,5},{2,6},{3,7},{4,0},{5,1},{6,2},{7,3},{8,12},{9,13},{10,... | collective-permute-start | bytes 884744 | tf_op jit(solution)/shard_map/ppermute | solution.py:282
  5.3 20.4 %collective-permute-start.1 = (f32[72,1024]{1,0:T(8,128)S(1)}, f32[72,1024]{1,0:T(8,128)S(1)}, u32[]{:S(2)}, u32[]{:S(2)}) collective-permute-start(f32[72,1024]{1,0:T(8,128)S(1)} %get-tuple-element.74), channel_id=1, source_target_pairs={{0,8},{1,9},{2,10},{3,11},{4,12},{5,13},{6,14},{7,15},{8,0},{9,1},... | collective-permute-start | bytes 884744 | tf_op jit(solution)/shard_map/ppermute | solution.py:282
  5.6 27.0 %collective-permute-start.2 = (f32[72,1024]{1,0:T(8,128)S(1)}, f32[72,1024]{1,0:T(8,128)S(1)}, u32[]{:S(2)}, u32[]{:S(2)}) collective-permute-start(f32[72,1024]{1,0:T(8,128)S(1)} %get-tuple-element.75), channel_id=1, source_target_pairs={{0,12},{1,13},{2,14},{3,15},{4,8},{5,9},{6,10},{7,11},{8,4},{9,5},... | collective-permute-start | bytes 884744 | tf_op jit(solution)/shard_map/ppermute | solution.py:282
  32.7 26.6 %collective-permute-start.3 = (f32[200,1024]{1,0:T(8,128)S(1)}, f32[200,1024]{1,0:T(8,128)S(1)}, u32[]{:S(2)}, u32[]{:S(2)}) collective-permute-start(f32[200,1024]{1,0:T(8,128)S(1)} %join.3.refs_1_.refs_9_), channel_id=1, source_target_pairs={{0,2},{1,3},{2,0},{3,1},{4,6},{5,7},{6,4},{7,5},{8,10},{9,11},{10,... | collective-permute-start | bytes 2457608 | tf_op jit(solution)/shard_map/ppermute | solution.py:282
  34.3 36.5 %collective-permute-start.9 = (f32[3,64,1024]{2,1,0:T(8,128)S(1)}, f32[3,64,1024]{2,1,0:T(8,128)S(1)}, u32[]{:S(2)}, u32[]{:S(2)}) collective-permute-start(f32[3,64,1024]{2,1,0:T(8,128)S(1)} %get-tuple-element.94.refs_0_.refs_2_.refs_8_), channel_id=1, source_target_pairs={{0,2},{1,3},{2,0},{3,1},{4,6},{5,7},{6,4},{7,5},{8,10},{9,11},{10,... | collective-permute-start | bytes 2359304 | tf_op jit(solution)/shard_map/ppermute | solution.py:282
  34.8 19.6 %collective-permute-start.5 = (f32[64,1024]{1,0:T(8,128)S(1)}, f32[64,1024]{1,0:T(8,128)S(1)}, u32[]{:S(2)}, u32[]{:S(2)}) collective-permute-start(f32[64,1024]{1,0:T(8,128)S(1)} %get-tuple-element.83), channel_id=1, source_target_pairs={{0,8},{1,9},{2,10},{3,11},{4,12},{5,13},{6,14},{7,15},{8,0},{9,1},... | collective-permute-start | bytes 786440 | tf_op jit(solution)/shard_map/ppermute | solution.py:282
  36.7 22.5 %collective-permute-start.6 = (f32[64,1024]{1,0:T(8,128)S(1)}, f32[64,1024]{1,0:T(8,128)S(1)}, u32[]{:S(2)}, u32[]{:S(2)}) collective-permute-start(f32[64,1024]{1,0:T(8,128)S(1)} %get-tuple-element.84), channel_id=1, source_target_pairs={{0,12},{1,13},{2,14},{3,15},{4,8},{5,9},{6,10},{7,11},{8,4},{9,5},... | collective-permute-start | bytes 786440 | tf_op jit(solution)/shard_map/ppermute | solution.py:282
  59.3 26.0 %collective-permute-start.7 = (f32[200,1024]{1,0:T(8,128)S(1)}, f32[200,1024]{1,0:T(8,128)S(1)}, u32[]{:S(2)}, u32[]{:S(2)}) collective-permute-start(f32[200,1024]{1,0:T(8,128)S(1)} %join.3.refs_1_.refs_9_), channel_id=1, source_target_pairs={{0,1},{1,0},{2,3},{3,2},{4,5},{5,4},{6,7},{7,6},{8,9},{9,8},{10,11... | collective-permute-start | bytes 2457608 | tf_op jit(solution)/shard_map/ppermute | solution.py:282
  59.4 27.9 %collective-permute-start.8 = (f32[200,1024]{1,0:T(8,128)S(1)}, f32[200,1024]{1,0:T(8,128)S(1)}, u32[]{:S(2)}, u32[]{:S(2)}) collective-permute-start(f32[200,1024]{1,0:T(8,128)S(1)} %collective-permute-done.3.refs_3_.refs_11_), channel_id=1, source_target_pairs={{0,1},{1,0},{2,3},{3,2},{4,5},{5,4},{6,7},{7,6},{8,9},{9,8},{10,11... | collective-permute-start | bytes 2457608 | tf_op jit(solution)/shard_map/ppermute | solution.py:282
  59.9 25.4 %collective-permute-start.10 = (f32[192,1024]{1,0:T(8,128)S(1)}, f32[192,1024]{1,0:T(8,128)S(1)}, u32[]{:S(2)}, u32[]{:S(2)}) collective-permute-start(f32[192,1024]{1,0:T(8,128)S(1)} %join.4.refs_3_.refs_1_), channel_id=1, source_target_pairs={{0,2},{1,3},{2,0},{3,1},{4,6},{5,7},{6,4},{7,5},{8,10},{9,11},{10,... | collective-permute-start | bytes 2359304 | tf_op jit(solution)/shard_map/ppermute | solution.py:282
  70.8 28.2 %collective-permute-start.16 = (f32[3,64,1024]{2,1,0:T(8,128)S(1)}, f32[3,64,1024]{2,1,0:T(8,128)}, u32[]{:S(2)}, u32[]{:S(2)}) collective-permute-start(f32[3,64,1024]{2,1,0:T(8,128)S(1)} %get-tuple-element.94.refs_0_.refs_2_.refs_8_), channel_id=1, source_target_pairs={{0,1},{1,0},{2,3},{3,2},{4,5},{5,4},{6,7},{7,6},{8,9},{9,8},{10,11... | collective-permute-start | bytes 2359304 | tf_op jit(solution)/shard_map/ppermute | solution.py:282
  70.8 28.3 %collective-permute-start.17 = (f32[3,64,1024]{2,1,0:T(8,128)S(1)}, f32[3,64,1024]{2,1,0:T(8,128)}, u32[]{:S(2)}, u32[]{:S(2)}) collective-permute-start(f32[3,64,1024]{2,1,0:T(8,128)S(1)} %collective-permute-done.9.refs_2_.refs_10_), channel_id=1, source_target_pairs={{0,1},{1,0},{2,3},{3,2},{4,5},{5,4},{6,7},{7,6},{8,9},{9,8},{10,11... | collective-permute-start | bytes 2359304 | tf_op jit(solution)/shard_map/ppermute | solution.py:282
  85.3 32.1 %collective-permute-start.13 = (f32[64,1024]{1,0:T(8,128)}, f32[64,1024]{1,0:T(8,128)}, u32[]{:S(2)}, u32[]{:S(2)}) collective-permute-start(f32[64,1024]{1,0:T(8,128)} %get-tuple-element.89), channel_id=1, source_target_pairs={{0,4},{1,5},{2,6},{3,7},{4,0},{5,1},{6,2},{7,3},{8,12},{9,13},{10,... | collective-permute-start | bytes 786440 | tf_op jit(solution)/shard_map/ppermute | solution.py:282
  85.3 32.1 %collective-permute-start.14 = (f32[64,1024]{1,0:T(8,128)}, f32[64,1024]{1,0:T(8,128)}, u32[]{:S(2)}, u32[]{:S(2)}) collective-permute-start(f32[64,1024]{1,0:T(8,128)} %get-tuple-element.90), channel_id=1, source_target_pairs={{0,8},{1,9},{2,10},{3,11},{4,12},{5,13},{6,14},{7,15},{8,0},{9,1},... | collective-permute-start | bytes 786440 | tf_op jit(solution)/shard_map/ppermute | solution.py:282
  87.3 30.1 %collective-permute-start.15 = (f32[64,1024]{1,0:T(8,128)}, f32[64,1024]{1,0:T(8,128)}, u32[]{:S(2)}, u32[]{:S(2)}) collective-permute-start(f32[64,1024]{1,0:T(8,128)} %get-tuple-element.91), channel_id=1, source_target_pairs={{0,12},{1,13},{2,14},{3,15},{4,8},{5,9},{6,10},{7,11},{8,4},{9,5},... | collective-permute-start | bytes 786440 | tf_op jit(solution)/shard_map/ppermute | solution.py:282
  99.1 21.1 %collective-permute-start.11 = (f32[192,1024]{1,0:T(8,128)S(1)}, f32[192,1024]{1,0:T(8,128)S(1)}, u32[]{:S(2)}, u32[]{:S(2)}) collective-permute-start(f32[192,1024]{1,0:T(8,128)S(1)} %join.4.refs_3_.refs_1_), channel_id=1, source_target_pairs={{0,1},{1,0},{2,3},{3,2},{4,5},{5,4},{6,7},{7,6},{8,9},{9,8},{10,11... | collective-permute-start | bytes 2359304 | tf_op jit(solution)/shard_map/ppermute | solution.py:282
  99.1 21.0 %collective-permute-start.12 = (f32[192,1024]{1,0:T(8,128)}, f32[192,1024]{1,0:T(8,128)S(1)}, u32[]{:S(2)}, u32[]{:S(2)}) collective-permute-start(f32[192,1024]{1,0:T(8,128)} %copy-done.8), channel_id=1, source_target_pairs={{0,1},{1,0},{2,3},{3,2},{4,5},{5,4},{6,7},{7,6},{8,9},{9,8},{10,11... | collective-permute-start | bytes 2359304 | tf_op jit(solution)/shard_map/ppermute | solution.py:282
  118.6 22.0 %collective-permute-start.18 = (f32[192,1024]{1,0:T(8,128)S(1)}, f32[192,1024]{1,0:T(8,128)S(1)}, u32[]{:S(2)}, u32[]{:S(2)}) collective-permute-start(f32[192,1024]{1,0:T(8,128)S(1)} %join.5.refs_1_), channel_id=1, source_target_pairs={{0,2},{1,3},{2,0},{3,1},{4,6},{5,7},{6,4},{7,5},{8,10},{9,11},{10,... | collective-permute-start | bytes 2359304 | tf_op jit(solution)/shard_map/ppermute | solution.py:282
  131.2 43.0 %collective-permute-start.25 = (f32[256,1024]{1,0:T(8,128)}, f32[256,1024]{1,0:T(8,128)}, u32[]{:S(2)}, u32[]{:S(2)}) collective-permute-start(f32[256,1024]{1,0:T(8,128)} %get-tuple-element.112.refs_0_.refs_4_), channel_id=1, source_target_pairs={{0,2},{1,3},{2,0},{3,1},{4,6},{5,7},{6,4},{7,5},{8,10},{9,11},{10,... | collective-permute-start | bytes 3145736 | tf_op jit(solution)/shard_map/ppermute | solution.py:282
  175.3 25.2 %collective-permute-start.31 = (f32[256,1024]{1,0:T(8,128)S(1)}, f32[256,1024]{1,0:T(8,128)}, u32[]{:S(2)}, u32[]{:S(2)}) collective-permute-start(f32[256,1024]{1,0:T(8,128)S(1)} %copy-done.1), channel_id=1, source_target_pairs={{0,2},{1,3},{2,0},{3,1},{4,6},{5,7},{6,4},{7,5},{8,10},{9,11},{10,... | collective-permute-start | bytes 3145736 | tf_op jit(solution)/shard_map/ppermute | solution.py:282
  200.5 14.6 %collective-permute-start.32 = (f32[256,1024]{1,0:T(8,128)S(1)}, f32[256,1024]{1,0:T(8,128)}, u32[]{:S(2)}, u32[]{:S(2)}) collective-permute-start(f32[256,1024]{1,0:T(8,128)S(1)} %copy-done.1), channel_id=1, source_target_pairs={{0,1},{1,0},{2,3},{3,2},{4,5},{5,4},{6,7},{7,6},{8,9},{9,8},{10,11... | collective-permute-start | bytes 3145736 | tf_op jit(solution)/shard_map/ppermute | solution.py:282
  200.5 14.6 %collective-permute-start.33 = (f32[256,1024]{1,0:T(8,128)}, f32[256,1024]{1,0:T(8,128)}, u32[]{:S(2)}, u32[]{:S(2)}) collective-permute-start(f32[256,1024]{1,0:T(8,128)} %collective-permute-done.31.refs_1_), channel_id=1, source_target_pairs={{0,1},{1,0},{2,3},{3,2},{4,5},{5,4},{6,7},{7,6},{8,9},{9,8},{10,11... | collective-permute-start | bytes 3145736 | tf_op jit(solution)/shard_map/ppermute | solution.py:282
  201.0 32.3 %collective-permute-start.37 = (f32[256,1024]{1,0:T(8,128)S(1)}, f32[256,1024]{1,0:T(8,128)}, u32[]{:S(2)}, u32[]{:S(2)}) collective-permute-start(f32[256,1024]{1,0:T(8,128)S(1)} %copy-done.4), channel_id=1, source_target_pairs={{0,2},{1,3},{2,0},{3,1},{4,6},{5,7},{6,4},{7,5},{8,10},{9,11},{10,... | collective-permute-start | bytes 3145736 | tf_op jit(solution)/shard_map/ppermute | solution.py:282
  202.5 12.6 %collective-permute-start.29 = (f32[64,1024]{1,0:T(8,128)S(1)}, f32[64,1024]{1,0:T(8,128)S(1)}, u32[]{:S(2)}, u32[]{:S(2)}) collective-permute-start(f32[64,1024]{1,0:T(8,128)S(1)} %get-tuple-element.117), channel_id=1, source_target_pairs={{0,8},{1,9},{2,10},{3,11},{4,12},{5,13},{6,14},{7,15},{8,0},{9,1},... | collective-permute-start | bytes 786440 | tf_op jit(solution)/shard_map/ppermute | solution.py:282
  212.3 21.5 %collective-permute-start.30 = (f32[64,1024]{1,0:T(8,128)S(1)}, f32[64,1024]{1,0:T(8,128)S(1)}, u32[]{:S(2)}, u32[]{:S(2)}) collective-permute-start(f32[64,1024]{1,0:T(8,128)S(1)} %get-tuple-element.118), channel_id=1, source_target_pairs={{0,12},{1,13},{2,14},{3,15},{4,8},{5,9},{6,10},{7,11},{8,4},{9,5},... | collective-permute-start | bytes 786440 | tf_op jit(solution)/shard_map/ppermute | solution.py:282
  223.7 16.6 %collective-permute-start.34 = (f32[64,1024]{1,0:T(8,128)S(1)}, f32[64,1024]{1,0:T(8,128)S(1)}, u32[]{:S(2)}, u32[]{:S(2)}) collective-permute-start(f32[64,1024]{1,0:T(8,128)S(1)} %get-tuple-element.131), channel_id=1, source_target_pairs={{0,4},{1,5},{2,6},{3,7},{4,0},{5,1},{6,2},{7,3},{8,12},{9,13},{10,... | collective-permute-start | bytes 786440 | tf_op jit(solution)/shard_map/ppermute | solution.py:282
  233.3 25.3 %collective-permute-start.38 = (f32[256,1024]{1,0:T(8,128)S(1)}, f32[256,1024]{1,0:T(8,128)}, u32[]{:S(2)}, u32[]{:S(2)}) collective-permute-start(f32[256,1024]{1,0:T(8,128)S(1)} %copy-done.4), channel_id=1, source_target_pairs={{0,1},{1,0},{2,3},{3,2},{4,5},{5,4},{6,7},{7,6},{8,9},{9,8},{10,11... | collective-permute-start | bytes 3145736 | tf_op jit(solution)/shard_map/ppermute | solution.py:282
  233.3 25.3 %collective-permute-start.39 = (f32[256,1024]{1,0:T(8,128)}, f32[256,1024]{1,0:T(8,128)}, u32[]{:S(2)}, u32[]{:S(2)}) collective-permute-start(f32[256,1024]{1,0:T(8,128)} %collective-permute-done.37), channel_id=1, source_target_pairs={{0,1},{1,0},{2,3},{3,2},{4,5},{5,4},{6,7},{7,6},{8,9},{9,8},{10,11... | collective-permute-start | bytes 3145736 | tf_op jit(solution)/shard_map/ppermute | solution.py:282
  233.8 17.5 %collective-permute-start.35 = (f32[64,1024]{1,0:T(8,128)S(1)}, f32[64,1024]{1,0:T(8,128)S(1)}, u32[]{:S(2)}, u32[]{:S(2)}) collective-permute-start(f32[64,1024]{1,0:T(8,128)S(1)} %get-tuple-element.132), channel_id=1, source_target_pairs={{0,8},{1,9},{2,10},{3,11},{4,12},{5,13},{6,14},{7,15},{8,0},{9,1},... | collective-permute-start | bytes 786440 | tf_op jit(solution)/shard_map/ppermute | solution.py:282
  233.9 24.7 %collective-permute-start.36 = (f32[64,1024]{1,0:T(8,128)S(1)}, f32[64,1024]{1,0:T(8,128)S(1)}, u32[]{:S(2)}, u32[]{:S(2)}) collective-permute-start(f32[64,1024]{1,0:T(8,128)S(1)} %get-tuple-element.133), channel_id=1, source_target_pairs={{0,12},{1,13},{2,14},{3,15},{4,8},{5,9},{6,10},{7,11},{8,4},{9,5},... | collective-permute-start | bytes 786440 | tf_op jit(solution)/shard_map/ppermute | solution.py:282
  266.2 19.9 %collective-permute-start.41 = (f32[64,1024]{1,0:T(8,128)S(1)}, f32[64,1024]{1,0:T(8,128)S(1)}, u32[]{:S(2)}, u32[]{:S(2)}) collective-permute-start(f32[64,1024]{1,0:T(8,128)S(1)} %get-tuple-element.146), channel_id=1, source_target_pairs={{0,8},{1,9},{2,10},{3,11},{4,12},{5,13},{6,14},{7,15},{8,0},{9,1},... | collective-permute-start | bytes 786440 | tf_op jit(solution)/shard_map/ppermute | solution.py:282
  268.1 23.6 %collective-permute-start.42 = (f32[64,1024]{1,0:T(8,128)S(1)}, f32[64,1024]{1,0:T(8,128)S(1)}, u32[]{:S(2)}, u32[]{:S(2)}) collective-permute-start(f32[64,1024]{1,0:T(8,128)S(1)} %get-tuple-element.148), channel_id=1, source_target_pairs={{0,12},{1,13},{2,14},{3,15},{4,8},{5,9},{6,10},{7,11},{8,4},{9,5},... | collective-permute-start | bytes 786440 | tf_op jit(solution)/shard_map/ppermute | solution.py:282
  (35 other events, 400.2 us)

commit v4 on v3

v4 whole, which is shorter than its diff:
```python
import functools

import jax
import jax.numpy as jnp
from jax import lax
from jax.experimental import pallas as pl
from jax.experimental.pallas import tpu as pltpu
from jax.sharding import PartitionSpec as P

viscosity = 0.2
power_input = 2.0
time_step = 0.5
first_weight = 8.0 / 15.0
second_weight = 5.0 / 12.0
back_weight = 17.0 / 60.0

BF16 = jnp.bfloat16
F32 = jnp.float32
VMEM_BYTES = 50 * 1024 * 1024


def halves(x):
    high = x.astype(BF16)
    return high, (x - high.astype(F32)).astype(BF16)


def product(a, b):
    return jnp.dot(a, b, preferred_element_type=F32)


def params():
    return pltpu.CompilerParams(vmem_limit_bytes=VMEM_BYTES)


def matrices_kernel(count, order_ref, own_ref, *refs):
    slope_parts, curve_parts = refs[:count], refs[count:2 * count]
    slope_ref, curve_ref, along_x_ref, along_y_ref, turned = refs[2 * count:]
    size = slope_parts[0].shape[0]
    for place, ref, scale in ((0, slope_ref, -0.5), (2, curve_ref, viscosity)):
        high, low = halves(ref[...] * scale)
        along_x_ref[place] = high
        along_x_ref[place + 1] = low
    for high_place, low_place, parts, scale in ((1, 0, slope_parts, -0.5), (2, 3, curve_parts, viscosity)):
        turned[...] = jnp.concatenate([part[...] for part in parts], axis=0).T
        for block in range(along_y_ref.shape[1] // size):
            source = pl.ds(pl.multiple_of(own_ref[block] * size, size), size)
            high, low = halves(turned[source, :] * scale)
            along_y_ref[high_place, block * size:(block + 1) * size, :] = high
            along_y_ref[low_place, block * size:(block + 1) * size, :] = low


def prepare_matrices(order, own, slope_matrix, curve_matrix, size):
    length = slope_matrix.shape[0]
    width = min(128, length)
    count = width // size
    kept = own.shape[0] * size

    def part(place):
        return pl.BlockSpec((size, length), lambda j, order_ref, own_ref: (order_ref[count * j + place], 0))

    parts = [part(place) for place in range(count)]
    straight = pl.BlockSpec((width, length), lambda j, order_ref, own_ref: (j, 0))
    return pl.pallas_call(
        functools.partial(matrices_kernel, count),
        grid_spec=pltpu.PrefetchScalarGridSpec(
            num_scalar_prefetch=2,
            grid=(length // width,),
            in_specs=parts + parts + [straight, straight],
            out_specs=[
                pl.BlockSpec((4, width, length), lambda j, order_ref, own_ref: (0, j, 0)),
                pl.BlockSpec((4, kept, width), lambda j, order_ref, own_ref: (0, 0, j)),
            ],
            scratch_shapes=[pltpu.VMEM((length, width), F32)],
        ),
        out_shape=[
            jax.ShapeDtypeStruct((4, length, length), BF16),
            jax.ShapeDtypeStruct((4, kept, length), BF16),
        ],
        compiler_params=params(),
        cost_estimate=pl.CostEstimate(flops=16 * length ** 3, bytes_accessed=32 * length * length, transcendentals=0),
    )(order, own, *([slope_matrix] * count), *([curve_matrix] * count), slope_matrix, curve_matrix)


def piece_spec(piece, width, column):
    _, component, rows = piece
    if component is None:
        return pl.BlockSpec((rows, width), lambda n: (0, column(n)))
    return pl.BlockSpec((None, rows, width), lambda n: (component, 0, column(n)))


def joined(refs, columns=slice(None)):
    return jnp.concatenate([ref[:, columns] for ref in refs], axis=0)


def pack_kernel(holds_squares, plane_ref, velocity_ref, squares_ref, *block_refs):
    components, planes, size, length = velocity_ref.shape
    plane = plane_ref[0]
    velocity = velocity_ref[...].reshape(components * planes * size // 8, 8, length)
    squares = jnp.sum(velocity * velocity, axis=0)
    squares_ref[...] = squares
    for i in range(components):
        for d in range(planes):
            ref = block_refs[i * planes + d]
            ref[0:size, :] = velocity_ref[i, plane ^ d]
            if i == holds_squares and d:
                ref[size:, :] = squares


def pack(plane, velocity, holds_squares):
    components, planes, size, length = velocity.shape
    whole = lambda *shape: pl.BlockSpec(shape, lambda n, plane_ref: (0,) * len(shape))
    shapes = [(8, length)]
    for i in range(components):
        for d in range(planes):
            shapes.append((size + (8 if i == holds_squares and d else 0), length))
    squares, *blocks = pl.pallas_call(
        functools.partial(pack_kernel, holds_squares),
        grid_spec=pltpu.PrefetchScalarGridSpec(
            num_scalar_prefetch=1,
            grid=(1,),
            in_specs=[whole(*velocity.shape)],
            out_specs=[whole(*shape) for shape in shapes],
        ),
        out_shape=[jax.ShapeDtypeStruct(shape, F32) for shape in shapes],
        compiler_params=params(),
        name="pack",
    )(plane.reshape(1).astype(jnp.int32), velocity)
    own = [blocks[i * planes] for i in range(components)]
    return own, squares, [blocks[i * planes + 1:(i + 1) * planes] for i in range(components)]


def join_kernel(size, extra, *refs):
    out_ref = refs[-1]
    blocks = refs[:-1]
    if extra:
        *blocks, squares_ref = blocks
        squares = squares_ref[...]
        for ref in blocks[1:]:
            squares = squares + ref[size:, :]
        out_ref[len(blocks) * size:, :] = squares
    for place, ref in enumerate(blocks):
        out_ref[place * size:(place + 1) * size, :] = ref[0:size, :]


def join(blocks, size, squares=None):
    extra = [] if squares is None else [squares]
    rows = len(blocks) * size + (8 if extra else 0)
    return pl.pallas_call(
        functools.partial(join_kernel, size, len(extra)),
        out_shape=jax.ShapeDtypeStruct((rows, blocks[0].shape[1]), F32),
        compiler_params=params(),
        name="join",
    )(*blocks, *extra)


def along_x_kernel(counts, *refs):
    fields, carriers, _, (matrix_ref, out_ref, stack) = cut(refs, counts)
    rows = out_ref.shape[0]
    carriers = carriers or fields

    @pl.when(pl.program_id(0) == 0)
    def _():
        field = joined(fields)
        high, low = halves(field)
        stack[0:rows] = low
        stack[rows:2 * rows] = high
        high, low = halves(joined(carriers) * field)
        stack[2 * rows:3 * rows] = high
        stack[3 * rows:4 * rows] = low

    tile = out_ref.shape[1]
    columns = pl.ds(pl.multiple_of(pl.program_id(0) * tile, tile), tile)
    a = product(stack[...], matrix_ref[0])
    b = product(stack[rows:3 * rows], matrix_ref[1])
    c = product(stack[0:2 * rows], matrix_ref[2])
    d = product(stack[rows:2 * rows], matrix_ref[3])
    slope = a[0:rows] + a[rows:2 * rows] + b[0:rows]
    rest = a[2 * rows:3 * rows] + a[3 * rows:] + b[rows:] + c[0:rows] + c[rows:] + d
    out_ref[...] = joined(carriers, columns) * slope + rest


def along_x(fields, carriers, matrix, name):
    rows, length = sum(piece[2] for piece in fields), fields[0][0].shape[-1]
    tile = min(256, length)
    pieces = fields + carriers
    return pl.pallas_call(
        functools.partial(along_x_kernel, (len(fields), len(carriers), 0)),
        grid=(length // tile,),
        in_specs=[piece_spec(piece, length, lambda n: 0) for piece in pieces]
        + [pl.BlockSpec((4, length, tile), lambda n: (0, 0, n))],
        out_specs=pl.BlockSpec((rows, tile), lambda n: (0, n)),
        out_shape=jax.ShapeDtypeStruct((rows, length), F32),
        scratch_shapes=[pltpu.VMEM((4 * rows, length), BF16)],
        compiler_params=params(),
        cost_estimate=pl.CostEstimate(
            flops=36 * rows * length * length, bytes_accessed=4 * rows * length, transcendentals=0
        ),
        name=name,
    )(*[piece[0] for piece in pieces], matrix)


def y_products(matrix_ref, own, fields, carriers):
    rows, length = matrix_ref.shape[1:]
    field = joined(fields)
    carrier = joined(carriers) if carriers else field
    field_high, field_low = halves(field)
    flux_high, flux_low = halves(field * carrier)
    matrix = matrix_ref[...].reshape(4 * rows, length)
    a = product(matrix, field_high)
    b = product(matrix[rows:3 * rows], field_low)
    c = product(matrix[0:2 * rows], flux_high)
    d = product(matrix[rows:2 * rows], flux_low)
    slope = a[0:rows] + a[rows:2 * rows] + b[0:rows]
    rest = a[2 * rows:3 * rows] + a[3 * rows:] + b[rows:] + c[0:rows] + c[rows:] + d
    return own[1][...] * slope + rest


def first_kernel(counts, forcing_ref, matrix_ref, *refs):
    own, fields, carriers, (x_ref, middle_ref, base_ref, square_ref) = cut(refs, counts)
    rows = matrix_ref.shape[1]
    field = own[0][...]
    first = y_products(matrix_ref, own, fields, carriers) + x_ref[...] + forcing_ref[0, 0] * field
    middle = field + (time_step * first_weight) * first
    middle_ref[...] = middle
    base_ref[...] = middle - (time_step * back_weight) * first
    square_ref[...] = jnp.sum((middle * middle).reshape(rows // 8, 8, middle.shape[1]), axis=0)


def second_kernel(counts, forcing_ref, matrix_ref, *refs):
    own, fields, carriers, (x_ref, base_ref, *out_refs) = cut(refs, counts)
    second = y_products(matrix_ref, own, fields, carriers) + x_ref[...] + forcing_ref[0, 0] * own[0][...]
    out = base_ref[...] + (time_step * second_weight) * second
    size = out_refs[0].shape[0]
    for place, out_ref in enumerate(out_refs):
        out_ref[...] = out[place * size:(place + 1) * size]


def cut(refs, counts):
    pieces, start = [], 0
    for count in counts:
        pieces.append(refs[start:start + count])
        start += count
    return *pieces, refs[start:]


def y_call(kernel, rows, matrix, own, fields, carriers, rest, out_rows, forcing, name):
    length = fields[0][0].shape[-1]
    tile = min(256, length)
    columns = lambda count: pl.BlockSpec((count, tile), lambda n: (0, n))
    pieces = own + fields + carriers + [(x, None, rows) for x in rest]
    return pl.pallas_call(
        functools.partial(kernel, (len(own), len(fields), len(carriers))),
        grid=(length // tile,),
        in_specs=[
            pl.BlockSpec(memory_space=pltpu.SMEM),
            pl.BlockSpec((4, rows, length), lambda n: (0, 0, 0)),
            *[piece_spec(piece, tile, lambda n: n) for piece in pieces],
        ],
        out_specs=[columns(count) for count in out_rows],
        out_shape=[jax.ShapeDtypeStruct((count, length), F32) for count in out_rows],
        compiler_params=params(),
        cost_estimate=pl.CostEstimate(
            flops=36 * rows * length * length, bytes_accessed=4 * rows * length, transcendentals=0
        ),
        name=name,
    )(forcing, matrix, *[piece[0] for piece in pieces])


def after(values, *earlier):
    return lax.optimization_barrier((values, earlier))[0]


def on_device(velocity, slope_matrix, curve_matrix):
    planes, size, length = velocity.shape[1:]
    devices = lax.axis_size("row")
    group = devices // planes
    chips = group // 2
    kept = length // group
    place = lax.axis_index("row")
    plane, member = place // group, place % group
    cells = 3 * planes * size * devices * length

    def swap(x, distance):
        return lax.ppermute(x, "row", [(r, r ^ distance) for r in range(devices)])

    def swap_sum(x, distances):
        for distance in distances:
            x = x + swap(x, distance)
        return x

    def doubling(start, stop):
        return [start << step for step in range((stop // start).bit_length() - 1)]

    def forcing_of(total):
        return (power_input / (jnp.sum(total) / cells)).reshape(1, 1)

    def send(blocks):
        return [swap(block, d * group) for d, block in enumerate(blocks, 1)]

    members = [[g * group + m for m in range(group)] for g in range(planes)]

    def gathered(x):
        return lax.all_gather(x, "row", axis_index_groups=members, axis=0)

    def whole_pieces(x):
        return [(x, m, kept) for m in range(group)]

    order = jnp.stack([(plane ^ d) * group + m for m in range(group) for d in range(planes)]).astype(jnp.int32)
    own_order = jnp.stack([(plane ^ d) * group + member for d in range(planes)]).astype(jnp.int32)

    own, squares, blocks = pack(plane, velocity, 1)
    arriving = [None] * 3
    for i in (1, 0, 2):
        arriving[i] = send(blocks[i])
    along_x_matrix, along_y_matrix = prepare_matrices(order, own_order, slope_matrix, curve_matrix, size)

    def own_pieces(i):
        return (near[i], None, kept)

    x_terms, near, whole = [None] * 3, [None] * 3, [None] * 3
    arriving[1] = after(arriving[1], along_x_matrix, along_y_matrix)
    near[1] = join([own[1]] + arriving[1], size, squares)
    whole[1] = gathered(near[1])
    near[0] = join([own[0]] + arriving[0], size)
    whole[0] = gathered(near[0])
    x_terms[1] = along_x([own_pieces(1)], [own_pieces(0)], along_x_matrix, "x_first_1")
    forcing = forcing_of(whole[1][:, kept:])

    def first_step(i):
        return y_call(
            first_kernel, kept, along_y_matrix, [own_pieces(i), own_pieces(1)], whole_pieces(whole[i]),
            whole_pieces(whole[1]) if i != 1 else [], [x_terms[i]], [kept, kept, 8], forcing, f"y_first_{i}",
        )

    middle, base, square, middle_whole = [None] * 3, [None] * 3, [None] * 3, [None] * 3
    middle[1], base[1], square[1] = first_step(1)
    x_terms[0] = along_x([(after(near[0], middle[1]), None, kept)], [], along_x_matrix, "x_first_0")
    arriving[2] = after(arriving[2], x_terms[0])
    near[2] = join([own[2]] + arriving[2], size)
    whole[2] = gathered(near[2])
    middle_whole[1] = gathered(after(middle[1], near[2]))
    whole[0] = after(whole[0], near[2])
    middle[0], base[0], square[0] = first_step(0)
    x_terms[2] = along_x([(after(near[2], middle[0]), None, kept)], [own_pieces(0)], along_x_matrix, "x_first_2")
    whole[2] = after(whole[2], x_terms[2])
    middle[2], base[2], square[2] = first_step(2)

    total = jnp.sum((square[0] + square[1] + square[2]).reshape(8, length // 128, 128), axis=1)
    total = swap_sum(total, doubling(group, devices) + doubling(1, group))
    forcing = forcing_of(total)

    def piece(x):
        return (x, None, kept)

    x_terms[1] = along_x([piece(after(middle[1], square[2]))], [piece(middle[0])], along_x_matrix, "x_second_1")
    middle_whole[1] = after(middle_whole[1], x_terms[1])
    middle_whole[0] = gathered(middle[0])

    def second_step(i):
        return y_call(
            second_kernel, kept, along_y_matrix, [piece(middle[i]), piece(middle[1])], whole_pieces(middle_whole[i]),
            whole_pieces(middle_whole[1]) if i != 1 else [], [x_terms[i], base[i]], [size] * planes, forcing,
            f"y_second_{i}",
        )

    ends = [None] * 3
    ends[1] = second_step(1)
    x_terms[0] = along_x([piece(after(middle[0], ends[1]))], [], along_x_matrix, "x_second_0")
    middle_whole[2] = gathered(middle[2])
    middle_whole[0] = after(middle_whole[0], x_terms[0])
    ends[0] = second_step(0)
    x_terms[2] = along_x([piece(after(middle[2], ends[0]))], [piece(middle[0])], along_x_matrix, "x_second_2")
    middle_whole[2] = after(middle_whole[2], x_terms[2])
    ends[2] = second_step(2)

    out = jnp.zeros(velocity.shape, F32)
    for i in (1, 0, 2):
        for d, block in enumerate(ends[i]):
            block = swap(block, d * group) if d else block
            out = lax.dynamic_update_slice(out, block[None, None], (i, plane ^ d, 0, 0))
    return out


def solution(mesh):
    placed = (P(None, "groups", "row", None), P(), P())
    return jax.shard_map(
        on_device,
        mesh=mesh,
        in_specs=placed,
        out_specs=P(None, "groups", "row", None),
        check_vma=False,
    )
```

time: 294 us -> 301 us (1.024)
  starting transfers between devices: 42.7 us -> 24.1 us
  between operations: 1.84 us -> 15.1 us
  local copies, waits for them, and re-layouts: 10.1 us -> 21.3 us
  waiting for transfers between devices: 119 us -> 111 us
  Pallas kernels: 110 us -> 117 us
    ppermute x43 -> x22, waiting for transfers between devices: 119 us -> 64.6 us  [swap(): return lax.ppermute(x, 'row', [(r, r ^ distance) for r in range(devices)])]
    all_gather x0 -> x6, waiting for transfers between devices: none -> 45.7 us  [gathered(): return lax.all_gather(x, 'row', axis_index_groups=members, axis=0)]
    ppermute x43 -> x22, starting transfers between devices: 42.7 us -> 23.7 us  [swap(): return lax.ppermute(x, 'row', [(r, r ^ distance) for r in range(devices)])]
    dynamic_update_slice x11, local copies, waits for them, and re-layouts: 0.93 us -> 10.8 us  [on_device(): out = lax.dynamic_update_slice(out, block[None, None], (i, plane ^ d, 0, 0))]
    pallas_call x5, Pallas kernels: 43.9 us -> 47.5 us  [y_call(): pl.pallas_call(functools.partial(kernel, (len(own), len(fields), len(carr...]
    unnamed x48 -> x24, local copies, waits for them, and re-layouts: 8.75 us -> 8.34 us
  transfers between devices with their start and end apart: 43 -> 28, of which waited for: 23 -> 16; matrix products, arithmetic and copies ran while one was open for 1% -> 5% of each run, Pallas kernels for 37% -> 38%
where the time goes in v4:
time: 301 us; the launch traced here: 299 us
  Pallas kernels  117 us (39%)
  waiting for transfers between devices  111 us (37%)
  starting transfers between devices  24.1 us (8%)
  local copies, waits for them, and re-layouts  21.3 us (7%)
  between operations  15.1 us (5%)
  other arithmetic  10.8 us (4%)
    ppermute x22, waiting for transfers between devices, swap(): return lax.ppermute(x, 'row', [(r, r ^ distance) for r in range(devices)])  64.6 us
    pallas_call x6, Pallas kernels, along_x(): pl.pallas_call(functools.partial(along_x_kernel, (len(fields), len(carrie...  50.2 us
    pallas_call x5, Pallas kernels, y_call(): pl.pallas_call(functools.partial(kernel, (len(own), len(fields), len(carr...  47.5 us
    all_gather x6, waiting for transfers between devices, gathered(): return lax.all_gather(x, 'row', axis_index_groups=members, axis=0)  45.7 us
    ppermute x22, starting transfers between devices, swap(): return lax.ppermute(x, 'row', [(r, r ^ distance) for r in range(devices)])  23.7 us
    pallas_call x1, Pallas kernels, prepare_matrices(): pl.pallas_call(functools.partial(matrices_kernel, count), grid_spec=pltpu...  13.5 us
    dynamic_update_slice x11, local copies, waits for them, and re-layouts, on_device(): out = lax.dynamic_update_slice(out, block[None, None], (i, plane ^ d, 0, 0))  10.8 us
    pallas_call x1, other arithmetic, y_call(): pl.pallas_call(functools.partial(kernel, (len(own), len(fields), len(carr...  8.51 us
  transfers between devices with their start and end apart: 28, of which 16 were waited for; matrix products, arithmetic and copies ran while one was open for 5% of the time, Pallas kernels for 38%

profile of v4, /device:TPU:18, one launch (start us, length us, event | category | flops | bytes accessed | tf_op | source)
XLA Modules:
  0.0 299.0 jit_solution(13468554743446216707)
XLA Ops:
  6.5 2.3 pack.1
  14.6 13.5 %shard_map.37 = (bf16[4,1024,1024]{2,1,0:T(8,128)(2,1)}, bf16[4,256,1024]{2,1,0:T(8,128)(2,1)S(1)}) custom-call(s32[16]{0:T(128)S(1)} %stack.82.order_ref, s32[4]{0:T(128)S(1)} %pad_add_fusion.own_ref, f32[1024,1024]{1,0:T(8,128)} %refs_4_.1, f32[1024,1024]{1,0:T(8,128)} %refs_4_.1, f32[1024,1024]{1,0:T(8,128)} %refs_5_.1, f32[1024,1024]{1,0:T(8,128)} %refs_5_.1, ...), custom_call_target="tpu_custom_call" | custom-call | flops 17179869184 | bytes 33554432 | tf_op jit(solution)/shard_map/pallas_call | solution.py:63
  29.5 3.5 %collective-permute-done.1.refs_2_ = f32[72,1024]{1,0:T(8,128)S(1)} collective-permute-done((f32[72,1024]{1,0:T(8,128)S(1)}, f32[72,1024]{1,0:T(8,128)S(1)}, u32[]{:S(2)}, u32[]{:S(2)}) %collective-permute-start.1) | collective-permute-done | bytes 294944 | tf_op jit(solution)/shard_map/ppermute | solution.py:284
  32.9 6.9 %collective-permute-done.2.refs_3_ = f32[72,1024]{1,0:T(8,128)S(1)} collective-permute-done((f32[72,1024]{1,0:T(8,128)S(1)}, f32[72,1024]{1,0:T(8,128)S(1)}, u32[]{:S(2)}, u32[]{:S(2)}) %collective-permute-start.2) | collective-permute-done | bytes 294944 | tf_op jit(solution)/shard_map/ppermute | solution.py:284
  41.1 1.9 collective-permute-start.4
  44.6 6.0 %collective-permute-done.3.refs_1_ = f32[64,1024]{1,0:T(8,128)S(1)} collective-permute-done((f32[64,1024]{1,0:T(8,128)}, f32[64,1024]{1,0:T(8,128)S(1)}, u32[]{:S(2)}, u32[]{:S(2)}) %collective-permute-start.3) | collective-permute-done | bytes 262176 | tf_op jit(solution)/shard_map/ppermute | solution.py:284
  50.5 10.8 %collective-permute-done.4.refs_2_ = f32[64,1024]{1,0:T(8,128)S(1)} collective-permute-done((f32[64,1024]{1,0:T(8,128)}, f32[64,1024]{1,0:T(8,128)S(1)}, u32[]{:S(2)}, u32[]{:S(2)}) %collective-permute-start.4) | collective-permute-done | bytes 262176 | tf_op jit(solution)/shard_map/ppermute | solution.py:284
  61.3 5.0 %collective-permute-done.5.refs_3_ = f32[64,1024]{1,0:T(8,128)S(1)} collective-permute-done((f32[64,1024]{1,0:T(8,128)S(1)}, f32[64,1024]{1,0:T(8,128)S(1)}, u32[]{:S(2)}, u32[]{:S(2)}) %collective-permute-start.5) | collective-permute-done | bytes 262176 | tf_op jit(solution)/shard_map/ppermute | solution.py:284
  71.0 8.5 %x_first_1.1.refs_6_ = f32[256,1024]{1,0:T(8,128)S(1)} custom-call(f32[264,1024]{1,0:T(8,128)} %join.3.refs_0_.refs_1_, f32[256,1024]{1,0:T(8,128)} %join.4.refs_1_.refs_0_, bf16[4,1024,1024]{2,1,0:T(8,128)(2,1)} %get-tuple-element.62.refs_2_.refs_1_), custom_call_target="tpu_custom_call" | custom-call | flops 9663676416 | bytes 1048576 | tf_op jit(solution)/shard_map/x_first_1/pallas_call | solution.py:186
  81.9 8.9 %y_first_1.1 = (f32[256,1024]{1,0:T(8,128)}, f32[256,1024]{1,0:T(8,128)S(1)}, f32[8,1024]{1,0:T(8,128)S(1)}) custom-call(f32[1,1]{1,0:T(1,128)} %bitcast.22.forcing_ref, bf16[4,256,1024]{2,1,0:T(8,128)(2,1)} %copy-done, f32[264,1024]{1,0:T(8,128)} %join.3.refs_0_.refs_1_, f32[264,1024]{1,0:T(8,128)} %join.3.refs_0_.refs_1_, f32[4,264,1024]{2,1,0:T(8,128)} %bitcast.56, ...), custom_call_target="tpu_custom_call" | custom-call | flops 9663676416 | bytes 1048576 | tf_op jit(solution)/shard_map/y_first_1/pallas_call | solution.py:251
  91.7 8.2 %x_first_0.1.refs_10_ = f32[256,1024]{1,0:T(8,128)S(1)} custom-call(f32[256,1024]{1,0:T(8,128)} %join.4.refs_1_.refs_0_, bf16[4,1024,1024]{2,1,0:T(8,128)(2,1)} %get-tuple-element.62.refs_2_.refs_1_), custom_call_target="tpu_custom_call" | custom-call | flops 9663676416 | bytes 1048576 | tf_op jit(solution)/shard_map/x_first_0/pallas_call | solution.py:186
  102.6 9.8 %all-gather.15.cloned.1.call-done = f32[1024,1024]{1,0:T(8,128)} async-done(((f32[256,1024]{1,0:T(8,128)}), f32[1024,1024]{1,0:T(8,128)}) %all-gather.15.cloned.1.call-update) | async-done | bytes 4194320 | tf_op jit(solution)/shard_map/all_gather | solution.py:303
  112.5 10.1 %y_first_0.1 = (f32[256,1024]{1,0:T(8,128)}, f32[256,1024]{1,0:T(8,128)S(1)}, f32[8,1024]{1,0:T(8,128)S(1)}) custom-call(f32[1,1]{1,0:T(1,128)} %bitcast.22.forcing_ref, bf16[4,256,1024]{2,1,0:T(8,128)(2,1)} %copy-done, f32[256,1024]{1,0:T(8,128)} %join.4.refs_1_.refs_0_, f32[264,1024]{1,0:T(8,128)} %join.3.refs_0_.refs_1_, f32[4,256,1024]{2,1,0:T(8,128)} %bitcast.68, ...), custom_call_target="tpu_custom_call" | custom-call | flops 9663676416 | bytes 1048576 | tf_op jit(solution)/shard_map/y_first_0/pallas_call | solution.py:251
  123.8 8.5 %x_first_2.1.refs_10_ = f32[256,1024]{1,0:T(8,128)S(1)} custom-call(f32[256,1024]{1,0:T(8,128)} %join.5.refs_0_, f32[256,1024]{1,0:T(8,128)} %join.4.refs_1_.refs_0_, bf16[4,1024,1024]{2,1,0:T(8,128)(2,1)} %get-tuple-element.62.refs_2_.refs_1_), custom_call_target="tpu_custom_call" | custom-call | flops 9663676416 | bytes 1048576 | tf_op jit(solution)/shard_map/x_first_2/pallas_call | solution.py:186
  133.3 15.2 %all-gather.17.cloned.1.call-done = f32[1024,1024]{1,0:T(8,128)} async-done(((f32[256,1024]{1,0:T(8,128)}), f32[1024,1024]{1,0:T(8,128)}) %all-gather.17.cloned.1.call-update) | async-done | bytes 4194320 | tf_op jit(solution)/shard_map/all_gather | solution.py:303
  148.5 10.1 %y_first_2.1 = (f32[256,1024]{1,0:T(8,128)}, f32[256,1024]{1,0:T(8,128)S(1)}, f32[8,1024]{1,0:T(8,128)S(1)}) custom-call(f32[1,1]{1,0:T(1,128)} %bitcast.22.forcing_ref, bf16[4,256,1024]{2,1,0:T(8,128)(2,1)} %copy-done, f32[256,1024]{1,0:T(8,128)} %join.5.refs_0_, f32[264,1024]{1,0:T(8,128)} %join.3.refs_0_.refs_1_, f32[4,256,1024]{2,1,0:T(8,128)} %bitcast.72, ...), custom_call_target="tpu_custom_call" | custom-call | flops 9663676416 | bytes 1048576 | tf_op jit(solution)/shard_map/y_first_2/pallas_call | solution.py:251
  160.2 2.1 collective-permute-done.9
  162.8 4.0 %collective-permute-done.10 = f32[8,128]{1,0:T(8,128)S(1)} collective-permute-done((f32[8,128]{1,0:T(8,128)S(1)}, f32[8,128]{1,0:T(8,128)S(1)}, u32[]{:S(2)}, u32[]{:S(2)}) %collective-permute-start.10) | collective-permute-done | bytes 4128 | tf_op jit(solution)/shard_map/ppermute | solution.py:284
  168.5 8.5 %x_second_1.1.refs_6_ = f32[256,1024]{1,0:T(8,128)S(1)} custom-call(f32[256,1024]{1,0:T(8,128)} %get-tuple-element.89.refs_0_.refs_1_, f32[256,1024]{1,0:T(8,128)} %get-tuple-element.96.refs_1_.refs_0_, bf16[4,1024,1024]{2,1,0:T(8,128)(2,1)} %get-tuple-element.62.refs_2_.refs_1_), custom_call_target="tpu_custom_call" | custom-call | flops 9663676416 | bytes 1048576 | tf_op jit(solution)/shard_map/x_second_1/pallas_call | solution.py:186
  177.0 7.6 %all-gather.19.cloned.1.call-done = f32[1024,1024]{1,0:T(8,128)} async-done(((f32[256,1024]{1,0:T(8,128)}), f32[1024,1024]{1,0:T(8,128)}) %all-gather.19.cloned.1.call-update) | async-done | bytes 4194320 | tf_op jit(solution)/shard_map/all_gather | solution.py:303
  185.9 8.9 %y_second_1.1 = (f32[64,1024]{1,0:T(8,128)S(1)}, f32[64,1024]{1,0:T(8,128)}, f32[64,1024]{1,0:T(8,128)}, f32[64,1024]{1,0:T(8,128)}) custom-call(f32[1,1]{1,0:T(1,128)} %bitcast.26.forcing_ref, bf16[4,256,1024]{2,1,0:T(8,128)(2,1)} %copy-done, f32[256,1024]{1,0:T(8,128)} %get-tuple-element.89.refs_0_.refs_1_, f32[256,1024]{1,0:T(8,128)} %get-tuple-element.89.refs_0_.refs_1_, ...), custom_call_target="tpu_custom_call" | custom-call | flops 9663676416 | bytes 1048576 | tf_op jit(solution)/shard_map/y_second_1/pallas_call | solution.py:251
  198.3 8.1 %x_second_0.1.refs_10_ = f32[256,1024]{1,0:T(8,128)S(1)} custom-call(f32[256,1024]{1,0:T(8,128)} %get-tuple-element.96.refs_1_.refs_0_, bf16[4,1024,1024]{2,1,0:T(8,128)(2,1)} %get-tuple-element.62.refs_2_.refs_1_), custom_call_target="tpu_custom_call" | custom-call | flops 9663676416 | bytes 1048576 | tf_op jit(solution)/shard_map/x_second_0/pallas_call | solution.py:186
  207.4 13.1 %all-gather.21.cloned.1.call-done = f32[1024,1024]{1,0:T(8,128)} async-done(((f32[256,1024]{1,0:T(8,128)}), f32[1024,1024]{1,0:T(8,128)}) %all-gather.21.cloned.1.call-update) | async-done | bytes 4194320 | tf_op jit(solution)/shard_map/all_gather | solution.py:303
  220.5 9.5 %y_second_0.1 = (f32[64,1024]{1,0:T(8,128)S(1)}, f32[64,1024]{1,0:T(8,128)S(1)}, f32[64,1024]{1,0:T(8,128)S(1)}, f32[64,1024]{1,0:T(8,128)S(1)}) custom-call(f32[1,1]{1,0:T(1,128)} %bitcast.26.forcing_ref, bf16[4,256,1024]{2,1,0:T(8,128)(2,1)} %copy-done, f32[256,1024]{1,0:T(8,128)} %get-tuple-element.96.refs_1_.refs_0_, ...), custom_call_target="tpu_custom_call" | custom-call | flops 9663676416 | bytes 1048576 | tf_op jit(solution)/shard_map/y_second_0/pallas_call | solution.py:251
  232.1 8.4 %x_second_2.1 = f32[256,1024]{1,0:T(8,128)S(1)} custom-call(f32[256,1024]{1,0:T(8,128)} %get-tuple-element.104.refs_0_, f32[256,1024]{1,0:T(8,128)} %get-tuple-element.96.refs_1_.refs_0_, bf16[4,1024,1024]{2,1,0:T(8,128)(2,1)} %get-tuple-element.62.refs_2_.refs_1_), custom_call_target="tpu_custom_call" | custom-call | flops 9663676416 | bytes 1048576 | tf_op jit(solution)/shard_map/x_second_2/pallas_call | solution.py:186
  240.6 2.1 broadcast_in_dim.39
  252.1 4.9 %collective-permute-done.18 = f32[64,1024]{1,0:T(8,128)S(1)} collective-permute-done((f32[64,1024]{1,0:T(8,128)S(1)}, f32[64,1024]{1,0:T(8,128)S(1)}, u32[]{:S(2)}, u32[]{:S(2)}) %collective-permute-start.18) | collective-permute-done | bytes 262176 | tf_op jit(solution)/shard_map/ppermute | solution.py:284
  257.7 8.5 %y_second_2.1 = (f32[3,4,64,1024]{3,2,1,0:T(8,128)}, f32[64,1024]{1,0:T(8,128)S(1)}, f32[64,1024]{1,0:T(8,128)S(1)}, f32[64,1024]{1,0:T(8,128)S(1)}) fusion(f32[3,4,64,1024]{3,2,1,0:T(8,128)} %bitcast_dynamic-update-slice_fusion.4, s32[]{:T(128)S(6)} %select_n.33, f32[1,1]{1,0:T(1,128)} %bitcast.26.forcing_ref, bf16[4,256,1024]{2,1,0:T(8,128)(2,1)S(1)} %copy-done.1, ...), kind=kCustom, calls=%fused_computation.3 | custom fusion | flops 9663676416 | bytes 15729156 | tf_op jit(solution)/shard_map/y_second_2/pallas_call | solution.py:251
  266.4 2.7 collective-permute-start.20
  269.7 7.0 %collective-permute-done.19 = f32[64,1024]{1,0:T(8,128)S(1)} collective-permute-done((f32[64,1024]{1,0:T(8,128)S(1)}, f32[64,1024]{1,0:T(8,128)S(1)}, u32[]{:S(2)}, u32[]{:S(2)}) %collective-permute-start.19) | collective-permute-done | bytes 262176 | tf_op jit(solution)/shard_map/ppermute | solution.py:284
  277.4 9.7 %collective-permute-done.20 = f32[64,1024]{1,0:T(8,128)S(1)} collective-permute-done((f32[64,1024]{1,0:T(8,128)S(1)}, f32[64,1024]{1,0:T(8,128)S(1)}, u32[]{:S(2)}, u32[]{:S(2)}) %collective-permute-start.20) | collective-permute-done | bytes 262176 | tf_op jit(solution)/shard_map/ppermute | solution.py:284
  287.8 3.6 %collective-permute-done.21 = f32[64,1024]{1,0:T(8,128)S(1)} collective-permute-done((f32[64,1024]{1,0:T(8,128)S(1)}, f32[64,1024]{1,0:T(8,128)S(1)}, u32[]{:S(2)}, u32[]{:S(2)}) %collective-permute-start.21) | collective-permute-done | bytes 262176 | tf_op jit(solution)/shard_map/ppermute | solution.py:284
  (91 shorter events, 46.0 us)
Async XLA Ops:
  6.5 73.0 %all-gather.13.cloned.1.call-start = ((), (), s32[]{:S(2)}) async-start(), calls=%async_computation | async-start | bytes 5406720 | tf_op jit(solution)/shard_map/all_gather | solution.py:303
  10.9 18.5 %collective-permute-start = (f32[72,1024]{1,0:T(8,128)S(1)}, f32[72,1024]{1,0:T(8,128)S(1)}, u32[]{:S(2)}, u32[]{:S(2)}) collective-permute-start(f32[72,1024]{1,0:T(8,128)S(1)} %get-tuple-element.59), channel_id=1, source_target_pairs={{0,4},{1,5},{2,6},{3,7},{4,0},{5,1},{6,2},{7,3},{8,12},{9,13},{10,... | collective-permute-start | bytes 884744 | tf_op jit(solution)/shard_map/ppermute | solution.py:284
  12.5 20.4 %collective-permute-start.1 = (f32[72,1024]{1,0:T(8,128)S(1)}, f32[72,1024]{1,0:T(8,128)S(1)}, u32[]{:S(2)}, u32[]{:S(2)}) collective-permute-start(f32[72,1024]{1,0:T(8,128)S(1)} %get-tuple-element.60), channel_id=1, source_target_pairs={{0,8},{1,9},{2,10},{3,11},{4,12},{5,13},{6,14},{7,15},{8,0},{9,1},... | collective-permute-start | bytes 884744 | tf_op jit(solution)/shard_map/ppermute | solution.py:284
  12.9 27.0 %collective-permute-start.2 = (f32[72,1024]{1,0:T(8,128)S(1)}, f32[72,1024]{1,0:T(8,128)S(1)}, u32[]{:S(2)}, u32[]{:S(2)}) collective-permute-start(f32[72,1024]{1,0:T(8,128)S(1)} %get-tuple-element.61), channel_id=1, source_target_pairs={{0,12},{1,13},{2,14},{3,15},{4,8},{5,9},{6,10},{7,11},{8,4},{9,5},... | collective-permute-start | bytes 884744 | tf_op jit(solution)/shard_map/ppermute | solution.py:284
  28.2 1.3 copy-start
  29.5 13.5 %copy-start.7 = (f32[64,1024]{1,0:T(8,128)S(1)}, f32[64,1024]{1,0:T(8,128)}, u32[]{:S(2)}) copy-start(f32[64,1024]{1,0:T(8,128)} %copy-done.6) | copy-start | bytes 786436
  41.0 71.5 %all-gather.15.cloned.1.call-start = ((), (), s32[]{:S(2)}) async-start(), calls=%async_computation.1 | async-start | bytes 5242880 | tf_op jit(solution)/shard_map/all_gather | solution.py:303
  41.0 9.5 %collective-permute-start.3 = (f32[64,1024]{1,0:T(8,128)}, f32[64,1024]{1,0:T(8,128)S(1)}, u32[]{:S(2)}, u32[]{:S(2)}) collective-permute-start(f32[64,1024]{1,0:T(8,128)} %copy-done.9), channel_id=1, source_target_pairs={{0,4},{1,5},{2,6},{3,7},{4,0},{5,1},{6,2},{7,3},{8,12},{9,13},{10,... | collective-permute-start | bytes 786440 | tf_op jit(solution)/shard_map/ppermute | solution.py:284
  41.1 20.2 %collective-permute-start.4 = (f32[64,1024]{1,0:T(8,128)}, f32[64,1024]{1,0:T(8,128)S(1)}, u32[]{:S(2)}, u32[]{:S(2)}) collective-permute-start(f32[64,1024]{1,0:T(8,128)} %copy-done.8), channel_id=1, source_target_pairs={{0,8},{1,9},{2,10},{3,11},{4,12},{5,13},{6,14},{7,15},{8,0},{9,1},... | collective-permute-start | bytes 786440 | tf_op jit(solution)/shard_map/ppermute | solution.py:284
  43.0 23.3 %collective-permute-start.5 = (f32[64,1024]{1,0:T(8,128)S(1)}, f32[64,1024]{1,0:T(8,128)S(1)}, u32[]{:S(2)}, u32[]{:S(2)}) collective-permute-start(f32[64,1024]{1,0:T(8,128)S(1)} %copy-done.7), channel_id=1, source_target_pairs={{0,12},{1,13},{2,14},{3,15},{4,8},{5,9},{6,10},{7,11},{8,4},{9,5},... | collective-permute-start | bytes 786440 | tf_op jit(solution)/shard_map/ppermute | solution.py:284
  67.4 81.1 %all-gather.17.cloned.1.call-start = ((), (), s32[]{:S(2)}) async-start(), calls=%async_computation.2 | async-start | bytes 5242880 | tf_op jit(solution)/shard_map/all_gather | solution.py:303
  67.4 33.5 %collective-permute-start.6 = (f32[64,1024]{1,0:T(8,128)S(1)}, f32[64,1024]{1,0:T(8,128)S(1)}, u32[]{:S(2)}, u32[]{:S(2)}) collective-permute-start(f32[64,1024]{1,0:T(8,128)S(1)} %get-tuple-element.73), channel_id=1, source_target_pairs={{0,4},{1,5},{2,6},{3,7},{4,0},{5,1},{6,2},{7,3},{8,12},{9,13},{10,... | collective-permute-start | bytes 786440 | tf_op jit(solution)/shard_map/ppermute | solution.py:284
  67.5 33.4 %collective-permute-start.7 = (f32[64,1024]{1,0:T(8,128)S(1)}, f32[64,1024]{1,0:T(8,128)S(1)}, u32[]{:S(2)}, u32[]{:S(2)}) collective-permute-start(f32[64,1024]{1,0:T(8,128)S(1)} %get-tuple-element.74), channel_id=1, source_target_pairs={{0,8},{1,9},{2,10},{3,11},{4,12},{5,13},{6,14},{7,15},{8,0},{9,1},... | collective-permute-start | bytes 786440 | tf_op jit(solution)/shard_map/ppermute | solution.py:284
  69.4 31.5 %collective-permute-start.8 = (f32[64,1024]{1,0:T(8,128)S(1)}, f32[64,1024]{1,0:T(8,128)S(1)}, u32[]{:S(2)}, u32[]{:S(2)}) collective-permute-start(f32[64,1024]{1,0:T(8,128)S(1)} %get-tuple-element.75), channel_id=1, source_target_pairs={{0,12},{1,13},{2,14},{3,15},{4,8},{5,9},{6,10},{7,11},{8,4},{9,5},... | collective-permute-start | bytes 786440 | tf_op jit(solution)/shard_map/ppermute | solution.py:284
  102.0 82.5 %all-gather.19.cloned.1.call-start = ((), (), s32[]{:S(2)}) async-start(), calls=%async_computation.3 | async-start | bytes 5242880 | tf_op jit(solution)/shard_map/all_gather | solution.py:303
  102.6 117.9 %all-gather.21.cloned.1.call-start = ((), (), s32[]{:S(2)}) async-start(), calls=%async_computation.4 | async-start | bytes 5242880 | tf_op jit(solution)/shard_map/all_gather | solution.py:303
  123.5 134.1 %all-gather.23.cloned.1.call-start = ((), (), s32[]{:S(2)}) async-start(), calls=%async_computation.5 | async-start | bytes 5242880 | tf_op jit(solution)/shard_map/all_gather | solution.py:303
  158.6 3.7 %collective-permute-start.9 = (f32[8,128]{1,0:T(8,128)S(1)}, f32[8,128]{1,0:T(8,128)S(1)}, u32[]{:S(2)}, u32[]{:S(2)}) collective-permute-start(f32[8,128]{1,0:T(8,128)S(1)} %bitcast_reduce_fusion), channel_id=1, source_target_pairs={{0,4},{1,5},{2,6},{3,7},{4,0},{5,1},{6,2},{7,3},{8,12},{9,13},{10,... | collective-permute-start | bytes 12296 | tf_op jit(solution)/shard_map/ppermute | solution.py:284
  162.3 4.5 %collective-permute-start.10 = (f32[8,128]{1,0:T(8,128)S(1)}, f32[8,128]{1,0:T(8,128)S(1)}, u32[]{:S(2)}, u32[]{:S(2)}) collective-permute-start(f32[8,128]{1,0:T(8,128)S(1)} %add.110), channel_id=1, source_target_pairs={{0,8},{1,9},{2,10},{3,11},{4,12},{5,13},{6,14},{7,15},{8,0},{9,1},... | collective-permute-start | bytes 12296 | tf_op jit(solution)/shard_map/ppermute | solution.py:284
  166.8 1.2 collective-permute-start.11
  168.0 16.6 %collective-permute-start.12 = (f32[8,128]{1,0:T(8,128)S(1)}, f32[8,128]{1,0:T(8,128)S(1)}, u32[]{:S(2)}, u32[]{:S(2)}) collective-permute-start(f32[8,128]{1,0:T(8,128)S(1)} %add.112), channel_id=1, source_target_pairs={{0,2},{1,3},{2,0},{3,1},{4,6},{5,7},{6,4},{7,5},{8,10},{9,11},{10,... | collective-permute-start | bytes 12296 | tf_op jit(solution)/shard_map/ppermute | solution.py:284
  194.8 48.6 %collective-permute-start.13 = (f32[64,1024]{1,0:T(8,128)}, f32[64,1024]{1,0:T(8,128)}, u32[]{:S(2)}, u32[]{:S(2)}) collective-permute-start(f32[64,1024]{1,0:T(8,128)} %get-tuple-element.93), channel_id=1, source_target_pairs={{0,4},{1,5},{2,6},{3,7},{4,0},{5,1},{6,2},{7,3},{8,12},{9,13},{10,... | collective-permute-start | bytes 786440 | tf_op jit(solution)/shard_map/ppermute | solution.py:284
  196.3 50.3 %collective-permute-start.14 = (f32[64,1024]{1,0:T(8,128)}, f32[64,1024]{1,0:T(8,128)}, u32[]{:S(2)}, u32[]{:S(2)}) collective-permute-start(f32[64,1024]{1,0:T(8,128)} %get-tuple-element.94), channel_id=1, source_target_pairs={{0,8},{1,9},{2,10},{3,11},{4,12},{5,13},{6,14},{7,15},{8,0},{9,1},... | collective-permute-start | bytes 786440 | tf_op jit(solution)/shard_map/ppermute | solution.py:284
  196.8 51.4 %collective-permute-start.15 = (f32[64,1024]{1,0:T(8,128)}, f32[64,1024]{1,0:T(8,128)}, u32[]{:S(2)}, u32[]{:S(2)}) collective-permute-start(f32[64,1024]{1,0:T(8,128)} %get-tuple-element.95), channel_id=1, source_target_pairs={{0,12},{1,13},{2,14},{3,15},{4,8},{5,9},{6,10},{7,11},{8,4},{9,5},... | collective-permute-start | bytes 786440 | tf_op jit(solution)/shard_map/ppermute | solution.py:284
  230.0 20.6 %collective-permute-start.16 = (f32[64,1024]{1,0:T(8,128)S(1)}, f32[64,1024]{1,0:T(8,128)S(1)}, u32[]{:S(2)}, u32[]{:S(2)}) collective-permute-start(f32[64,1024]{1,0:T(8,128)S(1)} %get-tuple-element.100), channel_id=1, source_target_pairs={{0,4},{1,5},{2,6},{3,7},{4,0},{5,1},{6,2},{7,3},{8,12},{9,13},{10,... | collective-permute-start | bytes 786440 | tf_op jit(solution)/shard_map/ppermute | solution.py:284
  231.6 19.8 %collective-permute-start.17 = (f32[64,1024]{1,0:T(8,128)S(1)}, f32[64,1024]{1,0:T(8,128)S(1)}, u32[]{:S(2)}, u32[]{:S(2)}) collective-permute-start(f32[64,1024]{1,0:T(8,128)S(1)} %get-tuple-element.101), channel_id=1, source_target_pairs={{0,8},{1,9},{2,10},{3,11},{4,12},{5,13},{6,14},{7,15},{8,0},{9,1},... | collective-permute-start | bytes 786440 | tf_op jit(solution)/shard_map/ppermute | solution.py:284
  240.6 10.8 %copy-start.11 = (f32[256,1024]{1,0:T(8,128)}, f32[256,1024]{1,0:T(8,128)S(1)}, u32[]{:S(2)}) copy-start(f32[256,1024]{1,0:T(8,128)S(1)} %x_second_2.1) | copy-start | bytes 3145732
  240.6 17.1 %copy-start.1 = (bf16[4,256,1024]{2,1,0:T(8,128)(2,1)S(1)}, bf16[4,256,1024]{2,1,0:T(8,128)(2,1)}, u32[]{:S(2)}) copy-start(bf16[4,256,1024]{2,1,0:T(8,128)(2,1)} %copy-done) | copy-start | bytes 6291460
  243.4 13.6 %collective-permute-start.18 = (f32[64,1024]{1,0:T(8,128)S(1)}, f32[64,1024]{1,0:T(8,128)S(1)}, u32[]{:S(2)}, u32[]{:S(2)}) collective-permute-start(f32[64,1024]{1,0:T(8,128)S(1)} %get-tuple-element.102), channel_id=1, source_target_pairs={{0,12},{1,13},{2,14},{3,15},{4,8},{5,9},{6,10},{7,11},{8,4},{9,5},... | collective-permute-start | bytes 786440 | tf_op jit(solution)/shard_map/ppermute | solution.py:284
  266.2 10.5 %collective-permute-start.19 = (f32[64,1024]{1,0:T(8,128)S(1)}, f32[64,1024]{1,0:T(8,128)S(1)}, u32[]{:S(2)}, u32[]{:S(2)}) collective-permute-start(f32[64,1024]{1,0:T(8,128)S(1)} %get-tuple-element.114), channel_id=1, source_target_pairs={{0,4},{1,5},{2,6},{3,7},{4,0},{5,1},{6,2},{7,3},{8,12},{9,13},{10,... | collective-permute-start | bytes 786440 | tf_op jit(solution)/shard_map/ppermute | solution.py:284
  266.4 20.7 %collective-permute-start.20 = (f32[64,1024]{1,0:T(8,128)S(1)}, f32[64,1024]{1,0:T(8,128)S(1)}, u32[]{:S(2)}, u32[]{:S(2)}) collective-permute-start(f32[64,1024]{1,0:T(8,128)S(1)} %get-tuple-element.116), channel_id=1, source_target_pairs={{0,8},{1,9},{2,10},{3,11},{4,12},{5,13},{6,14},{7,15},{8,0},{9,1},... | collective-permute-start | bytes 786440 | tf_op jit(solution)/shard_map/ppermute | solution.py:284
  269.1 22.3 %collective-permute-start.21 = (f32[64,1024]{1,0:T(8,128)S(1)}, f32[64,1024]{1,0:T(8,128)S(1)}, u32[]{:S(2)}, u32[]{:S(2)}) collective-permute-start(f32[64,1024]{1,0:T(8,128)S(1)} %get-tuple-element.118), channel_id=1, source_target_pairs={{0,12},{1,13},{2,14},{3,15},{4,8},{5,9},{6,10},{7,11},{8,4},{9,5},... | collective-permute-start | bytes 786440 | tf_op jit(solution)/shard_map/ppermute | solution.py:284
  (8 other events, 7.0 us)
Sparse Core Ops, SparseCore 0:
  41.1 35.2 all-gather.12
  77.9 34.4 all-gather.14
  114.0 34.4 all-gather.16
  150.0 34.5 all-gather.18
  186.0 34.4 all-gather.20
  221.9 34.4 all-gather.22

commit v5 on v4

v5 whole, which is shorter than its diff:
```python
import functools

import jax
import jax.numpy as jnp
from jax import lax
from jax.experimental import pallas as pl
from jax.experimental.pallas import tpu as pltpu
from jax.sharding import PartitionSpec as P

viscosity = 0.2
power_input = 2.0
time_step = 0.5
first_weight = 8.0 / 15.0
second_weight = 5.0 / 12.0
back_weight = 17.0 / 60.0

BF16 = jnp.bfloat16
F32 = jnp.float32
VMEM_BYTES = 50 * 1024 * 1024


def halves(x):
    high = x.astype(BF16)
    return high, (x - high.astype(F32)).astype(BF16)


def product(a, b):
    return jnp.dot(a, b, preferred_element_type=F32)


def params():
    return pltpu.CompilerParams(vmem_limit_bytes=VMEM_BYTES)


def matrices_kernel(count, order_ref, own_ref, *refs):
    slope_parts, curve_parts = refs[:count], refs[count:2 * count]
    slope_ref, curve_ref, along_x_ref, along_y_ref, turned = refs[2 * count:]
    size = slope_parts[0].shape[0]
    for place, ref, scale in ((0, slope_ref, -0.5), (2, curve_ref, viscosity)):
        high, low = halves(ref[...] * scale)
        along_x_ref[place] = high
        along_x_ref[place + 1] = low
    for high_place, low_place, parts, scale in ((1, 0, slope_parts, -0.5), (2, 3, curve_parts, viscosity)):
        turned[...] = jnp.concatenate([part[...] for part in parts], axis=0).T
        for block in range(along_y_ref.shape[1] // size):
            source = pl.ds(pl.multiple_of(own_ref[block] * size, size), size)
            high, low = halves(turned[source, :] * scale)
            along_y_ref[high_place, block * size:(block + 1) * size, :] = high
            along_y_ref[low_place, block * size:(block + 1) * size, :] = low


def prepare_matrices(order, own, slope_matrix, curve_matrix, size):
    length = slope_matrix.shape[0]
    width = min(128, length)
    count = width // size
    kept = own.shape[0] * size

    def part(place):
        return pl.BlockSpec((size, length), lambda j, order_ref, own_ref: (order_ref[count * j + place], 0))

    parts = [part(place) for place in range(count)]
    straight = pl.BlockSpec((width, length), lambda j, order_ref, own_ref: (j, 0))
    return pl.pallas_call(
        functools.partial(matrices_kernel, count),
        grid_spec=pltpu.PrefetchScalarGridSpec(
            num_scalar_prefetch=2,
            grid=(length // width,),
            in_specs=parts + parts + [straight, straight],
            out_specs=[
                pl.BlockSpec((4, width, length), lambda j, order_ref, own_ref: (0, j, 0)),
                pl.BlockSpec((4, kept, width), lambda j, order_ref, own_ref: (0, 0, j)),
            ],
            scratch_shapes=[pltpu.VMEM((length, width), F32)],
        ),
        out_shape=[
            jax.ShapeDtypeStruct((4, length, length), BF16),
            jax.ShapeDtypeStruct((4, kept, length), BF16),
        ],
        compiler_params=params(),
        cost_estimate=pl.CostEstimate(flops=16 * length ** 3, bytes_accessed=32 * length * length, transcendentals=0),
    )(order, own, *([slope_matrix] * count), *([curve_matrix] * count), slope_matrix, curve_matrix)


def piece_spec(piece, width, column):
    _, place, rows = piece
    return pl.BlockSpec((rows, width), lambda n: (place, column(n)))


def joined(refs, columns=slice(None)):
    return jnp.concatenate([ref[:, columns] for ref in refs], axis=0)


def cut(refs, counts):
    pieces, start = [], 0
    for count in counts:
        pieces.append(refs[start:start + count])
        start += count
    return *pieces, refs[start:]


def pack_kernel(plane_ref, velocity_ref, *block_refs):
    components, planes, size, length = velocity_ref.shape
    plane = plane_ref[0]
    velocity = velocity_ref[...].reshape(components * planes * size // 8, 8, length)
    squares = jnp.sum(velocity * velocity, axis=0)
    for d, ref in enumerate(block_refs):
        for i in range(components):
            ref[i * size:(i + 1) * size, :] = velocity_ref[i, plane ^ d]
        ref[components * size:, :] = squares


def pack(plane, velocity):
    components, planes, size, length = velocity.shape
    shape = (components * size + 8, length)
    return pl.pallas_call(
        pack_kernel,
        grid_spec=pltpu.PrefetchScalarGridSpec(
            num_scalar_prefetch=1,
            grid=(1,),
            in_specs=[pl.BlockSpec(velocity.shape, lambda n, plane_ref: (0, 0, 0, 0))],
            out_specs=[pl.BlockSpec(shape, lambda n, plane_ref: (0, 0))] * planes,
        ),
        out_shape=[jax.ShapeDtypeStruct(shape, F32)] * planes,
        compiler_params=params(),
        name="pack",
    )(plane.reshape(1).astype(jnp.int32), velocity)


def along_x_kernel(counts, copies, *refs):
    fields, carriers, (matrix_ref, out_ref, stack) = cut(refs, counts)
    rows = out_ref.shape[0]
    carriers = (carriers or fields) * copies

    @pl.when(pl.program_id(0) == 0)
    def _():
        field = joined(fields)
        high, low = halves(field)
        stack[0:rows] = low
        stack[rows:2 * rows] = high
        high, low = halves(joined(carriers) * field)
        stack[2 * rows:3 * rows] = high
        stack[3 * rows:4 * rows] = low

    tile = out_ref.shape[1]
    columns = pl.ds(pl.multiple_of(pl.program_id(0) * tile, tile), tile)
    a = product(stack[...], matrix_ref[0])
    b = product(stack[rows:3 * rows], matrix_ref[1])
    c = product(stack[0:2 * rows], matrix_ref[2])
    d = product(stack[rows:2 * rows], matrix_ref[3])
    slope = a[0:rows] + a[rows:2 * rows] + b[0:rows]
    rest = a[2 * rows:3 * rows] + a[3 * rows:] + b[rows:] + c[0:rows] + c[rows:] + d
    out_ref[...] = joined(carriers, columns) * slope + rest


def along_x(fields, carriers, matrix, name, weight=36):
    rows, length = sum(piece[2] for piece in fields), fields[0][0].shape[1]
    copies = len(fields) // len(carriers) if carriers else 1
    tile = min(256, length)
    pieces = fields + carriers
    return pl.pallas_call(
        functools.partial(along_x_kernel, (len(fields), len(carriers)), copies),
        grid=(length // tile,),
        in_specs=[piece_spec(piece, length, lambda n: 0) for piece in pieces]
        + [pl.BlockSpec((4, length, tile), lambda n: (0, 0, n))],
        out_specs=pl.BlockSpec((rows, tile), lambda n: (0, n)),
        out_shape=jax.ShapeDtypeStruct((rows, length), F32),
        scratch_shapes=[pltpu.VMEM((4 * rows, length), BF16)],
        compiler_params=params(),
        cost_estimate=pl.CostEstimate(
            flops=weight * rows * length * length, bytes_accessed=4 * rows * length, transcendentals=0
        ),
        name=name,
    )(*[piece[0] for piece in pieces], matrix)


def y_sums(matrix_ref, fields, carriers, sums):
    rows, length = matrix_ref.shape[1:]
    field = joined(fields)
    carrier = joined(carriers) if carriers else field
    field_high, field_low = halves(field)
    flux_high, flux_low = halves(field * carrier)
    matrix = matrix_ref[...].reshape(4 * rows, length)
    a = product(matrix, field_high)
    b = product(matrix[rows:3 * rows], field_low)
    c = product(matrix[0:2 * rows], flux_high)
    d = product(matrix[rows:2 * rows], flux_low)
    slope = a[0:rows] + a[rows:2 * rows] + b[0:rows]
    rest = a[2 * rows:3 * rows] + a[3 * rows:] + b[rows:] + c[0:rows] + c[rows:] + d
    if sums:
        slope, rest = slope + sums[0][...], rest + sums[1][...]
    return slope, rest


def partial_kernel(counts, matrix_ref, *refs):
    fields, carriers, sums, (slope_ref, rest_ref) = cut(refs, counts)
    slope_ref[...], rest_ref[...] = y_sums(matrix_ref, fields, carriers, sums)


def tendency(forcing_ref, field, carrier, x_terms, sums):
    return joined(x_terms) + joined(carrier) * sums[0] + sums[1] + forcing_ref[0, 0] * field


def first_kernel(counts, forcing_ref, matrix_ref, *refs):
    fields, carriers, sums, own, own_carrier, x_terms, (middle_ref, base_ref, square_ref) = cut(refs, counts)
    rows = matrix_ref.shape[1]
    field = joined(own)
    first = tendency(forcing_ref, field, own_carrier, x_terms, y_sums(matrix_ref, fields, carriers, sums))
    middle = field + (time_step * first_weight) * first
    middle_ref[...] = middle
    base_ref[...] = middle - (time_step * back_weight) * first
    square_ref[...] = jnp.sum((middle * middle).reshape(rows // 8, 8, middle.shape[1]), axis=0)


def second_kernel(counts, forcing_ref, matrix_ref, *refs):
    fields, carriers, sums, own, own_carrier, x_terms, (base_ref, *out_refs) = cut(refs, counts)
    field = joined(own)
    second = tendency(forcing_ref, field, own_carrier, x_terms, y_sums(matrix_ref, fields, carriers, sums))
    out = base_ref[...] + (time_step * second_weight) * second
    size = out_refs[0].shape[0]
    for place, out_ref in enumerate(out_refs):
        out_ref[...] = out[place * size:(place + 1) * size]


def y_call(kernel, forcing, matrix, part, groups, out_rows, name, weight=36):
    rows, length = matrix.shape[1], groups[0][0][0].shape[1]
    depth = sum(piece[2] for piece in groups[0])
    tile = min(256, length)
    pieces = [piece for group in groups for piece in group]
    return pl.pallas_call(
        functools.partial(kernel, tuple(len(group) for group in groups[:6])),
        grid=(length // tile,),
        in_specs=[pl.BlockSpec(memory_space=pltpu.SMEM)] * len(forcing)
        + [pl.BlockSpec((4, rows, depth), lambda n: (0, 0, part))]
        + [piece_spec(piece, tile, lambda n: n) for piece in pieces],
        out_specs=[pl.BlockSpec((count, tile), lambda n: (0, n)) for count in out_rows],
        out_shape=[jax.ShapeDtypeStruct((count, length), F32) for count in out_rows],
        compiler_params=params(),
        cost_estimate=pl.CostEstimate(
            flops=weight * rows * depth * length, bytes_accessed=4 * rows * length, transcendentals=0
        ),
        name=name,
    )(*forcing, matrix, *[piece[0] for piece in pieces])


def after(values, *earlier):
    return lax.optimization_barrier((values, earlier))[0]


def on_device(velocity, slope_matrix, curve_matrix):
    components, planes, size, length = velocity.shape
    devices = lax.axis_size("row")
    group = devices // planes
    chips = group // 2
    kept = length // group
    place = lax.axis_index("row")
    plane, member = place // group, place % group
    cells = components * planes * size * devices * length
    parts = [range(planes // 2), range(planes // 2, planes)]

    def swap(x, distance):
        return lax.ppermute(x, "row", [(r, r ^ distance) for r in range(devices)])

    def swap_sum(x, distances):
        for distance in distances:
            x = x + swap(x, distance)
        return x

    def doubling(start, stop):
        return [start << step for step in range((stop // start).bit_length() - 1)]

    def forcing_of(total):
        return (power_input / (jnp.sum(total) / cells)).reshape(1, 1)

    def across_chips(x):
        return [swap(x, 2 * h) for h in range(1, chips)]

    def across_cores(pieces):
        return [swap(piece, 1) for piece in pieces]

    order = jnp.stack([
        (plane ^ d) * group + (member ^ (2 * h + core))
        for part in parts for h in range(chips) for core in range(2) for d in part
    ]).astype(jnp.int32)
    own_order = jnp.stack([(plane ^ d) * group + member for d in range(planes)]).astype(jnp.int32)

    here, others, twins, fars = [None] * planes, [None] * planes, [None] * planes, [None] * planes

    def block_pieces(i, part):
        pieces = []
        for h in range(chips):
            for core in range(2):
                for d in parts[part]:
                    block = ([here[d]] + others[d])[h] if core == 0 else (twins[d] + fars[d])[h]
                    pieces.append((block, i, size))
        return pieces

    def here_pieces(i, distances):
        return [(here[d], i, size) for d in distances]

    def x_first(distances, name, weight=36):
        fields = [piece for i in range(components) for piece in here_pieces(i, distances)]
        return along_x(fields, here_pieces(0, distances), along_x_matrix, name, weight)

    blocks = list(pack(plane, velocity))
    here[0] = blocks[0]
    for d in parts[0][1:]:
        here[d] = swap(blocks[d], d * group)
    for d in parts[1][:-1]:
        here[d] = swap(blocks[d], d * group)
    others[0] = across_chips(here[0])
    along_x_matrix, along_y_matrix = prepare_matrices(order, own_order, slope_matrix, curve_matrix, size)

    for d in parts[0][1:]:
        here[d] = after(here[d], along_x_matrix, along_y_matrix)
        others[d] = across_chips(here[d])
    here[planes - 1] = swap(after(blocks[-1], here[1]), (planes - 1) * group)
    last = planes - 1
    x_terms = [x_first(parts[0], "x_first_near")]
    for d in parts[0]:
        twins[d] = across_cores([after(here[d], x_terms[0])])
    for d in parts[1][:-1]:
        here[d] = after(here[d], x_terms[0])
        others[d] = across_chips(here[d])
        x_terms.append(x_first([d], f"x_first_{d}"))
    for d in parts[0]:
        others[d] = after(others[d], x_terms[-1])
        fars[d] = across_cores(others[d])
    here[last] = after(here[last], x_terms[-1], [twins[d] for d in parts[0]])
    others[last] = across_chips(here[last])
    x_terms.append(x_first([last], f"x_first_{last}"))

    sums, previous = [None] * 3, x_terms[-1]
    for i in (1, 0, 2):
        fields = block_pieces(i, 0)
        fields = [(after(fields[0][0], previous), *fields[0][1:])] + fields[1:]
        sums[i] = y_call(
            partial_kernel, [], along_y_matrix, 0, [fields, block_pieces(1, 0) if i != 1 else [], []],
            [kept, kept], f"y_first_near_{i}",
        )
        previous = sums[i]
    for d in parts[1][:-1]:
        twins[d] = across_cores([after(here[d], sums[1])])
        others[d] = after(others[d], sums[1])
        fars[d] = across_cores(others[d])
    twins[last] = across_cores([after(here[last], sums[0])])
    others[last] = after(others[last], sums[2])
    fars[last] = across_cores(others[last])
    forcing = [forcing_of(sum(
        block[components * size:] for d in range(planes) for block in [here[d]] + others[d] + twins[d] + fars[d]
    ))]

    middle, base, square = [None] * 3, [None] * 3, [None] * 3
    middle_others, middle_twin, middle_far = [None] * 3, [None] * 3, [None] * 3

    def piece(x):
        return (x, 0, x.shape[0])

    for i in (1, 0, 2):
        fields = block_pieces(i, 1)
        fields = [(after(fields[0][0], previous), *fields[0][1:])] + fields[1:]
        own = here_pieces(i, range(planes))
        terms = [(x_terms[0], i, len(parts[0]) * size)] + [(x, i, size) for x in x_terms[1:]]
        middle[i], base[i], square[i] = y_call(
            first_kernel, forcing, along_y_matrix, 1,
            [fields, block_pieces(1, 1) if i != 1 else [], [piece(x) for x in sums[i]], own,
             here_pieces(1, range(planes)), terms], [kept, kept, 8], f"y_first_far_{i}",
        )
        previous = middle[i]
        if i == 1:
            middle_others[1] = across_chips(middle[1])
            middle_twin[1] = across_cores([middle[1]])

    total = jnp.sum((square[0] + square[1] + square[2]).reshape(8, length // 128, 128), axis=1)
    total = swap_sum(total, doubling(group, devices) + [1])
    middle_twin[0] = across_cores([after(middle[0], square[2])])
    middle_twin[2] = across_cores([middle[2]])
    x_terms = [None] * 3
    x_terms[1] = along_x([piece(after(middle[1], total))], [piece(middle[0])], along_x_matrix, "x_second_1")
    middle_others[1] = after(middle_others[1], x_terms[1])
    total = after(swap_sum(total, doubling(2, group)), middle_others[1], middle_twin[0], middle_twin[2])
    middle_others[0] = across_chips(after(middle[0], total))
    middle_others[2] = across_chips(after(middle[2], total))
    forcing = [forcing_of(total)]

    def middle_pieces(i):
        return [
            (x, part, kept // 2) for part in range(2) for pair in
            zip([middle[i]] + middle_others[i], middle_twin[i] + middle_far[i]) for x in pair
        ]

    def second_step(i):
        return y_call(
            second_kernel, forcing, along_y_matrix, 0,
            [middle_pieces(i), middle_pieces(1) if i != 1 else [], [], [piece(middle[i])], [piece(middle[1])],
             [piece(x_terms[i])], [piece(base[i])]], [size] * planes, f"y_second_{i}",
        )

    ends = [None] * 3
    middle_far[1] = across_cores(middle_others[1])
    ends[1] = second_step(1)
    x_terms[0] = along_x([piece(after(middle[0], ends[1]))], [], along_x_matrix, "x_second_0")
    middle_others[0] = after(middle_others[0], x_terms[0])
    middle_far[0] = across_cores(middle_others[0])
    x_terms[2] = along_x([piece(after(middle[2], x_terms[0]))], [piece(middle[0])], along_x_matrix, "x_second_2")
    middle_far[0] = after(middle_far[0], x_terms[2])
    ends[0] = second_step(0)
    middle_others[2] = after(middle_others[2], ends[0])
    middle_far[2] = across_cores(middle_others[2])
    ends[2] = second_step(2)

    out = jnp.zeros(velocity.shape, F32)
    for i in (1, 0, 2):
        for d, block in enumerate(ends[i]):
            block = swap(block, d * group) if d else block
            out = lax.dynamic_update_slice(out, block[None, None], (i, plane ^ d, 0, 0))
    return out


def solution(mesh):
    placed = (P(None, "groups", "row", None), P(), P())
    return jax.shard_map(
        on_device,
        mesh=mesh,
        in_specs=placed,
        out_specs=P(None, "groups", "row", None),
        check_vma=False,
    )
```

time: 301 us -> 303 us (level)
  waiting for transfers between devices: 111 us -> 128 us
  between operations: 15.1 us -> 1.87 us
  local copies, waits for them, and re-layouts: 21.3 us -> 15 us
  Pallas kernels: 117 us -> 122 us
    ppermute x22 -> x37, waiting for transfers between devices: 64.6 us -> 128 us  [swap(): return lax.ppermute(x, 'row', [(r, r ^ distance) for r in range(devices)])]
    all_gather x6 -> x0, waiting for transfers between devices: 45.7 us -> none  [gathered(): return lax.all_gather(x, 'row', axis_index_groups=members, axis=0)]
    dynamic_update_slice x11, local copies, waits for them, and re-layouts: 10.8 us -> 0.94 us  [on_device(): out = lax.dynamic_update_slice(out, block[None, None], (i, plane ^ d, 0, 0))]
    pallas_call x9, Pallas kernels: 53 us -> 59.3 us  [the longest x8 55.8 us: y_call(): pl.pallas_call(functools.partial(kernel, tuple((len(group) for group in g...]
    unnamed x24 -> x60, local copies, waits for them, and re-layouts: 8.34 us -> 13.6 us
    ppermute x22 -> x37, starting transfers between devices: 23.7 us -> 24.8 us  [swap(): return lax.ppermute(x, 'row', [(r, r ^ distance) for r in range(devices)])]
  transfers between devices with their start and end apart: 28 -> 37, of which waited for: 16 -> 14; matrix products, arithmetic and copies ran while one was open for 5% -> 0% of each run, Pallas kernels for 38% -> 37%
where the time goes in v5:
time: 303 us; the launch traced here: 302 us
  waiting for transfers between devices  128 us (42%)
  Pallas kernels  122 us (40%)
  starting transfers between devices  24.8 us (8%)
  local copies, waits for them, and re-layouts  15 us (5%)
  other arithmetic  9.93 us (3%)
    ppermute x37, waiting for transfers between devices, swap(): return lax.ppermute(x, 'row', [(r, r ^ distance) for r in range(devices)])  128 us
    pallas_call x8, Pallas kernels, y_call(): pl.pallas_call(functools.partial(kernel, tuple((len(group) for group in g...  55.8 us
    pallas_call x6, Pallas kernels, along_x(): pl.pallas_call(functools.partial(along_x_kernel, (len(fields), len(carrie...  49 us
    ppermute x37, starting transfers between devices, swap(): return lax.ppermute(x, 'row', [(r, r ^ distance) for r in range(devices)])  24.8 us
    unnamed x60, local copies, waits for them, and re-layouts  13.6 us
    pallas_call x1, Pallas kernels, prepare_matrices(): pl.pallas_call(functools.partial(matrices_kernel, count), grid_spec=pltpu...  13.3 us
    pallas_call x1, other arithmetic, y_call(): pl.pallas_call(functools.partial(kernel, tuple((len(group) for group in g...  7.72 us
  transfers between devices with their start and end apart: 37, of which 14 were waited for; matrix products, arithmetic and copies ran while one was open for 0% of the time, Pallas kernels for 37%

profile of v5, /device:TPU:18, one launch (start us, length us, event | category | flops | bytes accessed | tf_op | source)
XLA Modules:
  0.0 301.7 jit_solution(12392929960428224301)
XLA Ops:
  0.0 3.5 %pack.1 = (f32[200,1024]{1,0:T(8,128)S(1)}, f32[200,1024]{1,0:T(8,128)}, f32[200,1024]{1,0:T(8,128)}, f32[200,1024]{1,0:T(8,128)S(1)}) custom-call(s32[1]{0:T(128)} %bitcast.plane_ref, f32[3,4,64,1024]{3,2,1,0:T(8,128)} %velocity_ref.1), custom_call_target="tpu_custom_call" | custom-call | tf_op jit(solution)/shard_map/pack/pallas_call | solution.py:115
  8.0 13.3 %shard_map.37 = (bf16[4,1024,1024]{2,1,0:T(8,128)(2,1)}, bf16[4,256,1024]{2,1,0:T(8,128)(2,1)S(1)}) custom-call(s32[16]{0:T(128)S(1)} %stack.74.order_ref, s32[4]{0:T(128)S(1)} %pad_add_fusion.own_ref, f32[1024,1024]{1,0:T(8,128)} %refs_4_.1, f32[1024,1024]{1,0:T(8,128)} %refs_4_.1, f32[1024,1024]{1,0:T(8,128)} %refs_5_.1, f32[1024,1024]{1,0:T(8,128)} %refs_5_.1, ...), custom_call_target="tpu_custom_call" | custom-call | flops 17179869184 | bytes 33554432 | tf_op jit(solution)/shard_map/pallas_call | solution.py:63
  22.7 17.5 %collective-permute-done.2.refs_1_.refs_3_.refs_5_.refs_7_.refs_9_.refs_11_.refs_15_.refs_19_.refs_23_ = f32[200,1024]{1,0:T(8,128)S(1)} collective-permute-done((f32[200,1024]{1,0:T(8,128)}, f32[200,1024]{1,0:T(8,128)S(1)}, u32[]{:S(2)}, u32[]{:S(2)}) %collective-permute-start.2) | collective-permute-done | bytes 819232 | tf_op jit(solution)/shard_map/ppermute | solution.py:261
  41.7 10.3 %x_first_near.1.refs_18_.refs_26_ = f32[384,1024]{1,0:T(8,128)S(1)} custom-call(f32[200,1024]{1,0:T(8,128)S(1)} %get-tuple-element.89.refs_0_.refs_2_.refs_4_.refs_6_.refs_8_.refs_10_.refs_14_.refs_18_.refs_22_, f32[200,1024]{1,0:T(8,128)S(1)} %collective-permute-done.2.refs_1_.refs_3_.refs_5_.refs_7_.refs_9_.refs_11_.refs_15_.refs_19_.refs_23_, ...), custom_call_target="tpu_custom_call" | custom-call | flops 14495514624 | bytes 1572864 | tf_op jit(solution)/shard_map/x_first_near/pallas_call | solution.py:160
  54.1 6.9 %x_first_2.1.refs_19_.refs_27_ = f32[192,1024]{1,0:T(8,128)S(1)} custom-call(f32[200,1024]{1,0:T(8,128)S(1)} %collective-permute-done.1.refs_0_.refs_1_.refs_2_.refs_3_.refs_12_.refs_16_.refs_8_.refs_20_.refs_24_, f32[200,1024]{1,0:T(8,128)S(1)} %collective-permute-done.1.refs_0_.refs_1_.refs_2_.refs_3_.refs_12_.refs_16_.refs_8_.refs_20_.refs_24_, ...), custom_call_target="tpu_custom_call" | custom-call | flops 7247757312 | bytes 786432 | tf_op jit(solution)/shard_map/x_first_2/pallas_call | solution.py:160
  62.1 29.2 %collective-permute-done.9.refs_0_.refs_1_.refs_2_.refs_3_.refs_13_.refs_17_.refs_9_.refs_21_.refs_25_ = f32[200,1024]{1,0:T(8,128)S(1)} collective-permute-done((f32[200,1024]{1,0:T(8,128)S(1)}, f32[200,1024]{1,0:T(8,128)S(1)}, u32[]{:S(2)}, u32[]{:S(2)}) %collective-permute-start.9) | collective-permute-done | bytes 819232 | tf_op jit(solution)/shard_map/ppermute | solution.py:261
  91.9 6.9 %x_first_3.1.refs_20_.refs_28_ = f32[192,1024]{1,0:T(8,128)S(1)} custom-call(f32[200,1024]{1,0:T(8,128)S(1)} %collective-permute-done.9.refs_0_.refs_1_.refs_2_.refs_3_.refs_13_.refs_17_.refs_9_.refs_21_.refs_25_, f32[200,1024]{1,0:T(8,128)S(1)} %collective-permute-done.9.refs_0_.refs_1_.refs_2_.refs_3_.refs_13_.refs_17_.refs_9_.refs_21_.refs_25_, ...), custom_call_target="tpu_custom_call" | custom-call | flops 7247757312 | bytes 786432 | tf_op jit(solution)/shard_map/x_first_3/pallas_call | solution.py:160
  100.6 5.7 %y_first_near_1.1 = (f32[256,1024]{1,0:T(8,128)}, f32[256,1024]{1,0:T(8,128)}) custom-call(bf16[4,256,1024]{2,1,0:T(8,128)(2,1)} %copy-done.4, f32[200,1024]{1,0:T(8,128)S(1)} %get-tuple-element.89.refs_0_.refs_2_.refs_4_.refs_6_.refs_8_.refs_10_.refs_14_.refs_18_.refs_22_, ...), custom_call_target="tpu_custom_call" | custom-call | flops 4831838208 | bytes 1048576 | tf_op jit(solution)/shard_map/y_first_near_1/pallas_call | solution.py:229
  106.3 5.9 %y_first_near_0.1 = (f32[256,1024]{1,0:T(8,128)}, f32[256,1024]{1,0:T(8,128)}) custom-call(bf16[4,256,1024]{2,1,0:T(8,128)(2,1)} %copy-done.4, f32[200,1024]{1,0:T(8,128)S(1)} %get-tuple-element.89.refs_0_.refs_2_.refs_4_.refs_6_.refs_8_.refs_10_.refs_14_.refs_18_.refs_22_, ...), custom_call_target="tpu_custom_call" | custom-call | flops 4831838208 | bytes 1048576 | tf_op jit(solution)/shard_map/y_first_near_0/pallas_call | solution.py:229
  112.9 5.9 %y_first_near_2.1 = (f32[256,1024]{1,0:T(8,128)}, f32[256,1024]{1,0:T(8,128)}) custom-call(bf16[4,256,1024]{2,1,0:T(8,128)(2,1)} %copy-done.4, f32[200,1024]{1,0:T(8,128)S(1)} %get-tuple-element.89.refs_0_.refs_2_.refs_4_.refs_6_.refs_8_.refs_10_.refs_14_.refs_18_.refs_22_, ...), custom_call_target="tpu_custom_call" | custom-call | flops 4831838208 | bytes 1048576 | tf_op jit(solution)/shard_map/y_first_near_2/pallas_call | solution.py:229
  119.4 1.9 collective-permute-done.14.refs_7_.refs_15_
  128.8 6.7 %y_first_far_1.1 = (f32[256,1024]{1,0:T(8,128)}, f32[256,1024]{1,0:T(8,128)}, f32[8,1024]{1,0:T(8,128)S(1)}) custom-call(f32[1,1]{1,0:T(1,128)} %bitcast.17.forcing_ref, bf16[4,256,1024]{2,1,0:T(8,128)(2,1)} %copy-done.4, f32[200,1024]{1,0:T(8,128)S(1)} %collective-permute-done.1.refs_0_.refs_1_.refs_2_.refs_3_.refs_12_.refs_16_.refs_8_.refs_20_.refs_24_, ...), custom_call_target="tpu_custom_call" | custom-call | flops 4831838208 | bytes 1048576 | tf_op jit(solution)/shard_map/y_first_far_1/pallas_call | solution.py:229
  137.1 7.0 %y_first_far_0.1 = (f32[256,1024]{1,0:T(8,128)}, f32[256,1024]{1,0:T(8,128)}, f32[8,1024]{1,0:T(8,128)S(1)}) custom-call(f32[1,1]{1,0:T(1,128)} %bitcast.17.forcing_ref, bf16[4,256,1024]{2,1,0:T(8,128)(2,1)} %copy-done.4, f32[200,1024]{1,0:T(8,128)S(1)} %collective-permute-done.1.refs_0_.refs_1_.refs_2_.refs_3_.refs_12_.refs_16_.refs_8_.refs_20_.refs_24_, ...), custom_call_target="tpu_custom_call" | custom-call | flops 4831838208 | bytes 1048576 | tf_op jit(solution)/shard_map/y_first_far_0/pallas_call | solution.py:229
  144.1 7.1 %y_first_far_2.1 = (f32[256,1024]{1,0:T(8,128)}, f32[256,1024]{1,0:T(8,128)}, f32[8,1024]{1,0:T(8,128)S(1)}) custom-call(f32[1,1]{1,0:T(1,128)} %bitcast.17.forcing_ref, bf16[4,256,1024]{2,1,0:T(8,128)(2,1)} %copy-done.4, f32[200,1024]{1,0:T(8,128)S(1)} %collective-permute-done.1.refs_0_.refs_1_.refs_2_.refs_3_.refs_12_.refs_16_.refs_8_.refs_20_.refs_24_, ...), custom_call_target="tpu_custom_call" | custom-call | flops 4831838208 | bytes 1048576 | tf_op jit(solution)/shard_map/y_first_far_2/pallas_call | solution.py:229
  151.4 3.6 %collective-permute-done.15 = f32[8,128]{1,0:T(8,128)S(1)} collective-permute-done((f32[8,128]{1,0:T(8,128)S(1)}, f32[8,128]{1,0:T(8,128)S(1)}, u32[]{:S(2)}, u32[]{:S(2)}) %collective-permute-start.15) | collective-permute-done | bytes 4128 | tf_op jit(solution)/shard_map/ppermute | solution.py:261
  155.0 4.5 %collective-permute-done.16 = f32[8,128]{1,0:T(8,128)S(1)} collective-permute-done((f32[8,128]{1,0:T(8,128)S(1)}, f32[8,128]{1,0:T(8,128)S(1)}, u32[]{:S(2)}, u32[]{:S(2)}) %collective-permute-start.16) | collective-permute-done | bytes 4128 | tf_op jit(solution)/shard_map/ppermute | solution.py:261
  160.6 8.3 %x_second_1.1.refs_10_ = f32[256,1024]{1,0:T(8,128)S(1)} custom-call(f32[256,1024]{1,0:T(8,128)S(1)} %copy-done.11, f32[256,1024]{1,0:T(8,128)} %get-tuple-element.113.refs_1_.refs_0_.refs_4_.refs_16_, bf16[4,1024,1024]{2,1,0:T(8,128)(2,1)} %get-tuple-element.70.refs_8_.refs_4_.refs_2_.refs_1_), custom_call_target="tpu_custom_call" | custom-call | flops 9663676416 | bytes 1048576 | tf_op jit(solution)/shard_map/x_second_1/pallas_call | solution.py:160
  170.6 3.1 %collective-permute-done.18 = f32[8,128]{1,0:T(8,128)S(1)} collective-permute-done((f32[8,128]{1,0:T(8,128)S(1)}, f32[8,128]{1,0:T(8,128)S(1)}, u32[]{:S(2)}, u32[]{:S(2)}) %collective-permute-start.18) | collective-permute-done | bytes 4128 | tf_op jit(solution)/shard_map/ppermute | solution.py:261
  177.1 8.2 %y_second_1.1 = (f32[64,1024]{1,0:T(8,128)S(1)}, f32[64,1024]{1,0:T(8,128)S(1)}, f32[64,1024]{1,0:T(8,128)S(1)}, f32[64,1024]{1,0:T(8,128)S(1)}) custom-call(f32[1,1]{1,0:T(1,128)} %bitcast.19.forcing_ref, bf16[4,256,1024]{2,1,0:T(8,128)(2,1)} %copy-done.4, f32[256,1024]{1,0:T(8,128)S(1)} %copy-done.11, ...), custom_call_target="tpu_custom_call" | custom-call | flops 9663676416 | bytes 1048576 | tf_op jit(solution)/shard_map/y_second_1/pallas_call | solution.py:229
  185.4 1.9 collective-permute-start.25
  188.9 8.1 %x_second_0.1.refs_18_ = f32[256,1024]{1,0:T(8,128)S(1)} custom-call(f32[256,1024]{1,0:T(8,128)} %get-tuple-element.113.refs_1_.refs_0_.refs_4_.refs_16_, bf16[4,1024,1024]{2,1,0:T(8,128)(2,1)} %get-tuple-element.70.refs_8_.refs_4_.refs_2_.refs_1_), custom_call_target="tpu_custom_call" | custom-call | flops 9663676416 | bytes 1048576 | tf_op jit(solution)/shard_map/x_second_0/pallas_call | solution.py:160
  198.1 22.5 %collective-permute-done.27.refs_2_.refs_6_ = f32[256,1024]{1,0:T(8,128)S(1)} collective-permute-done((f32[256,1024]{1,0:T(8,128)}, f32[256,1024]{1,0:T(8,128)S(1)}, u32[]{:S(2)}, u32[]{:S(2)}) %collective-permute-start.27) | collective-permute-done | bytes 1048608 | tf_op jit(solution)/shard_map/ppermute | solution.py:261
  220.6 8.5 %x_second_2.1 = f32[256,1024]{1,0:T(8,128)S(1)} custom-call(f32[256,1024]{1,0:T(8,128)S(1)} %copy-done.13, f32[256,1024]{1,0:T(8,128)} %get-tuple-element.113.refs_1_.refs_0_.refs_4_.refs_16_, bf16[4,1024,1024]{2,1,0:T(8,128)(2,1)} %get-tuple-element.70.refs_8_.refs_4_.refs_2_.refs_1_), custom_call_target="tpu_custom_call" | custom-call | flops 9663676416 | bytes 1048576 | tf_op jit(solution)/shard_map/x_second_2/pallas_call | solution.py:160
  230.7 9.2 %y_second_0.1 = (f32[64,1024]{1,0:T(8,128)S(1)}, f32[64,1024]{1,0:T(8,128)S(1)}, f32[64,1024]{1,0:T(8,128)S(1)}, f32[64,1024]{1,0:T(8,128)S(1)}) custom-call(f32[1,1]{1,0:T(1,128)} %bitcast.19.forcing_ref, bf16[4,256,1024]{2,1,0:T(8,128)(2,1)} %copy-done.4, f32[256,1024]{1,0:T(8,128)} %get-tuple-element.113.refs_1_.refs_0_.refs_4_.refs_16_, ...), custom_call_target="tpu_custom_call" | custom-call | flops 9663676416 | bytes 1048576 | tf_op jit(solution)/shard_map/y_second_0/pallas_call | solution.py:229
  243.6 6.1 %collective-permute-done.29 = f32[64,1024]{1,0:T(8,128)S(1)} collective-permute-done((f32[64,1024]{1,0:T(8,128)S(1)}, f32[64,1024]{1,0:T(8,128)S(1)}, u32[]{:S(2)}, u32[]{:S(2)}) %collective-permute-start.29) | collective-permute-done | bytes 262176 | tf_op jit(solution)/shard_map/ppermute | solution.py:261
  249.7 10.2 %collective-permute-done.30 = f32[64,1024]{1,0:T(8,128)S(1)} collective-permute-done((f32[64,1024]{1,0:T(8,128)S(1)}, f32[64,1024]{1,0:T(8,128)S(1)}, u32[]{:S(2)}, u32[]{:S(2)}) %collective-permute-start.30) | collective-permute-done | bytes 262176 | tf_op jit(solution)/shard_map/ppermute | solution.py:261
  259.9 7.2 %collective-permute-done.31 = f32[64,1024]{1,0:T(8,128)S(1)} collective-permute-done((f32[64,1024]{1,0:T(8,128)S(1)}, f32[64,1024]{1,0:T(8,128)S(1)}, u32[]{:S(2)}, u32[]{:S(2)}) %collective-permute-start.31) | collective-permute-done | bytes 262176 | tf_op jit(solution)/shard_map/ppermute | solution.py:261
  267.2 7.7 %y_second_2.1 = (f32[3,4,64,1024]{3,2,1,0:T(8,128)S(1)}, f32[64,1024]{1,0:T(8,128)S(1)}, f32[64,1024]{1,0:T(8,128)S(1)}, f32[64,1024]{1,0:T(8,128)S(1)}) fusion(f32[3,4,64,1024]{3,2,1,0:T(8,128)S(1)} %bitcast_dynamic-update-slice_fusion.4, s32[]{:T(128)S(6)} %select_n.33, f32[1,1]{1,0:T(1,128)} %bitcast.19.forcing_ref, ...), kind=kCustom, calls=%fused_computation.3 | custom fusion | flops 9663676416 | bytes 13631496 | tf_op jit(solution)/shard_map/y_second_2/pallas_call | solution.py:229
  275.0 1.9 collective-permute-start.35
  278.5 6.5 %collective-permute-done.34 = f32[64,1024]{1,0:T(8,128)S(1)} collective-permute-done((f32[64,1024]{1,0:T(8,128)S(1)}, f32[64,1024]{1,0:T(8,128)S(1)}, u32[]{:S(2)}, u32[]{:S(2)}) %collective-permute-start.34) | collective-permute-done | bytes 262176 | tf_op jit(solution)/shard_map/ppermute | solution.py:261
  284.9 9.9 %collective-permute-done.35 = f32[64,1024]{1,0:T(8,128)S(1)} collective-permute-done((f32[64,1024]{1,0:T(8,128)S(1)}, f32[64,1024]{1,0:T(8,128)S(1)}, u32[]{:S(2)}, u32[]{:S(2)}) %collective-permute-start.35) | collective-permute-done | bytes 262176 | tf_op jit(solution)/shard_map/ppermute | solution.py:261
  294.9 6.1 %collective-permute-done.36 = f32[64,1024]{1,0:T(8,128)S(1)} collective-permute-done((f32[64,1024]{1,0:T(8,128)S(1)}, f32[64,1024]{1,0:T(8,128)S(1)}, u32[]{:S(2)}, u32[]{:S(2)}) %collective-permute-start.36) | collective-permute-done | bytes 262176 | tf_op jit(solution)/shard_map/ppermute | solution.py:261
  (140 shorter events, 38.4 us)
Async XLA Ops:
  4.4 35.7 %collective-permute-start.2 = (f32[200,1024]{1,0:T(8,128)}, f32[200,1024]{1,0:T(8,128)S(1)}, u32[]{:S(2)}, u32[]{:S(2)}) collective-permute-start(f32[200,1024]{1,0:T(8,128)} %get-tuple-element.69), channel_id=1, source_target_pairs={{0,4},{1,5},{2,6},{3,7},{4,0},{5,1},{6,2},{7,3},{8,12},{9,13},{10,... | collective-permute-start | bytes 2457608 | tf_op jit(solution)/shard_map/ppermute | solution.py:261
  6.0 47.1 %collective-permute-start.1 = (f32[200,1024]{1,0:T(8,128)}, f32[200,1024]{1,0:T(8,128)S(1)}, u32[]{:S(2)}, u32[]{:S(2)}) collective-permute-start(f32[200,1024]{1,0:T(8,128)} %get-tuple-element.68), channel_id=1, source_target_pairs={{0,8},{1,9},{2,10},{3,11},{4,12},{5,13},{6,14},{7,15},{8,0},{9,1},... | collective-permute-start | bytes 2457608 | tf_op jit(solution)/shard_map/ppermute | solution.py:261
  6.4 54.6 %collective-permute-start = (f32[200,1024]{1,0:T(8,128)S(1)}, f32[200,1024]{1,0:T(8,128)}, u32[]{:S(2)}, u32[]{:S(2)}) collective-permute-start(f32[200,1024]{1,0:T(8,128)S(1)} %get-tuple-element.89.refs_0_.refs_2_.refs_4_.refs_6_.refs_8_.refs_10_.refs_14_.refs_18_.refs_22_), channel_id=1, source_target_pairs={{0,2},{1,3},{2,0},{3,1},{4,6},{5,7},{6,4},{7,5},{8,10},{9,11},{10,... | collective-permute-start | bytes 2457608 | tf_op jit(solution)/shard_map/ppermute | solution.py:261
  40.2 20.9 %collective-permute-start.5 = (f32[200,1024]{1,0:T(8,128)S(1)}, f32[200,1024]{1,0:T(8,128)S(1)}, u32[]{:S(2)}, u32[]{:S(2)}) collective-permute-start(f32[200,1024]{1,0:T(8,128)S(1)} %collective-permute-done.2.refs_1_.refs_3_.refs_5_.refs_7_.refs_9_.refs_11_.refs_15_.refs_19_.refs_23_), channel_id=1, source_target_pairs={{0,2},{1,3},{2,0},{3,1},{4,6},{5,7},{6,4},{7,5},{8,10},{9,11},{10,... | collective-permute-start | bytes 2457608 | tf_op jit(solution)/shard_map/ppermute | solution.py:261
  53.1 8.5 %collective-permute-start.6 = (f32[200,1024]{1,0:T(8,128)S(1)}, f32[200,1024]{1,0:T(8,128)S(1)}, u32[]{:S(2)}, u32[]{:S(2)}) collective-permute-start(f32[200,1024]{1,0:T(8,128)S(1)} %collective-permute-done.2.refs_1_.refs_3_.refs_5_.refs_7_.refs_9_.refs_11_.refs_15_.refs_19_.refs_23_), channel_id=1, source_target_pairs={{0,1},{1,0},{2,3},{3,2},{4,5},{5,4},{6,7},{7,6},{8,9},{9,8},{10,11... | collective-permute-start | bytes 2457608 | tf_op jit(solution)/shard_map/ppermute | solution.py:261
  53.1 9.0 %collective-permute-start.3 = (f32[200,1024]{1,0:T(8,128)S(1)}, f32[200,1024]{1,0:T(8,128)S(1)}, u32[]{:S(2)}, u32[]{:S(2)}) collective-permute-start(f32[200,1024]{1,0:T(8,128)S(1)} %get-tuple-element.89.refs_0_.refs_2_.refs_4_.refs_6_.refs_8_.refs_10_.refs_14_.refs_18_.refs_22_), channel_id=1, source_target_pairs={{0,1},{1,0},{2,3},{3,2},{4,5},{5,4},{6,7},{7,6},{8,9},{9,8},{10,11... | collective-permute-start | bytes 2457608 | tf_op jit(solution)/shard_map/ppermute | solution.py:261
  53.6 37.7 %collective-permute-start.9 = (f32[200,1024]{1,0:T(8,128)S(1)}, f32[200,1024]{1,0:T(8,128)S(1)}, u32[]{:S(2)}, u32[]{:S(2)}) collective-permute-start(f32[200,1024]{1,0:T(8,128)S(1)} %copy-done.15), channel_id=1, source_target_pairs={{0,12},{1,13},{2,14},{3,15},{4,8},{5,9},{6,10},{7,11},{8,4},{9,5},... | collective-permute-start | bytes 2457608 | tf_op jit(solution)/shard_map/ppermute | solution.py:261
  61.0 37.8 %collective-permute-start.4 = (f32[200,1024]{1,0:T(8,128)}, f32[200,1024]{1,0:T(8,128)S(1)}, u32[]{:S(2)}, u32[]{:S(2)}) collective-permute-start(f32[200,1024]{1,0:T(8,128)} %collective-permute-done.refs_4_.refs_12_), channel_id=1, source_target_pairs={{0,1},{1,0},{2,3},{3,2},{4,5},{5,4},{6,7},{7,6},{8,9},{9,8},{10,11... | collective-permute-start | bytes 2457608 | tf_op jit(solution)/shard_map/ppermute | solution.py:261
  61.1 37.7 %collective-permute-start.7 = (f32[200,1024]{1,0:T(8,128)S(1)}, f32[200,1024]{1,0:T(8,128)S(1)}, u32[]{:S(2)}, u32[]{:S(2)}) collective-permute-start(f32[200,1024]{1,0:T(8,128)S(1)} %collective-permute-done.5.refs_5_.refs_13_), channel_id=1, source_target_pairs={{0,1},{1,0},{2,3},{3,2},{4,5},{5,4},{6,7},{7,6},{8,9},{9,8},{10,11... | collective-permute-start | bytes 2457608 | tf_op jit(solution)/shard_map/ppermute | solution.py:261
  61.6 50.7 %collective-permute-start.8 = (f32[200,1024]{1,0:T(8,128)S(1)}, f32[200,1024]{1,0:T(8,128)S(1)}, u32[]{:S(2)}, u32[]{:S(2)}) collective-permute-start(f32[200,1024]{1,0:T(8,128)S(1)} %collective-permute-done.1.refs_0_.refs_1_.refs_2_.refs_3_.refs_12_.refs_16_.refs_8_.refs_20_.refs_24_), channel_id=1, source_target_pairs={{0,2},{1,3},{2,0},{3,1},{4,6},{5,7},{6,4},{7,5},{8,10},{9,11},{10,... | collective-permute-start | bytes 2457608 | tf_op jit(solution)/shard_map/ppermute | solution.py:261
  91.3 27.5 %collective-permute-start.12 = (f32[200,1024]{1,0:T(8,128)S(1)}, f32[200,1024]{1,0:T(8,128)S(1)}, u32[]{:S(2)}, u32[]{:S(2)}) collective-permute-start(f32[200,1024]{1,0:T(8,128)S(1)} %collective-permute-done.9.refs_0_.refs_1_.refs_2_.refs_3_.refs_13_.refs_17_.refs_9_.refs_21_.refs_25_), channel_id=1, source_target_pairs={{0,2},{1,3},{2,0},{3,1},{4,6},{5,7},{6,4},{7,5},{8,10},{9,11},{10,... | collective-permute-start | bytes 2457608 | tf_op jit(solution)/shard_map/ppermute | solution.py:261
  112.3 7.0 %collective-permute-start.10 = (f32[200,1024]{1,0:T(8,128)S(1)}, f32[200,1024]{1,0:T(8,128)S(1)}, u32[]{:S(2)}, u32[]{:S(2)}) collective-permute-start(f32[200,1024]{1,0:T(8,128)S(1)} %collective-permute-done.1.refs_0_.refs_1_.refs_2_.refs_3_.refs_12_.refs_16_.refs_8_.refs_20_.refs_24_), channel_id=1, source_target_pairs={{0,1},{1,0},{2,3},{3,2},{4,5},{5,4},{6,7},{7,6},{8,9},{9,8},{10,11... | collective-permute-start | bytes 2457608 | tf_op jit(solution)/shard_map/ppermute | solution.py:261
  112.3 7.0 %collective-permute-start.11 = (f32[200,1024]{1,0:T(8,128)S(1)}, f32[200,1024]{1,0:T(8,128)S(1)}, u32[]{:S(2)}, u32[]{:S(2)}) collective-permute-start(f32[200,1024]{1,0:T(8,128)S(1)} %collective-permute-done.8.refs_4_.refs_12_), channel_id=1, source_target_pairs={{0,1},{1,0},{2,3},{3,2},{4,5},{5,4},{6,7},{7,6},{8,9},{9,8},{10,11... | collective-permute-start | bytes 2457608 | tf_op jit(solution)/shard_map/ppermute | solution.py:261
  112.8 6.5 %collective-permute-start.13 = (f32[200,1024]{1,0:T(8,128)S(1)}, f32[200,1024]{1,0:T(8,128)S(1)}, u32[]{:S(2)}, u32[]{:S(2)}) collective-permute-start(f32[200,1024]{1,0:T(8,128)S(1)} %collective-permute-done.9.refs_0_.refs_1_.refs_2_.refs_3_.refs_13_.refs_17_.refs_9_.refs_21_.refs_25_), channel_id=1, source_target_pairs={{0,1},{1,0},{2,3},{3,2},{4,5},{5,4},{6,7},{7,6},{8,9},{9,8},{10,11... | collective-permute-start | bytes 2457608 | tf_op jit(solution)/shard_map/ppermute | solution.py:261
  135.5 34.5 %collective-permute-start.19 = (f32[256,1024]{1,0:T(8,128)}, f32[256,1024]{1,0:T(8,128)}, u32[]{:S(2)}, u32[]{:S(2)}) collective-permute-start(f32[256,1024]{1,0:T(8,128)} %get-tuple-element.102.refs_0_.refs_4_.refs_8_.refs_9_.refs_12_.refs_17_), channel_id=1, source_target_pairs={{0,2},{1,3},{2,0},{3,1},{4,6},{5,7},{6,4},{7,5},{8,10},{9,11},{10,... | collective-permute-start | bytes 3145736 | tf_op jit(solution)/shard_map/ppermute | solution.py:261
  159.5 17.7 %collective-permute-start.22 = (f32[256,1024]{1,0:T(8,128)S(1)}, f32[256,1024]{1,0:T(8,128)}, u32[]{:S(2)}, u32[]{:S(2)}) collective-permute-start(f32[256,1024]{1,0:T(8,128)S(1)} %copy-done.11), channel_id=1, source_target_pairs={{0,1},{1,0},{2,3},{3,2},{4,5},{5,4},{6,7},{7,6},{8,9},{9,8},{10,11... | collective-permute-start | bytes 3145736 | tf_op jit(solution)/shard_map/ppermute | solution.py:261
  160.0 13.7 %collective-permute-start.20 = (f32[256,1024]{1,0:T(8,128)}, f32[256,1024]{1,0:T(8,128)}, u32[]{:S(2)}, u32[]{:S(2)}) collective-permute-start(f32[256,1024]{1,0:T(8,128)} %get-tuple-element.113.refs_1_.refs_0_.refs_4_.refs_16_), channel_id=1, source_target_pairs={{0,1},{1,0},{2,3},{3,2},{4,5},{5,4},{6,7},{7,6},{8,9},{9,8},{10,11... | collective-permute-start | bytes 3145736 | tf_op jit(solution)/shard_map/ppermute | solution.py:261
  160.0 13.6 %collective-permute-start.21 = (f32[256,1024]{1,0:T(8,128)}, f32[256,1024]{1,0:T(8,128)}, u32[]{:S(2)}, u32[]{:S(2)}) collective-permute-start(f32[256,1024]{1,0:T(8,128)} %get-tuple-element.122.refs_0_), channel_id=1, source_target_pairs={{0,1},{1,0},{2,3},{3,2},{4,5},{5,4},{6,7},{7,6},{8,9},{9,8},{10,11... | collective-permute-start | bytes 3145736 | tf_op jit(solution)/shard_map/ppermute | solution.py:261
  170.0 7.1 %collective-permute-start.23 = (f32[256,1024]{1,0:T(8,128)}, f32[256,1024]{1,0:T(8,128)}, u32[]{:S(2)}, u32[]{:S(2)}) collective-permute-start(f32[256,1024]{1,0:T(8,128)} %collective-permute-done.19.refs_2_.refs_6_.refs_10_.refs_14_), channel_id=1, source_target_pairs={{0,1},{1,0},{2,3},{3,2},{4,5},{5,4},{6,7},{7,6},{8,9},{9,8},{10,11... | collective-permute-start | bytes 3145736 | tf_op jit(solution)/shard_map/ppermute | solution.py:261
  173.7 66.2 %collective-permute-start.32 = (f32[256,1024]{1,0:T(8,128)S(1)}, f32[256,1024]{1,0:T(8,128)}, u32[]{:S(2)}, u32[]{:S(2)}) collective-permute-start(f32[256,1024]{1,0:T(8,128)S(1)} %copy-done.13), channel_id=1, source_target_pairs={{0,2},{1,3},{2,0},{3,1},{4,6},{5,7},{6,4},{7,5},{8,10},{9,11},{10,... | collective-permute-start | bytes 3145736 | tf_op jit(solution)/shard_map/ppermute | solution.py:261
  175.6 45.0 %collective-permute-start.27 = (f32[256,1024]{1,0:T(8,128)}, f32[256,1024]{1,0:T(8,128)S(1)}, u32[]{:S(2)}, u32[]{:S(2)}) collective-permute-start(f32[256,1024]{1,0:T(8,128)} %get-tuple-element.113.refs_1_.refs_0_.refs_4_.refs_16_), channel_id=1, source_target_pairs={{0,2},{1,3},{2,0},{3,1},{4,6},{5,7},{6,4},{7,5},{8,10},{9,11},{10,... | collective-permute-start | bytes 3145736 | tf_op jit(solution)/shard_map/ppermute | solution.py:261
  185.4 44.2 %collective-permute-start.24 = (f32[64,1024]{1,0:T(8,128)S(1)}, f32[64,1024]{1,0:T(8,128)S(1)}, u32[]{:S(2)}, u32[]{:S(2)}) collective-permute-start(f32[64,1024]{1,0:T(8,128)S(1)} %get-tuple-element.109), channel_id=1, source_target_pairs={{0,4},{1,5},{2,6},{3,7},{4,0},{5,1},{6,2},{7,3},{8,12},{9,13},{10,... | collective-permute-start | bytes 786440 | tf_op jit(solution)/shard_map/ppermute | solution.py:261
  185.4 44.2 %collective-permute-start.25 = (f32[64,1024]{1,0:T(8,128)S(1)}, f32[64,1024]{1,0:T(8,128)S(1)}, u32[]{:S(2)}, u32[]{:S(2)}) collective-permute-start(f32[64,1024]{1,0:T(8,128)S(1)} %get-tuple-element.110), channel_id=1, source_target_pairs={{0,8},{1,9},{2,10},{3,11},{4,12},{5,13},{6,14},{7,15},{8,0},{9,1},... | collective-permute-start | bytes 786440 | tf_op jit(solution)/shard_map/ppermute | solution.py:261
  187.3 52.8 %collective-permute-start.26 = (f32[64,1024]{1,0:T(8,128)S(1)}, f32[64,1024]{1,0:T(8,128)S(1)}, u32[]{:S(2)}, u32[]{:S(2)}) collective-permute-start(f32[64,1024]{1,0:T(8,128)S(1)} %get-tuple-element.111), channel_id=1, source_target_pairs={{0,12},{1,13},{2,14},{3,15},{4,8},{5,9},{6,10},{7,11},{8,4},{9,5},... | collective-permute-start | bytes 786440 | tf_op jit(solution)/shard_map/ppermute | solution.py:261
  220.6 9.0 %collective-permute-start.28 = (f32[256,1024]{1,0:T(8,128)S(1)}, f32[256,1024]{1,0:T(8,128)S(1)}, u32[]{:S(2)}, u32[]{:S(2)}) collective-permute-start(f32[256,1024]{1,0:T(8,128)S(1)} %collective-permute-done.27.refs_2_.refs_6_), channel_id=1, source_target_pairs={{0,1},{1,0},{2,3},{3,2},{4,5},{5,4},{6,7},{7,6},{8,9},{9,8},{10,11... | collective-permute-start | bytes 3145736 | tf_op jit(solution)/shard_map/ppermute | solution.py:261
  239.9 9.8 %collective-permute-start.29 = (f32[64,1024]{1,0:T(8,128)S(1)}, f32[64,1024]{1,0:T(8,128)S(1)}, u32[]{:S(2)}, u32[]{:S(2)}) collective-permute-start(f32[64,1024]{1,0:T(8,128)S(1)} %get-tuple-element.119), channel_id=1, source_target_pairs={{0,4},{1,5},{2,6},{3,7},{4,0},{5,1},{6,2},{7,3},{8,12},{9,13},{10,... | collective-permute-start | bytes 786440 | tf_op jit(solution)/shard_map/ppermute | solution.py:261
  240.0 27.2 %collective-permute-start.33 = (f32[256,1024]{1,0:T(8,128)}, f32[256,1024]{1,0:T(8,128)S(1)}, u32[]{:S(2)}, u32[]{:S(2)}) collective-permute-start(f32[256,1024]{1,0:T(8,128)} %collective-permute-done.32), channel_id=1, source_target_pairs={{0,1},{1,0},{2,3},{3,2},{4,5},{5,4},{6,7},{7,6},{8,9},{9,8},{10,11... | collective-permute-start | bytes 3145736 | tf_op jit(solution)/shard_map/ppermute | solution.py:261
  240.2 19.7 %collective-permute-start.30 = (f32[64,1024]{1,0:T(8,128)S(1)}, f32[64,1024]{1,0:T(8,128)S(1)}, u32[]{:S(2)}, u32[]{:S(2)}) collective-permute-start(f32[64,1024]{1,0:T(8,128)S(1)} %get-tuple-element.120), channel_id=1, source_target_pairs={{0,8},{1,9},{2,10},{3,11},{4,12},{5,13},{6,14},{7,15},{8,0},{9,1},... | collective-permute-start | bytes 786440 | tf_op jit(solution)/shard_map/ppermute | solution.py:261
  242.0 25.2 %collective-permute-start.31 = (f32[64,1024]{1,0:T(8,128)S(1)}, f32[64,1024]{1,0:T(8,128)S(1)}, u32[]{:S(2)}, u32[]{:S(2)}) collective-permute-start(f32[64,1024]{1,0:T(8,128)S(1)} %get-tuple-element.121), channel_id=1, source_target_pairs={{0,12},{1,13},{2,14},{3,15},{4,8},{5,9},{6,10},{7,11},{8,4},{9,5},... | collective-permute-start | bytes 786440 | tf_op jit(solution)/shard_map/ppermute | solution.py:261
  274.9 10.0 %collective-permute-start.34 = (f32[64,1024]{1,0:T(8,128)S(1)}, f32[64,1024]{1,0:T(8,128)S(1)}, u32[]{:S(2)}, u32[]{:S(2)}) collective-permute-start(f32[64,1024]{1,0:T(8,128)S(1)} %get-tuple-element.132), channel_id=1, source_target_pairs={{0,4},{1,5},{2,6},{3,7},{4,0},{5,1},{6,2},{7,3},{8,12},{9,13},{10,... | collective-permute-start | bytes 786440 | tf_op jit(solution)/shard_map/ppermute | solution.py:261
  275.0 19.9 %collective-permute-start.35 = (f32[64,1024]{1,0:T(8,128)S(1)}, f32[64,1024]{1,0:T(8,128)S(1)}, u32[]{:S(2)}, u32[]{:S(2)}) collective-permute-start(f32[64,1024]{1,0:T(8,128)S(1)} %get-tuple-element.134), channel_id=1, source_target_pairs={{0,8},{1,9},{2,10},{3,11},{4,12},{5,13},{6,14},{7,15},{8,0},{9,1},... | collective-permute-start | bytes 786440 | tf_op jit(solution)/shard_map/ppermute | solution.py:261
  276.9 24.1 %collective-permute-start.36 = (f32[64,1024]{1,0:T(8,128)S(1)}, f32[64,1024]{1,0:T(8,128)S(1)}, u32[]{:S(2)}, u32[]{:S(2)}) collective-permute-start(f32[64,1024]{1,0:T(8,128)S(1)} %get-tuple-element.136), channel_id=1, source_target_pairs={{0,12},{1,13},{2,14},{3,15},{4,8},{5,9},{6,10},{7,11},{8,4},{9,5},... | collective-permute-start | bytes 786440 | tf_op jit(solution)/shard_map/ppermute | solution.py:261
  (35 other events, 491.4 us)

commit v6 on v5

--- a/solution.py
+++ b/solution.py
@@ -16,7 +16,7 @@
 
 BF16 = jnp.bfloat16
 F32 = jnp.float32
-VMEM_BYTES = 50 * 1024 * 1024
+VMEM_BYTES = 24 * 1024 * 1024
 
 
 def halves(x):
@@ -313,15 +313,15 @@
     for d in parts[0][1:]:
         here[d] = after(here[d], along_x_matrix, along_y_matrix)
         others[d] = across_chips(here[d])
-    here[planes - 1] = swap(after(blocks[-1], here[1]), (planes - 1) * group)
+    here[planes - 1] = swap(blocks[-1], (planes - 1) * group)
     last = planes - 1
-    x_terms = [x_first(parts[0], "x_first_near")]
+    x_terms = [x_first(parts[0], "x_first_near", 1)]
     for d in parts[0]:
         twins[d] = across_cores([after(here[d], x_terms[0])])
     for d in parts[1][:-1]:
         here[d] = after(here[d], x_terms[0])
         others[d] = across_chips(here[d])
-        x_terms.append(x_first([d], f"x_first_{d}"))
+        x_terms.append(x_first([d], f"x_first_{d}", 1))
     for d in parts[0]:
         others[d] = after(others[d], x_terms[-1])
         fars[d] = across_cores(others[d])
@@ -379,7 +379,6 @@
     middle_others[1] = after(middle_others[1], x_terms[1])
     total = after(swap_sum(total, doubling(2, group)), middle_others[1], middle_twin[0], middle_twin[2])
     middle_others[0] = across_chips(after(middle[0], total))
-    middle_others[2] = across_chips(after(middle[2], total))
     forcing = [forcing_of(total)]
 
     def middle_pieces(i):
@@ -398,10 +397,11 @@
     ends = [None] * 3
     middle_far[1] = across_cores(middle_others[1])
     ends[1] = second_step(1)
-    x_terms[0] = along_x([piece(after(middle[0], ends[1]))], [], along_x_matrix, "x_second_0")
+    x_terms[0] = along_x([piece(after(middle[0], ends[1]))], [], along_x_matrix, "x_second_0", 1)
     middle_others[0] = after(middle_others[0], x_terms[0])
+    middle_others[2] = across_chips(after(middle[2], middle_others[0]))
     middle_far[0] = across_cores(middle_others[0])
-    x_terms[2] = along_x([piece(after(middle[2], x_terms[0]))], [piece(middle[0])], along_x_matrix, "x_second_2")
+    x_terms[2] = along_x([piece(after(middle[2], x_terms[0]))], [piece(middle[0])], along_x_matrix, "x_second_2", 1)
     middle_far[0] = after(middle_far[0], x_terms[2])
     ends[0] = second_step(0)
     middle_others[2] = after(middle_others[2], ends[0])

time: 303 us -> 300 us (0.990)
  local copies, waits for them, and re-layouts: 15 us -> 44.3 us
  Pallas kernels: 122 us -> 98.5 us
  waiting for transfers between devices: 128 us -> 118 us
    unnamed x60 -> x138, local copies, waits for them, and re-layouts: 13.6 us -> 42.9 us
    pallas_call x8, Pallas kernels: 55.8 us -> 43.8 us  [y_call(): pl.pallas_call(functools.partial(kernel, tuple((len(group) for group in g...]
    ppermute x37, waiting for transfers between devices: 128 us -> 118 us  [swap(): return lax.ppermute(x, 'row', [(r, r ^ distance) for r in range(devices)])]
    pallas_call x1, Pallas kernels: 13.3 us -> 7.16 us  [prepare_matrices(): pl.pallas_call(functools.partial(matrices_kernel, count), grid_spec=pltpu...]
  transfers between devices with their start and end apart: 37 -> 37, of which waited for: 14 -> 18; matrix products, arithmetic and copies ran while one was open for 0% -> 0% of each run, Pallas kernels for 37% -> 31%
where the time goes in v6:
time: 300 us; the launch traced here: 298 us
  waiting for transfers between devices  118 us (39%)
  Pallas kernels  98.5 us (33%)
  local copies, waits for them, and re-layouts  44.3 us (15%)
  starting transfers between devices  25.3 us (8%)
  other arithmetic  9.83 us (3%)
    ppermute x37, waiting for transfers between devices, swap(): return lax.ppermute(x, 'row', [(r, r ^ distance) for r in range(devices)])  118 us
    pallas_call x6, Pallas kernels, along_x(): pl.pallas_call(functools.partial(along_x_kernel, (len(fields), len(carrie...  46.3 us
    pallas_call x8, Pallas kernels, y_call(): pl.pallas_call(functools.partial(kernel, tuple((len(group) for group in g...  43.8 us
    unnamed x138, local copies, waits for them, and re-layouts  42.9 us
    ppermute x37, starting transfers between devices, swap(): return lax.ppermute(x, 'row', [(r, r ^ distance) for r in range(devices)])  25.3 us
    pallas_call x1, other arithmetic, y_call(): pl.pallas_call(functools.partial(kernel, tuple((len(group) for group in g...  7.66 us
    pallas_call x1, Pallas kernels, prepare_matrices(): pl.pallas_call(functools.partial(matrices_kernel, count), grid_spec=pltpu...  7.16 us
  transfers between devices with their start and end apart: 37, of which 18 were waited for; matrix products, arithmetic and copies ran while one was open for 0% of the time, Pallas kernels for 31%

profile of v6, /device:TPU:18, one launch (start us, length us, event | category | flops | bytes accessed | tf_op | source)
XLA Modules:
  0.0 298.1 jit_solution(17124239000921376164)
XLA Ops:
  12.1 7.2 %shard_map.37 = (bf16[4,1024,1024]{2,1,0:T(8,128)(2,1)S(1)}, bf16[4,256,1024]{2,1,0:T(8,128)(2,1)S(1)}) custom-call(s32[16]{0:T(128)S(1)} %stack.74.order_ref, s32[4]{0:T(128)S(1)} %pad_add_fusion.own_ref, f32[1024,1024]{1,0:T(8,128)S(1)} %copy-done.43, f32[1024,1024]{1,0:T(8,128)S(1)} %copy-done.43, f32[1024,1024]{1,0:T(8,128)S(1)} %copy-done.44, ...), custom_call_target="tpu_custom_call" | custom-call | flops 17179869184 | bytes 33554432 | tf_op jit(solution)/shard_map/pallas_call | solution.py:63
  19.3 20.0 %collective-permute-done.2.refs_1_.refs_3_.refs_5_.refs_7_.refs_9_.refs_11_.refs_15_.refs_19_.refs_23_ = f32[200,1024]{1,0:T(8,128)S(1)} collective-permute-done((f32[200,1024]{1,0:T(8,128)S(1)}, f32[200,1024]{1,0:T(8,128)S(1)}, u32[]{:S(2)}, u32[]{:S(2)}) %collective-permute-start.2) | collective-permute-done | bytes 819232 | tf_op jit(solution)/shard_map/ppermute | solution.py:261
  41.3 9.8 %x_first_near.1.refs_18_.refs_26_ = f32[384,1024]{1,0:T(8,128)S(1)} custom-call(f32[200,1024]{1,0:T(8,128)S(1)} %get-tuple-element.87.refs_0_.refs_2_.refs_4_.refs_6_.refs_8_.refs_10_.refs_14_.refs_18_.refs_22_, f32[200,1024]{1,0:T(8,128)S(1)} %collective-permute-done.2.refs_1_.refs_3_.refs_5_.refs_7_.refs_9_.refs_11_.refs_15_.refs_19_.refs_23_, ...), custom_call_target="tpu_custom_call" | custom-call | flops 402653184 | bytes 1572864 | tf_op jit(solution)/shard_map/x_first_near/pallas_call | solution.py:160
  51.6 5.8 %x_first_2.1.refs_19_.refs_27_ = f32[192,1024]{1,0:T(8,128)S(1)} custom-call(f32[200,1024]{1,0:T(8,128)S(1)} %collective-permute-done.1.refs_0_.refs_1_.refs_2_.refs_3_.refs_12_.refs_16_.refs_8_.refs_20_.refs_24_, f32[200,1024]{1,0:T(8,128)S(1)} %collective-permute-done.1.refs_0_.refs_1_.refs_2_.refs_3_.refs_12_.refs_16_.refs_8_.refs_20_.refs_24_, ...), custom_call_target="tpu_custom_call" | custom-call | flops 201326592 | bytes 786432 | tf_op jit(solution)/shard_map/x_first_2/pallas_call | solution.py:160
  58.4 19.8 %collective-permute-done.9.refs_0_.refs_1_.refs_2_.refs_3_.refs_13_.refs_17_.refs_9_.refs_21_.refs_25_ = f32[200,1024]{1,0:T(8,128)S(1)} collective-permute-done((f32[200,1024]{1,0:T(8,128)S(1)}, f32[200,1024]{1,0:T(8,128)S(1)}, u32[]{:S(2)}, u32[]{:S(2)}) %collective-permute-start.9) | collective-permute-done | bytes 819232 | tf_op jit(solution)/shard_map/ppermute | solution.py:261
  80.2 5.8 %x_first_3.1.refs_20_.refs_28_ = f32[192,1024]{1,0:T(8,128)S(1)} custom-call(f32[200,1024]{1,0:T(8,128)S(1)} %collective-permute-done.9.refs_0_.refs_1_.refs_2_.refs_3_.refs_13_.refs_17_.refs_9_.refs_21_.refs_25_, f32[200,1024]{1,0:T(8,128)S(1)} %collective-permute-done.9.refs_0_.refs_1_.refs_2_.refs_3_.refs_13_.refs_17_.refs_9_.refs_21_.refs_25_, ...), custom_call_target="tpu_custom_call" | custom-call | flops 7247757312 | bytes 786432 | tf_op jit(solution)/shard_map/x_first_3/pallas_call | solution.py:160
  86.1 4.4 %y_first_near_1.1 = (f32[256,1024]{1,0:T(8,128)S(1)}, f32[256,1024]{1,0:T(8,128)S(1)}) custom-call(bf16[4,256,1024]{2,1,0:T(8,128)(2,1)S(1)} %get-tuple-element.70.matrix_ref, f32[200,1024]{1,0:T(8,128)S(1)} %get-tuple-element.87.refs_0_.refs_2_.refs_4_.refs_6_.refs_8_.refs_10_.refs_14_.refs_18_.refs_22_, ...), custom_call_target="tpu_custom_call" | custom-call | flops 4831838208 | bytes 1048576 | tf_op jit(solution)/shard_map/y_first_near_1/pallas_call | solution.py:229
  92.6 4.5 %y_first_near_0.1 = (f32[256,1024]{1,0:T(8,128)S(1)}, f32[256,1024]{1,0:T(8,128)S(1)}) custom-call(bf16[4,256,1024]{2,1,0:T(8,128)(2,1)S(1)} %get-tuple-element.70.matrix_ref, f32[200,1024]{1,0:T(8,128)S(1)} %get-tuple-element.87.refs_0_.refs_2_.refs_4_.refs_6_.refs_8_.refs_10_.refs_14_.refs_18_.refs_22_, ...), custom_call_target="tpu_custom_call" | custom-call | flops 4831838208 | bytes 1048576 | tf_op jit(solution)/shard_map/y_first_near_0/pallas_call | solution.py:229
  99.9 4.5 %y_first_near_2.1 = (f32[256,1024]{1,0:T(8,128)S(1)}, f32[256,1024]{1,0:T(8,128)S(1)}) custom-call(bf16[4,256,1024]{2,1,0:T(8,128)(2,1)S(1)} %get-tuple-element.70.matrix_ref, f32[200,1024]{1,0:T(8,128)S(1)} %get-tuple-element.87.refs_0_.refs_2_.refs_4_.refs_6_.refs_8_.refs_10_.refs_14_.refs_18_.refs_22_, ...), custom_call_target="tpu_custom_call" | custom-call | flops 4831838208 | bytes 1048576 | tf_op jit(solution)/shard_map/y_first_near_2/pallas_call | solution.py:229
  106.4 8.3 %collective-permute-done.12.refs_5_.refs_13_ = f32[200,1024]{1,0:T(8,128)S(1)} collective-permute-done((f32[200,1024]{1,0:T(8,128)S(1)}, f32[200,1024]{1,0:T(8,128)S(1)}, u32[]{:S(2)}, u32[]{:S(2)}) %collective-permute-start.12) | collective-permute-done | bytes 819232 | tf_op jit(solution)/shard_map/ppermute | solution.py:261
  138.2 5.0 %y_first_far_1.1 = (f32[256,1024]{1,0:T(8,128)}, f32[256,1024]{1,0:T(8,128)S(1)}, f32[8,1024]{1,0:T(8,128)S(1)}) custom-call(f32[1,1]{1,0:T(1,128)} %bitcast.17.forcing_ref, bf16[4,256,1024]{2,1,0:T(8,128)(2,1)S(1)} %copy-done.22, f32[200,1024]{1,0:T(8,128)S(1)} %collective-permute-done.1.refs_0_.refs_1_.refs_2_.refs_3_.refs_12_.refs_16_.refs_8_.refs_20_.refs_24_, ...), custom_call_target="tpu_custom_call" | custom-call | flops 4831838208 | bytes 1048576 | tf_op jit(solution)/shard_map/y_first_far_1/pallas_call | solution.py:229
  145.8 5.3 %y_first_far_0.1 = (f32[256,1024]{1,0:T(8,128)}, f32[256,1024]{1,0:T(8,128)S(1)}, f32[8,1024]{1,0:T(8,128)S(1)}) custom-call(f32[1,1]{1,0:T(1,128)} %bitcast.17.forcing_ref, bf16[4,256,1024]{2,1,0:T(8,128)(2,1)S(1)} %copy-done.22, f32[200,1024]{1,0:T(8,128)S(1)} %collective-permute-done.1.refs_0_.refs_1_.refs_2_.refs_3_.refs_12_.refs_16_.refs_8_.refs_20_.refs_24_, ...), custom_call_target="tpu_custom_call" | custom-call | flops 4831838208 | bytes 1048576 | tf_op jit(solution)/shard_map/y_first_far_0/pallas_call | solution.py:229
  152.1 4.8 %y_first_far_2.1 = (f32[256,1024]{1,0:T(8,128)S(1)}, f32[256,1024]{1,0:T(8,128)S(1)}, f32[8,1024]{1,0:T(8,128)S(1)}) custom-call(f32[1,1]{1,0:T(1,128)} %bitcast.17.forcing_ref, bf16[4,256,1024]{2,1,0:T(8,128)(2,1)S(1)} %copy-done.22, f32[200,1024]{1,0:T(8,128)S(1)} %collective-permute-done.1.refs_0_.refs_1_.refs_2_.refs_3_.refs_12_.refs_16_.refs_8_.refs_20_.refs_24_, ...), custom_call_target="tpu_custom_call" | custom-call | flops 4831838208 | bytes 1048576 | tf_op jit(solution)/shard_map/y_first_far_2/pallas_call | solution.py:229
  157.0 3.6 %collective-permute-done.15 = f32[8,128]{1,0:T(8,128)S(1)} collective-permute-done((f32[8,128]{1,0:T(8,128)S(1)}, f32[8,128]{1,0:T(8,128)S(1)}, u32[]{:S(2)}, u32[]{:S(2)}) %collective-permute-start.15) | collective-permute-done | bytes 4128 | tf_op jit(solution)/shard_map/ppermute | solution.py:261
  161.6 3.5 %collective-permute-done.16 = f32[8,128]{1,0:T(8,128)S(1)} collective-permute-done((f32[8,128]{1,0:T(8,128)S(1)}, f32[8,128]{1,0:T(8,128)S(1)}, u32[]{:S(2)}, u32[]{:S(2)}) %collective-permute-start.16) | collective-permute-done | bytes 4128 | tf_op jit(solution)/shard_map/ppermute | solution.py:261
  166.3 8.6 %x_second_1.1.refs_10_ = f32[256,1024]{1,0:T(8,128)S(1)} custom-call(f32[256,1024]{1,0:T(8,128)} %get-tuple-element.100.refs_0_.refs_4_.refs_8_.refs_9_.refs_12_.refs_17_, f32[256,1024]{1,0:T(8,128)} %get-tuple-element.111.refs_1_.refs_0_.refs_4_.refs_16_, bf16[4,1024,1024]{2,1,0:T(8,128)(2,1)S(1)} %bitcast.46), custom_call_target="tpu_custom_call" | custom-call | flops 9663676416 | bytes 1048576 | tf_op jit(solution)/shard_map/x_second_1/pallas_call | solution.py:160
  176.6 3.0 %collective-permute-done.18 = f32[8,128]{1,0:T(8,128)S(1)} collective-permute-done((f32[8,128]{1,0:T(8,128)S(1)}, f32[8,128]{1,0:T(8,128)S(1)}, u32[]{:S(2)}, u32[]{:S(2)}) %collective-permute-start.18) | collective-permute-done | bytes 4128 | tf_op jit(solution)/shard_map/ppermute | solution.py:261
  186.8 7.5 %y_second_1.1 = (f32[64,1024]{1,0:T(8,128)S(1)}, f32[64,1024]{1,0:T(8,128)S(1)}, f32[64,1024]{1,0:T(8,128)S(1)}, f32[64,1024]{1,0:T(8,128)S(1)}) custom-call(f32[1,1]{1,0:T(1,128)} %bitcast.19.forcing_ref, bf16[4,256,1024]{2,1,0:T(8,128)(2,1)S(1)} %copy-done.23, f32[256,1024]{1,0:T(8,128)} %get-tuple-element.100.refs_0_.refs_4_.refs_8_.refs_9_.refs_12_.refs_17_, ...), custom_call_target="tpu_custom_call" | custom-call | flops 9663676416 | bytes 1048576 | tf_op jit(solution)/shard_map/y_second_1/pallas_call | solution.py:229
  194.5 8.1 %x_second_0.1.refs_18_ = f32[256,1024]{1,0:T(8,128)S(1)} custom-call(f32[256,1024]{1,0:T(8,128)} %get-tuple-element.111.refs_1_.refs_0_.refs_4_.refs_16_, bf16[4,1024,1024]{2,1,0:T(8,128)(2,1)S(1)} %bitcast.48), custom_call_target="tpu_custom_call" | custom-call | flops 268435456 | bytes 1048576 | tf_op jit(solution)/shard_map/x_second_0/pallas_call | solution.py:160
  202.6 3.7 %collective-permute-done.27.refs_2_.refs_6_ = f32[256,1024]{1,0:T(8,128)} collective-permute-done((f32[256,1024]{1,0:T(8,128)}, f32[256,1024]{1,0:T(8,128)}, u32[]{:S(2)}, u32[]{:S(2)}) %collective-permute-start.27) | collective-permute-done | bytes 1048608 | tf_op jit(solution)/shard_map/ppermute | solution.py:261
  206.4 2.9 collective-permute-start.25
  210.7 3.4 %copy-done.1 = bf16[4,1024,1024]{2,1,0:T(8,128)(2,1)S(1)} copy-done((bf16[4,1024,1024]{2,1,0:T(8,128)(2,1)S(1)}, bf16[4,1024,1024]{2,1,0:T(8,128)(2,1)}, u32[]{:S(2)}) %copy-start.1) | copy-done | bytes 8388632
  214.1 8.2 %x_second_2.1 = f32[256,1024]{1,0:T(8,128)S(1)} custom-call(f32[256,1024]{1,0:T(8,128)S(1)} %copy-done.42, f32[256,1024]{1,0:T(8,128)} %get-tuple-element.111.refs_1_.refs_0_.refs_4_.refs_16_, bf16[4,1024,1024]{2,1,0:T(8,128)(2,1)S(1)} %copy-done.1), custom_call_target="tpu_custom_call" | custom-call | flops 268435456 | bytes 1048576 | tf_op jit(solution)/shard_map/x_second_2/pallas_call | solution.py:160
  222.4 5.2 %collective-permute-done.25 = f32[64,1024]{1,0:T(8,128)S(1)} collective-permute-done((f32[64,1024]{1,0:T(8,128)}, f32[64,1024]{1,0:T(8,128)S(1)}, u32[]{:S(2)}, u32[]{:S(2)}) %collective-permute-start.25) | collective-permute-done | bytes 262176 | tf_op jit(solution)/shard_map/ppermute | solution.py:261
  227.6 7.9 %y_second_0.1 = (f32[64,1024]{1,0:T(8,128)S(1)}, f32[64,1024]{1,0:T(8,128)S(1)}, f32[64,1024]{1,0:T(8,128)S(1)}, f32[64,1024]{1,0:T(8,128)S(1)}) custom-call(f32[1,1]{1,0:T(1,128)} %bitcast.19.forcing_ref, bf16[4,256,1024]{2,1,0:T(8,128)(2,1)S(1)} %copy-done.23, f32[256,1024]{1,0:T(8,128)} %get-tuple-element.111.refs_1_.refs_0_.refs_4_.refs_16_, ...), custom_call_target="tpu_custom_call" | custom-call | flops 9663676416 | bytes 1048576 | tf_op jit(solution)/shard_map/y_second_0/pallas_call | solution.py:229
  239.6 4.8 %collective-permute-done.29 = f32[64,1024]{1,0:T(8,128)S(1)} collective-permute-done((f32[64,1024]{1,0:T(8,128)S(1)}, f32[64,1024]{1,0:T(8,128)S(1)}, u32[]{:S(2)}, u32[]{:S(2)}) %collective-permute-start.29) | collective-permute-done | bytes 262176 | tf_op jit(solution)/shard_map/ppermute | solution.py:261
  244.5 12.5 %collective-permute-done.30 = f32[64,1024]{1,0:T(8,128)S(1)} collective-permute-done((f32[64,1024]{1,0:T(8,128)S(1)}, f32[64,1024]{1,0:T(8,128)S(1)}, u32[]{:S(2)}, u32[]{:S(2)}) %collective-permute-start.30) | collective-permute-done | bytes 262176 | tf_op jit(solution)/shard_map/ppermute | solution.py:261
  257.0 6.4 %collective-permute-done.31 = f32[64,1024]{1,0:T(8,128)S(1)} collective-permute-done((f32[64,1024]{1,0:T(8,128)S(1)}, f32[64,1024]{1,0:T(8,128)S(1)}, u32[]{:S(2)}, u32[]{:S(2)}) %collective-permute-start.31) | collective-permute-done | bytes 262176 | tf_op jit(solution)/shard_map/ppermute | solution.py:261
  263.4 7.7 %y_second_2.1 = (f32[3,4,64,1024]{3,2,1,0:T(8,128)S(1)}, f32[64,1024]{1,0:T(8,128)S(1)}, f32[64,1024]{1,0:T(8,128)S(1)}, f32[64,1024]{1,0:T(8,128)S(1)}) fusion(f32[3,4,64,1024]{3,2,1,0:T(8,128)S(1)} %bitcast_dynamic-update-slice_fusion.4, s32[]{:T(128)S(6)} %select_n.33, f32[1,1]{1,0:T(1,128)} %bitcast.19.forcing_ref, ...), kind=kCustom, calls=%fused_computation.3 | custom fusion | flops 9663676416 | bytes 13631496 | tf_op jit(solution)/shard_map/y_second_2/pallas_call | solution.py:229
  274.7 7.1 %collective-permute-done.34 = f32[64,1024]{1,0:T(8,128)S(1)} collective-permute-done((f32[64,1024]{1,0:T(8,128)S(1)}, f32[64,1024]{1,0:T(8,128)S(1)}, u32[]{:S(2)}, u32[]{:S(2)}) %collective-permute-start.34) | collective-permute-done | bytes 262176 | tf_op jit(solution)/shard_map/ppermute | solution.py:261
  281.8 10.1 %collective-permute-done.35 = f32[64,1024]{1,0:T(8,128)S(1)} collective-permute-done((f32[64,1024]{1,0:T(8,128)S(1)}, f32[64,1024]{1,0:T(8,128)S(1)}, u32[]{:S(2)}, u32[]{:S(2)}) %collective-permute-start.35) | collective-permute-done | bytes 262176 | tf_op jit(solution)/shard_map/ppermute | solution.py:261
  292.0 5.4 %collective-permute-done.36 = f32[64,1024]{1,0:T(8,128)S(1)} collective-permute-done((f32[64,1024]{1,0:T(8,128)S(1)}, f32[64,1024]{1,0:T(8,128)S(1)}, u32[]{:S(2)}, u32[]{:S(2)}) %collective-permute-start.36) | collective-permute-done | bytes 262176 | tf_op jit(solution)/shard_map/ppermute | solution.py:261
  (220 shorter events, 71.4 us)
Async XLA Ops:
  4.1 35.2 %collective-permute-start.2 = (f32[200,1024]{1,0:T(8,128)S(1)}, f32[200,1024]{1,0:T(8,128)S(1)}, u32[]{:S(2)}, u32[]{:S(2)}) collective-permute-start(f32[200,1024]{1,0:T(8,128)S(1)} %get-tuple-element.68), channel_id=1, source_target_pairs={{0,4},{1,5},{2,6},{3,7},{4,0},{5,1},{6,2},{7,3},{8,12},{9,13},{10,... | collective-permute-start | bytes 2457608 | tf_op jit(solution)/shard_map/ppermute | solution.py:261
  5.7 45.4 %collective-permute-start.1 = (f32[200,1024]{1,0:T(8,128)}, f32[200,1024]{1,0:T(8,128)S(1)}, u32[]{:S(2)}, u32[]{:S(2)}) collective-permute-start(f32[200,1024]{1,0:T(8,128)} %get-tuple-element.67), channel_id=1, source_target_pairs={{0,8},{1,9},{2,10},{3,11},{4,12},{5,13},{6,14},{7,15},{8,0},{9,1},... | collective-permute-start | bytes 2457608 | tf_op jit(solution)/shard_map/ppermute | solution.py:261
  6.0 51.5 %collective-permute-start = (f32[200,1024]{1,0:T(8,128)S(1)}, f32[200,1024]{1,0:T(8,128)}, u32[]{:S(2)}, u32[]{:S(2)}) collective-permute-start(f32[200,1024]{1,0:T(8,128)S(1)} %get-tuple-element.87.refs_0_.refs_2_.refs_4_.refs_6_.refs_8_.refs_10_.refs_14_.refs_18_.refs_22_), channel_id=1, source_target_pairs={{0,2},{1,3},{2,0},{3,1},{4,6},{5,7},{6,4},{7,5},{8,10},{9,11},{10,... | collective-permute-start | bytes 2457608 | tf_op jit(solution)/shard_map/ppermute | solution.py:261
  39.3 19.1 %collective-permute-start.5 = (f32[200,1024]{1,0:T(8,128)S(1)}, f32[200,1024]{1,0:T(8,128)S(1)}, u32[]{:S(2)}, u32[]{:S(2)}) collective-permute-start(f32[200,1024]{1,0:T(8,128)S(1)} %collective-permute-done.2.refs_1_.refs_3_.refs_5_.refs_7_.refs_9_.refs_11_.refs_15_.refs_19_.refs_23_), channel_id=1, source_target_pairs={{0,2},{1,3},{2,0},{3,1},{4,6},{5,7},{6,4},{7,5},{8,10},{9,11},{10,... | collective-permute-start | bytes 2457608 | tf_op jit(solution)/shard_map/ppermute | solution.py:261
  40.8 37.4 %collective-permute-start.9 = (f32[200,1024]{1,0:T(8,128)S(1)}, f32[200,1024]{1,0:T(8,128)S(1)}, u32[]{:S(2)}, u32[]{:S(2)}) collective-permute-start(f32[200,1024]{1,0:T(8,128)S(1)} %copy-done.56), channel_id=1, source_target_pairs={{0,12},{1,13},{2,14},{3,15},{4,8},{5,9},{6,10},{7,11},{8,4},{9,5},... | collective-permute-start | bytes 2457608 | tf_op jit(solution)/shard_map/ppermute | solution.py:261
  51.1 28.7 %collective-permute-start.6 = (f32[200,1024]{1,0:T(8,128)S(1)}, f32[200,1024]{1,0:T(8,128)S(1)}, u32[]{:S(2)}, u32[]{:S(2)}) collective-permute-start(f32[200,1024]{1,0:T(8,128)S(1)} %collective-permute-done.2.refs_1_.refs_3_.refs_5_.refs_7_.refs_9_.refs_11_.refs_15_.refs_19_.refs_23_), channel_id=1, source_target_pairs={{0,1},{1,0},{2,3},{3,2},{4,5},{5,4},{6,7},{7,6},{8,9},{9,8},{10,11... | collective-permute-start | bytes 2457608 | tf_op jit(solution)/shard_map/ppermute | solution.py:261
  51.2 28.6 %collective-permute-start.3 = (f32[200,1024]{1,0:T(8,128)S(1)}, f32[200,1024]{1,0:T(8,128)S(1)}, u32[]{:S(2)}, u32[]{:S(2)}) collective-permute-start(f32[200,1024]{1,0:T(8,128)S(1)} %get-tuple-element.87.refs_0_.refs_2_.refs_4_.refs_6_.refs_8_.refs_10_.refs_14_.refs_18_.refs_22_), channel_id=1, source_target_pairs={{0,1},{1,0},{2,3},{3,2},{4,5},{5,4},{6,7},{7,6},{8,9},{9,8},{10,11... | collective-permute-start | bytes 2457608 | tf_op jit(solution)/shard_map/ppermute | solution.py:261
  57.5 28.6 %collective-permute-start.4 = (f32[200,1024]{1,0:T(8,128)}, f32[200,1024]{1,0:T(8,128)S(1)}, u32[]{:S(2)}, u32[]{:S(2)}) collective-permute-start(f32[200,1024]{1,0:T(8,128)} %collective-permute-done.refs_4_.refs_12_), channel_id=1, source_target_pairs={{0,1},{1,0},{2,3},{3,2},{4,5},{5,4},{6,7},{7,6},{8,9},{9,8},{10,11... | collective-permute-start | bytes 2457608 | tf_op jit(solution)/shard_map/ppermute | solution.py:261
  58.4 27.7 %collective-permute-start.7 = (f32[200,1024]{1,0:T(8,128)S(1)}, f32[200,1024]{1,0:T(8,128)S(1)}, u32[]{:S(2)}, u32[]{:S(2)}) collective-permute-start(f32[200,1024]{1,0:T(8,128)S(1)} %collective-permute-done.5.refs_5_.refs_13_), channel_id=1, source_target_pairs={{0,1},{1,0},{2,3},{3,2},{4,5},{5,4},{6,7},{7,6},{8,9},{9,8},{10,11... | collective-permute-start | bytes 2457608 | tf_op jit(solution)/shard_map/ppermute | solution.py:261
  78.2 21.2 %collective-permute-start.8 = (f32[200,1024]{1,0:T(8,128)S(1)}, f32[200,1024]{1,0:T(8,128)S(1)}, u32[]{:S(2)}, u32[]{:S(2)}) collective-permute-start(f32[200,1024]{1,0:T(8,128)S(1)} %collective-permute-done.1.refs_0_.refs_1_.refs_2_.refs_3_.refs_12_.refs_16_.refs_8_.refs_20_.refs_24_), channel_id=1, source_target_pairs={{0,2},{1,3},{2,0},{3,1},{4,6},{5,7},{6,4},{7,5},{8,10},{9,11},{10,... | collective-permute-start | bytes 2457608 | tf_op jit(solution)/shard_map/ppermute | solution.py:261
  79.7 34.9 %collective-permute-start.12 = (f32[200,1024]{1,0:T(8,128)S(1)}, f32[200,1024]{1,0:T(8,128)S(1)}, u32[]{:S(2)}, u32[]{:S(2)}) collective-permute-start(f32[200,1024]{1,0:T(8,128)S(1)} %collective-permute-done.9.refs_0_.refs_1_.refs_2_.refs_3_.refs_13_.refs_17_.refs_9_.refs_21_.refs_25_), channel_id=1, source_target_pairs={{0,2},{1,3},{2,0},{3,1},{4,6},{5,7},{6,4},{7,5},{8,10},{9,11},{10,... | collective-permute-start | bytes 2457608 | tf_op jit(solution)/shard_map/ppermute | solution.py:261
  98.0 16.7 %collective-permute-start.10 = (f32[200,1024]{1,0:T(8,128)S(1)}, f32[200,1024]{1,0:T(8,128)S(1)}, u32[]{:S(2)}, u32[]{:S(2)}) collective-permute-start(f32[200,1024]{1,0:T(8,128)S(1)} %collective-permute-done.1.refs_0_.refs_1_.refs_2_.refs_3_.refs_12_.refs_16_.refs_8_.refs_20_.refs_24_), channel_id=1, source_target_pairs={{0,1},{1,0},{2,3},{3,2},{4,5},{5,4},{6,7},{7,6},{8,9},{9,8},{10,11... | collective-permute-start | bytes 2457608 | tf_op jit(solution)/shard_map/ppermute | solution.py:261
  99.4 15.3 %collective-permute-start.11 = (f32[200,1024]{1,0:T(8,128)S(1)}, f32[200,1024]{1,0:T(8,128)S(1)}, u32[]{:S(2)}, u32[]{:S(2)}) collective-permute-start(f32[200,1024]{1,0:T(8,128)S(1)} %collective-permute-done.8.refs_4_.refs_12_), channel_id=1, source_target_pairs={{0,1},{1,0},{2,3},{3,2},{4,5},{5,4},{6,7},{7,6},{8,9},{9,8},{10,11... | collective-permute-start | bytes 2457608 | tf_op jit(solution)/shard_map/ppermute | solution.py:261
  99.4 15.3 %collective-permute-start.13 = (f32[200,1024]{1,0:T(8,128)S(1)}, f32[200,1024]{1,0:T(8,128)S(1)}, u32[]{:S(2)}, u32[]{:S(2)}) collective-permute-start(f32[200,1024]{1,0:T(8,128)S(1)} %collective-permute-done.9.refs_0_.refs_1_.refs_2_.refs_3_.refs_13_.refs_17_.refs_9_.refs_21_.refs_25_), channel_id=1, source_target_pairs={{0,1},{1,0},{2,3},{3,2},{4,5},{5,4},{6,7},{7,6},{8,9},{9,8},{10,11... | collective-permute-start | bytes 2457608 | tf_op jit(solution)/shard_map/ppermute | solution.py:261
  144.3 31.6 %collective-permute-start.19 = (f32[256,1024]{1,0:T(8,128)}, f32[256,1024]{1,0:T(8,128)}, u32[]{:S(2)}, u32[]{:S(2)}) collective-permute-start(f32[256,1024]{1,0:T(8,128)} %get-tuple-element.100.refs_0_.refs_4_.refs_8_.refs_9_.refs_12_.refs_17_), channel_id=1, source_target_pairs={{0,2},{1,3},{2,0},{3,1},{4,6},{5,7},{6,4},{7,5},{8,10},{9,11},{10,... | collective-permute-start | bytes 3145736 | tf_op jit(solution)/shard_map/ppermute | solution.py:261
  165.1 18.5 %collective-permute-start.22 = (f32[256,1024]{1,0:T(8,128)}, f32[256,1024]{1,0:T(8,128)S(1)}, u32[]{:S(2)}, u32[]{:S(2)}) collective-permute-start(f32[256,1024]{1,0:T(8,128)} %get-tuple-element.100.refs_0_.refs_4_.refs_8_.refs_9_.refs_12_.refs_17_), channel_id=1, source_target_pairs={{0,1},{1,0},{2,3},{3,2},{4,5},{5,4},{6,7},{7,6},{8,9},{9,8},{10,11... | collective-permute-start | bytes 3145736 | tf_op jit(solution)/shard_map/ppermute | solution.py:261
  165.6 14.1 %collective-permute-start.20 = (f32[256,1024]{1,0:T(8,128)}, f32[256,1024]{1,0:T(8,128)S(1)}, u32[]{:S(2)}, u32[]{:S(2)}) collective-permute-start(f32[256,1024]{1,0:T(8,128)} %get-tuple-element.111.refs_1_.refs_0_.refs_4_.refs_16_), channel_id=1, source_target_pairs={{0,1},{1,0},{2,3},{3,2},{4,5},{5,4},{6,7},{7,6},{8,9},{9,8},{10,11... | collective-permute-start | bytes 3145736 | tf_op jit(solution)/shard_map/ppermute | solution.py:261
  165.6 15.1 %collective-permute-start.21 = (f32[256,1024]{1,0:T(8,128)S(1)}, f32[256,1024]{1,0:T(8,128)S(1)}, u32[]{:S(2)}, u32[]{:S(2)}) collective-permute-start(f32[256,1024]{1,0:T(8,128)S(1)} %get-tuple-element.120.refs_0_), channel_id=1, source_target_pairs={{0,1},{1,0},{2,3},{3,2},{4,5},{5,4},{6,7},{7,6},{8,9},{9,8},{10,11... | collective-permute-start | bytes 3145736 | tf_op jit(solution)/shard_map/ppermute | solution.py:261
  175.9 7.8 %collective-permute-start.23 = (f32[256,1024]{1,0:T(8,128)}, f32[256,1024]{1,0:T(8,128)}, u32[]{:S(2)}, u32[]{:S(2)}) collective-permute-start(f32[256,1024]{1,0:T(8,128)} %collective-permute-done.19.refs_2_.refs_6_.refs_10_.refs_14_), channel_id=1, source_target_pairs={{0,1},{1,0},{2,3},{3,2},{4,5},{5,4},{6,7},{7,6},{8,9},{9,8},{10,11... | collective-permute-start | bytes 3145736 | tf_op jit(solution)/shard_map/ppermute | solution.py:261
  181.7 24.6 %collective-permute-start.27 = (f32[256,1024]{1,0:T(8,128)}, f32[256,1024]{1,0:T(8,128)}, u32[]{:S(2)}, u32[]{:S(2)}) collective-permute-start(f32[256,1024]{1,0:T(8,128)} %get-tuple-element.111.refs_1_.refs_0_.refs_4_.refs_16_), channel_id=1, source_target_pairs={{0,2},{1,3},{2,0},{3,1},{4,6},{5,7},{6,4},{7,5},{8,10},{9,11},{10,... | collective-permute-start | bytes 3145736 | tf_op jit(solution)/shard_map/ppermute | solution.py:261
  206.2 21.3 %collective-permute-start.28 = (f32[256,1024]{1,0:T(8,128)}, f32[256,1024]{1,0:T(8,128)}, u32[]{:S(2)}, u32[]{:S(2)}) collective-permute-start(f32[256,1024]{1,0:T(8,128)} %collective-permute-done.27.refs_2_.refs_6_), channel_id=1, source_target_pairs={{0,1},{1,0},{2,3},{3,2},{4,5},{5,4},{6,7},{7,6},{8,9},{9,8},{10,11... | collective-permute-start | bytes 3145736 | tf_op jit(solution)/shard_map/ppermute | solution.py:261
  206.2 16.1 %collective-permute-start.24 = (f32[64,1024]{1,0:T(8,128)}, f32[64,1024]{1,0:T(8,128)S(1)}, u32[]{:S(2)}, u32[]{:S(2)}) collective-permute-start(f32[64,1024]{1,0:T(8,128)} %copy-done.59), channel_id=1, source_target_pairs={{0,4},{1,5},{2,6},{3,7},{4,0},{5,1},{6,2},{7,3},{8,12},{9,13},{10,... | collective-permute-start | bytes 786440 | tf_op jit(solution)/shard_map/ppermute | solution.py:261
  206.4 21.2 %collective-permute-start.25 = (f32[64,1024]{1,0:T(8,128)}, f32[64,1024]{1,0:T(8,128)S(1)}, u32[]{:S(2)}, u32[]{:S(2)}) collective-permute-start(f32[64,1024]{1,0:T(8,128)} %copy-done.58), channel_id=1, source_target_pairs={{0,8},{1,9},{2,10},{3,11},{4,12},{5,13},{6,14},{7,15},{8,0},{9,1},... | collective-permute-start | bytes 786440 | tf_op jit(solution)/shard_map/ppermute | solution.py:261
  209.3 28.5 %collective-permute-start.26 = (f32[64,1024]{1,0:T(8,128)}, f32[64,1024]{1,0:T(8,128)S(1)}, u32[]{:S(2)}, u32[]{:S(2)}) collective-permute-start(f32[64,1024]{1,0:T(8,128)} %copy-done.57), channel_id=1, source_target_pairs={{0,12},{1,13},{2,14},{3,15},{4,8},{5,9},{6,10},{7,11},{8,4},{9,5},... | collective-permute-start | bytes 786440 | tf_op jit(solution)/shard_map/ppermute | solution.py:261
  209.7 28.1 %collective-permute-start.32 = (f32[256,1024]{1,0:T(8,128)}, f32[256,1024]{1,0:T(8,128)S(1)}, u32[]{:S(2)}, u32[]{:S(2)}) collective-permute-start(f32[256,1024]{1,0:T(8,128)} %copy-done.41), channel_id=1, source_target_pairs={{0,2},{1,3},{2,0},{3,1},{4,6},{5,7},{6,4},{7,5},{8,10},{9,11},{10,... | collective-permute-start | bytes 3145736 | tf_op jit(solution)/shard_map/ppermute | solution.py:261
  235.5 8.9 %collective-permute-start.29 = (f32[64,1024]{1,0:T(8,128)S(1)}, f32[64,1024]{1,0:T(8,128)S(1)}, u32[]{:S(2)}, u32[]{:S(2)}) collective-permute-start(f32[64,1024]{1,0:T(8,128)S(1)} %get-tuple-element.117), channel_id=1, source_target_pairs={{0,4},{1,5},{2,6},{3,7},{4,0},{5,1},{6,2},{7,3},{8,12},{9,13},{10,... | collective-permute-start | bytes 786440 | tf_op jit(solution)/shard_map/ppermute | solution.py:261
  237.8 25.6 %collective-permute-start.33 = (f32[256,1024]{1,0:T(8,128)S(1)}, f32[256,1024]{1,0:T(8,128)S(1)}, u32[]{:S(2)}, u32[]{:S(2)}) collective-permute-start(f32[256,1024]{1,0:T(8,128)S(1)} %collective-permute-done.32), channel_id=1, source_target_pairs={{0,1},{1,0},{2,3},{3,2},{4,5},{5,4},{6,7},{7,6},{8,9},{9,8},{10,11... | collective-permute-start | bytes 3145736 | tf_op jit(solution)/shard_map/ppermute | solution.py:261
  237.9 19.1 %collective-permute-start.30 = (f32[64,1024]{1,0:T(8,128)S(1)}, f32[64,1024]{1,0:T(8,128)S(1)}, u32[]{:S(2)}, u32[]{:S(2)}) collective-permute-start(f32[64,1024]{1,0:T(8,128)S(1)} %get-tuple-element.118), channel_id=1, source_target_pairs={{0,8},{1,9},{2,10},{3,11},{4,12},{5,13},{6,14},{7,15},{8,0},{9,1},... | collective-permute-start | bytes 786440 | tf_op jit(solution)/shard_map/ppermute | solution.py:261
  239.1 24.3 %collective-permute-start.31 = (f32[64,1024]{1,0:T(8,128)S(1)}, f32[64,1024]{1,0:T(8,128)S(1)}, u32[]{:S(2)}, u32[]{:S(2)}) collective-permute-start(f32[64,1024]{1,0:T(8,128)S(1)} %get-tuple-element.119), channel_id=1, source_target_pairs={{0,12},{1,13},{2,14},{3,15},{4,8},{5,9},{6,10},{7,11},{8,4},{9,5},... | collective-permute-start | bytes 786440 | tf_op jit(solution)/shard_map/ppermute | solution.py:261
  271.1 10.6 %collective-permute-start.34 = (f32[64,1024]{1,0:T(8,128)S(1)}, f32[64,1024]{1,0:T(8,128)S(1)}, u32[]{:S(2)}, u32[]{:S(2)}) collective-permute-start(f32[64,1024]{1,0:T(8,128)S(1)} %get-tuple-element.130), channel_id=1, source_target_pairs={{0,4},{1,5},{2,6},{3,7},{4,0},{5,1},{6,2},{7,3},{8,12},{9,13},{10,... | collective-permute-start | bytes 786440 | tf_op jit(solution)/shard_map/ppermute | solution.py:261
  271.2 20.7 %collective-permute-start.35 = (f32[64,1024]{1,0:T(8,128)S(1)}, f32[64,1024]{1,0:T(8,128)S(1)}, u32[]{:S(2)}, u32[]{:S(2)}) collective-permute-start(f32[64,1024]{1,0:T(8,128)S(1)} %get-tuple-element.132), channel_id=1, source_target_pairs={{0,8},{1,9},{2,10},{3,11},{4,12},{5,13},{6,14},{7,15},{8,0},{9,1},... | collective-permute-start | bytes 786440 | tf_op jit(solution)/shard_map/ppermute | solution.py:261
  273.9 23.5 %collective-permute-start.36 = (f32[64,1024]{1,0:T(8,128)S(1)}, f32[64,1024]{1,0:T(8,128)S(1)}, u32[]{:S(2)}, u32[]{:S(2)}) collective-permute-start(f32[64,1024]{1,0:T(8,128)S(1)} %get-tuple-element.134), channel_id=1, source_target_pairs={{0,12},{1,13},{2,14},{3,15},{4,8},{5,9},{6,10},{7,11},{8,4},{9,5},... | collective-permute-start | bytes 786440 | tf_op jit(solution)/shard_map/ppermute | solution.py:261
  (74 other events, 625.2 us)

commit v7 on v6

--- a/solution.py
+++ b/solution.py
@@ -196,42 +196,49 @@
     slope_ref[...], rest_ref[...] = y_sums(matrix_ref, fields, carriers, sums)
 
 
-def tendency(forcing_ref, field, carrier, x_terms, sums):
-    return joined(x_terms) + joined(carrier) * sums[0] + sums[1] + forcing_ref[0, 0] * field
-
-
-def first_kernel(counts, forcing_ref, matrix_ref, *refs):
-    fields, carriers, sums, own, own_carrier, x_terms, (middle_ref, base_ref, square_ref) = cut(refs, counts)
+def tendency(cells, totals, field, carrier, x_terms, sums):
+    total = jnp.sum(functools.reduce(jnp.add, [ref[...] for ref in totals]), keepdims=True)
+    forcing = power_input / (total / cells)
+    return joined(x_terms) + joined(carrier) * sums[0] + sums[1] + forcing * field
+
+
+def first_kernel(cells, counts, matrix_ref, *refs):
+    fields, carriers, sums, own, own_carrier, x_terms, totals, (middle_ref, base_ref, square_ref) = cut(refs, counts)
     rows = matrix_ref.shape[1]
     field = joined(own)
-    first = tendency(forcing_ref, field, own_carrier, x_terms, y_sums(matrix_ref, fields, carriers, sums))
+    first = tendency(cells, totals, field, own_carrier, x_terms, y_sums(matrix_ref, fields, carriers, sums))
     middle = field + (time_step * first_weight) * first
     middle_ref[...] = middle
     base_ref[...] = middle - (time_step * back_weight) * first
     square_ref[...] = jnp.sum((middle * middle).reshape(rows // 8, 8, middle.shape[1]), axis=0)
 
 
-def second_kernel(counts, forcing_ref, matrix_ref, *refs):
-    fields, carriers, sums, own, own_carrier, x_terms, (base_ref, *out_refs) = cut(refs, counts)
+def second_kernel(cells, counts, matrix_ref, *refs):
+    fields, carriers, sums, own, own_carrier, x_terms, totals, (base_ref, *out_refs) = cut(refs, counts)
     field = joined(own)
-    second = tendency(forcing_ref, field, own_carrier, x_terms, y_sums(matrix_ref, fields, carriers, sums))
+    second = tendency(cells, totals, field, own_carrier, x_terms, y_sums(matrix_ref, fields, carriers, sums))
     out = base_ref[...] + (time_step * second_weight) * second
     size = out_refs[0].shape[0]
     for place, out_ref in enumerate(out_refs):
         out_ref[...] = out[place * size:(place + 1) * size]
 
 
-def y_call(kernel, forcing, matrix, part, groups, out_rows, name, weight=36):
+def y_call(kernel, matrix, part, groups, out_rows, name, totals=(), weight=36):
     rows, length = matrix.shape[1], groups[0][0][0].shape[1]
     depth = sum(piece[2] for piece in groups[0])
     tile = min(256, length)
     pieces = [piece for group in groups for piece in group]
-    return pl.pallas_call(
-        functools.partial(kernel, tuple(len(group) for group in groups[:6])),
+    counts = [len(group) for group in groups]
+    specs = [piece_spec(piece, tile, lambda n: n) for piece in pieces]
+    if totals:
+        start = sum(counts[:6])
+        pieces[start:start] = totals
+        specs[start:start] = [piece_spec(piece, piece[0].shape[1], lambda n: 0) for piece in totals]
+        counts[6:] = [len(totals)]
+    return pl.pallas_call(
+        functools.partial(kernel, tuple(counts)),
         grid=(length // tile,),
-        in_specs=[pl.BlockSpec(memory_space=pltpu.SMEM)] * len(forcing)
-        + [pl.BlockSpec((4, rows, depth), lambda n: (0, 0, part))]
-        + [piece_spec(piece, tile, lambda n: n) for piece in pieces],
+        in_specs=[pl.BlockSpec((4, rows, depth), lambda n: (0, 0, part))] + specs,
         out_specs=[pl.BlockSpec((count, tile), lambda n: (0, n)) for count in out_rows],
         out_shape=[jax.ShapeDtypeStruct((count, length), F32) for count in out_rows],
         compiler_params=params(),
@@ -239,7 +246,50 @@
             flops=weight * rows * depth * length, bytes_accessed=4 * rows * length, transcendentals=0
         ),
         name=name,
-    )(*forcing, matrix, *[piece[0] for piece in pieces])
+    )(matrix, *[piece[0] for piece in pieces])
+
+
+def fold_kernel(*refs):
+    total = functools.reduce(jnp.add, [ref[...] for ref in refs[:-1]])
+    refs[-1][...] = functools.reduce(jnp.add, [total[:, k:k + 128] for k in range(0, total.shape[1], 128)])
+
+
+def fold(arrays, name):
+    return pl.pallas_call(
+        fold_kernel,
+        out_shape=jax.ShapeDtypeStruct((8, 128), F32),
+        compiler_params=params(),
+        name=name,
+    )(*arrays)
+
+
+def place_kernel(components, planes, plane_ref, *refs):
+    out_ref = refs[-1]
+    for n in range(components):
+        @pl.when(pl.program_id(0) == n)
+        def _():
+            for d in range(planes):
+                out_ref[plane_ref[0] ^ d] = refs[n * planes + d][...]
+
+
+def place_blocks(plane, blocks, components, shape, out):
+    planes, size, length = shape[1:]
+    first, step = components[0], components[-1] - components[0]
+    whole = pl.BlockSpec((size, length), lambda n, plane_ref: (0, 0))
+    arrays = [block for i in components for block in blocks[i]]
+    return pl.pallas_call(
+        functools.partial(place_kernel, len(components), planes),
+        grid_spec=pltpu.PrefetchScalarGridSpec(
+            num_scalar_prefetch=1,
+            grid=(len(components),),
+            in_specs=[whole] * len(arrays) + [pl.BlockSpec(memory_space=pl.ANY)] * (out is not None),
+            out_specs=pl.BlockSpec((None, planes, size, length), lambda n, plane_ref: (first + step * n, 0, 0, 0)),
+        ),
+        out_shape=jax.ShapeDtypeStruct(shape, F32),
+        input_output_aliases={} if out is None else {1 + len(arrays): 0},
+        compiler_params=params(),
+        name="place",
+    )(plane.reshape(1).astype(jnp.int32), *arrays, *([] if out is None else [out]))
 
 
 def after(values, *earlier):
@@ -259,17 +309,6 @@
 
     def swap(x, distance):
         return lax.ppermute(x, "row", [(r, r ^ distance) for r in range(devices)])
-
-    def swap_sum(x, distances):
-        for distance in distances:
-            x = x + swap(x, distance)
-        return x
-
-    def doubling(start, stop):
-        return [start << step for step in range((stop // start).bit_length() - 1)]
-
-    def forcing_of(total):
-        return (power_input / (jnp.sum(total) / cells)).reshape(1, 1)
 
     def across_chips(x):
         return [swap(x, 2 * h) for h in range(1, chips)]
@@ -325,7 +364,7 @@
     for d in parts[0]:
         others[d] = after(others[d], x_terms[-1])
         fars[d] = across_cores(others[d])
-    here[last] = after(here[last], x_terms[-1], [twins[d] for d in parts[0]])
+    here[last] = after(here[last], x_terms[-1], [twins[d] for d in parts[0]], [others[d] for d in parts[1][:-1]])
     others[last] = across_chips(here[last])
     x_terms.append(x_first([last], f"x_first_{last}"))
 
@@ -334,7 +373,7 @@
         fields = block_pieces(i, 0)
         fields = [(after(fields[0][0], previous), *fields[0][1:])] + fields[1:]
         sums[i] = y_call(
-            partial_kernel, [], along_y_matrix, 0, [fields, block_pieces(1, 0) if i != 1 else [], []],
+            partial_kernel, along_y_matrix, 0, [fields, block_pieces(1, 0) if i != 1 else [], []],
             [kept, kept], f"y_first_near_{i}",
         )
         previous = sums[i]
@@ -345,9 +384,10 @@
     twins[last] = across_cores([after(here[last], sums[0])])
     others[last] = after(others[last], sums[2])
     fars[last] = across_cores(others[last])
-    forcing = [forcing_of(sum(
-        block[components * size:] for d in range(planes) for block in [here[d]] + others[d] + twins[d] + fars[d]
-    ))]
+    totals = [
+        (block, components * size // 8, 8)
+        for d in range(planes) for block in [here[d]] + others[d] + twins[d] + fars[d]
+    ]
 
     middle, base, square = [None] * 3, [None] * 3, [None] * 3
     middle_others, middle_twin, middle_far = [None] * 3, [None] * 3, [None] * 3
@@ -361,25 +401,26 @@
         own = here_pieces(i, range(planes))
         terms = [(x_terms[0], i, len(parts[0]) * size)] + [(x, i, size) for x in x_terms[1:]]
         middle[i], base[i], square[i] = y_call(
-            first_kernel, forcing, along_y_matrix, 1,
+            functools.partial(first_kernel, cells), along_y_matrix, 1,
             [fields, block_pieces(1, 1) if i != 1 else [], [piece(x) for x in sums[i]], own,
-             here_pieces(1, range(planes)), terms], [kept, kept, 8], f"y_first_far_{i}",
+             here_pieces(1, range(planes)), terms], [kept, kept, 8], f"y_first_far_{i}", totals,
         )
         previous = middle[i]
         if i == 1:
             middle_others[1] = across_chips(middle[1])
             middle_twin[1] = across_cores([middle[1]])
 
-    total = jnp.sum((square[0] + square[1] + square[2]).reshape(8, length // 128, 128), axis=1)
-    total = swap_sum(total, doubling(group, devices) + [1])
+    total = fold(square, "fold_own")
+    total = fold([total] + [swap(total, d * group) for d in range(1, planes)], "fold_planes")
     middle_twin[0] = across_cores([after(middle[0], square[2])])
     middle_twin[2] = across_cores([middle[2]])
     x_terms = [None] * 3
     x_terms[1] = along_x([piece(after(middle[1], total))], [piece(middle[0])], along_x_matrix, "x_second_1")
     middle_others[1] = after(middle_others[1], x_terms[1])
-    total = after(swap_sum(total, doubling(2, group)), middle_others[1], middle_twin[0], middle_twin[2])
-    middle_others[0] = across_chips(after(middle[0], total))
-    forcing = [forcing_of(total)]
+    totals = [total] + [swap(total, m) for m in range(1, group)]
+    totals = after(totals, middle_others[1], middle_twin[0], middle_twin[2])
+    middle_others[0] = across_chips(after(middle[0], totals))
+    totals = [piece(x) for x in totals]
 
     def middle_pieces(i):
         return [
@@ -389,31 +430,36 @@
 
     def second_step(i):
         return y_call(
-            second_kernel, forcing, along_y_matrix, 0,
+            functools.partial(second_kernel, cells), along_y_matrix, 0,
             [middle_pieces(i), middle_pieces(1) if i != 1 else [], [], [piece(middle[i])], [piece(middle[1])],
-             [piece(x_terms[i])], [piece(base[i])]], [size] * planes, f"y_second_{i}",
+             [piece(x_terms[i])], [piece(base[i])]], [size] * planes, f"y_second_{i}", totals, {0: 36, 1: 36, 2: 36}[i],
         )
 
     ends = [None] * 3
     middle_far[1] = across_cores(middle_others[1])
+    def leave(i):
+        ends[i] = [swap(block, d * group) if d else block for d, block in enumerate(ends[i])]
+
     ends[1] = second_step(1)
-    x_terms[0] = along_x([piece(after(middle[0], ends[1]))], [], along_x_matrix, "x_second_0", 1)
+    x_terms[0] = along_x([piece(after(middle[0], ends[1]))], [], along_x_matrix, "x_second_0", 36)
+    leave(1)
     middle_others[0] = after(middle_others[0], x_terms[0])
     middle_others[2] = across_chips(after(middle[2], middle_others[0]))
     middle_far[0] = across_cores(middle_others[0])
-    x_terms[2] = along_x([piece(after(middle[2], x_terms[0]))], [piece(middle[0])], along_x_matrix, "x_second_2", 1)
+    x_terms[2] = along_x(
+        [piece(after(middle[2], x_terms[0]))], [piece(middle[0])], along_x_matrix, "x_second_2", 36
+    )
     middle_far[0] = after(middle_far[0], x_terms[2])
     ends[0] = second_step(0)
-    middle_others[2] = after(middle_others[2], ends[0])
+    ends[1] = after(ends[1], ends[0])
+    out = place_blocks(plane, ends, (1,), velocity.shape, None)
+    leave(0)
+    middle_others[2] = after(middle_others[2], out)
     middle_far[2] = across_cores(middle_others[2])
     ends[2] = second_step(2)
-
-    out = jnp.zeros(velocity.shape, F32)
-    for i in (1, 0, 2):
-        for d, block in enumerate(ends[i]):
-            block = swap(block, d * group) if d else block
-            out = lax.dynamic_update_slice(out, block[None, None], (i, plane ^ d, 0, 0))
-    return out
+    leave(2)
+    out = place_blocks(plane, ends, (0,), velocity.shape, out)
+    return place_blocks(plane, ends, (2,), velocity.shape, out)
 
 
 def solution(mesh):

time: 300 us -> 247 us (0.82)
  local copies, waits for them, and re-layouts: 44.3 us -> 8.21 us
  other arithmetic: 9.83 us -> 0.08 us
  waiting for transfers between devices: 118 us -> 110 us
    unnamed x138 -> x14, local copies, waits for them, and re-layouts: 42.9 us -> 8.12 us
    ppermute x37 -> x39, waiting for transfers between devices: 118 us -> 110 us  [swap(): return lax.ppermute(x, 'row', [(r, r ^ distance) for r in range(devices)])]
    pallas_call x1 -> x0, other arithmetic: 7.66 us -> none  [y_call(): pl.pallas_call(functools.partial(kernel, tuple((len(group) for group in g...]
    pallas_call x8 -> x14, Pallas kernels: 43.8 us -> 49 us  [the longest x9 45.9 us: y_call(): pl.pallas_call(functools.partial(kernel, tuple(counts)), grid=(length //...]
    pallas_call x6, Pallas kernels: 46.3 us -> 42.8 us  [along_x(): pl.pallas_call(functools.partial(along_x_kernel, (len(fields), len(carrie...]
    ppermute x37 -> x39, starting transfers between devices: 25.3 us -> 26.3 us  [swap(): return lax.ppermute(x, 'row', [(r, r ^ distance) for r in range(devices)])]
  transfers between devices with their start and end apart: 37 -> 39, of which waited for: 18 -> 19; matrix products, arithmetic and copies ran while one was open for 0% -> 0% of each run, Pallas kernels for 31% -> 38%
where the time goes in v7:
time: 247 us; the launch traced here: 245 us
  waiting for transfers between devices  110 us (45%)
  Pallas kernels  101 us (41%)
  starting transfers between devices  26.3 us (11%)
  local copies, waits for them, and re-layouts  8.21 us (3%)
    ppermute x39, waiting for transfers between devices, swap(): return lax.ppermute(x, 'row', [(r, r ^ distance) for r in range(devices)])  110 us
    pallas_call x9, Pallas kernels, y_call(): pl.pallas_call(functools.partial(kernel, tuple(counts)), grid=(length //...  45.9 us
    pallas_call x6, Pallas kernels, along_x(): pl.pallas_call(functools.partial(along_x_kernel, (len(fields), len(carrie...  42.8 us
    ppermute x39, starting transfers between devices, swap(): return lax.ppermute(x, 'row', [(r, r ^ distance) for r in range(devices)])  26.3 us
    unnamed x14, local copies, waits for them, and re-layouts  8.12 us
    pallas_call x1, Pallas kernels, prepare_matrices(): pl.pallas_call(functools.partial(matrices_kernel, count), grid_spec=pltpu...  7.16 us
  transfers between devices with their start and end apart: 39, of which 19 were waited for; matrix products, arithmetic and copies ran while one was open for 0% of the time, Pallas kernels for 38%

profile of v7, /device:TPU:18, one launch (start us, length us, event | category | flops | bytes accessed | tf_op | source)
XLA Modules:
  0.0 245.2 jit_solution(725095469421262756)
XLA Ops:
  8.0 2.2 copy-done.1
  10.2 2.2 copy-done.2
  12.4 7.2 %shard_map.37 = (bf16[4,1024,1024]{2,1,0:T(8,128)(2,1)S(1)}, bf16[4,256,1024]{2,1,0:T(8,128)(2,1)S(1)}) custom-call(s32[16]{0:T(128)S(1)} %stack.74.order_ref, s32[4]{0:T(128)S(1)} %pad_add_fusion.own_ref, f32[1024,1024]{1,0:T(8,128)S(1)} %copy-done.1, f32[1024,1024]{1,0:T(8,128)S(1)} %copy-done.1, f32[1024,1024]{1,0:T(8,128)S(1)} %copy-done.2, ...), custom_call_target="tpu_custom_call" | custom-call | flops 17179869184 | bytes 33554432 | tf_op jit(solution)/shard_map/pallas_call | solution.py:63
  19.5 22.5 %collective-permute-done.1.refs_1_.refs_3_.refs_5_.refs_7_.refs_9_.refs_11_.refs_15_.refs_25_.refs_19_.refs_23_.refs_33_ = f32[200,1024]{1,0:T(8,128)S(1)} collective-permute-done((f32[200,1024]{1,0:T(8,128)}, f32[200,1024]{1,0:T(8,128)S(1)}, u32[]{:S(2)}, u32[]{:S(2)}) %collective-permute-start.1) | collective-permute-done | bytes 819232 | tf_op jit(solution)/shard_map/ppermute | solution.py:311
  45.2 9.8 %x_first_near.1.refs_18_.refs_26_ = f32[384,1024]{1,0:T(8,128)S(1)} custom-call(f32[200,1024]{1,0:T(8,128)S(1)} %get-tuple-element.92.refs_0_.refs_2_.refs_4_.refs_6_.refs_8_.refs_10_.refs_14_.refs_21_.refs_18_.refs_22_.refs_29_, ...), custom_call_target="tpu_custom_call" | custom-call | flops 402653184 | bytes 1572864 | tf_op jit(solution)/shard_map/x_first_near/pallas_call | solution.py:160
  56.1 5.8 %x_first_2.1.refs_19_.refs_27_ = f32[192,1024]{1,0:T(8,128)S(1)} custom-call(f32[200,1024]{1,0:T(8,128)S(1)} %collective-permute-done.refs_0_.refs_1_.refs_2_.refs_3_.refs_12_.refs_16_.refs_29_.refs_8_.refs_20_.refs_24_.refs_37_, ...), custom_call_target="tpu_custom_call" | custom-call | flops 201326592 | bytes 786432 | tf_op jit(solution)/shard_map/x_first_2/pallas_call | solution.py:160
  63.3 16.8 %collective-permute-done.2.refs_0_.refs_1_.refs_2_.refs_3_.refs_13_.refs_17_.refs_33_.refs_9_.refs_21_.refs_25_.refs_41_ = f32[200,1024]{1,0:T(8,128)S(1)} collective-permute-done((f32[200,1024]{1,0:T(8,128)S(1)}, f32[200,1024]{1,0:T(8,128)S(1)}, u32[]{:S(2)}, u32[]{:S(2)}) %collective-permute-start.2) | collective-permute-done | bytes 819232 | tf_op jit(solution)/shard_map/ppermute | solution.py:311
  80.6 5.8 %x_first_3.1.refs_20_.refs_28_ = f32[192,1024]{1,0:T(8,128)S(1)} custom-call(f32[200,1024]{1,0:T(8,128)S(1)} %collective-permute-done.2.refs_0_.refs_1_.refs_2_.refs_3_.refs_13_.refs_17_.refs_33_.refs_9_.refs_21_.refs_25_.refs_41_, ...), custom_call_target="tpu_custom_call" | custom-call | flops 7247757312 | bytes 786432 | tf_op jit(solution)/shard_map/x_first_3/pallas_call | solution.py:160
  86.5 3.6 %y_first_near_1.1 = (f32[256,1024]{1,0:T(8,128)S(1)}, f32[256,1024]{1,0:T(8,128)S(1)}) custom-call(bf16[4,256,1024]{2,1,0:T(8,128)(2,1)S(1)} %get-tuple-element.73.matrix_ref, f32[200,1024]{1,0:T(8,128)S(1)} %get-tuple-element.92.refs_0_.refs_2_.refs_4_.refs_6_.refs_8_.refs_10_.refs_14_.refs_21_.refs_18_.refs_22_.refs_29_, ...), custom_call_target="tpu_custom_call" | custom-call | flops 4831838208 | bytes 1048576 | tf_op jit(solution)/shard_map/y_first_near_1/pallas_call | solution.py:238
  90.1 3.9 %y_first_near_0.1 = (f32[256,1024]{1,0:T(8,128)S(1)}, f32[256,1024]{1,0:T(8,128)S(1)}) custom-call(bf16[4,256,1024]{2,1,0:T(8,128)(2,1)S(1)} %get-tuple-element.73.matrix_ref, f32[200,1024]{1,0:T(8,128)S(1)} %get-tuple-element.92.refs_0_.refs_2_.refs_4_.refs_6_.refs_8_.refs_10_.refs_14_.refs_21_.refs_18_.refs_22_.refs_29_, ...), custom_call_target="tpu_custom_call" | custom-call | flops 4831838208 | bytes 1048576 | tf_op jit(solution)/shard_map/y_first_near_0/pallas_call | solution.py:238
  94.8 3.9 %y_first_near_2.1 = (f32[256,1024]{1,0:T(8,128)S(1)}, f32[256,1024]{1,0:T(8,128)S(1)}) custom-call(bf16[4,256,1024]{2,1,0:T(8,128)(2,1)S(1)} %get-tuple-element.73.matrix_ref, f32[200,1024]{1,0:T(8,128)S(1)} %get-tuple-element.92.refs_0_.refs_2_.refs_4_.refs_6_.refs_8_.refs_10_.refs_14_.refs_21_.refs_18_.refs_22_.refs_29_, ...), custom_call_target="tpu_custom_call" | custom-call | flops 4831838208 | bytes 1048576 | tf_op jit(solution)/shard_map/y_first_near_2/pallas_call | solution.py:238
  100.8 2.3 collective-permute-done.14.refs_7_.refs_36_.refs_15_.refs_44_
  103.1 4.3 %y_first_far_1.1 = (f32[256,1024]{1,0:T(8,128)S(1)}, f32[256,1024]{1,0:T(8,128)S(1)}, f32[8,1024]{1,0:T(8,128)S(1)}) custom-call(bf16[4,256,1024]{2,1,0:T(8,128)(2,1)S(1)} %get-tuple-element.73.matrix_ref, f32[200,1024]{1,0:T(8,128)S(1)} %collective-permute-done.refs_0_.refs_1_.refs_2_.refs_3_.refs_12_.refs_16_.refs_29_.refs_8_.refs_20_.refs_24_.refs_37_, ...), custom_call_target="tpu_custom_call" | custom-call | flops 4831838208 | bytes 1048576 | tf_op jit(solution)/shard_map/y_first_far_1/pallas_call | solution.py:238
  108.9 4.6 %y_first_far_0.1 = (f32[256,1024]{1,0:T(8,128)S(1)}, f32[256,1024]{1,0:T(8,128)S(1)}, f32[8,1024]{1,0:T(8,128)S(1)}) custom-call(bf16[4,256,1024]{2,1,0:T(8,128)(2,1)S(1)} %get-tuple-element.73.matrix_ref, f32[200,1024]{1,0:T(8,128)S(1)} %collective-permute-done.refs_0_.refs_1_.refs_2_.refs_3_.refs_12_.refs_16_.refs_29_.refs_8_.refs_20_.refs_24_.refs_37_, ...), custom_call_target="tpu_custom_call" | custom-call | flops 4831838208 | bytes 1048576 | tf_op jit(solution)/shard_map/y_first_far_0/pallas_call | solution.py:238
  113.5 4.9 %y_first_far_2.1 = (f32[256,1024]{1,0:T(8,128)S(1)}, f32[256,1024]{1,0:T(8,128)S(1)}, f32[8,1024]{1,0:T(8,128)S(1)}) custom-call(bf16[4,256,1024]{2,1,0:T(8,128)(2,1)S(1)} %get-tuple-element.73.matrix_ref, f32[200,1024]{1,0:T(8,128)S(1)} %collective-permute-done.refs_0_.refs_1_.refs_2_.refs_3_.refs_12_.refs_16_.refs_29_.refs_8_.refs_20_.refs_24_.refs_37_, ...), custom_call_target="tpu_custom_call" | custom-call | flops 4831838208 | bytes 1048576 | tf_op jit(solution)/shard_map/y_first_far_2/pallas_call | solution.py:238
  124.5 7.1 %x_second_1.1.refs_10_ = f32[256,1024]{1,0:T(8,128)S(1)} custom-call(f32[256,1024]{1,0:T(8,128)S(1)} %get-tuple-element.108.refs_0_.refs_4_.refs_8_.refs_9_.refs_12_.refs_17_, f32[256,1024]{1,0:T(8,128)S(1)} %get-tuple-element.121.refs_1_.refs_0_.refs_4_.refs_16_, bf16[4,1024,1024]{2,1,0:T(8,128)(2,1)S(1)} %get-tuple-element.77.refs_8_.refs_4_.refs_2_.refs_1_), custom_call_target="tpu_custom_call" | custom-call | flops 9663676416 | bytes 1048576 | tf_op jit(solution)/shard_map/x_second_1/pallas_call | solution.py:160
  134.2 2.4 collective-permute-done.21.refs_14_.refs_22_
  137.1 3.1 %collective-permute-done.20.refs_13_.refs_21_ = f32[8,128]{1,0:T(8,128)S(1)} collective-permute-done((f32[8,128]{1,0:T(8,128)S(1)}, f32[8,128]{1,0:T(8,128)S(1)}, u32[]{:S(2)}, u32[]{:S(2)}) %collective-permute-start.20) | collective-permute-done | bytes 4128 | tf_op jit(solution)/shard_map/ppermute | solution.py:311
  141.9 6.6 %y_second_1.1 = (f32[64,1024]{1,0:T(8,128)S(1)}, f32[64,1024]{1,0:T(8,128)S(1)}, f32[64,1024]{1,0:T(8,128)S(1)}, f32[64,1024]{1,0:T(8,128)S(1)}) custom-call(bf16[4,256,1024]{2,1,0:T(8,128)(2,1)S(1)} %get-tuple-element.73.matrix_ref, f32[256,1024]{1,0:T(8,128)S(1)} %get-tuple-element.108.refs_0_.refs_4_.refs_8_.refs_9_.refs_12_.refs_17_, ...), custom_call_target="tpu_custom_call" | custom-call | flops 9663676416 | bytes 1048576 | tf_op jit(solution)/shard_map/y_second_1/pallas_call | solution.py:238
  148.5 7.1 %x_second_0.1.refs_18_ = f32[256,1024]{1,0:T(8,128)S(1)} custom-call(f32[256,1024]{1,0:T(8,128)S(1)} %get-tuple-element.121.refs_1_.refs_0_.refs_4_.refs_16_, bf16[4,1024,1024]{2,1,0:T(8,128)(2,1)S(1)} %get-tuple-element.77.refs_8_.refs_4_.refs_2_.refs_1_), custom_call_target="tpu_custom_call" | custom-call | flops 9663676416 | bytes 1048576 | tf_op jit(solution)/shard_map/x_second_0/pallas_call | solution.py:160
  155.7 11.0 %collective-permute-done.24.refs_2_.refs_6_ = f32[256,1024]{1,0:T(8,128)S(1)} collective-permute-done((f32[256,1024]{1,0:T(8,128)S(1)}, f32[256,1024]{1,0:T(8,128)S(1)}, u32[]{:S(2)}, u32[]{:S(2)}) %collective-permute-start.24) | collective-permute-done | bytes 1048608 | tf_op jit(solution)/shard_map/ppermute | solution.py:311
  166.6 3.0 %collective-permute-start.29 = (f32[64,1024]{1,0:T(8,128)S(1)}, f32[64,1024]{1,0:T(8,128)S(1)}, u32[]{:S(2)}, u32[]{:S(2)}) collective-permute-start(f32[64,1024]{1,0:T(8,128)S(1)} %get-tuple-element.119), channel_id=1, source_target_pairs={{0,8},{1,9},{2,10},{3,11},{4,12},{5,13},{6,14},{7,15},{8,0},{9,1},... | collective-permute-start | bytes 786440 | tf_op jit(solution)/shard_map/ppermute | solution.py:311
  170.6 7.1 %x_second_2.1.refs_18_ = f32[256,1024]{1,0:T(8,128)S(1)} custom-call(f32[256,1024]{1,0:T(8,128)S(1)} %get-tuple-element.124.refs_0_.refs_4_.refs_16_, f32[256,1024]{1,0:T(8,128)S(1)} %get-tuple-element.121.refs_1_.refs_0_.refs_4_.refs_16_, bf16[4,1024,1024]{2,1,0:T(8,128)(2,1)S(1)} %get-tuple-element.77.refs_8_.refs_4_.refs_2_.refs_1_), custom_call_target="tpu_custom_call" | custom-call | flops 9663676416 | bytes 1048576 | tf_op jit(solution)/shard_map/x_second_2/pallas_call | solution.py:160
  177.8 7.1 %y_second_0.1 = (f32[64,1024]{1,0:T(8,128)S(1)}, f32[64,1024]{1,0:T(8,128)S(1)}, f32[64,1024]{1,0:T(8,128)S(1)}, f32[64,1024]{1,0:T(8,128)S(1)}) custom-call(bf16[4,256,1024]{2,1,0:T(8,128)(2,1)S(1)} %get-tuple-element.73.matrix_ref, f32[256,1024]{1,0:T(8,128)S(1)} %get-tuple-element.121.refs_1_.refs_0_.refs_4_.refs_16_, ...), custom_call_target="tpu_custom_call" | custom-call | flops 9663676416 | bytes 1048576 | tf_op jit(solution)/shard_map/y_second_0/pallas_call | solution.py:238
  184.8 2.7 %collective-permute-done.29.refs_2_ = f32[64,1024]{1,0:T(8,128)S(1)} collective-permute-done((f32[64,1024]{1,0:T(8,128)S(1)}, f32[64,1024]{1,0:T(8,128)S(1)}, u32[]{:S(2)}, u32[]{:S(2)}) %collective-permute-start.29) | collective-permute-done | bytes 262176 | tf_op jit(solution)/shard_map/ppermute | solution.py:311
  187.6 5.9 %collective-permute-done.30.refs_3_ = f32[64,1024]{1,0:T(8,128)S(1)} collective-permute-done((f32[64,1024]{1,0:T(8,128)S(1)}, f32[64,1024]{1,0:T(8,128)S(1)}, u32[]{:S(2)}, u32[]{:S(2)}) %collective-permute-start.30) | collective-permute-done | bytes 262176 | tf_op jit(solution)/shard_map/ppermute | solution.py:311
  198.4 7.0 %y_second_2.1 = (f32[64,1024]{1,0:T(8,128)S(1)}, f32[64,1024]{1,0:T(8,128)S(1)}, f32[64,1024]{1,0:T(8,128)S(1)}, f32[64,1024]{1,0:T(8,128)S(1)}) custom-call(bf16[4,256,1024]{2,1,0:T(8,128)(2,1)S(1)} %get-tuple-element.73.matrix_ref, f32[256,1024]{1,0:T(8,128)S(1)} %get-tuple-element.124.refs_0_.refs_4_.refs_16_, ...), custom_call_target="tpu_custom_call" | custom-call | flops 9663676416 | bytes 1048576 | tf_op jit(solution)/shard_map/y_second_2/pallas_call | solution.py:238
  205.4 2.2 collective-permute-start.33
  209.2 6.7 %collective-permute-done.37.refs_2_ = f32[64,1024]{1,0:T(8,128)S(1)} collective-permute-done((f32[64,1024]{1,0:T(8,128)S(1)}, f32[64,1024]{1,0:T(8,128)S(1)}, u32[]{:S(2)}, u32[]{:S(2)}) %collective-permute-start.37) | collective-permute-done | bytes 262176 | tf_op jit(solution)/shard_map/ppermute | solution.py:311
  215.8 17.8 %collective-permute-done.38.refs_3_ = f32[64,1024]{1,0:T(8,128)S(1)} collective-permute-done((f32[64,1024]{1,0:T(8,128)S(1)}, f32[64,1024]{1,0:T(8,128)S(1)}, u32[]{:S(2)}, u32[]{:S(2)}) %collective-permute-start.38) | collective-permute-done | bytes 262176 | tf_op jit(solution)/shard_map/ppermute | solution.py:311
  234.7 3.6 %collective-permute-done.34.refs_2_ = f32[64,1024]{1,0:T(8,128)S(1)} collective-permute-done((f32[64,1024]{1,0:T(8,128)S(1)}, f32[64,1024]{1,0:T(8,128)S(1)}, u32[]{:S(2)}, u32[]{:S(2)}) %collective-permute-start.34) | collective-permute-done | bytes 262176 | tf_op jit(solution)/shard_map/ppermute | solution.py:311
  238.3 5.9 %collective-permute-done.35.refs_3_ = f32[64,1024]{1,0:T(8,128)S(1)} collective-permute-done((f32[64,1024]{1,0:T(8,128)S(1)}, f32[64,1024]{1,0:T(8,128)S(1)}, u32[]{:S(2)}, u32[]{:S(2)}) %collective-permute-start.35) | collective-permute-done | bytes 262176 | tf_op jit(solution)/shard_map/ppermute | solution.py:311
  (84 shorter events, 38.9 us)
Async XLA Ops:
  4.4 50.6 %collective-permute-start = (f32[200,1024]{1,0:T(8,128)}, f32[200,1024]{1,0:T(8,128)S(1)}, u32[]{:S(2)}, u32[]{:S(2)}) collective-permute-start(f32[200,1024]{1,0:T(8,128)} %get-tuple-element.74), channel_id=1, source_target_pairs={{0,8},{1,9},{2,10},{3,11},{4,12},{5,13},{6,14},{7,15},{8,0},{9,1},... | collective-permute-start | bytes 2457608 | tf_op jit(solution)/shard_map/ppermute | solution.py:311
  4.7 37.3 %collective-permute-start.1 = (f32[200,1024]{1,0:T(8,128)}, f32[200,1024]{1,0:T(8,128)S(1)}, u32[]{:S(2)}, u32[]{:S(2)}) collective-permute-start(f32[200,1024]{1,0:T(8,128)} %get-tuple-element.76), channel_id=1, source_target_pairs={{0,4},{1,5},{2,6},{3,7},{4,0},{5,1},{6,2},{7,3},{8,12},{9,13},{10,... | collective-permute-start | bytes 2457608 | tf_op jit(solution)/shard_map/ppermute | solution.py:311
  6.3 49.2 %collective-permute-start.6 = (f32[200,1024]{1,0:T(8,128)S(1)}, f32[200,1024]{1,0:T(8,128)S(1)}, u32[]{:S(2)}, u32[]{:S(2)}) collective-permute-start(f32[200,1024]{1,0:T(8,128)S(1)} %get-tuple-element.92.refs_0_.refs_2_.refs_4_.refs_6_.refs_8_.refs_10_.refs_14_.refs_21_.refs_18_.refs_22_.refs_29_), channel_id=1, source_target_pairs={{0,2},{1,3},{2,0},{3,1},{4,6},{5,7},{6,4},{7,5},{8,10},{9,11},{10,... | collective-permute-start | bytes 2457608 | tf_op jit(solution)/shard_map/ppermute | solution.py:311
  42.1 21.2 %collective-permute-start.7 = (f32[200,1024]{1,0:T(8,128)S(1)}, f32[200,1024]{1,0:T(8,128)S(1)}, u32[]{:S(2)}, u32[]{:S(2)}) collective-permute-start(f32[200,1024]{1,0:T(8,128)S(1)} %collective-permute-done.1.refs_1_.refs_3_.refs_5_.refs_7_.refs_9_.refs_11_.refs_15_.refs_25_.refs_19_.refs_23_.refs_33_), channel_id=1, source_target_pairs={{0,2},{1,3},{2,0},{3,1},{4,6},{5,7},{6,4},{7,5},{8,10},{9,11},{10,... | collective-permute-start | bytes 2457608 | tf_op jit(solution)/shard_map/ppermute | solution.py:311
  43.6 36.4 %collective-permute-start.2 = (f32[200,1024]{1,0:T(8,128)S(1)}, f32[200,1024]{1,0:T(8,128)S(1)}, u32[]{:S(2)}, u32[]{:S(2)}) collective-permute-start(f32[200,1024]{1,0:T(8,128)S(1)} %copy-done.6), channel_id=1, source_target_pairs={{0,12},{1,13},{2,14},{3,15},{4,8},{5,9},{6,10},{7,11},{8,4},{9,5},... | collective-permute-start | bytes 2457608 | tf_op jit(solution)/shard_map/ppermute | solution.py:311
  55.0 25.1 %collective-permute-start.5 = (f32[200,1024]{1,0:T(8,128)S(1)}, f32[200,1024]{1,0:T(8,128)S(1)}, u32[]{:S(2)}, u32[]{:S(2)}) collective-permute-start(f32[200,1024]{1,0:T(8,128)S(1)} %collective-permute-done.refs_0_.refs_1_.refs_2_.refs_3_.refs_12_.refs_16_.refs_29_.refs_8_.refs_20_.refs_24_.refs_37_), channel_id=1, source_target_pairs={{0,2},{1,3},{2,0},{3,1},{4,6},{5,7},{6,4},{7,5},{8,10},{9,11},{10,... | collective-permute-start | bytes 2457608 | tf_op jit(solution)/shard_map/ppermute | solution.py:311
  55.5 24.5 %collective-permute-start.3 = (f32[200,1024]{1,0:T(8,128)S(1)}, f32[200,1024]{1,0:T(8,128)S(1)}, u32[]{:S(2)}, u32[]{:S(2)}) collective-permute-start(f32[200,1024]{1,0:T(8,128)S(1)} %get-tuple-element.92.refs_0_.refs_2_.refs_4_.refs_6_.refs_8_.refs_10_.refs_14_.refs_21_.refs_18_.refs_22_.refs_29_), channel_id=1, source_target_pairs={{0,1},{1,0},{2,3},{3,2},{4,5},{5,4},{6,7},{7,6},{8,9},{9,8},{10,11... | collective-permute-start | bytes 2457608 | tf_op jit(solution)/shard_map/ppermute | solution.py:311
  55.5 24.5 %collective-permute-start.4 = (f32[200,1024]{1,0:T(8,128)S(1)}, f32[200,1024]{1,0:T(8,128)S(1)}, u32[]{:S(2)}, u32[]{:S(2)}) collective-permute-start(f32[200,1024]{1,0:T(8,128)S(1)} %collective-permute-done.1.refs_1_.refs_3_.refs_5_.refs_7_.refs_9_.refs_11_.refs_15_.refs_25_.refs_19_.refs_23_.refs_33_), channel_id=1, source_target_pairs={{0,1},{1,0},{2,3},{3,2},{4,5},{5,4},{6,7},{7,6},{8,9},{9,8},{10,11... | collective-permute-start | bytes 2457608 | tf_op jit(solution)/shard_map/ppermute | solution.py:311
  63.3 23.2 %collective-permute-start.8 = (f32[200,1024]{1,0:T(8,128)S(1)}, f32[200,1024]{1,0:T(8,128)S(1)}, u32[]{:S(2)}, u32[]{:S(2)}) collective-permute-start(f32[200,1024]{1,0:T(8,128)S(1)} %collective-permute-done.6.refs_4_.refs_12_.refs_22_.refs_30_), channel_id=1, source_target_pairs={{0,1},{1,0},{2,3},{3,2},{4,5},{5,4},{6,7},{7,6},{8,9},{9,8},{10,11... | collective-permute-start | bytes 2457608 | tf_op jit(solution)/shard_map/ppermute | solution.py:311
  80.0 6.4 %collective-permute-start.9 = (f32[200,1024]{1,0:T(8,128)S(1)}, f32[200,1024]{1,0:T(8,128)S(1)}, u32[]{:S(2)}, u32[]{:S(2)}) collective-permute-start(f32[200,1024]{1,0:T(8,128)S(1)} %collective-permute-done.7.refs_5_.refs_13_.refs_26_.refs_34_), channel_id=1, source_target_pairs={{0,1},{1,0},{2,3},{3,2},{4,5},{5,4},{6,7},{7,6},{8,9},{9,8},{10,11... | collective-permute-start | bytes 2457608 | tf_op jit(solution)/shard_map/ppermute | solution.py:311
  80.0 20.7 %collective-permute-start.12 = (f32[200,1024]{1,0:T(8,128)S(1)}, f32[200,1024]{1,0:T(8,128)S(1)}, u32[]{:S(2)}, u32[]{:S(2)}) collective-permute-start(f32[200,1024]{1,0:T(8,128)S(1)} %collective-permute-done.2.refs_0_.refs_1_.refs_2_.refs_3_.refs_13_.refs_17_.refs_33_.refs_9_.refs_21_.refs_25_.refs_41_), channel_id=1, source_target_pairs={{0,2},{1,3},{2,0},{3,1},{4,6},{5,7},{6,4},{7,5},{8,10},{9,11},{10,... | collective-permute-start | bytes 2457608 | tf_op jit(solution)/shard_map/ppermute | solution.py:311
  94.0 6.8 %collective-permute-start.10 = (f32[200,1024]{1,0:T(8,128)S(1)}, f32[200,1024]{1,0:T(8,128)S(1)}, u32[]{:S(2)}, u32[]{:S(2)}) collective-permute-start(f32[200,1024]{1,0:T(8,128)S(1)} %collective-permute-done.refs_0_.refs_1_.refs_2_.refs_3_.refs_12_.refs_16_.refs_29_.refs_8_.refs_20_.refs_24_.refs_37_), channel_id=1, source_target_pairs={{0,1},{1,0},{2,3},{3,2},{4,5},{5,4},{6,7},{7,6},{8,9},{9,8},{10,11... | collective-permute-start | bytes 2457608 | tf_op jit(solution)/shard_map/ppermute | solution.py:311
  94.3 6.5 %collective-permute-start.13 = (f32[200,1024]{1,0:T(8,128)S(1)}, f32[200,1024]{1,0:T(8,128)S(1)}, u32[]{:S(2)}, u32[]{:S(2)}) collective-permute-start(f32[200,1024]{1,0:T(8,128)S(1)} %collective-permute-done.5.refs_4_.refs_30_.refs_12_.refs_38_), channel_id=1, source_target_pairs={{0,1},{1,0},{2,3},{3,2},{4,5},{5,4},{6,7},{7,6},{8,9},{9,8},{10,11... | collective-permute-start | bytes 2457608 | tf_op jit(solution)/shard_map/ppermute | solution.py:311
  94.6 6.2 %collective-permute-start.11 = (f32[200,1024]{1,0:T(8,128)S(1)}, f32[200,1024]{1,0:T(8,128)S(1)}, u32[]{:S(2)}, u32[]{:S(2)}) collective-permute-start(f32[200,1024]{1,0:T(8,128)S(1)} %collective-permute-done.2.refs_0_.refs_1_.refs_2_.refs_3_.refs_13_.refs_17_.refs_33_.refs_9_.refs_21_.refs_25_.refs_41_), channel_id=1, source_target_pairs={{0,1},{1,0},{2,3},{3,2},{4,5},{5,4},{6,7},{7,6},{8,9},{9,8},{10,11... | collective-permute-start | bytes 2457608 | tf_op jit(solution)/shard_map/ppermute | solution.py:311
  108.4 25.2 %collective-permute-start.22 = (f32[256,1024]{1,0:T(8,128)S(1)}, f32[256,1024]{1,0:T(8,128)S(1)}, u32[]{:S(2)}, u32[]{:S(2)}) collective-permute-start(f32[256,1024]{1,0:T(8,128)S(1)} %get-tuple-element.108.refs_0_.refs_4_.refs_8_.refs_9_.refs_12_.refs_17_), channel_id=1, source_target_pairs={{0,2},{1,3},{2,0},{3,1},{4,6},{5,7},{6,4},{7,5},{8,10},{9,11},{10,... | collective-permute-start | bytes 3145736 | tf_op jit(solution)/shard_map/ppermute | solution.py:311
  120.0 4.5 %collective-permute-start.16 = (f32[8,128]{1,0:T(8,128)S(1)}, f32[8,128]{1,0:T(8,128)S(1)}, u32[]{:S(2)}, u32[]{:S(2)}) collective-permute-start(f32[8,128]{1,0:T(8,128)S(1)} %fold_own.1.refs_0_), channel_id=1, source_target_pairs={{0,4},{1,5},{2,6},{3,7},{4,0},{5,1},{6,2},{7,3},{8,12},{9,13},{10,... | collective-permute-start | bytes 12296 | tf_op jit(solution)/shard_map/ppermute | solution.py:311
  122.0 19.9 %collective-permute-start.25 = (f32[256,1024]{1,0:T(8,128)S(1)}, f32[256,1024]{1,0:T(8,128)S(1)}, u32[]{:S(2)}, u32[]{:S(2)}) collective-permute-start(f32[256,1024]{1,0:T(8,128)S(1)} %get-tuple-element.108.refs_0_.refs_4_.refs_8_.refs_9_.refs_12_.refs_17_), channel_id=1, source_target_pairs={{0,1},{1,0},{2,3},{3,2},{4,5},{5,4},{6,7},{7,6},{8,9},{9,8},{10,11... | collective-permute-start | bytes 3145736 | tf_op jit(solution)/shard_map/ppermute | solution.py:311
  122.1 19.3 %collective-permute-start.23 = (f32[256,1024]{1,0:T(8,128)S(1)}, f32[256,1024]{1,0:T(8,128)S(1)}, u32[]{:S(2)}, u32[]{:S(2)}) collective-permute-start(f32[256,1024]{1,0:T(8,128)S(1)} %get-tuple-element.121.refs_1_.refs_0_.refs_4_.refs_16_), channel_id=1, source_target_pairs={{0,1},{1,0},{2,3},{3,2},{4,5},{5,4},{6,7},{7,6},{8,9},{9,8},{10,11... | collective-permute-start | bytes 3145736 | tf_op jit(solution)/shard_map/ppermute | solution.py:311
  124.5 16.9 %collective-permute-start.15 = (f32[256,1024]{1,0:T(8,128)S(1)}, f32[256,1024]{1,0:T(8,128)S(1)}, u32[]{:S(2)}, u32[]{:S(2)}) collective-permute-start(f32[256,1024]{1,0:T(8,128)S(1)} %get-tuple-element.124.refs_0_.refs_4_.refs_16_), channel_id=1, source_target_pairs={{0,1},{1,0},{2,3},{3,2},{4,5},{5,4},{6,7},{7,6},{8,9},{9,8},{10,11... | collective-permute-start | bytes 3145736 | tf_op jit(solution)/shard_map/ppermute | solution.py:311
  133.6 8.3 %collective-permute-start.26 = (f32[256,1024]{1,0:T(8,128)S(1)}, f32[256,1024]{1,0:T(8,128)S(1)}, u32[]{:S(2)}, u32[]{:S(2)}) collective-permute-start(f32[256,1024]{1,0:T(8,128)S(1)} %collective-permute-done.22.refs_2_.refs_6_.refs_10_.refs_14_), channel_id=1, source_target_pairs={{0,1},{1,0},{2,3},{3,2},{4,5},{5,4},{6,7},{7,6},{8,9},{9,8},{10,11... | collective-permute-start | bytes 3145736 | tf_op jit(solution)/shard_map/ppermute | solution.py:311
  141.4 25.2 %collective-permute-start.24 = (f32[256,1024]{1,0:T(8,128)S(1)}, f32[256,1024]{1,0:T(8,128)S(1)}, u32[]{:S(2)}, u32[]{:S(2)}) collective-permute-start(f32[256,1024]{1,0:T(8,128)S(1)} %get-tuple-element.121.refs_1_.refs_0_.refs_4_.refs_16_), channel_id=1, source_target_pairs={{0,2},{1,3},{2,0},{3,1},{4,6},{5,7},{6,4},{7,5},{8,10},{9,11},{10,... | collective-permute-start | bytes 3145736 | tf_op jit(solution)/shard_map/ppermute | solution.py:311
  166.6 11.1 %collective-permute-start.31 = (f32[256,1024]{1,0:T(8,128)S(1)}, f32[256,1024]{1,0:T(8,128)S(1)}, u32[]{:S(2)}, u32[]{:S(2)}) collective-permute-start(f32[256,1024]{1,0:T(8,128)S(1)} %collective-permute-done.24.refs_2_.refs_6_), channel_id=1, source_target_pairs={{0,1},{1,0},{2,3},{3,2},{4,5},{5,4},{6,7},{7,6},{8,9},{9,8},{10,11... | collective-permute-start | bytes 3145736 | tf_op jit(solution)/shard_map/ppermute | solution.py:311
  166.6 18.2 %collective-permute-start.28 = (f32[64,1024]{1,0:T(8,128)S(1)}, f32[64,1024]{1,0:T(8,128)S(1)}, u32[]{:S(2)}, u32[]{:S(2)}) collective-permute-start(f32[64,1024]{1,0:T(8,128)S(1)} %get-tuple-element.118), channel_id=1, source_target_pairs={{0,4},{1,5},{2,6},{3,7},{4,0},{5,1},{6,2},{7,3},{8,12},{9,13},{10,... | collective-permute-start | bytes 786440 | tf_op jit(solution)/shard_map/ppermute | solution.py:311
  166.6 20.9 %collective-permute-start.29 = (f32[64,1024]{1,0:T(8,128)S(1)}, f32[64,1024]{1,0:T(8,128)S(1)}, u32[]{:S(2)}, u32[]{:S(2)}) collective-permute-start(f32[64,1024]{1,0:T(8,128)S(1)} %get-tuple-element.119), channel_id=1, source_target_pairs={{0,8},{1,9},{2,10},{3,11},{4,12},{5,13},{6,14},{7,15},{8,0},{9,1},... | collective-permute-start | bytes 786440 | tf_op jit(solution)/shard_map/ppermute | solution.py:311
  169.6 23.8 %collective-permute-start.30 = (f32[64,1024]{1,0:T(8,128)S(1)}, f32[64,1024]{1,0:T(8,128)S(1)}, u32[]{:S(2)}, u32[]{:S(2)}) collective-permute-start(f32[64,1024]{1,0:T(8,128)S(1)} %get-tuple-element.120), channel_id=1, source_target_pairs={{0,12},{1,13},{2,14},{3,15},{4,8},{5,9},{6,10},{7,11},{8,4},{9,5},... | collective-permute-start | bytes 786440 | tf_op jit(solution)/shard_map/ppermute | solution.py:311
  170.1 24.7 %collective-permute-start.27 = (f32[256,1024]{1,0:T(8,128)S(1)}, f32[256,1024]{1,0:T(8,128)S(1)}, u32[]{:S(2)}, u32[]{:S(2)}) collective-permute-start(f32[256,1024]{1,0:T(8,128)S(1)} %get-tuple-element.124.refs_0_.refs_4_.refs_16_), channel_id=1, source_target_pairs={{0,2},{1,3},{2,0},{3,1},{4,6},{5,7},{6,4},{7,5},{8,10},{9,11},{10,... | collective-permute-start | bytes 3145736 | tf_op jit(solution)/shard_map/ppermute | solution.py:311
  194.9 13.7 %collective-permute-start.36 = (f32[64,1024]{1,0:T(8,128)S(1)}, f32[64,1024]{1,0:T(8,128)S(1)}, u32[]{:S(2)}, u32[]{:S(2)}) collective-permute-start(f32[64,1024]{1,0:T(8,128)S(1)} %get-tuple-element.128), channel_id=1, source_target_pairs={{0,4},{1,5},{2,6},{3,7},{4,0},{5,1},{6,2},{7,3},{8,12},{9,13},{10,... | collective-permute-start | bytes 786440 | tf_op jit(solution)/shard_map/ppermute | solution.py:311
  196.1 19.7 %collective-permute-start.37 = (f32[64,1024]{1,0:T(8,128)S(1)}, f32[64,1024]{1,0:T(8,128)S(1)}, u32[]{:S(2)}, u32[]{:S(2)}) collective-permute-start(f32[64,1024]{1,0:T(8,128)S(1)} %get-tuple-element.129), channel_id=1, source_target_pairs={{0,8},{1,9},{2,10},{3,11},{4,12},{5,13},{6,14},{7,15},{8,0},{9,1},... | collective-permute-start | bytes 786440 | tf_op jit(solution)/shard_map/ppermute | solution.py:311
  197.9 35.8 %collective-permute-start.38 = (f32[64,1024]{1,0:T(8,128)S(1)}, f32[64,1024]{1,0:T(8,128)S(1)}, u32[]{:S(2)}, u32[]{:S(2)}) collective-permute-start(f32[64,1024]{1,0:T(8,128)S(1)} %get-tuple-element.130), channel_id=1, source_target_pairs={{0,12},{1,13},{2,14},{3,15},{4,8},{5,9},{6,10},{7,11},{8,4},{9,5},... | collective-permute-start | bytes 786440 | tf_op jit(solution)/shard_map/ppermute | solution.py:311
  205.4 29.3 %collective-permute-start.33 = (f32[64,1024]{1,0:T(8,128)S(1)}, f32[64,1024]{1,0:T(8,128)S(1)}, u32[]{:S(2)}, u32[]{:S(2)}) collective-permute-start(f32[64,1024]{1,0:T(8,128)S(1)} %get-tuple-element.138), channel_id=1, source_target_pairs={{0,4},{1,5},{2,6},{3,7},{4,0},{5,1},{6,2},{7,3},{8,12},{9,13},{10,... | collective-permute-start | bytes 786440 | tf_op jit(solution)/shard_map/ppermute | solution.py:311
  207.6 30.7 %collective-permute-start.34 = (f32[64,1024]{1,0:T(8,128)S(1)}, f32[64,1024]{1,0:T(8,128)S(1)}, u32[]{:S(2)}, u32[]{:S(2)}) collective-permute-start(f32[64,1024]{1,0:T(8,128)S(1)} %get-tuple-element.139), channel_id=1, source_target_pairs={{0,8},{1,9},{2,10},{3,11},{4,12},{5,13},{6,14},{7,15},{8,0},{9,1},... | collective-permute-start | bytes 786440 | tf_op jit(solution)/shard_map/ppermute | solution.py:311
  208.6 35.6 %collective-permute-start.35 = (f32[64,1024]{1,0:T(8,128)S(1)}, f32[64,1024]{1,0:T(8,128)S(1)}, u32[]{:S(2)}, u32[]{:S(2)}) collective-permute-start(f32[64,1024]{1,0:T(8,128)S(1)} %get-tuple-element.140), channel_id=1, source_target_pairs={{0,12},{1,13},{2,14},{3,15},{4,8},{5,9},{6,10},{7,11},{8,4},{9,5},... | collective-permute-start | bytes 786440 | tf_op jit(solution)/shard_map/ppermute | solution.py:311
  (14 other events, 78.5 us)

commit v8 on v7

--- a/solution.py
+++ b/solution.py
@@ -340,32 +340,28 @@
         fields = [piece for i in range(components) for piece in here_pieces(i, distances)]
         return along_x(fields, here_pieces(0, distances), along_x_matrix, name, weight)
 
+    last = planes - 1
     blocks = list(pack(plane, velocity))
     here[0] = blocks[0]
-    for d in parts[0][1:]:
-        here[d] = swap(blocks[d], d * group)
-    for d in parts[1][:-1]:
+    for d in range(1, last):
         here[d] = swap(blocks[d], d * group)
     others[0] = across_chips(here[0])
+    others[1] = across_chips(blocks[1])
     along_x_matrix, along_y_matrix = prepare_matrices(order, own_order, slope_matrix, curve_matrix, size)
-
-    for d in parts[0][1:]:
-        here[d] = after(here[d], along_x_matrix, along_y_matrix)
+    here[last] = swap(after(blocks[last], along_x_matrix), last * group)
+    here[0] = after(here[0], along_x_matrix, along_y_matrix)
+    x_terms = [x_first([0], "x_first_0", 120)]
+    for d in range(1, last):
+        here[d] = after(here[d], x_terms[-1], others[0], others[1])
+        x_terms.append(x_first([d], f"x_first_{d}", 1))
+    others[1] = [swap(block, group) for block in others[1]]
+    for d in range(2, last):
         others[d] = across_chips(here[d])
-    here[planes - 1] = swap(blocks[-1], (planes - 1) * group)
-    last = planes - 1
-    x_terms = [x_first(parts[0], "x_first_near", 1)]
+    here[last] = after(here[last], x_terms[-1])
+    others[last] = across_chips(here[last])
     for d in parts[0]:
-        twins[d] = across_cores([after(here[d], x_terms[0])])
-    for d in parts[1][:-1]:
-        here[d] = after(here[d], x_terms[0])
-        others[d] = across_chips(here[d])
-        x_terms.append(x_first([d], f"x_first_{d}", 1))
-    for d in parts[0]:
-        others[d] = after(others[d], x_terms[-1])
-        fars[d] = across_cores(others[d])
-    here[last] = after(here[last], x_terms[-1], [twins[d] for d in parts[0]], [others[d] for d in parts[1][:-1]])
-    others[last] = across_chips(here[last])
+        twins[d] = across_cores([after(here[d], here[last], others[last - 1])])
+        fars[d] = across_cores(after(others[d], here[last], others[last - 1]))
     x_terms.append(x_first([last], f"x_first_{last}"))
 
     sums, previous = [None] * 3, x_terms[-1]
@@ -396,30 +392,29 @@
         return (x, 0, x.shape[0])
 
     for i in (1, 0, 2):
+        earlier = {1: [sums[2]], 0: [middle[1]], 2: [middle[0], middle_twin[1]]}[i]
         fields = block_pieces(i, 1)
-        fields = [(after(fields[0][0], previous), *fields[0][1:])] + fields[1:]
+        fields = [(after(fields[0][0], earlier), *fields[0][1:])] + fields[1:]
         own = here_pieces(i, range(planes))
-        terms = [(x_terms[0], i, len(parts[0]) * size)] + [(x, i, size) for x in x_terms[1:]]
+        terms = [(x, i, size) for x in x_terms]
         middle[i], base[i], square[i] = y_call(
             functools.partial(first_kernel, cells), along_y_matrix, 1,
             [fields, block_pieces(1, 1) if i != 1 else [], [piece(x) for x in sums[i]], own,
              here_pieces(1, range(planes)), terms], [kept, kept, 8], f"y_first_far_{i}", totals,
         )
-        previous = middle[i]
+        middle_twin[i] = across_cores([middle[i]])
         if i == 1:
             middle_others[1] = across_chips(middle[1])
-            middle_twin[1] = across_cores([middle[1]])
-
-    total = fold(square, "fold_own")
-    total = fold([total] + [swap(total, d * group) for d in range(1, planes)], "fold_planes")
-    middle_twin[0] = across_cores([after(middle[0], square[2])])
-    middle_twin[2] = across_cores([middle[2]])
+
+    total = fold(after(square, middle_twin[0]), "fold_own")
+    total = [total] + [swap(total, d * group) for d in range(1, planes)]
+    total = fold(after(total, middle_twin[2]), "fold_planes")
+    totals = [total] + [swap(total, m) for m in range(1, group)]
     x_terms = [None] * 3
     x_terms[1] = along_x([piece(after(middle[1], total))], [piece(middle[0])], along_x_matrix, "x_second_1")
-    middle_others[1] = after(middle_others[1], x_terms[1])
-    totals = [total] + [swap(total, m) for m in range(1, group)]
-    totals = after(totals, middle_others[1], middle_twin[0], middle_twin[2])
-    middle_others[0] = across_chips(after(middle[0], totals))
+    totals = after(totals, x_terms[1])
+    middle_others[1] = after(middle_others[1], totals)
+    middle_others[0] = across_chips(after(middle[0], middle_others[1]))
     totals = [piece(x) for x in totals]
 
     def middle_pieces(i):

time: 247 us -> 255 us (1.032)
  starting transfers between devices: 26.3 us -> 33 us
    ppermute x39 -> x40, starting transfers between devices: 26.3 us -> 33 us  [swap(): return lax.ppermute(x, 'row', [(r, r ^ distance) for r in range(devices)])]
    pallas_call x6 -> x7, Pallas kernels: 42.8 us -> 44.6 us  [along_x(): pl.pallas_call(functools.partial(along_x_kernel, (len(fields), len(carrie...]
    unnamed x14 -> x18, local copies, waits for them, and re-layouts: 8.12 us -> 9.15 us
    ppermute x39 -> x40, waiting for transfers between devices: 110 us -> 110 us  [swap(): return lax.ppermute(x, 'row', [(r, r ^ distance) for r in range(devices)])]
  transfers between devices with their start and end apart: 39 -> 40, of which waited for: 19 -> 20; matrix products, arithmetic and copies ran while one was open for 0% -> 0% of each run, Pallas kernels for 38% -> 37%
where the time goes in v8:
time: 255 us
  waiting for transfers between devices  110 us (43%)
  Pallas kernels  102 us (40%)
  starting transfers between devices  33 us (13%)
  local copies, waits for them, and re-layouts  9.24 us (4%)
    ppermute x40, waiting for transfers between devices, swap(): return lax.ppermute(x, 'row', [(r, r ^ distance) for r in range(devices)])  110 us
    pallas_call x9, Pallas kernels, y_call(): pl.pallas_call(functools.partial(kernel, tuple(counts)), grid=(length //...  45.6 us
    pallas_call x7, Pallas kernels, along_x(): pl.pallas_call(functools.partial(along_x_kernel, (len(fields), len(carrie...  44.6 us
    ppermute x40, starting transfers between devices, swap(): return lax.ppermute(x, 'row', [(r, r ^ distance) for r in range(devices)])  33 us
    unnamed x18, local copies, waits for them, and re-layouts  9.15 us
    pallas_call x1, Pallas kernels, prepare_matrices(): pl.pallas_call(functools.partial(matrices_kernel, count), grid_spec=pltpu...  7.16 us
  transfers between devices with their start and end apart: 40, of which 20 were waited for; matrix products, arithmetic and copies ran while one was open for 0% of the time, Pallas kernels for 37%

profile of v8, /device:TPU:18, one launch (start us, length us, event | category | flops | bytes accessed | tf_op | source)
XLA Modules:
  0.0 254.9 jit_solution(16038691180648983840)
XLA Ops:
  12.9 7.2 %shard_map.37 = (bf16[4,1024,1024]{2,1,0:T(8,128)(2,1)S(1)}, bf16[4,256,1024]{2,1,0:T(8,128)(2,1)S(1)}) custom-call(s32[16]{0:T(128)S(1)} %stack.74.order_ref, s32[4]{0:T(128)S(1)} %pad_add_fusion.own_ref, f32[1024,1024]{1,0:T(8,128)S(1)} %copy-done.1, f32[1024,1024]{1,0:T(8,128)S(1)} %copy-done.1, f32[1024,1024]{1,0:T(8,128)S(1)} %copy-done.2, ...), custom_call_target="tpu_custom_call" | custom-call | flops 17179869184 | bytes 33554432 | tf_op jit(solution)/shard_map/pallas_call | solution.py:63
  21.7 5.8 %x_first_0.1.refs_18_.refs_26_ = f32[192,1024]{1,0:T(8,128)S(1)} custom-call(f32[200,1024]{1,0:T(8,128)S(1)} %get-tuple-element.102.refs_0_.refs_1_.refs_2_.refs_3_.refs_8_.refs_10_.refs_14_.refs_22_.refs_18_.refs_30_, f32[200,1024]{1,0:T(8,128)S(1)} %get-tuple-element.102.refs_0_.refs_1_.refs_2_.refs_3_.refs_8_.refs_10_.refs_14_.refs_22_.refs_18_.refs_30_, ...), custom_call_target="tpu_custom_call" | custom-call | flops 24159191040 | bytes 786432 | tf_op jit(solution)/shard_map/x_first_0/pallas_call | solution.py:160
  27.5 14.6 %collective-permute-done.2.refs_4_.refs_12_.refs_23_.refs_31_ = f32[200,1024]{1,0:T(8,128)S(1)} collective-permute-done((f32[200,1024]{1,0:T(8,128)S(1)}, f32[200,1024]{1,0:T(8,128)S(1)}, u32[]{:S(2)}, u32[]{:S(2)}) %collective-permute-start.2) | collective-permute-done | bytes 819232 | tf_op jit(solution)/shard_map/ppermute | solution.py:311
  42.2 5.8 %x_first_1.1.refs_19_.refs_27_ = f32[192,1024]{1,0:T(8,128)S(1)} custom-call(f32[200,1024]{1,0:T(8,128)S(1)} %collective-permute-done.1.refs_0_.refs_1_.refs_2_.refs_3_.refs_9_.refs_11_.refs_15_.refs_26_.refs_19_.refs_23_.refs_34_, ...), custom_call_target="tpu_custom_call" | custom-call | flops 201326592 | bytes 786432 | tf_op jit(solution)/shard_map/x_first_1/pallas_call | solution.py:160
  48.0 14.5 %collective-permute-done.refs_0_.refs_1_.refs_2_.refs_3_.refs_12_.refs_16_.refs_30_.refs_8_.refs_20_.refs_24_.refs_38_ = f32[200,1024]{1,0:T(8,128)S(1)} collective-permute-done((f32[200,1024]{1,0:T(8,128)}, f32[200,1024]{1,0:T(8,128)S(1)}, u32[]{:S(2)}, u32[]{:S(2)}) %collective-permute-start) | collective-permute-done | bytes 819232 | tf_op jit(solution)/shard_map/ppermute | solution.py:311
  64.0 3.4 %collective-permute-start.8 = (f32[200,1024]{1,0:T(8,128)}, f32[200,1024]{1,0:T(8,128)S(1)}, u32[]{:S(2)}, u32[]{:S(2)}) collective-permute-start(f32[200,1024]{1,0:T(8,128)} %collective-permute-done.3), channel_id=1, source_target_pairs={{0,4},{1,5},{2,6},{3,7},{4,0},{5,1},{6,2},{7,3},{8,12},{9,13},{10,... | collective-permute-start | bytes 2457608 | tf_op jit(solution)/shard_map/ppermute | solution.py:311
  67.4 5.8 %x_first_2.1.refs_20_.refs_28_ = f32[192,1024]{1,0:T(8,128)S(1)} custom-call(f32[200,1024]{1,0:T(8,128)S(1)} %collective-permute-done.refs_0_.refs_1_.refs_2_.refs_3_.refs_12_.refs_16_.refs_30_.refs_8_.refs_20_.refs_24_.refs_38_, ...), custom_call_target="tpu_custom_call" | custom-call | flops 201326592 | bytes 786432 | tf_op jit(solution)/shard_map/x_first_2/pallas_call | solution.py:160
  73.2 6.8 %collective-permute-done.4.refs_0_.refs_1_.refs_2_.refs_3_.refs_13_.refs_17_.refs_34_.refs_9_.refs_21_.refs_25_.refs_42_ = f32[200,1024]{1,0:T(8,128)S(1)} collective-permute-done((f32[200,1024]{1,0:T(8,128)S(1)}, f32[200,1024]{1,0:T(8,128)S(1)}, u32[]{:S(2)}, u32[]{:S(2)}) %collective-permute-start.4) | collective-permute-done | bytes 819232 | tf_op jit(solution)/shard_map/ppermute | solution.py:311
  83.1 5.8 %x_first_3.1.refs_21_.refs_29_ = f32[192,1024]{1,0:T(8,128)S(1)} custom-call(f32[200,1024]{1,0:T(8,128)S(1)} %collective-permute-done.4.refs_0_.refs_1_.refs_2_.refs_3_.refs_13_.refs_17_.refs_34_.refs_9_.refs_21_.refs_25_.refs_42_, ...), custom_call_target="tpu_custom_call" | custom-call | flops 7247757312 | bytes 786432 | tf_op jit(solution)/shard_map/x_first_3/pallas_call | solution.py:160
  89.0 3.6 %y_first_near_1.1 = (f32[256,1024]{1,0:T(8,128)S(1)}, f32[256,1024]{1,0:T(8,128)S(1)}) custom-call(bf16[4,256,1024]{2,1,0:T(8,128)(2,1)S(1)} %get-tuple-element.81.matrix_ref, f32[200,1024]{1,0:T(8,128)S(1)} %get-tuple-element.102.refs_0_.refs_1_.refs_2_.refs_3_.refs_8_.refs_10_.refs_14_.refs_22_.refs_18_.refs_30_, ...), custom_call_target="tpu_custom_call" | custom-call | flops 4831838208 | bytes 1048576 | tf_op jit(solution)/shard_map/y_first_near_1/pallas_call | solution.py:238
  92.6 3.9 %y_first_near_0.1 = (f32[256,1024]{1,0:T(8,128)S(1)}, f32[256,1024]{1,0:T(8,128)S(1)}) custom-call(bf16[4,256,1024]{2,1,0:T(8,128)(2,1)S(1)} %get-tuple-element.81.matrix_ref, f32[200,1024]{1,0:T(8,128)S(1)} %get-tuple-element.102.refs_0_.refs_1_.refs_2_.refs_3_.refs_8_.refs_10_.refs_14_.refs_22_.refs_18_.refs_30_, ...), custom_call_target="tpu_custom_call" | custom-call | flops 4831838208 | bytes 1048576 | tf_op jit(solution)/shard_map/y_first_near_0/pallas_call | solution.py:238
  96.5 3.9 %y_first_near_2.1 = (f32[256,1024]{1,0:T(8,128)S(1)}, f32[256,1024]{1,0:T(8,128)S(1)}) custom-call(bf16[4,256,1024]{2,1,0:T(8,128)(2,1)S(1)} %get-tuple-element.81.matrix_ref, f32[200,1024]{1,0:T(8,128)S(1)} %get-tuple-element.102.refs_0_.refs_1_.refs_2_.refs_3_.refs_8_.refs_10_.refs_14_.refs_22_.refs_18_.refs_30_, ...), custom_call_target="tpu_custom_call" | custom-call | flops 4831838208 | bytes 1048576 | tf_op jit(solution)/shard_map/y_first_near_2/pallas_call | solution.py:238
  100.4 2.6 %collective-permute-done.13.refs_5_.refs_35_.refs_13_.refs_43_ = f32[200,1024]{1,0:T(8,128)S(1)} collective-permute-done((f32[200,1024]{1,0:T(8,128)S(1)}, f32[200,1024]{1,0:T(8,128)S(1)}, u32[]{:S(2)}, u32[]{:S(2)}) %collective-permute-start.13) | collective-permute-done | bytes 819232 | tf_op jit(solution)/shard_map/ppermute | solution.py:311
  108.9 4.3 %y_first_far_1.1 = (f32[256,1024]{1,0:T(8,128)S(1)}, f32[256,1024]{1,0:T(8,128)S(1)}, f32[8,1024]{1,0:T(8,128)S(1)}) custom-call(bf16[4,256,1024]{2,1,0:T(8,128)(2,1)S(1)} %get-tuple-element.81.matrix_ref, f32[200,1024]{1,0:T(8,128)S(1)} %collective-permute-done.refs_0_.refs_1_.refs_2_.refs_3_.refs_12_.refs_16_.refs_30_.refs_8_.refs_20_.refs_24_.refs_38_, ...), custom_call_target="tpu_custom_call" | custom-call | flops 4831838208 | bytes 1048576 | tf_op jit(solution)/shard_map/y_first_far_1/pallas_call | solution.py:238
  114.4 4.6 %y_first_far_0.1 = (f32[256,1024]{1,0:T(8,128)S(1)}, f32[256,1024]{1,0:T(8,128)S(1)}, f32[8,1024]{1,0:T(8,128)S(1)}) custom-call(bf16[4,256,1024]{2,1,0:T(8,128)(2,1)S(1)} %get-tuple-element.81.matrix_ref, f32[200,1024]{1,0:T(8,128)S(1)} %collective-permute-done.refs_0_.refs_1_.refs_2_.refs_3_.refs_12_.refs_16_.refs_30_.refs_8_.refs_20_.refs_24_.refs_38_, ...), custom_call_target="tpu_custom_call" | custom-call | flops 4831838208 | bytes 1048576 | tf_op jit(solution)/shard_map/y_first_far_0/pallas_call | solution.py:238
  119.4 4.6 %y_first_far_2.1 = (f32[256,1024]{1,0:T(8,128)S(1)}, f32[256,1024]{1,0:T(8,128)S(1)}, f32[8,1024]{1,0:T(8,128)S(1)}) custom-call(bf16[4,256,1024]{2,1,0:T(8,128)(2,1)S(1)} %get-tuple-element.81.matrix_ref, f32[200,1024]{1,0:T(8,128)S(1)} %collective-permute-done.refs_0_.refs_1_.refs_2_.refs_3_.refs_12_.refs_16_.refs_30_.refs_8_.refs_20_.refs_24_.refs_38_, ...), custom_call_target="tpu_custom_call" | custom-call | flops 4831838208 | bytes 1048576 | tf_op jit(solution)/shard_map/y_first_far_2/pallas_call | solution.py:238
  129.6 2.9 %collective-permute-done.21.refs_2_ = f32[8,128]{1,0:T(8,128)S(1)} collective-permute-done((f32[8,128]{1,0:T(8,128)S(1)}, f32[8,128]{1,0:T(8,128)S(1)}, u32[]{:S(2)}, u32[]{:S(2)}) %collective-permute-start.21) | collective-permute-done | bytes 4128 | tf_op jit(solution)/shard_map/ppermute | solution.py:311
  134.5 7.1 %x_second_1.1.refs_10_ = f32[256,1024]{1,0:T(8,128)S(1)} custom-call(f32[256,1024]{1,0:T(8,128)S(1)} %get-tuple-element.125.refs_0_.refs_4_.refs_8_.refs_9_.refs_12_.refs_17_, f32[256,1024]{1,0:T(8,128)S(1)} %get-tuple-element.137.refs_1_.refs_0_.refs_4_.refs_16_, bf16[4,1024,1024]{2,1,0:T(8,128)(2,1)S(1)} %get-tuple-element.85.refs_4_.refs_2_.refs_1_), custom_call_target="tpu_custom_call" | custom-call | flops 9663676416 | bytes 1048576 | tf_op jit(solution)/shard_map/x_second_1/pallas_call | solution.py:160
  141.6 8.2 %collective-permute-done.24.refs_13_.refs_21_ = f32[8,128]{1,0:T(8,128)S(1)} collective-permute-done((f32[8,128]{1,0:T(8,128)S(1)}, f32[8,128]{1,0:T(8,128)S(1)}, u32[]{:S(2)}, u32[]{:S(2)}) %collective-permute-start.24) | collective-permute-done | bytes 4128 | tf_op jit(solution)/shard_map/ppermute | solution.py:311
  152.5 6.6 %y_second_1.1 = (f32[64,1024]{1,0:T(8,128)S(1)}, f32[64,1024]{1,0:T(8,128)S(1)}, f32[64,1024]{1,0:T(8,128)S(1)}, f32[64,1024]{1,0:T(8,128)S(1)}) custom-call(bf16[4,256,1024]{2,1,0:T(8,128)(2,1)S(1)} %get-tuple-element.81.matrix_ref, f32[256,1024]{1,0:T(8,128)S(1)} %get-tuple-element.125.refs_0_.refs_4_.refs_8_.refs_9_.refs_12_.refs_17_, ...), custom_call_target="tpu_custom_call" | custom-call | flops 9663676416 | bytes 1048576 | tf_op jit(solution)/shard_map/y_second_1/pallas_call | solution.py:238
  159.1 7.1 %x_second_0.1.refs_18_ = f32[256,1024]{1,0:T(8,128)S(1)} custom-call(f32[256,1024]{1,0:T(8,128)S(1)} %get-tuple-element.137.refs_1_.refs_0_.refs_4_.refs_16_, bf16[4,1024,1024]{2,1,0:T(8,128)(2,1)S(1)} %get-tuple-element.85.refs_4_.refs_2_.refs_1_), custom_call_target="tpu_custom_call" | custom-call | flops 9663676416 | bytes 1048576 | tf_op jit(solution)/shard_map/x_second_0/pallas_call | solution.py:160
  166.2 9.2 %collective-permute-done.26.refs_2_.refs_6_ = f32[256,1024]{1,0:T(8,128)S(1)} collective-permute-done((f32[256,1024]{1,0:T(8,128)S(1)}, f32[256,1024]{1,0:T(8,128)S(1)}, u32[]{:S(2)}, u32[]{:S(2)}) %collective-permute-start.26) | collective-permute-done | bytes 1048608 | tf_op jit(solution)/shard_map/ppermute | solution.py:311
  179.5 7.1 %x_second_2.1.refs_18_ = f32[256,1024]{1,0:T(8,128)S(1)} custom-call(f32[256,1024]{1,0:T(8,128)S(1)} %get-tuple-element.140.refs_0_.refs_4_.refs_16_, f32[256,1024]{1,0:T(8,128)S(1)} %get-tuple-element.137.refs_1_.refs_0_.refs_4_.refs_16_, bf16[4,1024,1024]{2,1,0:T(8,128)(2,1)S(1)} %get-tuple-element.85.refs_4_.refs_2_.refs_1_), custom_call_target="tpu_custom_call" | custom-call | flops 9663676416 | bytes 1048576 | tf_op jit(solution)/shard_map/x_second_2/pallas_call | solution.py:160
  186.6 7.1 %y_second_0.1 = (f32[64,1024]{1,0:T(8,128)S(1)}, f32[64,1024]{1,0:T(8,128)S(1)}, f32[64,1024]{1,0:T(8,128)S(1)}, f32[64,1024]{1,0:T(8,128)S(1)}) custom-call(bf16[4,256,1024]{2,1,0:T(8,128)(2,1)S(1)} %get-tuple-element.81.matrix_ref, f32[256,1024]{1,0:T(8,128)S(1)} %get-tuple-element.137.refs_1_.refs_0_.refs_4_.refs_16_, f32[256,1024]{1,0:T(8,128)S(1)} %copy-done.4, ...), custom_call_target="tpu_custom_call" | custom-call | flops 9663676416 | bytes 1048576 | tf_op jit(solution)/shard_map/y_second_0/pallas_call | solution.py:238
  194.9 7.3 %collective-permute-done.31.refs_3_ = f32[64,1024]{1,0:T(8,128)S(1)} collective-permute-done((f32[64,1024]{1,0:T(8,128)S(1)}, f32[64,1024]{1,0:T(8,128)S(1)}, u32[]{:S(2)}, u32[]{:S(2)}) %collective-permute-start.31) | collective-permute-done | bytes 262176 | tf_op jit(solution)/shard_map/ppermute | solution.py:311
  203.7 2.6 %collective-permute-start.37 = (f32[64,1024]{1,0:T(8,128)S(1)}, f32[64,1024]{1,0:T(8,128)S(1)}, u32[]{:S(2)}, u32[]{:S(2)}) collective-permute-start(f32[64,1024]{1,0:T(8,128)S(1)} %get-tuple-element.144), channel_id=1, source_target_pairs={{0,4},{1,5},{2,6},{3,7},{4,0},{5,1},{6,2},{7,3},{8,12},{9,13},{10,... | collective-permute-start | bytes 786440 | tf_op jit(solution)/shard_map/ppermute | solution.py:311
  207.8 7.0 %y_second_2.1 = (f32[64,1024]{1,0:T(8,128)S(1)}, f32[64,1024]{1,0:T(8,128)S(1)}, f32[64,1024]{1,0:T(8,128)S(1)}, f32[64,1024]{1,0:T(8,128)S(1)}) custom-call(bf16[4,256,1024]{2,1,0:T(8,128)(2,1)S(1)} %get-tuple-element.81.matrix_ref, f32[256,1024]{1,0:T(8,128)S(1)} %get-tuple-element.140.refs_0_.refs_4_.refs_16_, ...), custom_call_target="tpu_custom_call" | custom-call | flops 9663676416 | bytes 1048576 | tf_op jit(solution)/shard_map/y_second_2/pallas_call | solution.py:238
  214.8 3.0 %collective-permute-start.34 = (f32[64,1024]{1,0:T(8,128)S(1)}, f32[64,1024]{1,0:T(8,128)S(1)}, u32[]{:S(2)}, u32[]{:S(2)}) collective-permute-start(f32[64,1024]{1,0:T(8,128)S(1)} %get-tuple-element.154), channel_id=1, source_target_pairs={{0,4},{1,5},{2,6},{3,7},{4,0},{5,1},{6,2},{7,3},{8,12},{9,13},{10,... | collective-permute-start | bytes 786440 | tf_op jit(solution)/shard_map/ppermute | solution.py:311
  219.3 4.8 %collective-permute-done.38.refs_2_ = f32[64,1024]{1,0:T(8,128)S(1)} collective-permute-done((f32[64,1024]{1,0:T(8,128)S(1)}, f32[64,1024]{1,0:T(8,128)S(1)}, u32[]{:S(2)}, u32[]{:S(2)}) %collective-permute-start.38) | collective-permute-done | bytes 262176 | tf_op jit(solution)/shard_map/ppermute | solution.py:311
  224.1 18.9 %collective-permute-done.39.refs_3_ = f32[64,1024]{1,0:T(8,128)S(1)} collective-permute-done((f32[64,1024]{1,0:T(8,128)S(1)}, f32[64,1024]{1,0:T(8,128)S(1)}, u32[]{:S(2)}, u32[]{:S(2)}) %collective-permute-start.39) | collective-permute-done | bytes 262176 | tf_op jit(solution)/shard_map/ppermute | solution.py:311
  244.1 2.7 %collective-permute-done.35.refs_2_ = f32[64,1024]{1,0:T(8,128)S(1)} collective-permute-done((f32[64,1024]{1,0:T(8,128)S(1)}, f32[64,1024]{1,0:T(8,128)S(1)}, u32[]{:S(2)}, u32[]{:S(2)}) %collective-permute-start.35) | collective-permute-done | bytes 262176 | tf_op jit(solution)/shard_map/ppermute | solution.py:311
  246.7 7.2 %collective-permute-done.36.refs_3_ = f32[64,1024]{1,0:T(8,128)S(1)} collective-permute-done((f32[64,1024]{1,0:T(8,128)S(1)}, f32[64,1024]{1,0:T(8,128)S(1)}, u32[]{:S(2)}, u32[]{:S(2)}) %collective-permute-start.36) | collective-permute-done | bytes 262176 | tf_op jit(solution)/shard_map/ppermute | solution.py:311
  (91 shorter events, 48.7 us)
Async XLA Ops:
  4.4 37.8 %collective-permute-start.3 = (f32[200,1024]{1,0:T(8,128)}, f32[200,1024]{1,0:T(8,128)}, u32[]{:S(2)}, u32[]{:S(2)}) collective-permute-start(f32[200,1024]{1,0:T(8,128)} %get-tuple-element.83), channel_id=1, source_target_pairs={{0,2},{1,3},{2,0},{3,1},{4,6},{5,7},{6,4},{7,5},{8,10},{9,11},{10,... | collective-permute-start | bytes 2457608 | tf_op jit(solution)/shard_map/ppermute | solution.py:311
  5.9 36.2 %collective-permute-start.1 = (f32[200,1024]{1,0:T(8,128)}, f32[200,1024]{1,0:T(8,128)S(1)}, u32[]{:S(2)}, u32[]{:S(2)}) collective-permute-start(f32[200,1024]{1,0:T(8,128)} %get-tuple-element.83), channel_id=1, source_target_pairs={{0,4},{1,5},{2,6},{3,7},{4,0},{5,1},{6,2},{7,3},{8,12},{9,13},{10,... | collective-permute-start | bytes 2457608 | tf_op jit(solution)/shard_map/ppermute | solution.py:311
  7.5 34.7 %collective-permute-start.2 = (f32[200,1024]{1,0:T(8,128)S(1)}, f32[200,1024]{1,0:T(8,128)S(1)}, u32[]{:S(2)}, u32[]{:S(2)}) collective-permute-start(f32[200,1024]{1,0:T(8,128)S(1)} %get-tuple-element.102.refs_0_.refs_1_.refs_2_.refs_3_.refs_8_.refs_10_.refs_14_.refs_22_.refs_18_.refs_30_), channel_id=1, source_target_pairs={{0,2},{1,3},{2,0},{3,1},{4,6},{5,7},{6,4},{7,5},{8,10},{9,11},{10,... | collective-permute-start | bytes 2457608 | tf_op jit(solution)/shard_map/ppermute | solution.py:311
  8.0 54.5 %collective-permute-start = (f32[200,1024]{1,0:T(8,128)}, f32[200,1024]{1,0:T(8,128)S(1)}, u32[]{:S(2)}, u32[]{:S(2)}) collective-permute-start(f32[200,1024]{1,0:T(8,128)} %get-tuple-element.82), channel_id=1, source_target_pairs={{0,8},{1,9},{2,10},{3,11},{4,12},{5,13},{6,14},{7,15},{8,0},{9,1},... | collective-permute-start | bytes 2457608 | tf_op jit(solution)/shard_map/ppermute | solution.py:311
  20.1 59.9 %collective-permute-start.4 = (f32[200,1024]{1,0:T(8,128)S(1)}, f32[200,1024]{1,0:T(8,128)S(1)}, u32[]{:S(2)}, u32[]{:S(2)}) collective-permute-start(f32[200,1024]{1,0:T(8,128)S(1)} %copy-done.8), channel_id=1, source_target_pairs={{0,12},{1,13},{2,14},{3,15},{4,8},{5,9},{6,10},{7,11},{8,4},{9,5},... | collective-permute-start | bytes 2457608 | tf_op jit(solution)/shard_map/ppermute | solution.py:311
  62.5 17.5 %collective-permute-start.5 = (f32[200,1024]{1,0:T(8,128)S(1)}, f32[200,1024]{1,0:T(8,128)S(1)}, u32[]{:S(2)}, u32[]{:S(2)}) collective-permute-start(f32[200,1024]{1,0:T(8,128)S(1)} %collective-permute-done.refs_0_.refs_1_.refs_2_.refs_3_.refs_12_.refs_16_.refs_30_.refs_8_.refs_20_.refs_24_.refs_38_), channel_id=1, source_target_pairs={{0,2},{1,3},{2,0},{3,1},{4,6},{5,7},{6,4},{7,5},{8,10},{9,11},{10,... | collective-permute-start | bytes 2457608 | tf_op jit(solution)/shard_map/ppermute | solution.py:311
  64.0 17.8 %collective-permute-start.8 = (f32[200,1024]{1,0:T(8,128)}, f32[200,1024]{1,0:T(8,128)S(1)}, u32[]{:S(2)}, u32[]{:S(2)}) collective-permute-start(f32[200,1024]{1,0:T(8,128)} %collective-permute-done.3), channel_id=1, source_target_pairs={{0,4},{1,5},{2,6},{3,7},{4,0},{5,1},{6,2},{7,3},{8,12},{9,13},{10,... | collective-permute-start | bytes 2457608 | tf_op jit(solution)/shard_map/ppermute | solution.py:311
  81.8 7.1 %collective-permute-start.10 = (f32[200,1024]{1,0:T(8,128)S(1)}, f32[200,1024]{1,0:T(8,128)S(1)}, u32[]{:S(2)}, u32[]{:S(2)}) collective-permute-start(f32[200,1024]{1,0:T(8,128)S(1)} %collective-permute-done.8.refs_5_.refs_13_.refs_27_.refs_35_), channel_id=1, source_target_pairs={{0,1},{1,0},{2,3},{3,2},{4,5},{5,4},{6,7},{7,6},{8,9},{9,8},{10,11... | collective-permute-start | bytes 2457608 | tf_op jit(solution)/shard_map/ppermute | solution.py:311
  81.8 7.1 %collective-permute-start.9 = (f32[200,1024]{1,0:T(8,128)S(1)}, f32[200,1024]{1,0:T(8,128)S(1)}, u32[]{:S(2)}, u32[]{:S(2)}) collective-permute-start(f32[200,1024]{1,0:T(8,128)S(1)} %collective-permute-done.2.refs_4_.refs_12_.refs_23_.refs_31_), channel_id=1, source_target_pairs={{0,1},{1,0},{2,3},{3,2},{4,5},{5,4},{6,7},{7,6},{8,9},{9,8},{10,11... | collective-permute-start | bytes 2457608 | tf_op jit(solution)/shard_map/ppermute | solution.py:311
  82.3 6.6 %collective-permute-start.7 = (f32[200,1024]{1,0:T(8,128)S(1)}, f32[200,1024]{1,0:T(8,128)S(1)}, u32[]{:S(2)}, u32[]{:S(2)}) collective-permute-start(f32[200,1024]{1,0:T(8,128)S(1)} %collective-permute-done.1.refs_0_.refs_1_.refs_2_.refs_3_.refs_9_.refs_11_.refs_15_.refs_26_.refs_19_.refs_23_.refs_34_), channel_id=1, source_target_pairs={{0,1},{1,0},{2,3},{3,2},{4,5},{5,4},{6,7},{7,6},{8,9},{9,8},{10,11... | collective-permute-start | bytes 2457608 | tf_op jit(solution)/shard_map/ppermute | solution.py:311
  82.3 6.6 %collective-permute-start.6 = (f32[200,1024]{1,0:T(8,128)S(1)}, f32[200,1024]{1,0:T(8,128)S(1)}, u32[]{:S(2)}, u32[]{:S(2)}) collective-permute-start(f32[200,1024]{1,0:T(8,128)S(1)} %get-tuple-element.102.refs_0_.refs_1_.refs_2_.refs_3_.refs_8_.refs_10_.refs_14_.refs_22_.refs_18_.refs_30_), channel_id=1, source_target_pairs={{0,1},{1,0},{2,3},{3,2},{4,5},{5,4},{6,7},{7,6},{8,9},{9,8},{10,11... | collective-permute-start | bytes 2457608 | tf_op jit(solution)/shard_map/ppermute | solution.py:311
  82.9 20.2 %collective-permute-start.13 = (f32[200,1024]{1,0:T(8,128)S(1)}, f32[200,1024]{1,0:T(8,128)S(1)}, u32[]{:S(2)}, u32[]{:S(2)}) collective-permute-start(f32[200,1024]{1,0:T(8,128)S(1)} %collective-permute-done.4.refs_0_.refs_1_.refs_2_.refs_3_.refs_13_.refs_17_.refs_34_.refs_9_.refs_21_.refs_25_.refs_42_), channel_id=1, source_target_pairs={{0,2},{1,3},{2,0},{3,1},{4,6},{5,7},{6,4},{7,5},{8,10},{9,11},{10,... | collective-permute-start | bytes 2457608 | tf_op jit(solution)/shard_map/ppermute | solution.py:311
  103.5 5.3 %collective-permute-start.11 = (f32[200,1024]{1,0:T(8,128)S(1)}, f32[200,1024]{1,0:T(8,128)S(1)}, u32[]{:S(2)}, u32[]{:S(2)}) collective-permute-start(f32[200,1024]{1,0:T(8,128)S(1)} %collective-permute-done.refs_0_.refs_1_.refs_2_.refs_3_.refs_12_.refs_16_.refs_30_.refs_8_.refs_20_.refs_24_.refs_38_), channel_id=1, source_target_pairs={{0,1},{1,0},{2,3},{3,2},{4,5},{5,4},{6,7},{7,6},{8,9},{9,8},{10,11... | collective-permute-start | bytes 2457608 | tf_op jit(solution)/shard_map/ppermute | solution.py:311
  114.2 5.2 %collective-permute-start.16 = (f32[256,1024]{1,0:T(8,128)S(1)}, f32[256,1024]{1,0:T(8,128)S(1)}, u32[]{:S(2)}, u32[]{:S(2)}) collective-permute-start(f32[256,1024]{1,0:T(8,128)S(1)} %get-tuple-element.125.refs_0_.refs_4_.refs_8_.refs_9_.refs_12_.refs_17_), channel_id=1, source_target_pairs={{0,1},{1,0},{2,3},{3,2},{4,5},{5,4},{6,7},{7,6},{8,9},{9,8},{10,11... | collective-permute-start | bytes 3145736 | tf_op jit(solution)/shard_map/ppermute | solution.py:311
  119.0 5.7 %collective-permute-start.19 = (f32[256,1024]{1,0:T(8,128)S(1)}, f32[256,1024]{1,0:T(8,128)S(1)}, u32[]{:S(2)}, u32[]{:S(2)}) collective-permute-start(f32[256,1024]{1,0:T(8,128)S(1)} %get-tuple-element.137.refs_1_.refs_0_.refs_4_.refs_16_), channel_id=1, source_target_pairs={{0,1},{1,0},{2,3},{3,2},{4,5},{5,4},{6,7},{7,6},{8,9},{9,8},{10,11... | collective-permute-start | bytes 3145736 | tf_op jit(solution)/shard_map/ppermute | solution.py:311
  124.0 8.5 %collective-permute-start.17 = (f32[256,1024]{1,0:T(8,128)S(1)}, f32[256,1024]{1,0:T(8,128)S(1)}, u32[]{:S(2)}, u32[]{:S(2)}) collective-permute-start(f32[256,1024]{1,0:T(8,128)S(1)} %get-tuple-element.140.refs_0_.refs_4_.refs_16_), channel_id=1, source_target_pairs={{0,1},{1,0},{2,3},{3,2},{4,5},{5,4},{6,7},{7,6},{8,9},{9,8},{10,11... | collective-permute-start | bytes 3145736 | tf_op jit(solution)/shard_map/ppermute | solution.py:311
  124.4 25.4 %collective-permute-start.18 = (f32[256,1024]{1,0:T(8,128)S(1)}, f32[256,1024]{1,0:T(8,128)S(1)}, u32[]{:S(2)}, u32[]{:S(2)}) collective-permute-start(f32[256,1024]{1,0:T(8,128)S(1)} %get-tuple-element.125.refs_0_.refs_4_.refs_8_.refs_9_.refs_12_.refs_17_), channel_id=1, source_target_pairs={{0,2},{1,3},{2,0},{3,1},{4,6},{5,7},{6,4},{7,5},{8,10},{9,11},{10,... | collective-permute-start | bytes 3145736 | tf_op jit(solution)/shard_map/ppermute | solution.py:311
  132.6 9.1 %collective-permute-start.23 = (f32[8,128]{1,0:T(8,128)S(1)}, f32[8,128]{1,0:T(8,128)S(1)}, u32[]{:S(2)}, u32[]{:S(2)}) collective-permute-start(f32[8,128]{1,0:T(8,128)S(1)} %fold_planes.1.refs_11_.refs_19_), channel_id=1, source_target_pairs={{0,1},{1,0},{2,3},{3,2},{4,5},{5,4},{6,7},{7,6},{8,9},{9,8},{10,11... | collective-permute-start | bytes 12296 | tf_op jit(solution)/shard_map/ppermute | solution.py:311
  132.6 17.2 %collective-permute-start.24 = (f32[8,128]{1,0:T(8,128)S(1)}, f32[8,128]{1,0:T(8,128)S(1)}, u32[]{:S(2)}, u32[]{:S(2)}) collective-permute-start(f32[8,128]{1,0:T(8,128)S(1)} %fold_planes.1.refs_11_.refs_19_), channel_id=1, source_target_pairs={{0,2},{1,3},{2,0},{3,1},{4,6},{5,7},{6,4},{7,5},{8,10},{9,11},{10,... | collective-permute-start | bytes 12296 | tf_op jit(solution)/shard_map/ppermute | solution.py:311
  133.9 15.9 %collective-permute-start.25 = (f32[8,128]{1,0:T(8,128)S(1)}, f32[8,128]{1,0:T(8,128)S(1)}, u32[]{:S(2)}, u32[]{:S(2)}) collective-permute-start(f32[8,128]{1,0:T(8,128)S(1)} %fold_planes.1.refs_11_.refs_19_), channel_id=1, source_target_pairs={{0,3},{1,2},{2,1},{3,0},{4,7},{5,6},{6,5},{7,4},{8,11},{9,10},{10,... | collective-permute-start | bytes 12296 | tf_op jit(solution)/shard_map/ppermute | solution.py:311
  149.9 25.5 %collective-permute-start.26 = (f32[256,1024]{1,0:T(8,128)S(1)}, f32[256,1024]{1,0:T(8,128)S(1)}, u32[]{:S(2)}, u32[]{:S(2)}) collective-permute-start(f32[256,1024]{1,0:T(8,128)S(1)} %get-tuple-element.137.refs_1_.refs_0_.refs_4_.refs_16_), channel_id=1, source_target_pairs={{0,2},{1,3},{2,0},{3,1},{4,6},{5,7},{6,4},{7,5},{8,10},{9,11},{10,... | collective-permute-start | bytes 3145736 | tf_op jit(solution)/shard_map/ppermute | solution.py:311
  175.4 11.2 %collective-permute-start.32 = (f32[256,1024]{1,0:T(8,128)S(1)}, f32[256,1024]{1,0:T(8,128)S(1)}, u32[]{:S(2)}, u32[]{:S(2)}) collective-permute-start(f32[256,1024]{1,0:T(8,128)S(1)} %collective-permute-done.26.refs_2_.refs_6_), channel_id=1, source_target_pairs={{0,1},{1,0},{2,3},{3,2},{4,5},{5,4},{6,7},{7,6},{8,9},{9,8},{10,11... | collective-permute-start | bytes 3145736 | tf_op jit(solution)/shard_map/ppermute | solution.py:311
  175.4 18.3 %collective-permute-start.29 = (f32[64,1024]{1,0:T(8,128)S(1)}, f32[64,1024]{1,0:T(8,128)S(1)}, u32[]{:S(2)}, u32[]{:S(2)}) collective-permute-start(f32[64,1024]{1,0:T(8,128)S(1)} %get-tuple-element.134), channel_id=1, source_target_pairs={{0,4},{1,5},{2,6},{3,7},{4,0},{5,1},{6,2},{7,3},{8,12},{9,13},{10,... | collective-permute-start | bytes 786440 | tf_op jit(solution)/shard_map/ppermute | solution.py:311
  177.2 17.8 %collective-permute-start.30 = (f32[64,1024]{1,0:T(8,128)S(1)}, f32[64,1024]{1,0:T(8,128)S(1)}, u32[]{:S(2)}, u32[]{:S(2)}) collective-permute-start(f32[64,1024]{1,0:T(8,128)S(1)} %get-tuple-element.135), channel_id=1, source_target_pairs={{0,8},{1,9},{2,10},{3,11},{4,12},{5,13},{6,14},{7,15},{8,0},{9,1},... | collective-permute-start | bytes 786440 | tf_op jit(solution)/shard_map/ppermute | solution.py:311
  177.2 25.1 %collective-permute-start.31 = (f32[64,1024]{1,0:T(8,128)S(1)}, f32[64,1024]{1,0:T(8,128)S(1)}, u32[]{:S(2)}, u32[]{:S(2)}) collective-permute-start(f32[64,1024]{1,0:T(8,128)S(1)} %get-tuple-element.136), channel_id=1, source_target_pairs={{0,12},{1,13},{2,14},{3,15},{4,8},{5,9},{6,10},{7,11},{8,4},{9,5},... | collective-permute-start | bytes 786440 | tf_op jit(solution)/shard_map/ppermute | solution.py:311
  178.9 24.7 %collective-permute-start.28 = (f32[256,1024]{1,0:T(8,128)S(1)}, f32[256,1024]{1,0:T(8,128)S(1)}, u32[]{:S(2)}, u32[]{:S(2)}) collective-permute-start(f32[256,1024]{1,0:T(8,128)S(1)} %get-tuple-element.140.refs_0_.refs_4_.refs_16_), channel_id=1, source_target_pairs={{0,2},{1,3},{2,0},{3,1},{4,6},{5,7},{6,4},{7,5},{8,10},{9,11},{10,... | collective-permute-start | bytes 3145736 | tf_op jit(solution)/shard_map/ppermute | solution.py:311
  203.7 14.1 %collective-permute-start.37 = (f32[64,1024]{1,0:T(8,128)S(1)}, f32[64,1024]{1,0:T(8,128)S(1)}, u32[]{:S(2)}, u32[]{:S(2)}) collective-permute-start(f32[64,1024]{1,0:T(8,128)S(1)} %get-tuple-element.144), channel_id=1, source_target_pairs={{0,4},{1,5},{2,6},{3,7},{4,0},{5,1},{6,2},{7,3},{8,12},{9,13},{10,... | collective-permute-start | bytes 786440 | tf_op jit(solution)/shard_map/ppermute | solution.py:311
  206.3 17.8 %collective-permute-start.38 = (f32[64,1024]{1,0:T(8,128)S(1)}, f32[64,1024]{1,0:T(8,128)S(1)}, u32[]{:S(2)}, u32[]{:S(2)}) collective-permute-start(f32[64,1024]{1,0:T(8,128)S(1)} %get-tuple-element.145), channel_id=1, source_target_pairs={{0,8},{1,9},{2,10},{3,11},{4,12},{5,13},{6,14},{7,15},{8,0},{9,1},... | collective-permute-start | bytes 786440 | tf_op jit(solution)/shard_map/ppermute | solution.py:311
  206.3 36.7 %collective-permute-start.39 = (f32[64,1024]{1,0:T(8,128)S(1)}, f32[64,1024]{1,0:T(8,128)S(1)}, u32[]{:S(2)}, u32[]{:S(2)}) collective-permute-start(f32[64,1024]{1,0:T(8,128)S(1)} %get-tuple-element.146), channel_id=1, source_target_pairs={{0,12},{1,13},{2,14},{3,15},{4,8},{5,9},{6,10},{7,11},{8,4},{9,5},... | collective-permute-start | bytes 786440 | tf_op jit(solution)/shard_map/ppermute | solution.py:311
  214.8 29.2 %collective-permute-start.34 = (f32[64,1024]{1,0:T(8,128)S(1)}, f32[64,1024]{1,0:T(8,128)S(1)}, u32[]{:S(2)}, u32[]{:S(2)}) collective-permute-start(f32[64,1024]{1,0:T(8,128)S(1)} %get-tuple-element.154), channel_id=1, source_target_pairs={{0,4},{1,5},{2,6},{3,7},{4,0},{5,1},{6,2},{7,3},{8,12},{9,13},{10,... | collective-permute-start | bytes 786440 | tf_op jit(solution)/shard_map/ppermute | solution.py:311
  217.8 28.9 %collective-permute-start.35 = (f32[64,1024]{1,0:T(8,128)S(1)}, f32[64,1024]{1,0:T(8,128)S(1)}, u32[]{:S(2)}, u32[]{:S(2)}) collective-permute-start(f32[64,1024]{1,0:T(8,128)S(1)} %get-tuple-element.155), channel_id=1, source_target_pairs={{0,8},{1,9},{2,10},{3,11},{4,12},{5,13},{6,14},{7,15},{8,0},{9,1},... | collective-permute-start | bytes 786440 | tf_op jit(solution)/shard_map/ppermute | solution.py:311
  217.8 36.1 %collective-permute-start.36 = (f32[64,1024]{1,0:T(8,128)S(1)}, f32[64,1024]{1,0:T(8,128)S(1)}, u32[]{:S(2)}, u32[]{:S(2)}) collective-permute-start(f32[64,1024]{1,0:T(8,128)S(1)} %get-tuple-element.156), channel_id=1, source_target_pairs={{0,12},{1,13},{2,14},{3,15},{4,8},{5,9},{6,10},{7,11},{8,4},{9,5},... | collective-permute-start | bytes 786440 | tf_op jit(solution)/shard_map/ppermute | solution.py:311
  (17 other events, 86.4 us)

commit v9 on v8

--- a/solution.py
+++ b/solution.py
@@ -103,24 +103,27 @@
     plane = plane_ref[0]
     velocity = velocity_ref[...].reshape(components * planes * size // 8, 8, length)
     squares = jnp.sum(velocity * velocity, axis=0)
+    *block_refs, tail_ref = block_refs
     for d, ref in enumerate(block_refs):
-        for i in range(components):
+        count = components if d < planes - 1 else components - 1
+        for i in range(count):
             ref[i * size:(i + 1) * size, :] = velocity_ref[i, plane ^ d]
-        ref[components * size:, :] = squares
+        ref[count * size:, :] = squares
+    tail_ref[...] = velocity_ref[components - 1, plane ^ (planes - 1)]
 
 
 def pack(plane, velocity):
     components, planes, size, length = velocity.shape
-    shape = (components * size + 8, length)
+    rows = [components * size + 8] * (planes - 1) + [(components - 1) * size + 8, size]
     return pl.pallas_call(
         pack_kernel,
         grid_spec=pltpu.PrefetchScalarGridSpec(
             num_scalar_prefetch=1,
             grid=(1,),
             in_specs=[pl.BlockSpec(velocity.shape, lambda n, plane_ref: (0, 0, 0, 0))],
-            out_specs=[pl.BlockSpec(shape, lambda n, plane_ref: (0, 0))] * planes,
+            out_specs=[pl.BlockSpec((count, length), lambda n, plane_ref: (0, 0)) for count in rows],
         ),
-        out_shape=[jax.ShapeDtypeStruct(shape, F32)] * planes,
+        out_shape=[jax.ShapeDtypeStruct((count, length), F32) for count in rows],
         compiler_params=params(),
         name="pack",
     )(plane.reshape(1).astype(jnp.int32), velocity)
@@ -322,25 +325,28 @@
     ]).astype(jnp.int32)
     own_order = jnp.stack([(plane ^ d) * group + member for d in range(planes)]).astype(jnp.int32)
 
-    here, others, twins, fars = [None] * planes, [None] * planes, [None] * planes, [None] * planes
+    last = planes - 1
+    here, others, twins, fars = ([None] * (planes + 1) for _ in range(4))
+
+    def piece_of(store, i, d):
+        block = store[planes] if d == last and i == components - 1 else store[d]
+        return lambda h: (block[h], 0 if d == last and i == components - 1 else i, size)
 
     def block_pieces(i, part):
-        pieces = []
-        for h in range(chips):
-            for core in range(2):
-                for d in parts[part]:
-                    block = ([here[d]] + others[d])[h] if core == 0 else (twins[d] + fars[d])[h]
-                    pieces.append((block, i, size))
-        return pieces
+        near = [[here[d]] + (others[d] or []) for d in range(planes + 1)]
+        far = [(twins[d] or []) + (fars[d] or []) for d in range(planes + 1)]
+        return [
+            piece_of(store, i, d)(h) for h in range(chips) for store in (near, far) for d in parts[part]
+        ]
 
     def here_pieces(i, distances):
-        return [(here[d], i, size) for d in distances]
-
-    def x_first(distances, name, weight=36):
-        fields = [piece for i in range(components) for piece in here_pieces(i, distances)]
+        return [piece_of([[block] for block in here], i, d)(0) for d in distances]
+
+    def x_first(components, distances, name, weight=36):
+        fields = [piece for i in components for piece in here_pieces(i, distances)]
         return along_x(fields, here_pieces(0, distances), along_x_matrix, name, weight)
 
-    last = planes - 1
+    every = range(components)
     blocks = list(pack(plane, velocity))
     here[0] = blocks[0]
     for d in range(1, last):
@@ -348,40 +354,47 @@
     others[0] = across_chips(here[0])
     others[1] = across_chips(blocks[1])
     along_x_matrix, along_y_matrix = prepare_matrices(order, own_order, slope_matrix, curve_matrix, size)
-    here[last] = swap(after(blocks[last], along_x_matrix), last * group)
-    here[0] = after(here[0], along_x_matrix, along_y_matrix)
-    x_terms = [x_first([0], "x_first_0", 120)]
-    for d in range(1, last):
-        here[d] = after(here[d], x_terms[-1], others[0], others[1])
-        x_terms.append(x_first([d], f"x_first_{d}", 1))
-    others[1] = [swap(block, group) for block in others[1]]
-    for d in range(2, last):
-        others[d] = across_chips(here[d])
-    here[last] = after(here[last], x_terms[-1])
+
+    here[1] = after(here[1], along_x_matrix, along_y_matrix)
+    others[1] = [swap(after(block, here[1]), group) for block in others[1]]
+    here[last] = swap(after(blocks[last], here[1]), last * group)
+    here[planes] = swap(after(blocks[planes], here[last - 1]), last * group)
+    x_near = x_first(every, parts[0], "x_first_near", 1)
+    here[2] = after(here[2], x_near, others[0])
+    others[2] = across_chips(here[2])
+    x_two = x_first(every, [2], "x_first_2", 1)
+    for d in parts[0]:
+        twins[d] = across_cores([after(here[d], x_near)])
+    here[last] = after(here[last], x_two)
     others[last] = across_chips(here[last])
     for d in parts[0]:
-        twins[d] = across_cores([after(here[d], here[last], others[last - 1])])
-        fars[d] = across_cores(after(others[d], here[last], others[last - 1]))
-    x_terms.append(x_first([last], f"x_first_{last}"))
-
-    sums, previous = [None] * 3, x_terms[-1]
-    for i in (1, 0, 2):
+        others[d] = after(others[d], here[last])
+        fars[d] = across_cores(others[d])
+    sums = [None] * 3
+
+    def near_sums(i, earlier):
         fields = block_pieces(i, 0)
-        fields = [(after(fields[0][0], previous), *fields[0][1:])] + fields[1:]
+        fields = [(after(fields[0][0], earlier), *fields[0][1:])] + fields[1:]
         sums[i] = y_call(
             partial_kernel, along_y_matrix, 0, [fields, block_pieces(1, 0) if i != 1 else [], []],
-            [kept, kept], f"y_first_near_{i}",
+            [kept, kept], f"y_first_near_{i}", (), 36,
         )
-        previous = sums[i]
-    for d in parts[1][:-1]:
-        twins[d] = across_cores([after(here[d], sums[1])])
-        others[d] = after(others[d], sums[1])
-        fars[d] = across_cores(others[d])
-    twins[last] = across_cores([after(here[last], sums[0])])
+
+    near_sums(1, here[last])
+    twins[2] = across_cores([after(here[2], here[last])])
+    others[2] = after(others[2], here[last])
+    fars[2] = across_cores(others[2])
+    here[last] = after(here[last], sums[1])
+    x_last = x_first(every[:-1], [last], "x_first_last", 36)
+    near_sums(0, x_last)
+    here[planes] = after(here[planes], sums[0])
+    others[planes] = across_chips(here[planes])
+    twins[last] = across_cores([after(here[last], sums[1], twins[2], fars[2])])
+    near_sums(2, here[planes])
     others[last] = after(others[last], sums[2])
     fars[last] = across_cores(others[last])
     totals = [
-        (block, components * size // 8, 8)
+        (block, block.shape[0] // 8 - 1, 8)
         for d in range(planes) for block in [here[d]] + others[d] + twins[d] + fars[d]
     ]
 
@@ -391,29 +404,37 @@
     def piece(x):
         return (x, 0, x.shape[0])
 
-    for i in (1, 0, 2):
-        earlier = {1: [sums[2]], 0: [middle[1]], 2: [middle[0], middle_twin[1]]}[i]
+    def first_step(i, terms, earlier, weight=36):
         fields = block_pieces(i, 1)
         fields = [(after(fields[0][0], earlier), *fields[0][1:])] + fields[1:]
-        own = here_pieces(i, range(planes))
-        terms = [(x, i, size) for x in x_terms]
         middle[i], base[i], square[i] = y_call(
             functools.partial(first_kernel, cells), along_y_matrix, 1,
-            [fields, block_pieces(1, 1) if i != 1 else [], [piece(x) for x in sums[i]], own,
-             here_pieces(1, range(planes)), terms], [kept, kept, 8], f"y_first_far_{i}", totals,
+            [fields, block_pieces(1, 1) if i != 1 else [], [piece(x) for x in sums[i]],
+             here_pieces(i, range(planes)), here_pieces(1, range(planes)), terms],
+            [kept, kept, 8], f"y_first_far_{i}", totals, weight,
         )
-        middle_twin[i] = across_cores([middle[i]])
-        if i == 1:
-            middle_others[1] = across_chips(middle[1])
-
-    total = fold(after(square, middle_twin[0]), "fold_own")
+
+    def terms_of(i):
+        return [(x_near, i, len(parts[0]) * size), (x_two, i, size), (x_last, i, size)]
+
+    first_step(1, terms_of(1), sums[2])
+    middle_others[1] = across_chips(middle[1])
+    first_step(0, terms_of(0), [middle[1], others[planes]], 36)
+    twins[planes] = across_cores([after(here[planes], middle[1])])
+    x_tail = x_first(every[-1:], [last], "x_first_tail", 36)
+    others[planes] = after(others[planes], middle[1])
+    fars[planes] = across_cores(others[planes])
+    first_step(2, terms_of(2)[:-1] + [(x_tail, 0, size)], middle[0], 36)
+
+    total = fold(square, "fold_own")
     total = [total] + [swap(total, d * group) for d in range(1, planes)]
-    total = fold(after(total, middle_twin[2]), "fold_planes")
-    totals = [total] + [swap(total, m) for m in range(1, group)]
+    total = fold(total, "fold_planes")
+    for i in range(3):
+        middle_twin[i] = across_cores([after(middle[i], square[2])])
     x_terms = [None] * 3
-    x_terms[1] = along_x([piece(after(middle[1], total))], [piece(middle[0])], along_x_matrix, "x_second_1")
-    totals = after(totals, x_terms[1])
-    middle_others[1] = after(middle_others[1], totals)
+    x_terms[1] = along_x([piece(after(middle[1], total))], [piece(middle[0])], along_x_matrix, "x_second_1", 36)
+    middle_others[1] = after(middle_others[1], x_terms[1], middle_twin)
+    totals = [total] + [swap(after(total, middle_others[1]), m) for m in range(1, group)]
     middle_others[0] = across_chips(after(middle[0], middle_others[1]))
     totals = [piece(x) for x in totals]
 

time: 255 us -> 242 us (0.949)
  waiting for transfers between devices: 110 us -> 92 us
  starting transfers between devices: 33 us -> 39.7 us
    ppermute x40 -> x44, waiting for transfers between devices: 110 us -> 92 us  [swap(): return lax.ppermute(x, 'row', [(r, r ^ distance) for r in range(devices)])]
    ppermute x40 -> x44, starting transfers between devices: 33 us -> 39.7 us  [swap(): return lax.ppermute(x, 'row', [(r, r ^ distance) for r in range(devices)])]
    unnamed x18 -> x14, local copies, waits for them, and re-layouts: 9.15 us -> 7.09 us
  transfers between devices with their start and end apart: 40 -> 44, of which waited for: 20 -> 15; matrix products, arithmetic and copies ran while one was open for 0% -> 0% of each run, Pallas kernels for 37% -> 41%
where the time goes in v9:
time: 242 us
  Pallas kernels  102 us (42%)
  waiting for transfers between devices  92 us (38%)
  starting transfers between devices  39.7 us (16%)
  local copies, waits for them, and re-layouts  7.19 us (3%)
    ppermute x44, waiting for transfers between devices, swap(): return lax.ppermute(x, 'row', [(r, r ^ distance) for r in range(devices)])  92 us
    pallas_call x9, Pallas kernels, y_call(): pl.pallas_call(functools.partial(kernel, tuple(counts)), grid=(length //...  45.8 us
    pallas_call x7, Pallas kernels, along_x(): pl.pallas_call(functools.partial(along_x_kernel, (len(fields), len(carrie...  44.7 us
    ppermute x44, starting transfers between devices, swap(): return lax.ppermute(x, 'row', [(r, r ^ distance) for r in range(devices)])  39.7 us
    pallas_call x1, Pallas kernels, prepare_matrices(): pl.pallas_call(functools.partial(matrices_kernel, count), grid_spec=pltpu...  7.16 us
    unnamed x14, local copies, waits for them, and re-layouts  7.09 us
  transfers between devices with their start and end apart: 44, of which 15 were waited for; matrix products, arithmetic and copies ran while one was open for 0% of the time, Pallas kernels for 41%

profile of v9, /device:TPU:18, one launch (start us, length us, event | category | flops | bytes accessed | tf_op | source)
XLA Modules:
  0.0 241.7 jit_solution(4334084481178827148)
XLA Ops:
  10.6 2.2 copy-done.2
  12.8 7.2 %shard_map.37 = (bf16[4,1024,1024]{2,1,0:T(8,128)(2,1)S(1)}, bf16[4,256,1024]{2,1,0:T(8,128)(2,1)S(1)}) custom-call(s32[16]{0:T(128)S(1)} %stack.74.order_ref, s32[4]{0:T(128)S(1)} %pad_add_fusion.own_ref, f32[1024,1024]{1,0:T(8,128)S(1)} %copy-done.1, f32[1024,1024]{1,0:T(8,128)S(1)} %copy-done.1, f32[1024,1024]{1,0:T(8,128)S(1)} %copy-done.2, ...), custom_call_target="tpu_custom_call" | custom-call | flops 17179869184 | bytes 33554432 | tf_op jit(solution)/shard_map/pallas_call | solution.py:63
  20.0 21.3 %collective-permute-done.1.refs_1_.refs_3_.refs_5_.refs_7_.refs_9_.refs_11_.refs_15_.refs_25_.refs_19_.refs_23_.refs_33_ = f32[200,1024]{1,0:T(8,128)S(1)} collective-permute-done((f32[200,1024]{1,0:T(8,128)}, f32[200,1024]{1,0:T(8,128)S(1)}, u32[]{:S(2)}, u32[]{:S(2)}) %collective-permute-start.1) | collective-permute-done | bytes 819232 | tf_op jit(solution)/shard_map/ppermute | solution.py:314
  41.3 2.4 collective-permute-start.8
  44.1 9.8 %x_first_near.1.refs_18_.refs_26_ = f32[384,1024]{1,0:T(8,128)S(1)} custom-call(f32[200,1024]{1,0:T(8,128)S(1)} %get-tuple-element.105.refs_0_.refs_2_.refs_4_.refs_6_.refs_8_.refs_10_.refs_14_.refs_21_.refs_18_.refs_22_.refs_29_, ...), custom_call_target="tpu_custom_call" | custom-call | flops 402653184 | bytes 1572864 | tf_op jit(solution)/shard_map/x_first_near/pallas_call | solution.py:163
  54.5 5.8 %x_first_2.1.refs_19_.refs_27_ = f32[192,1024]{1,0:T(8,128)S(1)} custom-call(f32[200,1024]{1,0:T(8,128)S(1)} %collective-permute-done.refs_0_.refs_1_.refs_2_.refs_3_.refs_12_.refs_16_.refs_29_.refs_8_.refs_20_.refs_24_.refs_37_, ...), custom_call_target="tpu_custom_call" | custom-call | flops 201326592 | bytes 786432 | tf_op jit(solution)/shard_map/x_first_2/pallas_call | solution.py:163
  61.0 12.2 %collective-permute-done.8.refs_5_.refs_13_.refs_26_.refs_34_ = f32[200,1024]{1,0:T(8,128)S(1)} collective-permute-done((f32[200,1024]{1,0:T(8,128)}, f32[200,1024]{1,0:T(8,128)S(1)}, u32[]{:S(2)}, u32[]{:S(2)}) %collective-permute-start.8) | collective-permute-done | bytes 819232 | tf_op jit(solution)/shard_map/ppermute | solution.py:314
  75.5 3.6 %y_first_near_1.1 = (f32[256,1024]{1,0:T(8,128)S(1)}, f32[256,1024]{1,0:T(8,128)S(1)}) custom-call(bf16[4,256,1024]{2,1,0:T(8,128)(2,1)S(1)} %get-tuple-element.80.matrix_ref, f32[200,1024]{1,0:T(8,128)S(1)} %get-tuple-element.105.refs_0_.refs_2_.refs_4_.refs_6_.refs_8_.refs_10_.refs_14_.refs_21_.refs_18_.refs_22_.refs_29_, ...), custom_call_target="tpu_custom_call" | custom-call | flops 4831838208 | bytes 1048576 | tf_op jit(solution)/shard_map/y_first_near_1/pallas_call | solution.py:241
  79.1 4.5 %x_first_last.1.refs_20_.refs_28_ = f32[128,1024]{1,0:T(8,128)S(1)} custom-call(f32[136,1024]{1,0:T(8,128)S(1)} %collective-permute-done.4.refs_0_.refs_1_.refs_2_.refs_13_.refs_17_.refs_33_.refs_9_.refs_21_.refs_25_.refs_41_, f32[136,1024]{1,0:T(8,128)S(1)} %collective-permute-done.4.refs_0_.refs_1_.refs_2_.refs_13_.refs_17_.refs_33_.refs_9_.refs_21_.refs_25_.refs_41_, ...), custom_call_target="tpu_custom_call" | custom-call | flops 4831838208 | bytes 524288 | tf_op jit(solution)/shard_map/x_first_last/pallas_call | solution.py:163
  83.8 3.9 %y_first_near_0.1 = (f32[256,1024]{1,0:T(8,128)S(1)}, f32[256,1024]{1,0:T(8,128)S(1)}) custom-call(bf16[4,256,1024]{2,1,0:T(8,128)(2,1)S(1)} %get-tuple-element.80.matrix_ref, f32[200,1024]{1,0:T(8,128)S(1)} %get-tuple-element.105.refs_0_.refs_2_.refs_4_.refs_6_.refs_8_.refs_10_.refs_14_.refs_21_.refs_18_.refs_22_.refs_29_, ...), custom_call_target="tpu_custom_call" | custom-call | flops 4831838208 | bytes 1048576 | tf_op jit(solution)/shard_map/y_first_near_0/pallas_call | solution.py:241
  87.6 3.9 %y_first_near_2.1 = (f32[256,1024]{1,0:T(8,128)S(1)}, f32[256,1024]{1,0:T(8,128)S(1)}) custom-call(bf16[4,256,1024]{2,1,0:T(8,128)(2,1)S(1)} %get-tuple-element.80.matrix_ref, f32[200,1024]{1,0:T(8,128)S(1)} %get-tuple-element.105.refs_0_.refs_2_.refs_4_.refs_6_.refs_8_.refs_10_.refs_14_.refs_21_.refs_18_.refs_22_.refs_29_, ...), custom_call_target="tpu_custom_call" | custom-call | flops 4831838208 | bytes 1048576 | tf_op jit(solution)/shard_map/y_first_near_2/pallas_call | solution.py:241
  93.1 3.3 %x_first_tail.1.refs_28_ = f32[64,1024]{1,0:T(8,128)S(1)} custom-call(f32[64,1024]{1,0:T(8,128)S(1)} %collective-permute-done.3.refs_0_.refs_1_.refs_21_, f32[136,1024]{1,0:T(8,128)S(1)} %collective-permute-done.4.refs_0_.refs_1_.refs_2_.refs_13_.refs_17_.refs_33_.refs_9_.refs_21_.refs_25_.refs_41_, ...), custom_call_target="tpu_custom_call" | custom-call | flops 2415919104 | bytes 262144 | tf_op jit(solution)/shard_map/x_first_tail/pallas_call | solution.py:163
  96.4 4.4 %y_first_far_1.1 = (f32[256,1024]{1,0:T(8,128)S(1)}, f32[256,1024]{1,0:T(8,128)S(1)}, f32[8,1024]{1,0:T(8,128)S(1)}) custom-call(bf16[4,256,1024]{2,1,0:T(8,128)(2,1)S(1)} %get-tuple-element.80.matrix_ref, f32[200,1024]{1,0:T(8,128)S(1)} %collective-permute-done.refs_0_.refs_1_.refs_2_.refs_3_.refs_12_.refs_16_.refs_29_.refs_8_.refs_20_.refs_24_.refs_37_, ...), custom_call_target="tpu_custom_call" | custom-call | flops 4831838208 | bytes 1048576 | tf_op jit(solution)/shard_map/y_first_far_1/pallas_call | solution.py:241
  102.3 4.6 %y_first_far_0.1 = (f32[256,1024]{1,0:T(8,128)S(1)}, f32[256,1024]{1,0:T(8,128)S(1)}, f32[8,1024]{1,0:T(8,128)S(1)}) custom-call(bf16[4,256,1024]{2,1,0:T(8,128)(2,1)S(1)} %get-tuple-element.80.matrix_ref, f32[200,1024]{1,0:T(8,128)S(1)} %collective-permute-done.refs_0_.refs_1_.refs_2_.refs_3_.refs_12_.refs_16_.refs_29_.refs_8_.refs_20_.refs_24_.refs_37_, ...), custom_call_target="tpu_custom_call" | custom-call | flops 4831838208 | bytes 1048576 | tf_op jit(solution)/shard_map/y_first_far_0/pallas_call | solution.py:241
  107.0 4.7 %y_first_far_2.1 = (f32[256,1024]{1,0:T(8,128)S(1)}, f32[256,1024]{1,0:T(8,128)S(1)}, f32[8,1024]{1,0:T(8,128)S(1)}) custom-call(bf16[4,256,1024]{2,1,0:T(8,128)(2,1)S(1)} %get-tuple-element.80.matrix_ref, f32[200,1024]{1,0:T(8,128)S(1)} %collective-permute-done.refs_0_.refs_1_.refs_2_.refs_3_.refs_12_.refs_16_.refs_29_.refs_8_.refs_20_.refs_24_.refs_37_, ...), custom_call_target="tpu_custom_call" | custom-call | flops 4831838208 | bytes 1048576 | tf_op jit(solution)/shard_map/y_first_far_2/pallas_call | solution.py:241
  113.2 2.8 %collective-permute-done.24.refs_3_ = f32[8,128]{1,0:T(8,128)S(1)} collective-permute-done((f32[8,128]{1,0:T(8,128)S(1)}, f32[8,128]{1,0:T(8,128)S(1)}, u32[]{:S(2)}, u32[]{:S(2)}) %collective-permute-start.24) | collective-permute-done | bytes 4128 | tf_op jit(solution)/shard_map/ppermute | solution.py:314
  116.0 5.3 %collective-permute-start.23 = (f32[8,128]{1,0:T(8,128)S(1)}, f32[8,128]{1,0:T(8,128)S(1)}, u32[]{:S(2)}, u32[]{:S(2)}) collective-permute-start(f32[8,128]{1,0:T(8,128)S(1)} %fold_own.1.refs_0_), channel_id=1, source_target_pairs={{0,8},{1,9},{2,10},{3,11},{4,12},{5,13},{6,14},{7,15},{8,0},{9,1},... | collective-permute-start | bytes 12296 | tf_op jit(solution)/shard_map/ppermute | solution.py:314
  122.9 2.4 %collective-permute-start.22 = (f32[8,128]{1,0:T(8,128)S(1)}, f32[8,128]{1,0:T(8,128)S(1)}, u32[]{:S(2)}, u32[]{:S(2)}) collective-permute-start(f32[8,128]{1,0:T(8,128)S(1)} %fold_own.1.refs_0_), channel_id=1, source_target_pairs={{0,4},{1,5},{2,6},{3,7},{4,0},{5,1},{6,2},{7,3},{8,12},{9,13},{10,... | collective-permute-start | bytes 12296 | tf_op jit(solution)/shard_map/ppermute | solution.py:314
  127.0 7.1 %x_second_1.1.refs_10_ = f32[256,1024]{1,0:T(8,128)S(1)} custom-call(f32[256,1024]{1,0:T(8,128)S(1)} %get-tuple-element.126.refs_0_.refs_4_.refs_8_.refs_9_.refs_12_.refs_17_, f32[256,1024]{1,0:T(8,128)S(1)} %get-tuple-element.135.refs_1_.refs_0_.refs_4_.refs_16_, bf16[4,1024,1024]{2,1,0:T(8,128)(2,1)S(1)} %get-tuple-element.84.refs_8_.refs_4_.refs_3_.refs_2_.refs_1_), custom_call_target="tpu_custom_call" | custom-call | flops 9663676416 | bytes 1048576 | tf_op jit(solution)/shard_map/x_second_1/pallas_call | solution.py:163
  139.4 6.6 %y_second_1.1 = (f32[64,1024]{1,0:T(8,128)S(1)}, f32[64,1024]{1,0:T(8,128)S(1)}, f32[64,1024]{1,0:T(8,128)S(1)}, f32[64,1024]{1,0:T(8,128)S(1)}) custom-call(bf16[4,256,1024]{2,1,0:T(8,128)(2,1)S(1)} %get-tuple-element.80.matrix_ref, f32[256,1024]{1,0:T(8,128)S(1)} %get-tuple-element.126.refs_0_.refs_4_.refs_8_.refs_9_.refs_12_.refs_17_, ...), custom_call_target="tpu_custom_call" | custom-call | flops 9663676416 | bytes 1048576 | tf_op jit(solution)/shard_map/y_second_1/pallas_call | solution.py:241
  146.0 7.1 %x_second_0.1.refs_18_ = f32[256,1024]{1,0:T(8,128)S(1)} custom-call(f32[256,1024]{1,0:T(8,128)S(1)} %get-tuple-element.135.refs_1_.refs_0_.refs_4_.refs_16_, bf16[4,1024,1024]{2,1,0:T(8,128)(2,1)S(1)} %get-tuple-element.84.refs_8_.refs_4_.refs_3_.refs_2_.refs_1_), custom_call_target="tpu_custom_call" | custom-call | flops 9663676416 | bytes 1048576 | tf_op jit(solution)/shard_map/x_second_0/pallas_call | solution.py:163
  153.2 8.7 %collective-permute-done.27.refs_2_.refs_6_ = f32[256,1024]{1,0:T(8,128)S(1)} collective-permute-done((f32[256,1024]{1,0:T(8,128)S(1)}, f32[256,1024]{1,0:T(8,128)S(1)}, u32[]{:S(2)}, u32[]{:S(2)}) %collective-permute-start.27) | collective-permute-done | bytes 1048608 | tf_op jit(solution)/shard_map/ppermute | solution.py:314
  166.9 7.1 %x_second_2.1.refs_18_ = f32[256,1024]{1,0:T(8,128)S(1)} custom-call(f32[256,1024]{1,0:T(8,128)S(1)} %get-tuple-element.138.refs_0_.refs_4_.refs_16_, f32[256,1024]{1,0:T(8,128)S(1)} %get-tuple-element.135.refs_1_.refs_0_.refs_4_.refs_16_, bf16[4,1024,1024]{2,1,0:T(8,128)(2,1)S(1)} %get-tuple-element.84.refs_8_.refs_4_.refs_3_.refs_2_.refs_1_), custom_call_target="tpu_custom_call" | custom-call | flops 9663676416 | bytes 1048576 | tf_op jit(solution)/shard_map/x_second_2/pallas_call | solution.py:163
  174.0 7.1 %y_second_0.1 = (f32[64,1024]{1,0:T(8,128)S(1)}, f32[64,1024]{1,0:T(8,128)S(1)}, f32[64,1024]{1,0:T(8,128)S(1)}, f32[64,1024]{1,0:T(8,128)S(1)}) custom-call(bf16[4,256,1024]{2,1,0:T(8,128)(2,1)S(1)} %get-tuple-element.80.matrix_ref, f32[256,1024]{1,0:T(8,128)S(1)} %get-tuple-element.135.refs_1_.refs_0_.refs_4_.refs_16_, ...), custom_call_target="tpu_custom_call" | custom-call | flops 9663676416 | bytes 1048576 | tf_op jit(solution)/shard_map/y_second_0/pallas_call | solution.py:241
  182.3 6.7 %collective-permute-done.35.refs_3_ = f32[64,1024]{1,0:T(8,128)S(1)} collective-permute-done((f32[64,1024]{1,0:T(8,128)S(1)}, f32[64,1024]{1,0:T(8,128)S(1)}, u32[]{:S(2)}, u32[]{:S(2)}) %collective-permute-start.35) | collective-permute-done | bytes 262176 | tf_op jit(solution)/shard_map/ppermute | solution.py:314
  190.4 2.6 %collective-permute-start.41 = (f32[64,1024]{1,0:T(8,128)S(1)}, f32[64,1024]{1,0:T(8,128)S(1)}, u32[]{:S(2)}, u32[]{:S(2)}) collective-permute-start(f32[64,1024]{1,0:T(8,128)S(1)} %get-tuple-element.142), channel_id=1, source_target_pairs={{0,4},{1,5},{2,6},{3,7},{4,0},{5,1},{6,2},{7,3},{8,12},{9,13},{10,... | collective-permute-start | bytes 786440 | tf_op jit(solution)/shard_map/ppermute | solution.py:314
  194.5 7.0 %y_second_2.1 = (f32[64,1024]{1,0:T(8,128)S(1)}, f32[64,1024]{1,0:T(8,128)S(1)}, f32[64,1024]{1,0:T(8,128)S(1)}, f32[64,1024]{1,0:T(8,128)S(1)}) custom-call(bf16[4,256,1024]{2,1,0:T(8,128)(2,1)S(1)} %get-tuple-element.80.matrix_ref, f32[256,1024]{1,0:T(8,128)S(1)} %get-tuple-element.138.refs_0_.refs_4_.refs_16_, ...), custom_call_target="tpu_custom_call" | custom-call | flops 9663676416 | bytes 1048576 | tf_op jit(solution)/shard_map/y_second_2/pallas_call | solution.py:241
  201.6 3.0 %collective-permute-start.38 = (f32[64,1024]{1,0:T(8,128)S(1)}, f32[64,1024]{1,0:T(8,128)S(1)}, u32[]{:S(2)}, u32[]{:S(2)}) collective-permute-start(f32[64,1024]{1,0:T(8,128)S(1)} %get-tuple-element.152), channel_id=1, source_target_pairs={{0,4},{1,5},{2,6},{3,7},{4,0},{5,1},{6,2},{7,3},{8,12},{9,13},{10,... | collective-permute-start | bytes 786440 | tf_op jit(solution)/shard_map/ppermute | solution.py:314
  206.1 5.4 %collective-permute-done.42.refs_2_ = f32[64,1024]{1,0:T(8,128)S(1)} collective-permute-done((f32[64,1024]{1,0:T(8,128)S(1)}, f32[64,1024]{1,0:T(8,128)S(1)}, u32[]{:S(2)}, u32[]{:S(2)}) %collective-permute-start.42) | collective-permute-done | bytes 262176 | tf_op jit(solution)/shard_map/ppermute | solution.py:314
  211.5 18.3 %collective-permute-done.43.refs_3_ = f32[64,1024]{1,0:T(8,128)S(1)} collective-permute-done((f32[64,1024]{1,0:T(8,128)S(1)}, f32[64,1024]{1,0:T(8,128)S(1)}, u32[]{:S(2)}, u32[]{:S(2)}) %collective-permute-start.43) | collective-permute-done | bytes 262176 | tf_op jit(solution)/shard_map/ppermute | solution.py:314
  230.8 3.1 %collective-permute-done.39.refs_2_ = f32[64,1024]{1,0:T(8,128)S(1)} collective-permute-done((f32[64,1024]{1,0:T(8,128)S(1)}, f32[64,1024]{1,0:T(8,128)S(1)}, u32[]{:S(2)}, u32[]{:S(2)}) %collective-permute-start.39) | collective-permute-done | bytes 262176 | tf_op jit(solution)/shard_map/ppermute | solution.py:314
  234.0 6.7 %collective-permute-done.40.refs_3_ = f32[64,1024]{1,0:T(8,128)S(1)} collective-permute-done((f32[64,1024]{1,0:T(8,128)S(1)}, f32[64,1024]{1,0:T(8,128)S(1)}, u32[]{:S(2)}, u32[]{:S(2)}) %collective-permute-start.40) | collective-permute-done | bytes 262176 | tf_op jit(solution)/shard_map/ppermute | solution.py:314
  (95 shorter events, 40.6 us)
Async XLA Ops:
  4.3 37.0 %collective-permute-start.7 = (f32[200,1024]{1,0:T(8,128)}, f32[200,1024]{1,0:T(8,128)}, u32[]{:S(2)}, u32[]{:S(2)}) collective-permute-start(f32[200,1024]{1,0:T(8,128)} %get-tuple-element.83), channel_id=1, source_target_pairs={{0,2},{1,3},{2,0},{3,1},{4,6},{5,7},{6,4},{7,5},{8,10},{9,11},{10,... | collective-permute-start | bytes 2457608 | tf_op jit(solution)/shard_map/ppermute | solution.py:314
  5.9 35.4 %collective-permute-start.1 = (f32[200,1024]{1,0:T(8,128)}, f32[200,1024]{1,0:T(8,128)S(1)}, u32[]{:S(2)}, u32[]{:S(2)}) collective-permute-start(f32[200,1024]{1,0:T(8,128)} %get-tuple-element.83), channel_id=1, source_target_pairs={{0,4},{1,5},{2,6},{3,7},{4,0},{5,1},{6,2},{7,3},{8,12},{9,13},{10,... | collective-permute-start | bytes 2457608 | tf_op jit(solution)/shard_map/ppermute | solution.py:314
  7.4 46.5 %collective-permute-start = (f32[200,1024]{1,0:T(8,128)}, f32[200,1024]{1,0:T(8,128)S(1)}, u32[]{:S(2)}, u32[]{:S(2)}) collective-permute-start(f32[200,1024]{1,0:T(8,128)} %get-tuple-element.81), channel_id=1, source_target_pairs={{0,8},{1,9},{2,10},{3,11},{4,12},{5,13},{6,14},{7,15},{8,0},{9,1},... | collective-permute-start | bytes 2457608 | tf_op jit(solution)/shard_map/ppermute | solution.py:314
  7.8 46.1 %collective-permute-start.2 = (f32[200,1024]{1,0:T(8,128)S(1)}, f32[200,1024]{1,0:T(8,128)S(1)}, u32[]{:S(2)}, u32[]{:S(2)}) collective-permute-start(f32[200,1024]{1,0:T(8,128)S(1)} %get-tuple-element.105.refs_0_.refs_2_.refs_4_.refs_6_.refs_8_.refs_10_.refs_14_.refs_21_.refs_18_.refs_22_.refs_29_), channel_id=1, source_target_pairs={{0,2},{1,3},{2,0},{3,1},{4,6},{5,7},{6,4},{7,5},{8,10},{9,11},{10,... | collective-permute-start | bytes 2457608 | tf_op jit(solution)/shard_map/ppermute | solution.py:314
  41.3 31.8 %collective-permute-start.8 = (f32[200,1024]{1,0:T(8,128)}, f32[200,1024]{1,0:T(8,128)S(1)}, u32[]{:S(2)}, u32[]{:S(2)}) collective-permute-start(f32[200,1024]{1,0:T(8,128)} %collective-permute-done.7), channel_id=1, source_target_pairs={{0,4},{1,5},{2,6},{3,7},{4,0},{5,1},{6,2},{7,3},{8,12},{9,13},{10,... | collective-permute-start | bytes 2457608 | tf_op jit(solution)/shard_map/ppermute | solution.py:314
  43.7 17.2 %collective-permute-start.4 = (f32[136,1024]{1,0:T(8,128)S(1)}, f32[136,1024]{1,0:T(8,128)S(1)}, u32[]{:S(2)}, u32[]{:S(2)}) collective-permute-start(f32[136,1024]{1,0:T(8,128)S(1)} %copy-done.6), channel_id=1, source_target_pairs={{0,12},{1,13},{2,14},{3,15},{4,8},{5,9},{6,10},{7,11},{8,4},{9,5},... | collective-permute-start | bytes 1671176 | tf_op jit(solution)/shard_map/ppermute | solution.py:314
  53.9 19.2 %collective-permute-start.12 = (f32[200,1024]{1,0:T(8,128)S(1)}, f32[200,1024]{1,0:T(8,128)S(1)}, u32[]{:S(2)}, u32[]{:S(2)}) collective-permute-start(f32[200,1024]{1,0:T(8,128)S(1)} %collective-permute-done.refs_0_.refs_1_.refs_2_.refs_3_.refs_12_.refs_16_.refs_29_.refs_8_.refs_20_.refs_24_.refs_37_), channel_id=1, source_target_pairs={{0,2},{1,3},{2,0},{3,1},{4,6},{5,7},{6,4},{7,5},{8,10},{9,11},{10,... | collective-permute-start | bytes 2457608 | tf_op jit(solution)/shard_map/ppermute | solution.py:314
  54.5 19.6 %collective-permute-start.5 = (f32[200,1024]{1,0:T(8,128)S(1)}, f32[200,1024]{1,0:T(8,128)S(1)}, u32[]{:S(2)}, u32[]{:S(2)}) collective-permute-start(f32[200,1024]{1,0:T(8,128)S(1)} %get-tuple-element.105.refs_0_.refs_2_.refs_4_.refs_6_.refs_8_.refs_10_.refs_14_.refs_21_.refs_18_.refs_22_.refs_29_), channel_id=1, source_target_pairs={{0,1},{1,0},{2,3},{3,2},{4,5},{5,4},{6,7},{7,6},{8,9},{9,8},{10,11... | collective-permute-start | bytes 2457608 | tf_op jit(solution)/shard_map/ppermute | solution.py:314
  60.3 14.2 %collective-permute-start.6 = (f32[200,1024]{1,0:T(8,128)S(1)}, f32[200,1024]{1,0:T(8,128)S(1)}, u32[]{:S(2)}, u32[]{:S(2)}) collective-permute-start(f32[200,1024]{1,0:T(8,128)S(1)} %collective-permute-done.1.refs_1_.refs_3_.refs_5_.refs_7_.refs_9_.refs_11_.refs_15_.refs_25_.refs_19_.refs_23_.refs_33_), channel_id=1, source_target_pairs={{0,1},{1,0},{2,3},{3,2},{4,5},{5,4},{6,7},{7,6},{8,9},{9,8},{10,11... | collective-permute-start | bytes 2457608 | tf_op jit(solution)/shard_map/ppermute | solution.py:314
  60.9 13.7 %collective-permute-start.9 = (f32[200,1024]{1,0:T(8,128)S(1)}, f32[200,1024]{1,0:T(8,128)S(1)}, u32[]{:S(2)}, u32[]{:S(2)}) collective-permute-start(f32[200,1024]{1,0:T(8,128)S(1)} %collective-permute-done.2.refs_4_.refs_12_.refs_22_.refs_30_), channel_id=1, source_target_pairs={{0,1},{1,0},{2,3},{3,2},{4,5},{5,4},{6,7},{7,6},{8,9},{9,8},{10,11... | collective-permute-start | bytes 2457608 | tf_op jit(solution)/shard_map/ppermute | solution.py:314
  73.1 14.5 %collective-permute-start.3 = (f32[64,1024]{1,0:T(8,128)S(1)}, f32[64,1024]{1,0:T(8,128)S(1)}, u32[]{:S(2)}, u32[]{:S(2)}) collective-permute-start(f32[64,1024]{1,0:T(8,128)S(1)} %get-tuple-element.88), channel_id=1, source_target_pairs={{0,12},{1,13},{2,14},{3,15},{4,8},{5,9},{6,10},{7,11},{8,4},{9,5},... | collective-permute-start | bytes 786440 | tf_op jit(solution)/shard_map/ppermute | solution.py:314
  74.0 17.5 %collective-permute-start.15 = (f32[136,1024]{1,0:T(8,128)S(1)}, f32[136,1024]{1,0:T(8,128)S(1)}, u32[]{:S(2)}, u32[]{:S(2)}) collective-permute-start(f32[136,1024]{1,0:T(8,128)S(1)} %collective-permute-done.4.refs_0_.refs_1_.refs_2_.refs_13_.refs_17_.refs_33_.refs_9_.refs_21_.refs_25_.refs_41_), channel_id=1, source_target_pairs={{0,2},{1,3},{2,0},{3,1},{4,6},{5,7},{6,4},{7,5},{8,10},{9,11},{10,... | collective-permute-start | bytes 1671176 | tf_op jit(solution)/shard_map/ppermute | solution.py:314
  74.5 9.0 %collective-permute-start.11 = (f32[200,1024]{1,0:T(8,128)S(1)}, f32[200,1024]{1,0:T(8,128)S(1)}, u32[]{:S(2)}, u32[]{:S(2)}) collective-permute-start(f32[200,1024]{1,0:T(8,128)S(1)} %collective-permute-done.refs_0_.refs_1_.refs_2_.refs_3_.refs_12_.refs_16_.refs_29_.refs_8_.refs_20_.refs_24_.refs_37_), channel_id=1, source_target_pairs={{0,1},{1,0},{2,3},{3,2},{4,5},{5,4},{6,7},{7,6},{8,9},{9,8},{10,11... | collective-permute-start | bytes 2457608 | tf_op jit(solution)/shard_map/ppermute | solution.py:314
  74.6 9.0 %collective-permute-start.13 = (f32[200,1024]{1,0:T(8,128)S(1)}, f32[200,1024]{1,0:T(8,128)S(1)}, u32[]{:S(2)}, u32[]{:S(2)}) collective-permute-start(f32[200,1024]{1,0:T(8,128)S(1)} %collective-permute-done.12.refs_4_.refs_30_.refs_12_.refs_38_), channel_id=1, source_target_pairs={{0,1},{1,0},{2,3},{3,2},{4,5},{5,4},{6,7},{7,6},{8,9},{9,8},{10,11... | collective-permute-start | bytes 2457608 | tf_op jit(solution)/shard_map/ppermute | solution.py:314
  83.6 12.8 %collective-permute-start.14 = (f32[136,1024]{1,0:T(8,128)S(1)}, f32[136,1024]{1,0:T(8,128)S(1)}, u32[]{:S(2)}, u32[]{:S(2)}) collective-permute-start(f32[136,1024]{1,0:T(8,128)S(1)} %collective-permute-done.4.refs_0_.refs_1_.refs_2_.refs_13_.refs_17_.refs_33_.refs_9_.refs_21_.refs_25_.refs_41_), channel_id=1, source_target_pairs={{0,1},{1,0},{2,3},{3,2},{4,5},{5,4},{6,7},{7,6},{8,9},{9,8},{10,11... | collective-permute-start | bytes 1671176 | tf_op jit(solution)/shard_map/ppermute | solution.py:314
  92.0 9.8 %collective-permute-start.17 = (f32[64,1024]{1,0:T(8,128)S(1)}, f32[64,1024]{1,0:T(8,128)S(1)}, u32[]{:S(2)}, u32[]{:S(2)}) collective-permute-start(f32[64,1024]{1,0:T(8,128)S(1)} %collective-permute-done.3.refs_0_.refs_1_.refs_21_), channel_id=1, source_target_pairs={{0,2},{1,3},{2,0},{3,1},{4,6},{5,7},{6,4},{7,5},{8,10},{9,11},{10,... | collective-permute-start | bytes 786440 | tf_op jit(solution)/shard_map/ppermute | solution.py:314
  100.8 33.3 %collective-permute-start.21 = (f32[256,1024]{1,0:T(8,128)S(1)}, f32[256,1024]{1,0:T(8,128)S(1)}, u32[]{:S(2)}, u32[]{:S(2)}) collective-permute-start(f32[256,1024]{1,0:T(8,128)S(1)} %get-tuple-element.126.refs_0_.refs_4_.refs_8_.refs_9_.refs_12_.refs_17_), channel_id=1, source_target_pairs={{0,2},{1,3},{2,0},{3,1},{4,6},{5,7},{6,4},{7,5},{8,10},{9,11},{10,... | collective-permute-start | bytes 3145736 | tf_op jit(solution)/shard_map/ppermute | solution.py:314
  111.7 22.4 %collective-permute-start.25 = (f32[256,1024]{1,0:T(8,128)S(1)}, f32[256,1024]{1,0:T(8,128)S(1)}, u32[]{:S(2)}, u32[]{:S(2)}) collective-permute-start(f32[256,1024]{1,0:T(8,128)S(1)} %get-tuple-element.135.refs_1_.refs_0_.refs_4_.refs_16_), channel_id=1, source_target_pairs={{0,1},{1,0},{2,3},{3,2},{4,5},{5,4},{6,7},{7,6},{8,9},{9,8},{10,11... | collective-permute-start | bytes 3145736 | tf_op jit(solution)/shard_map/ppermute | solution.py:314
  111.7 22.4 %collective-permute-start.26 = (f32[256,1024]{1,0:T(8,128)S(1)}, f32[256,1024]{1,0:T(8,128)S(1)}, u32[]{:S(2)}, u32[]{:S(2)}) collective-permute-start(f32[256,1024]{1,0:T(8,128)S(1)} %get-tuple-element.126.refs_0_.refs_4_.refs_8_.refs_9_.refs_12_.refs_17_), channel_id=1, source_target_pairs={{0,1},{1,0},{2,3},{3,2},{4,5},{5,4},{6,7},{7,6},{8,9},{9,8},{10,11... | collective-permute-start | bytes 3145736 | tf_op jit(solution)/shard_map/ppermute | solution.py:314
  112.2 21.9 %collective-permute-start.20 = (f32[256,1024]{1,0:T(8,128)S(1)}, f32[256,1024]{1,0:T(8,128)S(1)}, u32[]{:S(2)}, u32[]{:S(2)}) collective-permute-start(f32[256,1024]{1,0:T(8,128)S(1)} %get-tuple-element.138.refs_0_.refs_4_.refs_16_), channel_id=1, source_target_pairs={{0,1},{1,0},{2,3},{3,2},{4,5},{5,4},{6,7},{7,6},{8,9},{9,8},{10,11... | collective-permute-start | bytes 3145736 | tf_op jit(solution)/shard_map/ppermute | solution.py:314
  136.4 25.6 %collective-permute-start.27 = (f32[256,1024]{1,0:T(8,128)S(1)}, f32[256,1024]{1,0:T(8,128)S(1)}, u32[]{:S(2)}, u32[]{:S(2)}) collective-permute-start(f32[256,1024]{1,0:T(8,128)S(1)} %get-tuple-element.135.refs_1_.refs_0_.refs_4_.refs_16_), channel_id=1, source_target_pairs={{0,2},{1,3},{2,0},{3,1},{4,6},{5,7},{6,4},{7,5},{8,10},{9,11},{10,... | collective-permute-start | bytes 3145736 | tf_op jit(solution)/shard_map/ppermute | solution.py:314
  161.9 12.1 %collective-permute-start.36 = (f32[256,1024]{1,0:T(8,128)S(1)}, f32[256,1024]{1,0:T(8,128)S(1)}, u32[]{:S(2)}, u32[]{:S(2)}) collective-permute-start(f32[256,1024]{1,0:T(8,128)S(1)} %collective-permute-done.27.refs_2_.refs_6_), channel_id=1, source_target_pairs={{0,1},{1,0},{2,3},{3,2},{4,5},{5,4},{6,7},{7,6},{8,9},{9,8},{10,11... | collective-permute-start | bytes 3145736 | tf_op jit(solution)/shard_map/ppermute | solution.py:314
  161.9 19.2 %collective-permute-start.33 = (f32[64,1024]{1,0:T(8,128)S(1)}, f32[64,1024]{1,0:T(8,128)S(1)}, u32[]{:S(2)}, u32[]{:S(2)}) collective-permute-start(f32[64,1024]{1,0:T(8,128)S(1)} %get-tuple-element.132), channel_id=1, source_target_pairs={{0,4},{1,5},{2,6},{3,7},{4,0},{5,1},{6,2},{7,3},{8,12},{9,13},{10,... | collective-permute-start | bytes 786440 | tf_op jit(solution)/shard_map/ppermute | solution.py:314
  164.0 18.4 %collective-permute-start.34 = (f32[64,1024]{1,0:T(8,128)S(1)}, f32[64,1024]{1,0:T(8,128)S(1)}, u32[]{:S(2)}, u32[]{:S(2)}) collective-permute-start(f32[64,1024]{1,0:T(8,128)S(1)} %get-tuple-element.133), channel_id=1, source_target_pairs={{0,8},{1,9},{2,10},{3,11},{4,12},{5,13},{6,14},{7,15},{8,0},{9,1},... | collective-permute-start | bytes 786440 | tf_op jit(solution)/shard_map/ppermute | solution.py:314
  164.4 24.6 %collective-permute-start.35 = (f32[64,1024]{1,0:T(8,128)S(1)}, f32[64,1024]{1,0:T(8,128)S(1)}, u32[]{:S(2)}, u32[]{:S(2)}) collective-permute-start(f32[64,1024]{1,0:T(8,128)S(1)} %get-tuple-element.134), channel_id=1, source_target_pairs={{0,12},{1,13},{2,14},{3,15},{4,8},{5,9},{6,10},{7,11},{8,4},{9,5},... | collective-permute-start | bytes 786440 | tf_op jit(solution)/shard_map/ppermute | solution.py:314
  165.4 25.0 %collective-permute-start.32 = (f32[256,1024]{1,0:T(8,128)S(1)}, f32[256,1024]{1,0:T(8,128)S(1)}, u32[]{:S(2)}, u32[]{:S(2)}) collective-permute-start(f32[256,1024]{1,0:T(8,128)S(1)} %get-tuple-element.138.refs_0_.refs_4_.refs_16_), channel_id=1, source_target_pairs={{0,2},{1,3},{2,0},{3,1},{4,6},{5,7},{6,4},{7,5},{8,10},{9,11},{10,... | collective-permute-start | bytes 3145736 | tf_op jit(solution)/shard_map/ppermute | solution.py:314
  190.4 14.7 %collective-permute-start.41 = (f32[64,1024]{1,0:T(8,128)S(1)}, f32[64,1024]{1,0:T(8,128)S(1)}, u32[]{:S(2)}, u32[]{:S(2)}) collective-permute-start(f32[64,1024]{1,0:T(8,128)S(1)} %get-tuple-element.142), channel_id=1, source_target_pairs={{0,4},{1,5},{2,6},{3,7},{4,0},{5,1},{6,2},{7,3},{8,12},{9,13},{10,... | collective-permute-start | bytes 786440 | tf_op jit(solution)/shard_map/ppermute | solution.py:314
  193.1 18.4 %collective-permute-start.42 = (f32[64,1024]{1,0:T(8,128)S(1)}, f32[64,1024]{1,0:T(8,128)S(1)}, u32[]{:S(2)}, u32[]{:S(2)}) collective-permute-start(f32[64,1024]{1,0:T(8,128)S(1)} %get-tuple-element.143), channel_id=1, source_target_pairs={{0,8},{1,9},{2,10},{3,11},{4,12},{5,13},{6,14},{7,15},{8,0},{9,1},... | collective-permute-start | bytes 786440 | tf_op jit(solution)/shard_map/ppermute | solution.py:314
  193.6 36.2 %collective-permute-start.43 = (f32[64,1024]{1,0:T(8,128)S(1)}, f32[64,1024]{1,0:T(8,128)S(1)}, u32[]{:S(2)}, u32[]{:S(2)}) collective-permute-start(f32[64,1024]{1,0:T(8,128)S(1)} %get-tuple-element.144), channel_id=1, source_target_pairs={{0,12},{1,13},{2,14},{3,15},{4,8},{5,9},{6,10},{7,11},{8,4},{9,5},... | collective-permute-start | bytes 786440 | tf_op jit(solution)/shard_map/ppermute | solution.py:314
  201.6 29.3 %collective-permute-start.38 = (f32[64,1024]{1,0:T(8,128)S(1)}, f32[64,1024]{1,0:T(8,128)S(1)}, u32[]{:S(2)}, u32[]{:S(2)}) collective-permute-start(f32[64,1024]{1,0:T(8,128)S(1)} %get-tuple-element.152), channel_id=1, source_target_pairs={{0,4},{1,5},{2,6},{3,7},{4,0},{5,1},{6,2},{7,3},{8,12},{9,13},{10,... | collective-permute-start | bytes 786440 | tf_op jit(solution)/shard_map/ppermute | solution.py:314
  204.6 29.4 %collective-permute-start.39 = (f32[64,1024]{1,0:T(8,128)S(1)}, f32[64,1024]{1,0:T(8,128)S(1)}, u32[]{:S(2)}, u32[]{:S(2)}) collective-permute-start(f32[64,1024]{1,0:T(8,128)S(1)} %get-tuple-element.153), channel_id=1, source_target_pairs={{0,8},{1,9},{2,10},{3,11},{4,12},{5,13},{6,14},{7,15},{8,0},{9,1},... | collective-permute-start | bytes 786440 | tf_op jit(solution)/shard_map/ppermute | solution.py:314
  205.1 35.5 %collective-permute-start.40 = (f32[64,1024]{1,0:T(8,128)S(1)}, f32[64,1024]{1,0:T(8,128)S(1)}, u32[]{:S(2)}, u32[]{:S(2)}) collective-permute-start(f32[64,1024]{1,0:T(8,128)S(1)} %get-tuple-element.154), channel_id=1, source_target_pairs={{0,12},{1,13},{2,14},{3,15},{4,8},{5,9},{6,10},{7,11},{8,4},{9,5},... | collective-permute-start | bytes 786440 | tf_op jit(solution)/shard_map/ppermute | solution.py:314
  (19 other events, 108.3 us)

commit v10 on v9

--- a/solution.py
+++ b/solution.py
@@ -428,12 +428,12 @@
 
     total = fold(square, "fold_own")
     total = [total] + [swap(total, d * group) for d in range(1, planes)]
-    total = fold(total, "fold_planes")
+    x_terms = [None] * 3
+    x_terms[1] = along_x([piece(after(middle[1], total[0]))], [piece(middle[0])], along_x_matrix, "x_second_1")
+    total = fold(after(total, x_terms[1]), "fold_planes")
     for i in range(3):
-        middle_twin[i] = across_cores([after(middle[i], square[2])])
-    x_terms = [None] * 3
-    x_terms[1] = along_x([piece(after(middle[1], total))], [piece(middle[0])], along_x_matrix, "x_second_1", 36)
-    middle_others[1] = after(middle_others[1], x_terms[1], middle_twin)
+        middle_twin[i] = across_cores([after(middle[i], total)])
+    middle_others[1] = after(middle_others[1], total)
     totals = [total] + [swap(after(total, middle_others[1]), m) for m in range(1, group)]
     middle_others[0] = across_chips(after(middle[0], middle_others[1]))
     totals = [piece(x) for x in totals]
@@ -448,7 +448,7 @@
         return y_call(
             functools.partial(second_kernel, cells), along_y_matrix, 0,
             [middle_pieces(i), middle_pieces(1) if i != 1 else [], [], [piece(middle[i])], [piece(middle[1])],
-             [piece(x_terms[i])], [piece(base[i])]], [size] * planes, f"y_second_{i}", totals, {0: 36, 1: 36, 2: 36}[i],
+             [piece(x_terms[i])], [piece(base[i])]], [size] * planes, f"y_second_{i}", totals, {0: 1, 1: 36, 2: 1}[i],
         )
 
     ends = [None] * 3
@@ -457,24 +457,23 @@
         ends[i] = [swap(block, d * group) if d else block for d, block in enumerate(ends[i])]
 
     ends[1] = second_step(1)
-    x_terms[0] = along_x([piece(after(middle[0], ends[1]))], [], along_x_matrix, "x_second_0", 36)
+    x_terms[0] = along_x([piece(after(middle[0], ends[1]))], [], along_x_matrix, "x_second_0", 1)
     leave(1)
-    middle_others[0] = after(middle_others[0], x_terms[0])
+    x_terms[2] = along_x(
+        [piece(after(middle[2], x_terms[0]))], [piece(middle[0])], along_x_matrix, "x_second_2", 1
+    )
+    ends[1] = after(ends[1], x_terms[2])
+    out = place_blocks(plane, ends, (1,), velocity.shape, None)
+    middle_others[0] = after(middle_others[0], out)
     middle_others[2] = across_chips(after(middle[2], middle_others[0]))
     middle_far[0] = across_cores(middle_others[0])
-    x_terms[2] = along_x(
-        [piece(after(middle[2], x_terms[0]))], [piece(middle[0])], along_x_matrix, "x_second_2", 36
-    )
-    middle_far[0] = after(middle_far[0], x_terms[2])
     ends[0] = second_step(0)
-    ends[1] = after(ends[1], ends[0])
-    out = place_blocks(plane, ends, (1,), velocity.shape, None)
     leave(0)
+    out = place_blocks(plane, ends, (0,), velocity.shape, out)
     middle_others[2] = after(middle_others[2], out)
     middle_far[2] = across_cores(middle_others[2])
     ends[2] = second_step(2)
     leave(2)
-    out = place_blocks(plane, ends, (0,), velocity.shape, out)
     return place_blocks(plane, ends, (2,), velocity.shape, out)
 
 

time: 242 us -> 241 us (level)
  starting transfers between devices: 39.7 us -> 35 us
  waiting for transfers between devices: 92 us -> 94.9 us
    ppermute x44, starting transfers between devices: 39.7 us -> 35 us  [swap(): return lax.ppermute(x, 'row', [(r, r ^ distance) for r in range(devices)])]
    ppermute x44, waiting for transfers between devices: 92 us -> 94.9 us  [swap(): return lax.ppermute(x, 'row', [(r, r ^ distance) for r in range(devices)])]
  transfers between devices with their start and end apart: 44 -> 44, of which waited for: 15 -> 16; matrix products, arithmetic and copies ran while one was open for 0% -> 0% of each run, Pallas kernels for 41% -> 39%
where the time goes in v10:
time: 241 us; the launch traced here: 240 us
  Pallas kernels  102 us (42%)
  waiting for transfers between devices  94.9 us (39%)
  starting transfers between devices  35 us (15%)
  local copies, waits for them, and re-layouts  7.18 us (3%)
    ppermute x44, waiting for transfers between devices, swap(): return lax.ppermute(x, 'row', [(r, r ^ distance) for r in range(devices)])  94.9 us
    pallas_call x9, Pallas kernels, y_call(): pl.pallas_call(functools.partial(kernel, tuple(counts)), grid=(length //...  45.7 us
    pallas_call x7, Pallas kernels, along_x(): pl.pallas_call(functools.partial(along_x_kernel, (len(fields), len(carrie...  44.7 us
    ppermute x44, starting transfers between devices, swap(): return lax.ppermute(x, 'row', [(r, r ^ distance) for r in range(devices)])  35 us
    pallas_call x1, Pallas kernels, prepare_matrices(): pl.pallas_call(functools.partial(matrices_kernel, count), grid_spec=pltpu...  7.16 us
    unnamed x14, local copies, waits for them, and re-layouts  7.09 us
  transfers between devices with their start and end apart: 44, of which 16 were waited for; matrix products, arithmetic and copies ran while one was open for 0% of the time, Pallas kernels for 39%

profile of v10, /device:TPU:18, one launch (start us, length us, event | category | flops | bytes accessed | tf_op | source)
XLA Modules:
  0.0 239.8 jit_solution(611229222000904884)
XLA Ops:
  12.8 7.2 %shard_map.37 = (bf16[4,1024,1024]{2,1,0:T(8,128)(2,1)S(1)}, bf16[4,256,1024]{2,1,0:T(8,128)(2,1)S(1)}) custom-call(s32[16]{0:T(128)S(1)} %stack.74.order_ref, s32[4]{0:T(128)S(1)} %pad_add_fusion.own_ref, f32[1024,1024]{1,0:T(8,128)S(1)} %copy-done.3, f32[1024,1024]{1,0:T(8,128)S(1)} %copy-done.3, f32[1024,1024]{1,0:T(8,128)S(1)} %copy-done.4, ...), custom_call_target="tpu_custom_call" | custom-call | flops 17179869184 | bytes 33554432 | tf_op jit(solution)/shard_map/pallas_call | solution.py:63
  20.0 21.3 %collective-permute-done.1.refs_1_.refs_3_.refs_5_.refs_7_.refs_9_.refs_11_.refs_15_.refs_25_.refs_19_.refs_23_.refs_33_ = f32[200,1024]{1,0:T(8,128)S(1)} collective-permute-done((f32[200,1024]{1,0:T(8,128)}, f32[200,1024]{1,0:T(8,128)S(1)}, u32[]{:S(2)}, u32[]{:S(2)}) %collective-permute-start.1) | collective-permute-done | bytes 819232 | tf_op jit(solution)/shard_map/ppermute | solution.py:314
  44.1 9.8 %x_first_near.1.refs_18_.refs_26_ = f32[384,1024]{1,0:T(8,128)S(1)} custom-call(f32[200,1024]{1,0:T(8,128)S(1)} %get-tuple-element.108.refs_0_.refs_2_.refs_4_.refs_6_.refs_8_.refs_10_.refs_14_.refs_21_.refs_18_.refs_22_.refs_29_, ...), custom_call_target="tpu_custom_call" | custom-call | flops 402653184 | bytes 1572864 | tf_op jit(solution)/shard_map/x_first_near/pallas_call | solution.py:163
  54.5 5.8 %x_first_2.1.refs_19_.refs_27_ = f32[192,1024]{1,0:T(8,128)S(1)} custom-call(f32[200,1024]{1,0:T(8,128)S(1)} %collective-permute-done.refs_0_.refs_1_.refs_2_.refs_3_.refs_12_.refs_16_.refs_29_.refs_8_.refs_20_.refs_24_.refs_37_, ...), custom_call_target="tpu_custom_call" | custom-call | flops 201326592 | bytes 786432 | tf_op jit(solution)/shard_map/x_first_2/pallas_call | solution.py:163
  61.0 12.2 %collective-permute-done.8.refs_5_.refs_13_.refs_26_.refs_34_ = f32[200,1024]{1,0:T(8,128)S(1)} collective-permute-done((f32[200,1024]{1,0:T(8,128)}, f32[200,1024]{1,0:T(8,128)S(1)}, u32[]{:S(2)}, u32[]{:S(2)}) %collective-permute-start.8) | collective-permute-done | bytes 819232 | tf_op jit(solution)/shard_map/ppermute | solution.py:314
  75.5 3.6 %y_first_near_1.1 = (f32[256,1024]{1,0:T(8,128)S(1)}, f32[256,1024]{1,0:T(8,128)S(1)}) custom-call(bf16[4,256,1024]{2,1,0:T(8,128)(2,1)S(1)} %get-tuple-element.83.matrix_ref, f32[200,1024]{1,0:T(8,128)S(1)} %get-tuple-element.108.refs_0_.refs_2_.refs_4_.refs_6_.refs_8_.refs_10_.refs_14_.refs_21_.refs_18_.refs_22_.refs_29_, ...), custom_call_target="tpu_custom_call" | custom-call | flops 4831838208 | bytes 1048576 | tf_op jit(solution)/shard_map/y_first_near_1/pallas_call | solution.py:241
  79.1 4.5 %x_first_last.1.refs_20_.refs_28_ = f32[128,1024]{1,0:T(8,128)S(1)} custom-call(f32[136,1024]{1,0:T(8,128)S(1)} %collective-permute-done.4.refs_0_.refs_1_.refs_2_.refs_13_.refs_17_.refs_33_.refs_9_.refs_21_.refs_25_.refs_41_, f32[136,1024]{1,0:T(8,128)S(1)} %collective-permute-done.4.refs_0_.refs_1_.refs_2_.refs_13_.refs_17_.refs_33_.refs_9_.refs_21_.refs_25_.refs_41_, ...), custom_call_target="tpu_custom_call" | custom-call | flops 4831838208 | bytes 524288 | tf_op jit(solution)/shard_map/x_first_last/pallas_call | solution.py:163
  83.8 3.9 %y_first_near_0.1 = (f32[256,1024]{1,0:T(8,128)S(1)}, f32[256,1024]{1,0:T(8,128)S(1)}) custom-call(bf16[4,256,1024]{2,1,0:T(8,128)(2,1)S(1)} %get-tuple-element.83.matrix_ref, f32[200,1024]{1,0:T(8,128)S(1)} %get-tuple-element.108.refs_0_.refs_2_.refs_4_.refs_6_.refs_8_.refs_10_.refs_14_.refs_21_.refs_18_.refs_22_.refs_29_, ...), custom_call_target="tpu_custom_call" | custom-call | flops 4831838208 | bytes 1048576 | tf_op jit(solution)/shard_map/y_first_near_0/pallas_call | solution.py:241
  87.6 3.9 %y_first_near_2.1 = (f32[256,1024]{1,0:T(8,128)S(1)}, f32[256,1024]{1,0:T(8,128)S(1)}) custom-call(bf16[4,256,1024]{2,1,0:T(8,128)(2,1)S(1)} %get-tuple-element.83.matrix_ref, f32[200,1024]{1,0:T(8,128)S(1)} %get-tuple-element.108.refs_0_.refs_2_.refs_4_.refs_6_.refs_8_.refs_10_.refs_14_.refs_21_.refs_18_.refs_22_.refs_29_, ...), custom_call_target="tpu_custom_call" | custom-call | flops 4831838208 | bytes 1048576 | tf_op jit(solution)/shard_map/y_first_near_2/pallas_call | solution.py:241
  93.1 3.3 %x_first_tail.1.refs_28_ = f32[64,1024]{1,0:T(8,128)S(1)} custom-call(f32[64,1024]{1,0:T(8,128)S(1)} %collective-permute-done.3.refs_0_.refs_1_.refs_21_, f32[136,1024]{1,0:T(8,128)S(1)} %collective-permute-done.4.refs_0_.refs_1_.refs_2_.refs_13_.refs_17_.refs_33_.refs_9_.refs_21_.refs_25_.refs_41_, ...), custom_call_target="tpu_custom_call" | custom-call | flops 2415919104 | bytes 262144 | tf_op jit(solution)/shard_map/x_first_tail/pallas_call | solution.py:163
  96.4 4.4 %y_first_far_1.1 = (f32[256,1024]{1,0:T(8,128)S(1)}, f32[256,1024]{1,0:T(8,128)S(1)}, f32[8,1024]{1,0:T(8,128)S(1)}) custom-call(bf16[4,256,1024]{2,1,0:T(8,128)(2,1)S(1)} %get-tuple-element.83.matrix_ref, f32[200,1024]{1,0:T(8,128)S(1)} %collective-permute-done.refs_0_.refs_1_.refs_2_.refs_3_.refs_12_.refs_16_.refs_29_.refs_8_.refs_20_.refs_24_.refs_37_, ...), custom_call_target="tpu_custom_call" | custom-call | flops 4831838208 | bytes 1048576 | tf_op jit(solution)/shard_map/y_first_far_1/pallas_call | solution.py:241
  102.3 4.6 %y_first_far_0.1 = (f32[256,1024]{1,0:T(8,128)S(1)}, f32[256,1024]{1,0:T(8,128)S(1)}, f32[8,1024]{1,0:T(8,128)S(1)}) custom-call(bf16[4,256,1024]{2,1,0:T(8,128)(2,1)S(1)} %get-tuple-element.83.matrix_ref, f32[200,1024]{1,0:T(8,128)S(1)} %collective-permute-done.refs_0_.refs_1_.refs_2_.refs_3_.refs_12_.refs_16_.refs_29_.refs_8_.refs_20_.refs_24_.refs_37_, ...), custom_call_target="tpu_custom_call" | custom-call | flops 4831838208 | bytes 1048576 | tf_op jit(solution)/shard_map/y_first_far_0/pallas_call | solution.py:241
  106.9 4.7 %y_first_far_2.1 = (f32[256,1024]{1,0:T(8,128)S(1)}, f32[256,1024]{1,0:T(8,128)S(1)}, f32[8,1024]{1,0:T(8,128)S(1)}) custom-call(bf16[4,256,1024]{2,1,0:T(8,128)(2,1)S(1)} %get-tuple-element.83.matrix_ref, f32[200,1024]{1,0:T(8,128)S(1)} %collective-permute-done.refs_0_.refs_1_.refs_2_.refs_3_.refs_12_.refs_16_.refs_29_.refs_8_.refs_20_.refs_24_.refs_37_, ...), custom_call_target="tpu_custom_call" | custom-call | flops 4831838208 | bytes 1048576 | tf_op jit(solution)/shard_map/y_first_far_2/pallas_call | solution.py:241
  112.5 4.7 %collective-permute-start.21 = (f32[8,128]{1,0:T(8,128)S(1)}, f32[8,128]{1,0:T(8,128)S(1)}, u32[]{:S(2)}, u32[]{:S(2)}) collective-permute-start(f32[8,128]{1,0:T(8,128)S(1)} %fold_own.1.refs_0_), channel_id=1, source_target_pairs={{0,8},{1,9},{2,10},{3,11},{4,12},{5,13},{6,14},{7,15},{8,0},{9,1},... | collective-permute-start | bytes 12296 | tf_op jit(solution)/shard_map/ppermute | solution.py:314
  117.2 7.1 %x_second_1.1.refs_10_ = f32[256,1024]{1,0:T(8,128)S(1)} custom-call(f32[256,1024]{1,0:T(8,128)S(1)} %get-tuple-element.134.refs_0_.refs_4_.refs_8_.refs_9_.refs_12_.refs_17_, f32[256,1024]{1,0:T(8,128)S(1)} %get-tuple-element.149.refs_1_.refs_0_.refs_4_.refs_16_, bf16[4,1024,1024]{2,1,0:T(8,128)(2,1)S(1)} %get-tuple-element.87.refs_8_.refs_4_.refs_3_.refs_2_.refs_1_), custom_call_target="tpu_custom_call" | custom-call | flops 9663676416 | bytes 1048576 | tf_op jit(solution)/shard_map/x_second_1/pallas_call | solution.py:163
  130.5 6.6 %y_second_1.1 = (f32[64,1024]{1,0:T(8,128)S(1)}, f32[64,1024]{1,0:T(8,128)S(1)}, f32[64,1024]{1,0:T(8,128)S(1)}, f32[64,1024]{1,0:T(8,128)S(1)}) custom-call(bf16[4,256,1024]{2,1,0:T(8,128)(2,1)S(1)} %get-tuple-element.83.matrix_ref, f32[256,1024]{1,0:T(8,128)S(1)} %get-tuple-element.134.refs_0_.refs_4_.refs_8_.refs_9_.refs_12_.refs_17_, ...), custom_call_target="tpu_custom_call" | custom-call | flops 9663676416 | bytes 1048576 | tf_op jit(solution)/shard_map/y_second_1/pallas_call | solution.py:241
  137.1 3.0 %collective-permute-start.31 = (f32[64,1024]{1,0:T(8,128)S(1)}, f32[64,1024]{1,0:T(8,128)S(1)}, u32[]{:S(2)}, u32[]{:S(2)}) collective-permute-start(f32[64,1024]{1,0:T(8,128)S(1)} %get-tuple-element.138), channel_id=1, source_target_pairs={{0,4},{1,5},{2,6},{3,7},{4,0},{5,1},{6,2},{7,3},{8,12},{9,13},{10,... | collective-permute-start | bytes 786440 | tf_op jit(solution)/shard_map/ppermute | solution.py:314
  141.7 7.1 %x_second_0.1.refs_18_ = f32[256,1024]{1,0:T(8,128)S(1)} custom-call(f32[256,1024]{1,0:T(8,128)S(1)} %get-tuple-element.149.refs_1_.refs_0_.refs_4_.refs_16_, bf16[4,1024,1024]{2,1,0:T(8,128)(2,1)S(1)} %get-tuple-element.87.refs_8_.refs_4_.refs_3_.refs_2_.refs_1_), custom_call_target="tpu_custom_call" | custom-call | flops 268435456 | bytes 1048576 | tf_op jit(solution)/shard_map/x_second_0/pallas_call | solution.py:163
  148.8 7.1 %x_second_2.1.refs_18_ = f32[256,1024]{1,0:T(8,128)S(1)} custom-call(f32[256,1024]{1,0:T(8,128)S(1)} %get-tuple-element.148.refs_0_.refs_4_.refs_16_, f32[256,1024]{1,0:T(8,128)S(1)} %get-tuple-element.149.refs_1_.refs_0_.refs_4_.refs_16_, bf16[4,1024,1024]{2,1,0:T(8,128)(2,1)S(1)} %get-tuple-element.87.refs_8_.refs_4_.refs_3_.refs_2_.refs_1_), custom_call_target="tpu_custom_call" | custom-call | flops 268435456 | bytes 1048576 | tf_op jit(solution)/shard_map/x_second_2/pallas_call | solution.py:163
  156.0 2.7 %collective-permute-done.32.refs_2_ = f32[64,1024]{1,0:T(8,128)S(1)} collective-permute-done((f32[64,1024]{1,0:T(8,128)S(1)}, f32[64,1024]{1,0:T(8,128)S(1)}, u32[]{:S(2)}, u32[]{:S(2)}) %collective-permute-start.32) | collective-permute-done | bytes 262176 | tf_op jit(solution)/shard_map/ppermute | solution.py:314
  158.7 5.6 %collective-permute-done.33.refs_3_ = f32[64,1024]{1,0:T(8,128)S(1)} collective-permute-done((f32[64,1024]{1,0:T(8,128)S(1)}, f32[64,1024]{1,0:T(8,128)S(1)}, u32[]{:S(2)}, u32[]{:S(2)}) %collective-permute-start.33) | collective-permute-done | bytes 262176 | tf_op jit(solution)/shard_map/ppermute | solution.py:314
  168.0 7.0 %y_second_0.1 = (f32[64,1024]{1,0:T(8,128)S(1)}, f32[64,1024]{1,0:T(8,128)S(1)}, f32[64,1024]{1,0:T(8,128)S(1)}, f32[64,1024]{1,0:T(8,128)S(1)}) custom-call(bf16[4,256,1024]{2,1,0:T(8,128)(2,1)S(1)} %get-tuple-element.83.matrix_ref, f32[256,1024]{1,0:T(8,128)S(1)} %get-tuple-element.149.refs_1_.refs_0_.refs_4_.refs_16_, ...), custom_call_target="tpu_custom_call" | custom-call | flops 268435456 | bytes 1048576 | tf_op jit(solution)/shard_map/y_second_0/pallas_call | solution.py:241
  175.1 2.5 %collective-permute-start.38 = (f32[64,1024]{1,0:T(8,128)S(1)}, f32[64,1024]{1,0:T(8,128)S(1)}, u32[]{:S(2)}, u32[]{:S(2)}) collective-permute-start(f32[64,1024]{1,0:T(8,128)S(1)} %get-tuple-element.153), channel_id=1, source_target_pairs={{0,8},{1,9},{2,10},{3,11},{4,12},{5,13},{6,14},{7,15},{8,0},{9,1},... | collective-permute-start | bytes 786440 | tf_op jit(solution)/shard_map/ppermute | solution.py:314
  178.6 7.4 %collective-permute-done.37.refs_1_ = f32[64,1024]{1,0:T(8,128)S(1)} collective-permute-done((f32[64,1024]{1,0:T(8,128)S(1)}, f32[64,1024]{1,0:T(8,128)S(1)}, u32[]{:S(2)}, u32[]{:S(2)}) %collective-permute-start.37) | collective-permute-done | bytes 262176 | tf_op jit(solution)/shard_map/ppermute | solution.py:314
  186.0 9.6 %collective-permute-done.38.refs_2_ = f32[64,1024]{1,0:T(8,128)S(1)} collective-permute-done((f32[64,1024]{1,0:T(8,128)S(1)}, f32[64,1024]{1,0:T(8,128)S(1)}, u32[]{:S(2)}, u32[]{:S(2)}) %collective-permute-start.38) | collective-permute-done | bytes 262176 | tf_op jit(solution)/shard_map/ppermute | solution.py:314
  195.6 5.9 %collective-permute-done.39.refs_3_ = f32[64,1024]{1,0:T(8,128)S(1)} collective-permute-done((f32[64,1024]{1,0:T(8,128)S(1)}, f32[64,1024]{1,0:T(8,128)S(1)}, u32[]{:S(2)}, u32[]{:S(2)}) %collective-permute-start.39) | collective-permute-done | bytes 262176 | tf_op jit(solution)/shard_map/ppermute | solution.py:314
  202.6 2.7 %collective-permute-done.40.refs_3_.refs_7_ = f32[256,1024]{1,0:T(8,128)S(1)} collective-permute-done((f32[256,1024]{1,0:T(8,128)S(1)}, f32[256,1024]{1,0:T(8,128)S(1)}, u32[]{:S(2)}, u32[]{:S(2)}) %collective-permute-start.40) | collective-permute-done | bytes 1048608 | tf_op jit(solution)/shard_map/ppermute | solution.py:314
  205.3 7.0 %y_second_2.1 = (f32[64,1024]{1,0:T(8,128)S(1)}, f32[64,1024]{1,0:T(8,128)S(1)}, f32[64,1024]{1,0:T(8,128)S(1)}, f32[64,1024]{1,0:T(8,128)S(1)}) custom-call(bf16[4,256,1024]{2,1,0:T(8,128)(2,1)S(1)} %get-tuple-element.83.matrix_ref, f32[256,1024]{1,0:T(8,128)S(1)} %get-tuple-element.148.refs_0_.refs_4_.refs_16_, ...), custom_call_target="tpu_custom_call" | custom-call | flops 268435456 | bytes 1048576 | tf_op jit(solution)/shard_map/y_second_2/pallas_call | solution.py:241
  212.4 2.5 %collective-permute-start.42 = (f32[64,1024]{1,0:T(8,128)S(1)}, f32[64,1024]{1,0:T(8,128)S(1)}, u32[]{:S(2)}, u32[]{:S(2)}) collective-permute-start(f32[64,1024]{1,0:T(8,128)S(1)} %get-tuple-element.159), channel_id=1, source_target_pairs={{0,8},{1,9},{2,10},{3,11},{4,12},{5,13},{6,14},{7,15},{8,0},{9,1},... | collective-permute-start | bytes 786440 | tf_op jit(solution)/shard_map/ppermute | solution.py:314
  215.9 7.4 %collective-permute-done.41.refs_1_ = f32[64,1024]{1,0:T(8,128)S(1)} collective-permute-done((f32[64,1024]{1,0:T(8,128)S(1)}, f32[64,1024]{1,0:T(8,128)S(1)}, u32[]{:S(2)}, u32[]{:S(2)}) %collective-permute-start.41) | collective-permute-done | bytes 262176 | tf_op jit(solution)/shard_map/ppermute | solution.py:314
  223.3 9.6 %collective-permute-done.42.refs_2_ = f32[64,1024]{1,0:T(8,128)S(1)} collective-permute-done((f32[64,1024]{1,0:T(8,128)S(1)}, f32[64,1024]{1,0:T(8,128)S(1)}, u32[]{:S(2)}, u32[]{:S(2)}) %collective-permute-start.42) | collective-permute-done | bytes 262176 | tf_op jit(solution)/shard_map/ppermute | solution.py:314
  232.9 5.9 %collective-permute-done.43.refs_3_ = f32[64,1024]{1,0:T(8,128)S(1)} collective-permute-done((f32[64,1024]{1,0:T(8,128)S(1)}, f32[64,1024]{1,0:T(8,128)S(1)}, u32[]{:S(2)}, u32[]{:S(2)}) %collective-permute-start.43) | collective-permute-done | bytes 262176 | tf_op jit(solution)/shard_map/ppermute | solution.py:314
  (95 shorter events, 38.8 us)
Async XLA Ops:
  4.3 37.0 %collective-permute-start.7 = (f32[200,1024]{1,0:T(8,128)}, f32[200,1024]{1,0:T(8,128)}, u32[]{:S(2)}, u32[]{:S(2)}) collective-permute-start(f32[200,1024]{1,0:T(8,128)} %get-tuple-element.86), channel_id=1, source_target_pairs={{0,2},{1,3},{2,0},{3,1},{4,6},{5,7},{6,4},{7,5},{8,10},{9,11},{10,... | collective-permute-start | bytes 2457608 | tf_op jit(solution)/shard_map/ppermute | solution.py:314
  5.9 35.4 %collective-permute-start.1 = (f32[200,1024]{1,0:T(8,128)}, f32[200,1024]{1,0:T(8,128)S(1)}, u32[]{:S(2)}, u32[]{:S(2)}) collective-permute-start(f32[200,1024]{1,0:T(8,128)} %get-tuple-element.86), channel_id=1, source_target_pairs={{0,4},{1,5},{2,6},{3,7},{4,0},{5,1},{6,2},{7,3},{8,12},{9,13},{10,... | collective-permute-start | bytes 2457608 | tf_op jit(solution)/shard_map/ppermute | solution.py:314
  7.4 46.5 %collective-permute-start = (f32[200,1024]{1,0:T(8,128)}, f32[200,1024]{1,0:T(8,128)S(1)}, u32[]{:S(2)}, u32[]{:S(2)}) collective-permute-start(f32[200,1024]{1,0:T(8,128)} %get-tuple-element.84), channel_id=1, source_target_pairs={{0,8},{1,9},{2,10},{3,11},{4,12},{5,13},{6,14},{7,15},{8,0},{9,1},... | collective-permute-start | bytes 2457608 | tf_op jit(solution)/shard_map/ppermute | solution.py:314
  7.8 46.1 %collective-permute-start.2 = (f32[200,1024]{1,0:T(8,128)S(1)}, f32[200,1024]{1,0:T(8,128)S(1)}, u32[]{:S(2)}, u32[]{:S(2)}) collective-permute-start(f32[200,1024]{1,0:T(8,128)S(1)} %get-tuple-element.108.refs_0_.refs_2_.refs_4_.refs_6_.refs_8_.refs_10_.refs_14_.refs_21_.refs_18_.refs_22_.refs_29_), channel_id=1, source_target_pairs={{0,2},{1,3},{2,0},{3,1},{4,6},{5,7},{6,4},{7,5},{8,10},{9,11},{10,... | collective-permute-start | bytes 2457608 | tf_op jit(solution)/shard_map/ppermute | solution.py:314
  41.3 31.8 %collective-permute-start.8 = (f32[200,1024]{1,0:T(8,128)}, f32[200,1024]{1,0:T(8,128)S(1)}, u32[]{:S(2)}, u32[]{:S(2)}) collective-permute-start(f32[200,1024]{1,0:T(8,128)} %collective-permute-done.7), channel_id=1, source_target_pairs={{0,4},{1,5},{2,6},{3,7},{4,0},{5,1},{6,2},{7,3},{8,12},{9,13},{10,... | collective-permute-start | bytes 2457608 | tf_op jit(solution)/shard_map/ppermute | solution.py:314
  43.7 17.2 %collective-permute-start.4 = (f32[136,1024]{1,0:T(8,128)S(1)}, f32[136,1024]{1,0:T(8,128)S(1)}, u32[]{:S(2)}, u32[]{:S(2)}) collective-permute-start(f32[136,1024]{1,0:T(8,128)S(1)} %copy-done.6), channel_id=1, source_target_pairs={{0,12},{1,13},{2,14},{3,15},{4,8},{5,9},{6,10},{7,11},{8,4},{9,5},... | collective-permute-start | bytes 1671176 | tf_op jit(solution)/shard_map/ppermute | solution.py:314
  53.9 19.2 %collective-permute-start.12 = (f32[200,1024]{1,0:T(8,128)S(1)}, f32[200,1024]{1,0:T(8,128)S(1)}, u32[]{:S(2)}, u32[]{:S(2)}) collective-permute-start(f32[200,1024]{1,0:T(8,128)S(1)} %collective-permute-done.refs_0_.refs_1_.refs_2_.refs_3_.refs_12_.refs_16_.refs_29_.refs_8_.refs_20_.refs_24_.refs_37_), channel_id=1, source_target_pairs={{0,2},{1,3},{2,0},{3,1},{4,6},{5,7},{6,4},{7,5},{8,10},{9,11},{10,... | collective-permute-start | bytes 2457608 | tf_op jit(solution)/shard_map/ppermute | solution.py:314
  54.5 19.6 %collective-permute-start.5 = (f32[200,1024]{1,0:T(8,128)S(1)}, f32[200,1024]{1,0:T(8,128)S(1)}, u32[]{:S(2)}, u32[]{:S(2)}) collective-permute-start(f32[200,1024]{1,0:T(8,128)S(1)} %get-tuple-element.108.refs_0_.refs_2_.refs_4_.refs_6_.refs_8_.refs_10_.refs_14_.refs_21_.refs_18_.refs_22_.refs_29_), channel_id=1, source_target_pairs={{0,1},{1,0},{2,3},{3,2},{4,5},{5,4},{6,7},{7,6},{8,9},{9,8},{10,11... | collective-permute-start | bytes 2457608 | tf_op jit(solution)/shard_map/ppermute | solution.py:314
  60.3 14.2 %collective-permute-start.6 = (f32[200,1024]{1,0:T(8,128)S(1)}, f32[200,1024]{1,0:T(8,128)S(1)}, u32[]{:S(2)}, u32[]{:S(2)}) collective-permute-start(f32[200,1024]{1,0:T(8,128)S(1)} %collective-permute-done.1.refs_1_.refs_3_.refs_5_.refs_7_.refs_9_.refs_11_.refs_15_.refs_25_.refs_19_.refs_23_.refs_33_), channel_id=1, source_target_pairs={{0,1},{1,0},{2,3},{3,2},{4,5},{5,4},{6,7},{7,6},{8,9},{9,8},{10,11... | collective-permute-start | bytes 2457608 | tf_op jit(solution)/shard_map/ppermute | solution.py:314
  60.9 13.7 %collective-permute-start.9 = (f32[200,1024]{1,0:T(8,128)S(1)}, f32[200,1024]{1,0:T(8,128)S(1)}, u32[]{:S(2)}, u32[]{:S(2)}) collective-permute-start(f32[200,1024]{1,0:T(8,128)S(1)} %collective-permute-done.2.refs_4_.refs_12_.refs_22_.refs_30_), channel_id=1, source_target_pairs={{0,1},{1,0},{2,3},{3,2},{4,5},{5,4},{6,7},{7,6},{8,9},{9,8},{10,11... | collective-permute-start | bytes 2457608 | tf_op jit(solution)/shard_map/ppermute | solution.py:314
  73.1 14.5 %collective-permute-start.3 = (f32[64,1024]{1,0:T(8,128)S(1)}, f32[64,1024]{1,0:T(8,128)S(1)}, u32[]{:S(2)}, u32[]{:S(2)}) collective-permute-start(f32[64,1024]{1,0:T(8,128)S(1)} %get-tuple-element.91), channel_id=1, source_target_pairs={{0,12},{1,13},{2,14},{3,15},{4,8},{5,9},{6,10},{7,11},{8,4},{9,5},... | collective-permute-start | bytes 786440 | tf_op jit(solution)/shard_map/ppermute | solution.py:314
  74.0 17.5 %collective-permute-start.15 = (f32[136,1024]{1,0:T(8,128)S(1)}, f32[136,1024]{1,0:T(8,128)S(1)}, u32[]{:S(2)}, u32[]{:S(2)}) collective-permute-start(f32[136,1024]{1,0:T(8,128)S(1)} %collective-permute-done.4.refs_0_.refs_1_.refs_2_.refs_13_.refs_17_.refs_33_.refs_9_.refs_21_.refs_25_.refs_41_), channel_id=1, source_target_pairs={{0,2},{1,3},{2,0},{3,1},{4,6},{5,7},{6,4},{7,5},{8,10},{9,11},{10,... | collective-permute-start | bytes 1671176 | tf_op jit(solution)/shard_map/ppermute | solution.py:314
  74.5 9.0 %collective-permute-start.11 = (f32[200,1024]{1,0:T(8,128)S(1)}, f32[200,1024]{1,0:T(8,128)S(1)}, u32[]{:S(2)}, u32[]{:S(2)}) collective-permute-start(f32[200,1024]{1,0:T(8,128)S(1)} %collective-permute-done.refs_0_.refs_1_.refs_2_.refs_3_.refs_12_.refs_16_.refs_29_.refs_8_.refs_20_.refs_24_.refs_37_), channel_id=1, source_target_pairs={{0,1},{1,0},{2,3},{3,2},{4,5},{5,4},{6,7},{7,6},{8,9},{9,8},{10,11... | collective-permute-start | bytes 2457608 | tf_op jit(solution)/shard_map/ppermute | solution.py:314
  74.6 9.0 %collective-permute-start.13 = (f32[200,1024]{1,0:T(8,128)S(1)}, f32[200,1024]{1,0:T(8,128)S(1)}, u32[]{:S(2)}, u32[]{:S(2)}) collective-permute-start(f32[200,1024]{1,0:T(8,128)S(1)} %collective-permute-done.12.refs_4_.refs_30_.refs_12_.refs_38_), channel_id=1, source_target_pairs={{0,1},{1,0},{2,3},{3,2},{4,5},{5,4},{6,7},{7,6},{8,9},{9,8},{10,11... | collective-permute-start | bytes 2457608 | tf_op jit(solution)/shard_map/ppermute | solution.py:314
  83.6 12.8 %collective-permute-start.14 = (f32[136,1024]{1,0:T(8,128)S(1)}, f32[136,1024]{1,0:T(8,128)S(1)}, u32[]{:S(2)}, u32[]{:S(2)}) collective-permute-start(f32[136,1024]{1,0:T(8,128)S(1)} %collective-permute-done.4.refs_0_.refs_1_.refs_2_.refs_13_.refs_17_.refs_33_.refs_9_.refs_21_.refs_25_.refs_41_), channel_id=1, source_target_pairs={{0,1},{1,0},{2,3},{3,2},{4,5},{5,4},{6,7},{7,6},{8,9},{9,8},{10,11... | collective-permute-start | bytes 1671176 | tf_op jit(solution)/shard_map/ppermute | solution.py:314
  92.0 9.8 %collective-permute-start.17 = (f32[64,1024]{1,0:T(8,128)S(1)}, f32[64,1024]{1,0:T(8,128)S(1)}, u32[]{:S(2)}, u32[]{:S(2)}) collective-permute-start(f32[64,1024]{1,0:T(8,128)S(1)} %collective-permute-done.3.refs_0_.refs_1_.refs_21_), channel_id=1, source_target_pairs={{0,2},{1,3},{2,0},{3,1},{4,6},{5,7},{6,4},{7,5},{8,10},{9,11},{10,... | collective-permute-start | bytes 786440 | tf_op jit(solution)/shard_map/ppermute | solution.py:314
  100.8 24.9 %collective-permute-start.24 = (f32[256,1024]{1,0:T(8,128)S(1)}, f32[256,1024]{1,0:T(8,128)S(1)}, u32[]{:S(2)}, u32[]{:S(2)}) collective-permute-start(f32[256,1024]{1,0:T(8,128)S(1)} %get-tuple-element.134.refs_0_.refs_4_.refs_8_.refs_9_.refs_12_.refs_17_), channel_id=1, source_target_pairs={{0,2},{1,3},{2,0},{3,1},{4,6},{5,7},{6,4},{7,5},{8,10},{9,11},{10,... | collective-permute-start | bytes 3145736 | tf_op jit(solution)/shard_map/ppermute | solution.py:314
  111.7 12.6 %collective-permute-start.22 = (f32[8,128]{1,0:T(8,128)S(1)}, f32[8,128]{1,0:T(8,128)S(1)}, u32[]{:S(2)}, u32[]{:S(2)}) collective-permute-start(f32[8,128]{1,0:T(8,128)S(1)} %fold_own.1.refs_0_), channel_id=1, source_target_pairs={{0,12},{1,13},{2,14},{3,15},{4,8},{5,9},{6,10},{7,11},{8,4},{9,5},... | collective-permute-start | bytes 12296 | tf_op jit(solution)/shard_map/ppermute | solution.py:314
  112.5 11.8 %collective-permute-start.21 = (f32[8,128]{1,0:T(8,128)S(1)}, f32[8,128]{1,0:T(8,128)S(1)}, u32[]{:S(2)}, u32[]{:S(2)}) collective-permute-start(f32[8,128]{1,0:T(8,128)S(1)} %fold_own.1.refs_0_), channel_id=1, source_target_pairs={{0,8},{1,9},{2,10},{3,11},{4,12},{5,13},{6,14},{7,15},{8,0},{9,1},... | collective-permute-start | bytes 12296 | tf_op jit(solution)/shard_map/ppermute | solution.py:314
  128.8 36.6 %collective-permute-start.25 = (f32[256,1024]{1,0:T(8,128)S(1)}, f32[256,1024]{1,0:T(8,128)S(1)}, u32[]{:S(2)}, u32[]{:S(2)}) collective-permute-start(f32[256,1024]{1,0:T(8,128)S(1)} %get-tuple-element.149.refs_1_.refs_0_.refs_4_.refs_16_), channel_id=1, source_target_pairs={{0,2},{1,3},{2,0},{3,1},{4,6},{5,7},{6,4},{7,5},{8,10},{9,11},{10,... | collective-permute-start | bytes 3145736 | tf_op jit(solution)/shard_map/ppermute | solution.py:314
  137.1 18.9 %collective-permute-start.31 = (f32[64,1024]{1,0:T(8,128)S(1)}, f32[64,1024]{1,0:T(8,128)S(1)}, u32[]{:S(2)}, u32[]{:S(2)}) collective-permute-start(f32[64,1024]{1,0:T(8,128)S(1)} %get-tuple-element.138), channel_id=1, source_target_pairs={{0,4},{1,5},{2,6},{3,7},{4,0},{5,1},{6,2},{7,3},{8,12},{9,13},{10,... | collective-permute-start | bytes 786440 | tf_op jit(solution)/shard_map/ppermute | solution.py:314
  140.1 18.6 %collective-permute-start.32 = (f32[64,1024]{1,0:T(8,128)S(1)}, f32[64,1024]{1,0:T(8,128)S(1)}, u32[]{:S(2)}, u32[]{:S(2)}) collective-permute-start(f32[64,1024]{1,0:T(8,128)S(1)} %get-tuple-element.139), channel_id=1, source_target_pairs={{0,8},{1,9},{2,10},{3,11},{4,12},{5,13},{6,14},{7,15},{8,0},{9,1},... | collective-permute-start | bytes 786440 | tf_op jit(solution)/shard_map/ppermute | solution.py:314
  140.7 23.6 %collective-permute-start.33 = (f32[64,1024]{1,0:T(8,128)S(1)}, f32[64,1024]{1,0:T(8,128)S(1)}, u32[]{:S(2)}, u32[]{:S(2)}) collective-permute-start(f32[64,1024]{1,0:T(8,128)S(1)} %get-tuple-element.140), channel_id=1, source_target_pairs={{0,12},{1,13},{2,14},{3,15},{4,8},{5,9},{6,10},{7,11},{8,4},{9,5},... | collective-permute-start | bytes 786440 | tf_op jit(solution)/shard_map/ppermute | solution.py:314
  141.7 25.2 %collective-permute-start.35 = (f32[256,1024]{1,0:T(8,128)S(1)}, f32[256,1024]{1,0:T(8,128)S(1)}, u32[]{:S(2)}, u32[]{:S(2)}) collective-permute-start(f32[256,1024]{1,0:T(8,128)S(1)} %get-tuple-element.149.refs_1_.refs_0_.refs_4_.refs_16_), channel_id=1, source_target_pairs={{0,1},{1,0},{2,3},{3,2},{4,5},{5,4},{6,7},{7,6},{8,9},{9,8},{10,11... | collective-permute-start | bytes 3145736 | tf_op jit(solution)/shard_map/ppermute | solution.py:314
  165.4 37.2 %collective-permute-start.34 = (f32[256,1024]{1,0:T(8,128)S(1)}, f32[256,1024]{1,0:T(8,128)S(1)}, u32[]{:S(2)}, u32[]{:S(2)}) collective-permute-start(f32[256,1024]{1,0:T(8,128)S(1)} %get-tuple-element.148.refs_0_.refs_4_.refs_16_), channel_id=1, source_target_pairs={{0,2},{1,3},{2,0},{3,1},{4,6},{5,7},{6,4},{7,5},{8,10},{9,11},{10,... | collective-permute-start | bytes 3145736 | tf_op jit(solution)/shard_map/ppermute | solution.py:314
  175.1 11.0 %collective-permute-start.37 = (f32[64,1024]{1,0:T(8,128)S(1)}, f32[64,1024]{1,0:T(8,128)S(1)}, u32[]{:S(2)}, u32[]{:S(2)}) collective-permute-start(f32[64,1024]{1,0:T(8,128)S(1)} %get-tuple-element.152), channel_id=1, source_target_pairs={{0,4},{1,5},{2,6},{3,7},{4,0},{5,1},{6,2},{7,3},{8,12},{9,13},{10,... | collective-permute-start | bytes 786440 | tf_op jit(solution)/shard_map/ppermute | solution.py:314
  175.1 20.5 %collective-permute-start.38 = (f32[64,1024]{1,0:T(8,128)S(1)}, f32[64,1024]{1,0:T(8,128)S(1)}, u32[]{:S(2)}, u32[]{:S(2)}) collective-permute-start(f32[64,1024]{1,0:T(8,128)S(1)} %get-tuple-element.153), channel_id=1, source_target_pairs={{0,8},{1,9},{2,10},{3,11},{4,12},{5,13},{6,14},{7,15},{8,0},{9,1},... | collective-permute-start | bytes 786440 | tf_op jit(solution)/shard_map/ppermute | solution.py:314
  177.7 23.9 %collective-permute-start.39 = (f32[64,1024]{1,0:T(8,128)S(1)}, f32[64,1024]{1,0:T(8,128)S(1)}, u32[]{:S(2)}, u32[]{:S(2)}) collective-permute-start(f32[64,1024]{1,0:T(8,128)S(1)} %get-tuple-element.154), channel_id=1, source_target_pairs={{0,12},{1,13},{2,14},{3,15},{4,8},{5,9},{6,10},{7,11},{8,4},{9,5},... | collective-permute-start | bytes 786440 | tf_op jit(solution)/shard_map/ppermute | solution.py:314
  178.6 24.0 %collective-permute-start.23 = (f32[256,1024]{1,0:T(8,128)S(1)}, f32[256,1024]{1,0:T(8,128)S(1)}, u32[]{:S(2)}, u32[]{:S(2)}) collective-permute-start(f32[256,1024]{1,0:T(8,128)S(1)} %get-tuple-element.148.refs_0_.refs_4_.refs_16_), channel_id=1, source_target_pairs={{0,1},{1,0},{2,3},{3,2},{4,5},{5,4},{6,7},{7,6},{8,9},{9,8},{10,11... | collective-permute-start | bytes 3145736 | tf_op jit(solution)/shard_map/ppermute | solution.py:314
  212.3 11.0 %collective-permute-start.41 = (f32[64,1024]{1,0:T(8,128)S(1)}, f32[64,1024]{1,0:T(8,128)S(1)}, u32[]{:S(2)}, u32[]{:S(2)}) collective-permute-start(f32[64,1024]{1,0:T(8,128)S(1)} %get-tuple-element.158), channel_id=1, source_target_pairs={{0,4},{1,5},{2,6},{3,7},{4,0},{5,1},{6,2},{7,3},{8,12},{9,13},{10,... | collective-permute-start | bytes 786440 | tf_op jit(solution)/shard_map/ppermute | solution.py:314
  212.4 20.5 %collective-permute-start.42 = (f32[64,1024]{1,0:T(8,128)S(1)}, f32[64,1024]{1,0:T(8,128)S(1)}, u32[]{:S(2)}, u32[]{:S(2)}) collective-permute-start(f32[64,1024]{1,0:T(8,128)S(1)} %get-tuple-element.159), channel_id=1, source_target_pairs={{0,8},{1,9},{2,10},{3,11},{4,12},{5,13},{6,14},{7,15},{8,0},{9,1},... | collective-permute-start | bytes 786440 | tf_op jit(solution)/shard_map/ppermute | solution.py:314
  214.9 23.9 %collective-permute-start.43 = (f32[64,1024]{1,0:T(8,128)S(1)}, f32[64,1024]{1,0:T(8,128)S(1)}, u32[]{:S(2)}, u32[]{:S(2)}) collective-permute-start(f32[64,1024]{1,0:T(8,128)S(1)} %get-tuple-element.160), channel_id=1, source_target_pairs={{0,12},{1,13},{2,14},{3,15},{4,8},{5,9},{6,10},{7,11},{8,4},{9,5},... | collective-permute-start | bytes 786440 | tf_op jit(solution)/shard_map/ppermute | solution.py:314
  (19 other events, 104.7 us)

commit v11 on v10

--- a/solution.py
+++ b/solution.py
@@ -221,9 +221,10 @@
     field = joined(own)
     second = tendency(cells, totals, field, own_carrier, x_terms, y_sums(matrix_ref, fields, carriers, sums))
     out = base_ref[...] + (time_step * second_weight) * second
-    size = out_refs[0].shape[0]
-    for place, out_ref in enumerate(out_refs):
-        out_ref[...] = out[place * size:(place + 1) * size]
+    start = 0
+    for out_ref in out_refs:
+        out_ref[...] = out[start:start + out_ref.shape[0]]
+        start += out_ref.shape[0]
 
 
 def y_call(kernel, matrix, part, groups, out_rows, name, totals=(), weight=36):
@@ -266,33 +267,29 @@
     )(*arrays)
 
 
-def place_kernel(components, planes, plane_ref, *refs):
+def place_kernel(spots, plane_ref, *refs):
     out_ref = refs[-1]
-    for n in range(components):
-        @pl.when(pl.program_id(0) == n)
-        def _():
-            for d in range(planes):
-                out_ref[plane_ref[0] ^ d] = refs[n * planes + d][...]
-
-
-def place_blocks(plane, blocks, components, shape, out):
+    for (d, start, rows), ref in zip(spots, refs):
+        out_ref[plane_ref[0] ^ d, start:start + rows, :] = ref[...]
+
+
+def place_blocks(plane, arrays, spots, component, shape, out):
     planes, size, length = shape[1:]
-    first, step = components[0], components[-1] - components[0]
-    whole = pl.BlockSpec((size, length), lambda n, plane_ref: (0, 0))
-    arrays = [block for i in components for block in blocks[i]]
-    return pl.pallas_call(
-        functools.partial(place_kernel, len(components), planes),
+    before = [] if out is None else [out]
+    return pl.pallas_call(
+        functools.partial(place_kernel, spots),
         grid_spec=pltpu.PrefetchScalarGridSpec(
             num_scalar_prefetch=1,
-            grid=(len(components),),
-            in_specs=[whole] * len(arrays) + [pl.BlockSpec(memory_space=pl.ANY)] * (out is not None),
-            out_specs=pl.BlockSpec((None, planes, size, length), lambda n, plane_ref: (first + step * n, 0, 0, 0)),
+            grid=(1,),
+            in_specs=[pl.BlockSpec((rows, length), lambda n, plane_ref: (0, 0)) for _, _, rows in spots]
+            + [pl.BlockSpec(memory_space=pl.ANY)] * len(before),
+            out_specs=pl.BlockSpec((None, planes, size, length), lambda n, plane_ref: (component, 0, 0, 0)),
         ),
         out_shape=jax.ShapeDtypeStruct(shape, F32),
-        input_output_aliases={} if out is None else {1 + len(arrays): 0},
+        input_output_aliases={1 + len(arrays): 0} if before else {},
         compiler_params=params(),
         name="place",
-    )(plane.reshape(1).astype(jnp.int32), *arrays, *([] if out is None else [out]))
+    )(plane.reshape(1).astype(jnp.int32), *arrays, *before)
 
 
 def after(values, *earlier):
@@ -448,33 +445,46 @@
         return y_call(
             functools.partial(second_kernel, cells), along_y_matrix, 0,
             [middle_pieces(i), middle_pieces(1) if i != 1 else [], [], [piece(middle[i])], [piece(middle[1])],
-             [piece(x_terms[i])], [piece(base[i])]], [size] * planes, f"y_second_{i}", totals, {0: 1, 1: 36, 2: 1}[i],
+             [piece(x_terms[i])], [piece(base[i])]], [rows for _, _, rows in spots[i]], f"y_second_{i}", totals, {0: 1, 1: 36, 2: 1}[i],
         )
 
+    whole = [(d, 0, size) for d in range(planes)]
+    halved = [(d, 0, size) for d in parts[0]]
+    halved += [(d, start, size // 2) for d in parts[1] for start in (0, size // 2)]
+    spots = [halved, halved, whole]
     ends = [None] * 3
+
+    def leave(i, second):
+        gone = []
+        for place, (d, start, _) in enumerate(spots[i]):
+            if d and (start > 0) == second:
+                ends[i][place] = swap(ends[i][place], d * group)
+                gone.append(ends[i][place])
+        return gone
+
+    def put(i, out):
+        return place_blocks(plane, ends[i], spots[i], i, velocity.shape, out)
+
     middle_far[1] = across_cores(middle_others[1])
-    def leave(i):
-        ends[i] = [swap(block, d * group) if d else block for d, block in enumerate(ends[i])]
-
-    ends[1] = second_step(1)
+    ends[1] = list(second_step(1))
     x_terms[0] = along_x([piece(after(middle[0], ends[1]))], [], along_x_matrix, "x_second_0", 1)
-    leave(1)
+    gone = leave(1, False)
     x_terms[2] = along_x(
-        [piece(after(middle[2], x_terms[0]))], [piece(middle[0])], along_x_matrix, "x_second_2", 1
+        [piece(after(middle[2], x_terms[0], gone, middle_twin[0]))], [piece(middle[0])], along_x_matrix, "x_second_2", 1
     )
-    ends[1] = after(ends[1], x_terms[2])
-    out = place_blocks(plane, ends, (1,), velocity.shape, None)
-    middle_others[0] = after(middle_others[0], out)
+    leave(1, True)
+    middle_others[0] = after(middle_others[0], x_terms[2])
     middle_others[2] = across_chips(after(middle[2], middle_others[0]))
     middle_far[0] = across_cores(middle_others[0])
-    ends[0] = second_step(0)
-    leave(0)
-    out = place_blocks(plane, ends, (0,), velocity.shape, out)
-    middle_others[2] = after(middle_others[2], out)
+    ends[0] = list(second_step(0))
+    gone = leave(0, False)
+    out = put(1, None)
+    middle_others[2] = after(middle_others[2], gone, out)
+    rest = leave(0, True)
     middle_far[2] = across_cores(middle_others[2])
-    ends[2] = second_step(2)
-    leave(2)
-    return place_blocks(plane, ends, (2,), velocity.shape, out)
+    ends[2] = list(after(second_step(2), rest))
+    leave(2, False)
+    return put(2, put(0, out))
 
 
 def solution(mesh):

time: 241 us -> 232 us (0.963)
  waiting for transfers between devices: 94.9 us -> 81.5 us
  starting transfers between devices: 35 us -> 39.9 us
    ppermute x44 -> x48, waiting for transfers between devices: 94.9 us -> 81.5 us  [swap(): return lax.ppermute(x, 'row', [(r, r ^ distance) for r in range(devices)])]
    ppermute x44 -> x48, starting transfers between devices: 35 us -> 39.9 us  [swap(): return lax.ppermute(x, 'row', [(r, r ^ distance) for r in range(devices)])]
  transfers between devices with their start and end apart: 44 -> 48, of which waited for: 16 -> 18; matrix products, arithmetic and copies ran while one was open for 0% -> 0% of each run, Pallas kernels for 39% -> 43%
where the time goes in v11:
time: 232 us; the launch traced here: 231 us
  Pallas kernels  102 us (44%)
  waiting for transfers between devices  81.5 us (35%)
  starting transfers between devices  39.9 us (17%)
  local copies, waits for them, and re-layouts  7.18 us (3%)
    ppermute x48, waiting for transfers between devices, swap(): return lax.ppermute(x, 'row', [(r, r ^ distance) for r in range(devices)])  81.5 us
    pallas_call x9, Pallas kernels, y_call(): pl.pallas_call(functools.partial(kernel, tuple(counts)), grid=(length //...  45.8 us
    pallas_call x7, Pallas kernels, along_x(): pl.pallas_call(functools.partial(along_x_kernel, (len(fields), len(carrie...  44.7 us
    ppermute x48, starting transfers between devices, swap(): return lax.ppermute(x, 'row', [(r, r ^ distance) for r in range(devices)])  39.9 us
    pallas_call x1, Pallas kernels, prepare_matrices(): pl.pallas_call(functools.partial(matrices_kernel, count), grid_spec=pltpu...  7.16 us
    unnamed x14, local copies, waits for them, and re-layouts  7.09 us
  transfers between devices with their start and end apart: 48, of which 18 were waited for; matrix products, arithmetic and copies ran while one was open for 0% of the time, Pallas kernels for 43%

profile of v11, /device:TPU:18, one launch (start us, length us, event | category | flops | bytes accessed | tf_op | source)
XLA Modules:
  0.0 231.4 jit_solution(6271359624764167671)
XLA Ops:
  10.6 2.2 copy-done.4
  12.8 7.2 %shard_map.37 = (bf16[4,1024,1024]{2,1,0:T(8,128)(2,1)S(1)}, bf16[4,256,1024]{2,1,0:T(8,128)(2,1)S(1)}) custom-call(s32[16]{0:T(128)S(1)} %stack.74.order_ref, s32[4]{0:T(128)S(1)} %pad_add_fusion.own_ref, f32[1024,1024]{1,0:T(8,128)S(1)} %copy-done.3, f32[1024,1024]{1,0:T(8,128)S(1)} %copy-done.3, f32[1024,1024]{1,0:T(8,128)S(1)} %copy-done.4, ...), custom_call_target="tpu_custom_call" | custom-call | flops 17179869184 | bytes 33554432 | tf_op jit(solution)/shard_map/pallas_call | solution.py:63
  20.0 21.3 %collective-permute-done.1.refs_1_.refs_3_.refs_5_.refs_7_.refs_9_.refs_11_.refs_15_.refs_25_.refs_19_.refs_23_.refs_33_ = f32[200,1024]{1,0:T(8,128)S(1)} collective-permute-done((f32[200,1024]{1,0:T(8,128)}, f32[200,1024]{1,0:T(8,128)S(1)}, u32[]{:S(2)}, u32[]{:S(2)}) %collective-permute-start.1) | collective-permute-done | bytes 819232 | tf_op jit(solution)/shard_map/ppermute | solution.py:311
  41.3 2.4 %collective-permute-start.8 = (f32[200,1024]{1,0:T(8,128)}, f32[200,1024]{1,0:T(8,128)S(1)}, u32[]{:S(2)}, u32[]{:S(2)}) collective-permute-start(f32[200,1024]{1,0:T(8,128)} %collective-permute-done.7), channel_id=1, source_target_pairs={{0,4},{1,5},{2,6},{3,7},{4,0},{5,1},{6,2},{7,3},{8,12},{9,13},{10,... | collective-permute-start | bytes 2457608 | tf_op jit(solution)/shard_map/ppermute | solution.py:311
  44.1 9.8 %x_first_near.1.refs_18_.refs_26_ = f32[384,1024]{1,0:T(8,128)S(1)} custom-call(f32[200,1024]{1,0:T(8,128)S(1)} %get-tuple-element.112.refs_0_.refs_2_.refs_4_.refs_6_.refs_8_.refs_10_.refs_14_.refs_21_.refs_18_.refs_22_.refs_29_, ...), custom_call_target="tpu_custom_call" | custom-call | flops 402653184 | bytes 1572864 | tf_op jit(solution)/shard_map/x_first_near/pallas_call | solution.py:163
  54.5 5.8 %x_first_2.1.refs_19_.refs_27_ = f32[192,1024]{1,0:T(8,128)S(1)} custom-call(f32[200,1024]{1,0:T(8,128)S(1)} %collective-permute-done.refs_0_.refs_1_.refs_2_.refs_3_.refs_12_.refs_16_.refs_29_.refs_8_.refs_20_.refs_24_.refs_37_, ...), custom_call_target="tpu_custom_call" | custom-call | flops 201326592 | bytes 786432 | tf_op jit(solution)/shard_map/x_first_2/pallas_call | solution.py:163
  60.9 12.2 %collective-permute-done.8.refs_5_.refs_13_.refs_26_.refs_34_ = f32[200,1024]{1,0:T(8,128)S(1)} collective-permute-done((f32[200,1024]{1,0:T(8,128)}, f32[200,1024]{1,0:T(8,128)S(1)}, u32[]{:S(2)}, u32[]{:S(2)}) %collective-permute-start.8) | collective-permute-done | bytes 819232 | tf_op jit(solution)/shard_map/ppermute | solution.py:311
  75.4 3.6 %y_first_near_1.1 = (f32[256,1024]{1,0:T(8,128)S(1)}, f32[256,1024]{1,0:T(8,128)S(1)}) custom-call(bf16[4,256,1024]{2,1,0:T(8,128)(2,1)S(1)} %get-tuple-element.87.matrix_ref, f32[200,1024]{1,0:T(8,128)S(1)} %get-tuple-element.112.refs_0_.refs_2_.refs_4_.refs_6_.refs_8_.refs_10_.refs_14_.refs_21_.refs_18_.refs_22_.refs_29_, ...), custom_call_target="tpu_custom_call" | custom-call | flops 4831838208 | bytes 1048576 | tf_op jit(solution)/shard_map/y_first_near_1/pallas_call | solution.py:242
  79.0 4.5 %x_first_last.1.refs_20_.refs_28_ = f32[128,1024]{1,0:T(8,128)S(1)} custom-call(f32[136,1024]{1,0:T(8,128)S(1)} %collective-permute-done.4.refs_0_.refs_1_.refs_2_.refs_13_.refs_17_.refs_33_.refs_9_.refs_21_.refs_25_.refs_41_, f32[136,1024]{1,0:T(8,128)S(1)} %collective-permute-done.4.refs_0_.refs_1_.refs_2_.refs_13_.refs_17_.refs_33_.refs_9_.refs_21_.refs_25_.refs_41_, ...), custom_call_target="tpu_custom_call" | custom-call | flops 4831838208 | bytes 524288 | tf_op jit(solution)/shard_map/x_first_last/pallas_call | solution.py:163
  83.7 3.9 %y_first_near_0.1 = (f32[256,1024]{1,0:T(8,128)S(1)}, f32[256,1024]{1,0:T(8,128)S(1)}) custom-call(bf16[4,256,1024]{2,1,0:T(8,128)(2,1)S(1)} %get-tuple-element.87.matrix_ref, f32[200,1024]{1,0:T(8,128)S(1)} %get-tuple-element.112.refs_0_.refs_2_.refs_4_.refs_6_.refs_8_.refs_10_.refs_14_.refs_21_.refs_18_.refs_22_.refs_29_, ...), custom_call_target="tpu_custom_call" | custom-call | flops 4831838208 | bytes 1048576 | tf_op jit(solution)/shard_map/y_first_near_0/pallas_call | solution.py:242
  87.6 3.9 %y_first_near_2.1 = (f32[256,1024]{1,0:T(8,128)S(1)}, f32[256,1024]{1,0:T(8,128)S(1)}) custom-call(bf16[4,256,1024]{2,1,0:T(8,128)(2,1)S(1)} %get-tuple-element.87.matrix_ref, f32[200,1024]{1,0:T(8,128)S(1)} %get-tuple-element.112.refs_0_.refs_2_.refs_4_.refs_6_.refs_8_.refs_10_.refs_14_.refs_21_.refs_18_.refs_22_.refs_29_, ...), custom_call_target="tpu_custom_call" | custom-call | flops 4831838208 | bytes 1048576 | tf_op jit(solution)/shard_map/y_first_near_2/pallas_call | solution.py:242
  93.1 3.3 %x_first_tail.1.refs_28_ = f32[64,1024]{1,0:T(8,128)S(1)} custom-call(f32[64,1024]{1,0:T(8,128)S(1)} %collective-permute-done.3.refs_0_.refs_1_.refs_21_, f32[136,1024]{1,0:T(8,128)S(1)} %collective-permute-done.4.refs_0_.refs_1_.refs_2_.refs_13_.refs_17_.refs_33_.refs_9_.refs_21_.refs_25_.refs_41_, ...), custom_call_target="tpu_custom_call" | custom-call | flops 2415919104 | bytes 262144 | tf_op jit(solution)/shard_map/x_first_tail/pallas_call | solution.py:163
  96.4 4.4 %y_first_far_1.1 = (f32[256,1024]{1,0:T(8,128)S(1)}, f32[256,1024]{1,0:T(8,128)S(1)}, f32[8,1024]{1,0:T(8,128)S(1)}) custom-call(bf16[4,256,1024]{2,1,0:T(8,128)(2,1)S(1)} %get-tuple-element.87.matrix_ref, f32[200,1024]{1,0:T(8,128)S(1)} %collective-permute-done.refs_0_.refs_1_.refs_2_.refs_3_.refs_12_.refs_16_.refs_29_.refs_8_.refs_20_.refs_24_.refs_37_, ...), custom_call_target="tpu_custom_call" | custom-call | flops 4831838208 | bytes 1048576 | tf_op jit(solution)/shard_map/y_first_far_1/pallas_call | solution.py:242
  102.3 4.6 %y_first_far_0.1 = (f32[256,1024]{1,0:T(8,128)S(1)}, f32[256,1024]{1,0:T(8,128)S(1)}, f32[8,1024]{1,0:T(8,128)S(1)}) custom-call(bf16[4,256,1024]{2,1,0:T(8,128)(2,1)S(1)} %get-tuple-element.87.matrix_ref, f32[200,1024]{1,0:T(8,128)S(1)} %collective-permute-done.refs_0_.refs_1_.refs_2_.refs_3_.refs_12_.refs_16_.refs_29_.refs_8_.refs_20_.refs_24_.refs_37_, ...), custom_call_target="tpu_custom_call" | custom-call | flops 4831838208 | bytes 1048576 | tf_op jit(solution)/shard_map/y_first_far_0/pallas_call | solution.py:242
  107.0 4.7 %y_first_far_2.1 = (f32[256,1024]{1,0:T(8,128)S(1)}, f32[256,1024]{1,0:T(8,128)S(1)}, f32[8,1024]{1,0:T(8,128)S(1)}) custom-call(bf16[4,256,1024]{2,1,0:T(8,128)(2,1)S(1)} %get-tuple-element.87.matrix_ref, f32[200,1024]{1,0:T(8,128)S(1)} %collective-permute-done.refs_0_.refs_1_.refs_2_.refs_3_.refs_12_.refs_16_.refs_29_.refs_8_.refs_20_.refs_24_.refs_37_, ...), custom_call_target="tpu_custom_call" | custom-call | flops 4831838208 | bytes 1048576 | tf_op jit(solution)/shard_map/y_first_far_2/pallas_call | solution.py:242
  112.5 4.6 %collective-permute-start.21 = (f32[8,128]{1,0:T(8,128)S(1)}, f32[8,128]{1,0:T(8,128)S(1)}, u32[]{:S(2)}, u32[]{:S(2)}) collective-permute-start(f32[8,128]{1,0:T(8,128)S(1)} %fold_own.1.refs_0_), channel_id=1, source_target_pairs={{0,8},{1,9},{2,10},{3,11},{4,12},{5,13},{6,14},{7,15},{8,0},{9,1},... | collective-permute-start | bytes 12296 | tf_op jit(solution)/shard_map/ppermute | solution.py:311
  117.1 7.1 %x_second_1.1.refs_10_ = f32[256,1024]{1,0:T(8,128)S(1)} custom-call(f32[256,1024]{1,0:T(8,128)S(1)} %get-tuple-element.138.refs_0_.refs_4_.refs_8_.refs_9_.refs_12_.refs_17_, f32[256,1024]{1,0:T(8,128)S(1)} %get-tuple-element.148.refs_1_.refs_0_.refs_4_.refs_16_, bf16[4,1024,1024]{2,1,0:T(8,128)(2,1)S(1)} %get-tuple-element.91.refs_8_.refs_4_.refs_3_.refs_2_.refs_1_), custom_call_target="tpu_custom_call" | custom-call | flops 9663676416 | bytes 1048576 | tf_op jit(solution)/shard_map/x_second_1/pallas_call | solution.py:163
  131.5 6.6 %y_second_1.1 = (f32[64,1024]{1,0:T(8,128)S(1)}, f32[64,1024]{1,0:T(8,128)S(1)}, f32[32,1024]{1,0:T(8,128)S(1)}, f32[32,1024]{1,0:T(8,128)S(1)}, f32[32,1024]{1,0:T(8,128)S(1)}, /*index=5*/f32[32,1024]{1,0:T(8,128)S(1)}) custom-call(bf16[4,256,1024]{2,1,0:T(8,128)(2,1)S(1)} %get-tuple-element.87.matrix_ref, ...), custom_call_target="tpu_custom_call" | custom-call | flops 9663676416 | bytes 1048576 | tf_op jit(solution)/shard_map/y_second_1/pallas_call | solution.py:242
  138.2 3.5 %collective-permute-start.31 = (f32[64,1024]{1,0:T(8,128)S(1)}, f32[64,1024]{1,0:T(8,128)S(1)}, u32[]{:S(2)}, u32[]{:S(2)}) collective-permute-start(f32[64,1024]{1,0:T(8,128)S(1)} %get-tuple-element.142), channel_id=1, source_target_pairs={{0,4},{1,5},{2,6},{3,7},{4,0},{5,1},{6,2},{7,3},{8,12},{9,13},{10,... | collective-permute-start | bytes 786440 | tf_op jit(solution)/shard_map/ppermute | solution.py:311
  143.2 7.1 %x_second_0.1.refs_18_ = f32[256,1024]{1,0:T(8,128)S(1)} custom-call(f32[256,1024]{1,0:T(8,128)S(1)} %get-tuple-element.148.refs_1_.refs_0_.refs_4_.refs_16_, bf16[4,1024,1024]{2,1,0:T(8,128)(2,1)S(1)} %get-tuple-element.91.refs_8_.refs_4_.refs_3_.refs_2_.refs_1_), custom_call_target="tpu_custom_call" | custom-call | flops 268435456 | bytes 1048576 | tf_op jit(solution)/shard_map/x_second_0/pallas_call | solution.py:163
  151.4 2.2 collective-permute-done.33.refs_4_
  153.6 7.1 %x_second_2.1.refs_18_ = f32[256,1024]{1,0:T(8,128)S(1)} custom-call(f32[256,1024]{1,0:T(8,128)S(1)} %get-tuple-element.151.refs_0_.refs_4_.refs_16_, f32[256,1024]{1,0:T(8,128)S(1)} %get-tuple-element.148.refs_1_.refs_0_.refs_4_.refs_16_, bf16[4,1024,1024]{2,1,0:T(8,128)(2,1)S(1)} %get-tuple-element.91.refs_8_.refs_4_.refs_3_.refs_2_.refs_1_), custom_call_target="tpu_custom_call" | custom-call | flops 268435456 | bytes 1048576 | tf_op jit(solution)/shard_map/x_second_2/pallas_call | solution.py:163
  163.5 7.1 %y_second_0.1 = (f32[64,1024]{1,0:T(8,128)S(1)}, f32[64,1024]{1,0:T(8,128)S(1)}, f32[32,1024]{1,0:T(8,128)S(1)}, f32[32,1024]{1,0:T(8,128)S(1)}, f32[32,1024]{1,0:T(8,128)S(1)}, /*index=5*/f32[32,1024]{1,0:T(8,128)S(1)}) custom-call(bf16[4,256,1024]{2,1,0:T(8,128)(2,1)S(1)} %get-tuple-element.87.matrix_ref, ...), custom_call_target="tpu_custom_call" | custom-call | flops 268435456 | bytes 1048576 | tf_op jit(solution)/shard_map/y_second_0/pallas_call | solution.py:242
  172.6 2.5 %collective-permute-start.38 = (f32[32,1024]{1,0:T(8,128)S(1)}, f32[32,1024]{1,0:T(8,128)S(1)}, u32[]{:S(2)}, u32[]{:S(2)}) collective-permute-start(f32[32,1024]{1,0:T(8,128)S(1)} %get-tuple-element.154), channel_id=1, source_target_pairs={{0,8},{1,9},{2,10},{3,11},{4,12},{5,13},{6,14},{7,15},{8,0},{9,1},... | collective-permute-start | bytes 393224 | tf_op jit(solution)/shard_map/ppermute | solution.py:311
  178.0 8.4 %collective-permute-done.35.refs_2_.refs_6_ = f32[256,1024]{1,0:T(8,128)S(1)} collective-permute-done((f32[256,1024]{1,0:T(8,128)S(1)}, f32[256,1024]{1,0:T(8,128)S(1)}, u32[]{:S(2)}, u32[]{:S(2)}) %collective-permute-start.35) | collective-permute-done | bytes 1048608 | tf_op jit(solution)/shard_map/ppermute | solution.py:311
  187.5 3.2 %collective-permute-done.39.refs_4_ = f32[32,1024]{1,0:T(8,128)S(1)} collective-permute-done((f32[32,1024]{1,0:T(8,128)S(1)}, f32[32,1024]{1,0:T(8,128)S(1)}, u32[]{:S(2)}, u32[]{:S(2)}) %collective-permute-start.39) | collective-permute-done | bytes 131104 | tf_op jit(solution)/shard_map/ppermute | solution.py:311
  193.4 7.0 %y_second_2.1 = (f32[64,1024]{1,0:T(8,128)S(1)}, f32[64,1024]{1,0:T(8,128)S(1)}, f32[64,1024]{1,0:T(8,128)S(1)}, f32[64,1024]{1,0:T(8,128)S(1)}) custom-call(bf16[4,256,1024]{2,1,0:T(8,128)(2,1)S(1)} %get-tuple-element.87.matrix_ref, f32[256,1024]{1,0:T(8,128)S(1)} %get-tuple-element.151.refs_0_.refs_4_.refs_16_, ...), custom_call_target="tpu_custom_call" | custom-call | flops 268435456 | bytes 1048576 | tf_op jit(solution)/shard_map/y_second_2/pallas_call | solution.py:242
  200.4 3.9 %collective-permute-done.44.refs_5_ = f32[32,1024]{1,0:T(8,128)S(1)} collective-permute-done((f32[32,1024]{1,0:T(8,128)S(1)}, f32[32,1024]{1,0:T(8,128)S(1)}, u32[]{:S(2)}, u32[]{:S(2)}) %collective-permute-start.44) | collective-permute-done | bytes 131104 | tf_op jit(solution)/shard_map/ppermute | solution.py:311
  204.3 2.4 %collective-permute-start.46 = (f32[64,1024]{1,0:T(8,128)S(1)}, f32[64,1024]{1,0:T(8,128)S(1)}, u32[]{:S(2)}, u32[]{:S(2)}) collective-permute-start(f32[64,1024]{1,0:T(8,128)S(1)} %get-tuple-element.166), channel_id=1, source_target_pairs={{0,8},{1,9},{2,10},{3,11},{4,12},{5,13},{6,14},{7,15},{8,0},{9,1},... | collective-permute-start | bytes 786440 | tf_op jit(solution)/shard_map/ppermute | solution.py:311
  208.9 5.8 %collective-permute-done.45.refs_1_ = f32[64,1024]{1,0:T(8,128)S(1)} collective-permute-done((f32[64,1024]{1,0:T(8,128)S(1)}, f32[64,1024]{1,0:T(8,128)S(1)}, u32[]{:S(2)}, u32[]{:S(2)}) %collective-permute-start.45) | collective-permute-done | bytes 262176 | tf_op jit(solution)/shard_map/ppermute | solution.py:311
  214.6 10.1 %collective-permute-done.46.refs_2_ = f32[64,1024]{1,0:T(8,128)S(1)} collective-permute-done((f32[64,1024]{1,0:T(8,128)S(1)}, f32[64,1024]{1,0:T(8,128)S(1)}, u32[]{:S(2)}, u32[]{:S(2)}) %collective-permute-start.46) | collective-permute-done | bytes 262176 | tf_op jit(solution)/shard_map/ppermute | solution.py:311
  224.8 5.6 %collective-permute-done.47.refs_3_ = f32[64,1024]{1,0:T(8,128)S(1)} collective-permute-done((f32[64,1024]{1,0:T(8,128)S(1)}, f32[64,1024]{1,0:T(8,128)S(1)}, u32[]{:S(2)}, u32[]{:S(2)}) %collective-permute-start.47) | collective-permute-done | bytes 262176 | tf_op jit(solution)/shard_map/ppermute | solution.py:311
  (103 shorter events, 43.1 us)
Async XLA Ops:
  4.3 37.0 %collective-permute-start.7 = (f32[200,1024]{1,0:T(8,128)}, f32[200,1024]{1,0:T(8,128)}, u32[]{:S(2)}, u32[]{:S(2)}) collective-permute-start(f32[200,1024]{1,0:T(8,128)} %get-tuple-element.90), channel_id=1, source_target_pairs={{0,2},{1,3},{2,0},{3,1},{4,6},{5,7},{6,4},{7,5},{8,10},{9,11},{10,... | collective-permute-start | bytes 2457608 | tf_op jit(solution)/shard_map/ppermute | solution.py:311
  5.8 35.4 %collective-permute-start.1 = (f32[200,1024]{1,0:T(8,128)}, f32[200,1024]{1,0:T(8,128)S(1)}, u32[]{:S(2)}, u32[]{:S(2)}) collective-permute-start(f32[200,1024]{1,0:T(8,128)} %get-tuple-element.90), channel_id=1, source_target_pairs={{0,4},{1,5},{2,6},{3,7},{4,0},{5,1},{6,2},{7,3},{8,12},{9,13},{10,... | collective-permute-start | bytes 2457608 | tf_op jit(solution)/shard_map/ppermute | solution.py:311
  7.4 46.5 %collective-permute-start = (f32[200,1024]{1,0:T(8,128)}, f32[200,1024]{1,0:T(8,128)S(1)}, u32[]{:S(2)}, u32[]{:S(2)}) collective-permute-start(f32[200,1024]{1,0:T(8,128)} %get-tuple-element.88), channel_id=1, source_target_pairs={{0,8},{1,9},{2,10},{3,11},{4,12},{5,13},{6,14},{7,15},{8,0},{9,1},... | collective-permute-start | bytes 2457608 | tf_op jit(solution)/shard_map/ppermute | solution.py:311
  7.7 46.1 %collective-permute-start.2 = (f32[200,1024]{1,0:T(8,128)S(1)}, f32[200,1024]{1,0:T(8,128)S(1)}, u32[]{:S(2)}, u32[]{:S(2)}) collective-permute-start(f32[200,1024]{1,0:T(8,128)S(1)} %get-tuple-element.112.refs_0_.refs_2_.refs_4_.refs_6_.refs_8_.refs_10_.refs_14_.refs_21_.refs_18_.refs_22_.refs_29_), channel_id=1, source_target_pairs={{0,2},{1,3},{2,0},{3,1},{4,6},{5,7},{6,4},{7,5},{8,10},{9,11},{10,... | collective-permute-start | bytes 2457608 | tf_op jit(solution)/shard_map/ppermute | solution.py:311
  41.3 31.8 %collective-permute-start.8 = (f32[200,1024]{1,0:T(8,128)}, f32[200,1024]{1,0:T(8,128)S(1)}, u32[]{:S(2)}, u32[]{:S(2)}) collective-permute-start(f32[200,1024]{1,0:T(8,128)} %collective-permute-done.7), channel_id=1, source_target_pairs={{0,4},{1,5},{2,6},{3,7},{4,0},{5,1},{6,2},{7,3},{8,12},{9,13},{10,... | collective-permute-start | bytes 2457608 | tf_op jit(solution)/shard_map/ppermute | solution.py:311
  43.6 17.2 %collective-permute-start.4 = (f32[136,1024]{1,0:T(8,128)S(1)}, f32[136,1024]{1,0:T(8,128)S(1)}, u32[]{:S(2)}, u32[]{:S(2)}) collective-permute-start(f32[136,1024]{1,0:T(8,128)S(1)} %copy-done.6), channel_id=1, source_target_pairs={{0,12},{1,13},{2,14},{3,15},{4,8},{5,9},{6,10},{7,11},{8,4},{9,5},... | collective-permute-start | bytes 1671176 | tf_op jit(solution)/shard_map/ppermute | solution.py:311
  53.9 19.2 %collective-permute-start.12 = (f32[200,1024]{1,0:T(8,128)S(1)}, f32[200,1024]{1,0:T(8,128)S(1)}, u32[]{:S(2)}, u32[]{:S(2)}) collective-permute-start(f32[200,1024]{1,0:T(8,128)S(1)} %collective-permute-done.refs_0_.refs_1_.refs_2_.refs_3_.refs_12_.refs_16_.refs_29_.refs_8_.refs_20_.refs_24_.refs_37_), channel_id=1, source_target_pairs={{0,2},{1,3},{2,0},{3,1},{4,6},{5,7},{6,4},{7,5},{8,10},{9,11},{10,... | collective-permute-start | bytes 2457608 | tf_op jit(solution)/shard_map/ppermute | solution.py:311
  54.4 19.6 %collective-permute-start.5 = (f32[200,1024]{1,0:T(8,128)S(1)}, f32[200,1024]{1,0:T(8,128)S(1)}, u32[]{:S(2)}, u32[]{:S(2)}) collective-permute-start(f32[200,1024]{1,0:T(8,128)S(1)} %get-tuple-element.112.refs_0_.refs_2_.refs_4_.refs_6_.refs_8_.refs_10_.refs_14_.refs_21_.refs_18_.refs_22_.refs_29_), channel_id=1, source_target_pairs={{0,1},{1,0},{2,3},{3,2},{4,5},{5,4},{6,7},{7,6},{8,9},{9,8},{10,11... | collective-permute-start | bytes 2457608 | tf_op jit(solution)/shard_map/ppermute | solution.py:311
  60.3 14.2 %collective-permute-start.6 = (f32[200,1024]{1,0:T(8,128)S(1)}, f32[200,1024]{1,0:T(8,128)S(1)}, u32[]{:S(2)}, u32[]{:S(2)}) collective-permute-start(f32[200,1024]{1,0:T(8,128)S(1)} %collective-permute-done.1.refs_1_.refs_3_.refs_5_.refs_7_.refs_9_.refs_11_.refs_15_.refs_25_.refs_19_.refs_23_.refs_33_), channel_id=1, source_target_pairs={{0,1},{1,0},{2,3},{3,2},{4,5},{5,4},{6,7},{7,6},{8,9},{9,8},{10,11... | collective-permute-start | bytes 2457608 | tf_op jit(solution)/shard_map/ppermute | solution.py:311
  60.9 13.7 %collective-permute-start.9 = (f32[200,1024]{1,0:T(8,128)S(1)}, f32[200,1024]{1,0:T(8,128)S(1)}, u32[]{:S(2)}, u32[]{:S(2)}) collective-permute-start(f32[200,1024]{1,0:T(8,128)S(1)} %collective-permute-done.2.refs_4_.refs_12_.refs_22_.refs_30_), channel_id=1, source_target_pairs={{0,1},{1,0},{2,3},{3,2},{4,5},{5,4},{6,7},{7,6},{8,9},{9,8},{10,11... | collective-permute-start | bytes 2457608 | tf_op jit(solution)/shard_map/ppermute | solution.py:311
  73.1 14.5 %collective-permute-start.3 = (f32[64,1024]{1,0:T(8,128)S(1)}, f32[64,1024]{1,0:T(8,128)S(1)}, u32[]{:S(2)}, u32[]{:S(2)}) collective-permute-start(f32[64,1024]{1,0:T(8,128)S(1)} %get-tuple-element.95), channel_id=1, source_target_pairs={{0,12},{1,13},{2,14},{3,15},{4,8},{5,9},{6,10},{7,11},{8,4},{9,5},... | collective-permute-start | bytes 786440 | tf_op jit(solution)/shard_map/ppermute | solution.py:311
  74.0 17.5 %collective-permute-start.15 = (f32[136,1024]{1,0:T(8,128)S(1)}, f32[136,1024]{1,0:T(8,128)S(1)}, u32[]{:S(2)}, u32[]{:S(2)}) collective-permute-start(f32[136,1024]{1,0:T(8,128)S(1)} %collective-permute-done.4.refs_0_.refs_1_.refs_2_.refs_13_.refs_17_.refs_33_.refs_9_.refs_21_.refs_25_.refs_41_), channel_id=1, source_target_pairs={{0,2},{1,3},{2,0},{3,1},{4,6},{5,7},{6,4},{7,5},{8,10},{9,11},{10,... | collective-permute-start | bytes 1671176 | tf_op jit(solution)/shard_map/ppermute | solution.py:311
  83.5 12.8 %collective-permute-start.14 = (f32[136,1024]{1,0:T(8,128)S(1)}, f32[136,1024]{1,0:T(8,128)S(1)}, u32[]{:S(2)}, u32[]{:S(2)}) collective-permute-start(f32[136,1024]{1,0:T(8,128)S(1)} %collective-permute-done.4.refs_0_.refs_1_.refs_2_.refs_13_.refs_17_.refs_33_.refs_9_.refs_21_.refs_25_.refs_41_), channel_id=1, source_target_pairs={{0,1},{1,0},{2,3},{3,2},{4,5},{5,4},{6,7},{7,6},{8,9},{9,8},{10,11... | collective-permute-start | bytes 1671176 | tf_op jit(solution)/shard_map/ppermute | solution.py:311
  92.0 9.8 %collective-permute-start.17 = (f32[64,1024]{1,0:T(8,128)S(1)}, f32[64,1024]{1,0:T(8,128)S(1)}, u32[]{:S(2)}, u32[]{:S(2)}) collective-permute-start(f32[64,1024]{1,0:T(8,128)S(1)} %collective-permute-done.3.refs_0_.refs_1_.refs_21_), channel_id=1, source_target_pairs={{0,2},{1,3},{2,0},{3,1},{4,6},{5,7},{6,4},{7,5},{8,10},{9,11},{10,... | collective-permute-start | bytes 786440 | tf_op jit(solution)/shard_map/ppermute | solution.py:311
  100.8 24.9 %collective-permute-start.24 = (f32[256,1024]{1,0:T(8,128)S(1)}, f32[256,1024]{1,0:T(8,128)S(1)}, u32[]{:S(2)}, u32[]{:S(2)}) collective-permute-start(f32[256,1024]{1,0:T(8,128)S(1)} %get-tuple-element.138.refs_0_.refs_4_.refs_8_.refs_9_.refs_12_.refs_17_), channel_id=1, source_target_pairs={{0,2},{1,3},{2,0},{3,1},{4,6},{5,7},{6,4},{7,5},{8,10},{9,11},{10,... | collective-permute-start | bytes 3145736 | tf_op jit(solution)/shard_map/ppermute | solution.py:311
  111.7 12.6 %collective-permute-start.22 = (f32[8,128]{1,0:T(8,128)S(1)}, f32[8,128]{1,0:T(8,128)S(1)}, u32[]{:S(2)}, u32[]{:S(2)}) collective-permute-start(f32[8,128]{1,0:T(8,128)S(1)} %fold_own.1.refs_0_), channel_id=1, source_target_pairs={{0,12},{1,13},{2,14},{3,15},{4,8},{5,9},{6,10},{7,11},{8,4},{9,5},... | collective-permute-start | bytes 12296 | tf_op jit(solution)/shard_map/ppermute | solution.py:311
  112.5 11.8 %collective-permute-start.21 = (f32[8,128]{1,0:T(8,128)S(1)}, f32[8,128]{1,0:T(8,128)S(1)}, u32[]{:S(2)}, u32[]{:S(2)}) collective-permute-start(f32[8,128]{1,0:T(8,128)S(1)} %fold_own.1.refs_0_), channel_id=1, source_target_pairs={{0,8},{1,9},{2,10},{3,11},{4,12},{5,13},{6,14},{7,15},{8,0},{9,1},... | collective-permute-start | bytes 12296 | tf_op jit(solution)/shard_map/ppermute | solution.py:311
  128.8 21.5 %collective-permute-start.34 = (f32[256,1024]{1,0:T(8,128)S(1)}, f32[256,1024]{1,0:T(8,128)S(1)}, u32[]{:S(2)}, u32[]{:S(2)}) collective-permute-start(f32[256,1024]{1,0:T(8,128)S(1)} %get-tuple-element.148.refs_1_.refs_0_.refs_4_.refs_16_), channel_id=1, source_target_pairs={{0,1},{1,0},{2,3},{3,2},{4,5},{5,4},{6,7},{7,6},{8,9},{9,8},{10,11... | collective-permute-start | bytes 3145736 | tf_op jit(solution)/shard_map/ppermute | solution.py:311
  130.4 30.3 %collective-permute-start.25 = (f32[256,1024]{1,0:T(8,128)S(1)}, f32[256,1024]{1,0:T(8,128)S(1)}, u32[]{:S(2)}, u32[]{:S(2)}) collective-permute-start(f32[256,1024]{1,0:T(8,128)S(1)} %get-tuple-element.148.refs_1_.refs_0_.refs_4_.refs_16_), channel_id=1, source_target_pairs={{0,2},{1,3},{2,0},{3,1},{4,6},{5,7},{6,4},{7,5},{8,10},{9,11},{10,... | collective-permute-start | bytes 3145736 | tf_op jit(solution)/shard_map/ppermute | solution.py:311
  138.2 15.4 %collective-permute-start.31 = (f32[64,1024]{1,0:T(8,128)S(1)}, f32[64,1024]{1,0:T(8,128)S(1)}, u32[]{:S(2)}, u32[]{:S(2)}) collective-permute-start(f32[64,1024]{1,0:T(8,128)S(1)} %get-tuple-element.142), channel_id=1, source_target_pairs={{0,4},{1,5},{2,6},{3,7},{4,0},{5,1},{6,2},{7,3},{8,12},{9,13},{10,... | collective-permute-start | bytes 786440 | tf_op jit(solution)/shard_map/ppermute | solution.py:311
  141.6 9.8 %collective-permute-start.32 = (f32[32,1024]{1,0:T(8,128)S(1)}, f32[32,1024]{1,0:T(8,128)S(1)}, u32[]{:S(2)}, u32[]{:S(2)}) collective-permute-start(f32[32,1024]{1,0:T(8,128)S(1)} %get-tuple-element.143), channel_id=1, source_target_pairs={{0,8},{1,9},{2,10},{3,11},{4,12},{5,13},{6,14},{7,15},{8,0},{9,1},... | collective-permute-start | bytes 393224 | tf_op jit(solution)/shard_map/ppermute | solution.py:311
  142.1 11.5 %collective-permute-start.33 = (f32[32,1024]{1,0:T(8,128)S(1)}, f32[32,1024]{1,0:T(8,128)S(1)}, u32[]{:S(2)}, u32[]{:S(2)}) collective-permute-start(f32[32,1024]{1,0:T(8,128)S(1)} %get-tuple-element.145), channel_id=1, source_target_pairs={{0,12},{1,13},{2,14},{3,15},{4,8},{5,9},{6,10},{7,11},{8,4},{9,5},... | collective-permute-start | bytes 393224 | tf_op jit(solution)/shard_map/ppermute | solution.py:311
  160.8 25.6 %collective-permute-start.35 = (f32[256,1024]{1,0:T(8,128)S(1)}, f32[256,1024]{1,0:T(8,128)S(1)}, u32[]{:S(2)}, u32[]{:S(2)}) collective-permute-start(f32[256,1024]{1,0:T(8,128)S(1)} %get-tuple-element.151.refs_0_.refs_4_.refs_16_), channel_id=1, source_target_pairs={{0,2},{1,3},{2,0},{3,1},{4,6},{5,7},{6,4},{7,5},{8,10},{9,11},{10,... | collective-permute-start | bytes 3145736 | tf_op jit(solution)/shard_map/ppermute | solution.py:311
  161.9 13.2 %collective-permute-start.40 = (f32[32,1024]{1,0:T(8,128)S(1)}, f32[32,1024]{1,0:T(8,128)S(1)}, u32[]{:S(2)}, u32[]{:S(2)}) collective-permute-start(f32[32,1024]{1,0:T(8,128)S(1)} %get-tuple-element.144), channel_id=1, source_target_pairs={{0,8},{1,9},{2,10},{3,11},{4,12},{5,13},{6,14},{7,15},{8,0},{9,1},... | collective-permute-start | bytes 393224 | tf_op jit(solution)/shard_map/ppermute | solution.py:311
  170.6 20.1 %collective-permute-start.37 = (f32[64,1024]{1,0:T(8,128)S(1)}, f32[64,1024]{1,0:T(8,128)S(1)}, u32[]{:S(2)}, u32[]{:S(2)}) collective-permute-start(f32[64,1024]{1,0:T(8,128)S(1)} %get-tuple-element.153), channel_id=1, source_target_pairs={{0,4},{1,5},{2,6},{3,7},{4,0},{5,1},{6,2},{7,3},{8,12},{9,13},{10,... | collective-permute-start | bytes 786440 | tf_op jit(solution)/shard_map/ppermute | solution.py:311
  172.6 14.9 %collective-permute-start.38 = (f32[32,1024]{1,0:T(8,128)S(1)}, f32[32,1024]{1,0:T(8,128)S(1)}, u32[]{:S(2)}, u32[]{:S(2)}) collective-permute-start(f32[32,1024]{1,0:T(8,128)S(1)} %get-tuple-element.154), channel_id=1, source_target_pairs={{0,8},{1,9},{2,10},{3,11},{4,12},{5,13},{6,14},{7,15},{8,0},{9,1},... | collective-permute-start | bytes 393224 | tf_op jit(solution)/shard_map/ppermute | solution.py:311
  175.1 15.6 %collective-permute-start.39 = (f32[32,1024]{1,0:T(8,128)S(1)}, f32[32,1024]{1,0:T(8,128)S(1)}, u32[]{:S(2)}, u32[]{:S(2)}) collective-permute-start(f32[32,1024]{1,0:T(8,128)S(1)} %get-tuple-element.155), channel_id=1, source_target_pairs={{0,12},{1,13},{2,14},{3,15},{4,8},{5,9},{6,10},{7,11},{8,4},{9,5},... | collective-permute-start | bytes 393224 | tf_op jit(solution)/shard_map/ppermute | solution.py:311
  177.0 14.9 %collective-permute-start.23 = (f32[256,1024]{1,0:T(8,128)S(1)}, f32[256,1024]{1,0:T(8,128)S(1)}, u32[]{:S(2)}, u32[]{:S(2)}) collective-permute-start(f32[256,1024]{1,0:T(8,128)S(1)} %get-tuple-element.151.refs_0_.refs_4_.refs_16_), channel_id=1, source_target_pairs={{0,1},{1,0},{2,3},{3,2},{4,5},{5,4},{6,7},{7,6},{8,9},{9,8},{10,11... | collective-permute-start | bytes 3145736 | tf_op jit(solution)/shard_map/ppermute | solution.py:311
  190.9 13.4 %collective-permute-start.44 = (f32[32,1024]{1,0:T(8,128)S(1)}, f32[32,1024]{1,0:T(8,128)S(1)}, u32[]{:S(2)}, u32[]{:S(2)}) collective-permute-start(f32[32,1024]{1,0:T(8,128)S(1)} %get-tuple-element.163), channel_id=1, source_target_pairs={{0,12},{1,13},{2,14},{3,15},{4,8},{5,9},{6,10},{7,11},{8,4},{9,5},... | collective-permute-start | bytes 393224 | tf_op jit(solution)/shard_map/ppermute | solution.py:311
  204.3 10.3 %collective-permute-start.45 = (f32[64,1024]{1,0:T(8,128)S(1)}, f32[64,1024]{1,0:T(8,128)S(1)}, u32[]{:S(2)}, u32[]{:S(2)}) collective-permute-start(f32[64,1024]{1,0:T(8,128)S(1)} %get-tuple-element.165), channel_id=1, source_target_pairs={{0,4},{1,5},{2,6},{3,7},{4,0},{5,1},{6,2},{7,3},{8,12},{9,13},{10,... | collective-permute-start | bytes 786440 | tf_op jit(solution)/shard_map/ppermute | solution.py:311
  204.3 20.4 %collective-permute-start.46 = (f32[64,1024]{1,0:T(8,128)S(1)}, f32[64,1024]{1,0:T(8,128)S(1)}, u32[]{:S(2)}, u32[]{:S(2)}) collective-permute-start(f32[64,1024]{1,0:T(8,128)S(1)} %get-tuple-element.166), channel_id=1, source_target_pairs={{0,8},{1,9},{2,10},{3,11},{4,12},{5,13},{6,14},{7,15},{8,0},{9,1},... | collective-permute-start | bytes 786440 | tf_op jit(solution)/shard_map/ppermute | solution.py:311
  206.8 23.6 %collective-permute-start.47 = (f32[64,1024]{1,0:T(8,128)S(1)}, f32[64,1024]{1,0:T(8,128)S(1)}, u32[]{:S(2)}, u32[]{:S(2)}) collective-permute-start(f32[64,1024]{1,0:T(8,128)S(1)} %get-tuple-element.167), channel_id=1, source_target_pairs={{0,12},{1,13},{2,14},{3,15},{4,8},{5,9},{6,10},{7,11},{8,4},{9,5},... | collective-permute-start | bytes 786440 | tf_op jit(solution)/shard_map/ppermute | solution.py:311
  (23 other events, 139.0 us)

commit v12 on v11

--- a/solution.py
+++ b/solution.py
@@ -469,16 +469,19 @@
     ends[1] = list(second_step(1))
     x_terms[0] = along_x([piece(after(middle[0], ends[1]))], [], along_x_matrix, "x_second_0", 1)
     gone = leave(1, False)
+    leave(1, True)
+    middle_others[0] = after(middle_others[0], x_terms[0], gone, middle_twin[0])
+    middle_others[2] = across_chips(after(middle[2], middle_others[0]))
     x_terms[2] = along_x(
-        [piece(after(middle[2], x_terms[0], gone, middle_twin[0]))], [piece(middle[0])], along_x_matrix, "x_second_2", 1
+        [piece(after(middle[2], middle_others[0]))], [piece(middle[0])], along_x_matrix, "x_second_2", 36
     )
-    leave(1, True)
-    middle_others[0] = after(middle_others[0], x_terms[2])
-    middle_others[2] = across_chips(after(middle[2], middle_others[0]))
     middle_far[0] = across_cores(middle_others[0])
+    middle_far[0] = after(middle_far[0], x_terms[2])
     ends[0] = list(second_step(0))
+    ends[1] = after(ends[1], ends[0])
+    out = put(1, None)
+    ends[0][1:] = after(ends[0][1:], [ends[1][place] for place, spot in enumerate(spots[1]) if spot[1]])
     gone = leave(0, False)
-    out = put(1, None)
     middle_others[2] = after(middle_others[2], gone, out)
     rest = leave(0, True)
     middle_far[2] = across_cores(middle_others[2])

time: 232 us -> 232 us (level)
  waiting for transfers between devices: 81.5 us -> 78.3 us
  starting transfers between devices: 39.9 us -> 42.7 us
    ppermute x48, waiting for transfers between devices: 81.5 us -> 78.3 us  [swap(): return lax.ppermute(x, 'row', [(r, r ^ distance) for r in range(devices)])]
    ppermute x48, starting transfers between devices: 39.9 us -> 42.7 us  [swap(): return lax.ppermute(x, 'row', [(r, r ^ distance) for r in range(devices)])]
  transfers between devices with their start and end apart: 48 -> 48, of which waited for: 18 -> 16; matrix products, arithmetic and copies ran while one was open for 0% -> 0% of each run, Pallas kernels for 43% -> 43%
where the time goes in v12:
time: 232 us; the launch traced here: 231 us
  Pallas kernels  102 us (44%)
  waiting for transfers between devices  78.3 us (34%)
  starting transfers between devices  42.7 us (18%)
  local copies, waits for them, and re-layouts  7.18 us (3%)
    ppermute x48, waiting for transfers between devices, swap(): return lax.ppermute(x, 'row', [(r, r ^ distance) for r in range(devices)])  78.3 us
    pallas_call x9, Pallas kernels, y_call(): pl.pallas_call(functools.partial(kernel, tuple(counts)), grid=(length //...  45.9 us
    pallas_call x7, Pallas kernels, along_x(): pl.pallas_call(functools.partial(along_x_kernel, (len(fields), len(carrie...  44.7 us
    ppermute x48, starting transfers between devices, swap(): return lax.ppermute(x, 'row', [(r, r ^ distance) for r in range(devices)])  42.7 us
    pallas_call x1, Pallas kernels, prepare_matrices(): pl.pallas_call(functools.partial(matrices_kernel, count), grid_spec=pltpu...  7.16 us
    unnamed x14, local copies, waits for them, and re-layouts  7.09 us
  transfers between devices with their start and end apart: 48, of which 16 were waited for; matrix products, arithmetic and copies ran while one was open for 0% of the time, Pallas kernels for 43%

profile of v12, /device:TPU:18, one launch (start us, length us, event | category | flops | bytes accessed | tf_op | source)
XLA Modules:
  0.0 231.1 jit_solution(12892980209586818026)
XLA Ops:
  10.6 2.2 copy-done.4
  12.8 7.2 %shard_map.37 = (bf16[4,1024,1024]{2,1,0:T(8,128)(2,1)S(1)}, bf16[4,256,1024]{2,1,0:T(8,128)(2,1)S(1)}) custom-call(s32[16]{0:T(128)S(1)} %stack.74.order_ref, s32[4]{0:T(128)S(1)} %pad_add_fusion.own_ref, f32[1024,1024]{1,0:T(8,128)S(1)} %copy-done.3, f32[1024,1024]{1,0:T(8,128)S(1)} %copy-done.3, f32[1024,1024]{1,0:T(8,128)S(1)} %copy-done.4, ...), custom_call_target="tpu_custom_call" | custom-call | flops 17179869184 | bytes 33554432 | tf_op jit(solution)/shard_map/pallas_call | solution.py:63
  20.0 21.3 %collective-permute-done.1.refs_1_.refs_3_.refs_5_.refs_7_.refs_9_.refs_11_.refs_15_.refs_25_.refs_19_.refs_23_.refs_33_ = f32[200,1024]{1,0:T(8,128)S(1)} collective-permute-done((f32[200,1024]{1,0:T(8,128)}, f32[200,1024]{1,0:T(8,128)S(1)}, u32[]{:S(2)}, u32[]{:S(2)}) %collective-permute-start.1) | collective-permute-done | bytes 819232 | tf_op jit(solution)/shard_map/ppermute | solution.py:311
  41.3 2.4 %collective-permute-start.8 = (f32[200,1024]{1,0:T(8,128)}, f32[200,1024]{1,0:T(8,128)S(1)}, u32[]{:S(2)}, u32[]{:S(2)}) collective-permute-start(f32[200,1024]{1,0:T(8,128)} %collective-permute-done.7), channel_id=1, source_target_pairs={{0,4},{1,5},{2,6},{3,7},{4,0},{5,1},{6,2},{7,3},{8,12},{9,13},{10,... | collective-permute-start | bytes 2457608 | tf_op jit(solution)/shard_map/ppermute | solution.py:311
  44.1 9.8 %x_first_near.1.refs_18_.refs_26_ = f32[384,1024]{1,0:T(8,128)S(1)} custom-call(f32[200,1024]{1,0:T(8,128)S(1)} %get-tuple-element.123.refs_0_.refs_2_.refs_4_.refs_6_.refs_8_.refs_10_.refs_14_.refs_21_.refs_18_.refs_22_.refs_29_, ...), custom_call_target="tpu_custom_call" | custom-call | flops 402653184 | bytes 1572864 | tf_op jit(solution)/shard_map/x_first_near/pallas_call | solution.py:163
  54.5 5.8 %x_first_2.1.refs_19_.refs_27_ = f32[192,1024]{1,0:T(8,128)S(1)} custom-call(f32[200,1024]{1,0:T(8,128)S(1)} %collective-permute-done.refs_0_.refs_1_.refs_2_.refs_3_.refs_12_.refs_16_.refs_29_.refs_8_.refs_20_.refs_24_.refs_37_, ...), custom_call_target="tpu_custom_call" | custom-call | flops 201326592 | bytes 786432 | tf_op jit(solution)/shard_map/x_first_2/pallas_call | solution.py:163
  60.9 12.2 %collective-permute-done.8.refs_5_.refs_13_.refs_26_.refs_34_ = f32[200,1024]{1,0:T(8,128)S(1)} collective-permute-done((f32[200,1024]{1,0:T(8,128)}, f32[200,1024]{1,0:T(8,128)S(1)}, u32[]{:S(2)}, u32[]{:S(2)}) %collective-permute-start.8) | collective-permute-done | bytes 819232 | tf_op jit(solution)/shard_map/ppermute | solution.py:311
  75.4 3.6 %y_first_near_1.1 = (f32[256,1024]{1,0:T(8,128)S(1)}, f32[256,1024]{1,0:T(8,128)S(1)}) custom-call(bf16[4,256,1024]{2,1,0:T(8,128)(2,1)S(1)} %get-tuple-element.98.matrix_ref, f32[200,1024]{1,0:T(8,128)S(1)} %get-tuple-element.123.refs_0_.refs_2_.refs_4_.refs_6_.refs_8_.refs_10_.refs_14_.refs_21_.refs_18_.refs_22_.refs_29_, ...), custom_call_target="tpu_custom_call" | custom-call | flops 4831838208 | bytes 1048576 | tf_op jit(solution)/shard_map/y_first_near_1/pallas_call | solution.py:242
  79.0 4.5 %x_first_last.1.refs_20_.refs_28_ = f32[128,1024]{1,0:T(8,128)S(1)} custom-call(f32[136,1024]{1,0:T(8,128)S(1)} %collective-permute-done.4.refs_0_.refs_1_.refs_2_.refs_13_.refs_17_.refs_33_.refs_9_.refs_21_.refs_25_.refs_41_, f32[136,1024]{1,0:T(8,128)S(1)} %collective-permute-done.4.refs_0_.refs_1_.refs_2_.refs_13_.refs_17_.refs_33_.refs_9_.refs_21_.refs_25_.refs_41_, ...), custom_call_target="tpu_custom_call" | custom-call | flops 4831838208 | bytes 524288 | tf_op jit(solution)/shard_map/x_first_last/pallas_call | solution.py:163
  83.7 3.9 %y_first_near_0.1 = (f32[256,1024]{1,0:T(8,128)S(1)}, f32[256,1024]{1,0:T(8,128)S(1)}) custom-call(bf16[4,256,1024]{2,1,0:T(8,128)(2,1)S(1)} %get-tuple-element.98.matrix_ref, f32[200,1024]{1,0:T(8,128)S(1)} %get-tuple-element.123.refs_0_.refs_2_.refs_4_.refs_6_.refs_8_.refs_10_.refs_14_.refs_21_.refs_18_.refs_22_.refs_29_, ...), custom_call_target="tpu_custom_call" | custom-call | flops 4831838208 | bytes 1048576 | tf_op jit(solution)/shard_map/y_first_near_0/pallas_call | solution.py:242
  87.6 3.9 %y_first_near_2.1 = (f32[256,1024]{1,0:T(8,128)S(1)}, f32[256,1024]{1,0:T(8,128)S(1)}) custom-call(bf16[4,256,1024]{2,1,0:T(8,128)(2,1)S(1)} %get-tuple-element.98.matrix_ref, f32[200,1024]{1,0:T(8,128)S(1)} %get-tuple-element.123.refs_0_.refs_2_.refs_4_.refs_6_.refs_8_.refs_10_.refs_14_.refs_21_.refs_18_.refs_22_.refs_29_, ...), custom_call_target="tpu_custom_call" | custom-call | flops 4831838208 | bytes 1048576 | tf_op jit(solution)/shard_map/y_first_near_2/pallas_call | solution.py:242
  93.1 3.3 %x_first_tail.1.refs_28_ = f32[64,1024]{1,0:T(8,128)S(1)} custom-call(f32[64,1024]{1,0:T(8,128)S(1)} %collective-permute-done.3.refs_0_.refs_1_.refs_21_, f32[136,1024]{1,0:T(8,128)S(1)} %collective-permute-done.4.refs_0_.refs_1_.refs_2_.refs_13_.refs_17_.refs_33_.refs_9_.refs_21_.refs_25_.refs_41_, ...), custom_call_target="tpu_custom_call" | custom-call | flops 2415919104 | bytes 262144 | tf_op jit(solution)/shard_map/x_first_tail/pallas_call | solution.py:163
  96.4 4.4 %y_first_far_1.1 = (f32[256,1024]{1,0:T(8,128)S(1)}, f32[256,1024]{1,0:T(8,128)S(1)}, f32[8,1024]{1,0:T(8,128)S(1)}) custom-call(bf16[4,256,1024]{2,1,0:T(8,128)(2,1)S(1)} %get-tuple-element.98.matrix_ref, f32[200,1024]{1,0:T(8,128)S(1)} %collective-permute-done.refs_0_.refs_1_.refs_2_.refs_3_.refs_12_.refs_16_.refs_29_.refs_8_.refs_20_.refs_24_.refs_37_, ...), custom_call_target="tpu_custom_call" | custom-call | flops 4831838208 | bytes 1048576 | tf_op jit(solution)/shard_map/y_first_far_1/pallas_call | solution.py:242
  102.3 4.6 %y_first_far_0.1 = (f32[256,1024]{1,0:T(8,128)S(1)}, f32[256,1024]{1,0:T(8,128)S(1)}, f32[8,1024]{1,0:T(8,128)S(1)}) custom-call(bf16[4,256,1024]{2,1,0:T(8,128)(2,1)S(1)} %get-tuple-element.98.matrix_ref, f32[200,1024]{1,0:T(8,128)S(1)} %collective-permute-done.refs_0_.refs_1_.refs_2_.refs_3_.refs_12_.refs_16_.refs_29_.refs_8_.refs_20_.refs_24_.refs_37_, ...), custom_call_target="tpu_custom_call" | custom-call | flops 4831838208 | bytes 1048576 | tf_op jit(solution)/shard_map/y_first_far_0/pallas_call | solution.py:242
  106.9 4.7 %y_first_far_2.1 = (f32[256,1024]{1,0:T(8,128)S(1)}, f32[256,1024]{1,0:T(8,128)S(1)}, f32[8,1024]{1,0:T(8,128)S(1)}) custom-call(bf16[4,256,1024]{2,1,0:T(8,128)(2,1)S(1)} %get-tuple-element.98.matrix_ref, f32[200,1024]{1,0:T(8,128)S(1)} %collective-permute-done.refs_0_.refs_1_.refs_2_.refs_3_.refs_12_.refs_16_.refs_29_.refs_8_.refs_20_.refs_24_.refs_37_, ...), custom_call_target="tpu_custom_call" | custom-call | flops 4831838208 | bytes 1048576 | tf_op jit(solution)/shard_map/y_first_far_2/pallas_call | solution.py:242
  112.5 4.6 %collective-permute-start.21 = (f32[8,128]{1,0:T(8,128)S(1)}, f32[8,128]{1,0:T(8,128)S(1)}, u32[]{:S(2)}, u32[]{:S(2)}) collective-permute-start(f32[8,128]{1,0:T(8,128)S(1)} %fold_own.1.refs_0_), channel_id=1, source_target_pairs={{0,8},{1,9},{2,10},{3,11},{4,12},{5,13},{6,14},{7,15},{8,0},{9,1},... | collective-permute-start | bytes 12296 | tf_op jit(solution)/shard_map/ppermute | solution.py:311
  117.1 7.1 %x_second_1.1.refs_10_ = f32[256,1024]{1,0:T(8,128)S(1)} custom-call(f32[256,1024]{1,0:T(8,128)S(1)} %get-tuple-element.149.refs_0_.refs_4_.refs_8_.refs_9_.refs_12_.refs_17_, f32[256,1024]{1,0:T(8,128)S(1)} %get-tuple-element.159.refs_1_.refs_0_.refs_4_.refs_16_, bf16[4,1024,1024]{2,1,0:T(8,128)(2,1)S(1)} %get-tuple-element.102.refs_8_.refs_4_.refs_3_.refs_2_.refs_1_), custom_call_target="tpu_custom_call" | custom-call | flops 9663676416 | bytes 1048576 | tf_op jit(solution)/shard_map/x_second_1/pallas_call | solution.py:163
  131.5 6.6 %y_second_1.1 = (f32[64,1024]{1,0:T(8,128)S(1)}, f32[64,1024]{1,0:T(8,128)S(1)}, f32[32,1024]{1,0:T(8,128)S(1)}, f32[32,1024]{1,0:T(8,128)S(1)}, f32[32,1024]{1,0:T(8,128)S(1)}, /*index=5*/f32[32,1024]{1,0:T(8,128)S(1)}) custom-call(bf16[4,256,1024]{2,1,0:T(8,128)(2,1)S(1)} %get-tuple-element.98.matrix_ref, ...), custom_call_target="tpu_custom_call" | custom-call | flops 9663676416 | bytes 1048576 | tf_op jit(solution)/shard_map/y_second_1/pallas_call | solution.py:242
  138.2 3.5 %collective-permute-start.31 = (f32[64,1024]{1,0:T(8,128)S(1)}, f32[64,1024]{1,0:T(8,128)S(1)}, u32[]{:S(2)}, u32[]{:S(2)}) collective-permute-start(f32[64,1024]{1,0:T(8,128)S(1)} %get-tuple-element.153), channel_id=1, source_target_pairs={{0,4},{1,5},{2,6},{3,7},{4,0},{5,1},{6,2},{7,3},{8,12},{9,13},{10,... | collective-permute-start | bytes 786440 | tf_op jit(solution)/shard_map/ppermute | solution.py:311
  143.2 7.1 %x_second_0.1.refs_18_ = f32[256,1024]{1,0:T(8,128)S(1)} custom-call(f32[256,1024]{1,0:T(8,128)S(1)} %get-tuple-element.159.refs_1_.refs_0_.refs_4_.refs_16_, bf16[4,1024,1024]{2,1,0:T(8,128)(2,1)S(1)} %get-tuple-element.102.refs_8_.refs_4_.refs_3_.refs_2_.refs_1_), custom_call_target="tpu_custom_call" | custom-call | flops 268435456 | bytes 1048576 | tf_op jit(solution)/shard_map/x_second_0/pallas_call | solution.py:163
  150.3 4.1 %collective-permute-done.25.refs_2_.refs_6_ = f32[256,1024]{1,0:T(8,128)S(1)} collective-permute-done((f32[256,1024]{1,0:T(8,128)S(1)}, f32[256,1024]{1,0:T(8,128)S(1)}, u32[]{:S(2)}, u32[]{:S(2)}) %collective-permute-start.25) | collective-permute-done | bytes 1048608 | tf_op jit(solution)/shard_map/ppermute | solution.py:311
  154.5 3.9 %collective-permute-start.37 = (f32[32,1024]{1,0:T(8,128)S(1)}, f32[32,1024]{1,0:T(8,128)S(1)}, u32[]{:S(2)}, u32[]{:S(2)}) collective-permute-start(f32[32,1024]{1,0:T(8,128)S(1)} %get-tuple-element.155), channel_id=1, source_target_pairs={{0,8},{1,9},{2,10},{3,11},{4,12},{5,13},{6,14},{7,15},{8,0},{9,1},... | collective-permute-start | bytes 393224 | tf_op jit(solution)/shard_map/ppermute | solution.py:311
  160.5 7.1 %x_second_2.1.refs_18_ = f32[256,1024]{1,0:T(8,128)S(1)} custom-call(f32[256,1024]{1,0:T(8,128)S(1)} %get-tuple-element.161.refs_0_.refs_4_.refs_16_, f32[256,1024]{1,0:T(8,128)S(1)} %get-tuple-element.159.refs_1_.refs_0_.refs_4_.refs_16_, bf16[4,1024,1024]{2,1,0:T(8,128)(2,1)S(1)} %get-tuple-element.102.refs_8_.refs_4_.refs_3_.refs_2_.refs_1_), custom_call_target="tpu_custom_call" | custom-call | flops 9663676416 | bytes 1048576 | tf_op jit(solution)/shard_map/x_second_2/pallas_call | solution.py:163
  167.6 7.2 %y_second_0.1 = (f32[64,1024]{1,0:T(8,128)S(1)}, f32[64,1024]{1,0:T(8,128)S(1)}, f32[32,1024]{1,0:T(8,128)S(1)}, f32[32,1024]{1,0:T(8,128)S(1)}, f32[32,1024]{1,0:T(8,128)S(1)}, /*index=5*/f32[32,1024]{1,0:T(8,128)S(1)}) custom-call(bf16[4,256,1024]{2,1,0:T(8,128)(2,1)S(1)} %get-tuple-element.98.matrix_ref, ...), custom_call_target="tpu_custom_call" | custom-call | flops 268435456 | bytes 1048576 | tf_op jit(solution)/shard_map/y_second_0/pallas_call | solution.py:242
  179.4 5.0 %collective-permute-done.35.refs_2_.refs_6_ = f32[256,1024]{1,0:T(8,128)S(1)} collective-permute-done((f32[256,1024]{1,0:T(8,128)S(1)}, f32[256,1024]{1,0:T(8,128)S(1)}, u32[]{:S(2)}, u32[]{:S(2)}) %collective-permute-start.35) | collective-permute-done | bytes 1048608 | tf_op jit(solution)/shard_map/ppermute | solution.py:311
  184.4 3.1 %collective-permute-done.40.refs_2_ = f32[32,1024]{1,0:T(8,128)S(1)} collective-permute-done((f32[32,1024]{1,0:T(8,128)S(1)}, f32[32,1024]{1,0:T(8,128)S(1)}, u32[]{:S(2)}, u32[]{:S(2)}) %collective-permute-start.40) | collective-permute-done | bytes 131104 | tf_op jit(solution)/shard_map/ppermute | solution.py:311
  192.2 7.0 %y_second_2.1 = (f32[64,1024]{1,0:T(8,128)S(1)}, f32[64,1024]{1,0:T(8,128)S(1)}, f32[64,1024]{1,0:T(8,128)S(1)}, f32[64,1024]{1,0:T(8,128)S(1)}) custom-call(bf16[4,256,1024]{2,1,0:T(8,128)(2,1)S(1)} %get-tuple-element.98.matrix_ref, f32[256,1024]{1,0:T(8,128)S(1)} %get-tuple-element.161.refs_0_.refs_4_.refs_16_, ...), custom_call_target="tpu_custom_call" | custom-call | flops 268435456 | bytes 1048576 | tf_op jit(solution)/shard_map/y_second_2/pallas_call | solution.py:242
  200.2 3.9 %collective-permute-done.44.refs_5_ = f32[32,1024]{1,0:T(8,128)S(1)} collective-permute-done((f32[32,1024]{1,0:T(8,128)S(1)}, f32[32,1024]{1,0:T(8,128)S(1)}, u32[]{:S(2)}, u32[]{:S(2)}) %collective-permute-start.44) | collective-permute-done | bytes 131104 | tf_op jit(solution)/shard_map/ppermute | solution.py:311
  204.1 2.5 %collective-permute-start.46 = (f32[64,1024]{1,0:T(8,128)S(1)}, f32[64,1024]{1,0:T(8,128)S(1)}, u32[]{:S(2)}, u32[]{:S(2)}) collective-permute-start(f32[64,1024]{1,0:T(8,128)S(1)} %get-tuple-element.189), channel_id=1, source_target_pairs={{0,8},{1,9},{2,10},{3,11},{4,12},{5,13},{6,14},{7,15},{8,0},{9,1},... | collective-permute-start | bytes 786440 | tf_op jit(solution)/shard_map/ppermute | solution.py:311
  208.6 5.7 %collective-permute-done.45.refs_1_ = f32[64,1024]{1,0:T(8,128)S(1)} collective-permute-done((f32[64,1024]{1,0:T(8,128)S(1)}, f32[64,1024]{1,0:T(8,128)S(1)}, u32[]{:S(2)}, u32[]{:S(2)}) %collective-permute-start.45) | collective-permute-done | bytes 262176 | tf_op jit(solution)/shard_map/ppermute | solution.py:311
  214.3 10.2 %collective-permute-done.46.refs_2_ = f32[64,1024]{1,0:T(8,128)S(1)} collective-permute-done((f32[64,1024]{1,0:T(8,128)S(1)}, f32[64,1024]{1,0:T(8,128)S(1)}, u32[]{:S(2)}, u32[]{:S(2)}) %collective-permute-start.46) | collective-permute-done | bytes 262176 | tf_op jit(solution)/shard_map/ppermute | solution.py:311
  224.6 5.5 %collective-permute-done.47.refs_3_ = f32[64,1024]{1,0:T(8,128)S(1)} collective-permute-done((f32[64,1024]{1,0:T(8,128)S(1)}, f32[64,1024]{1,0:T(8,128)S(1)}, u32[]{:S(2)}, u32[]{:S(2)}) %collective-permute-start.47) | collective-permute-done | bytes 262176 | tf_op jit(solution)/shard_map/ppermute | solution.py:311
  (103 shorter events, 43.0 us)
Async XLA Ops:
  4.3 37.0 %collective-permute-start.7 = (f32[200,1024]{1,0:T(8,128)}, f32[200,1024]{1,0:T(8,128)}, u32[]{:S(2)}, u32[]{:S(2)}) collective-permute-start(f32[200,1024]{1,0:T(8,128)} %get-tuple-element.101), channel_id=1, source_target_pairs={{0,2},{1,3},{2,0},{3,1},{4,6},{5,7},{6,4},{7,5},{8,10},{9,11},{10,... | collective-permute-start | bytes 2457608 | tf_op jit(solution)/shard_map/ppermute | solution.py:311
  5.8 35.4 %collective-permute-start.1 = (f32[200,1024]{1,0:T(8,128)}, f32[200,1024]{1,0:T(8,128)S(1)}, u32[]{:S(2)}, u32[]{:S(2)}) collective-permute-start(f32[200,1024]{1,0:T(8,128)} %get-tuple-element.101), channel_id=1, source_target_pairs={{0,4},{1,5},{2,6},{3,7},{4,0},{5,1},{6,2},{7,3},{8,12},{9,13},{10,... | collective-permute-start | bytes 2457608 | tf_op jit(solution)/shard_map/ppermute | solution.py:311
  7.4 46.5 %collective-permute-start = (f32[200,1024]{1,0:T(8,128)}, f32[200,1024]{1,0:T(8,128)S(1)}, u32[]{:S(2)}, u32[]{:S(2)}) collective-permute-start(f32[200,1024]{1,0:T(8,128)} %get-tuple-element.99), channel_id=1, source_target_pairs={{0,8},{1,9},{2,10},{3,11},{4,12},{5,13},{6,14},{7,15},{8,0},{9,1},... | collective-permute-start | bytes 2457608 | tf_op jit(solution)/shard_map/ppermute | solution.py:311
  7.7 46.1 %collective-permute-start.2 = (f32[200,1024]{1,0:T(8,128)S(1)}, f32[200,1024]{1,0:T(8,128)S(1)}, u32[]{:S(2)}, u32[]{:S(2)}) collective-permute-start(f32[200,1024]{1,0:T(8,128)S(1)} %get-tuple-element.123.refs_0_.refs_2_.refs_4_.refs_6_.refs_8_.refs_10_.refs_14_.refs_21_.refs_18_.refs_22_.refs_29_), channel_id=1, source_target_pairs={{0,2},{1,3},{2,0},{3,1},{4,6},{5,7},{6,4},{7,5},{8,10},{9,11},{10,... | collective-permute-start | bytes 2457608 | tf_op jit(solution)/shard_map/ppermute | solution.py:311
  41.3 31.8 %collective-permute-start.8 = (f32[200,1024]{1,0:T(8,128)}, f32[200,1024]{1,0:T(8,128)S(1)}, u32[]{:S(2)}, u32[]{:S(2)}) collective-permute-start(f32[200,1024]{1,0:T(8,128)} %collective-permute-done.7), channel_id=1, source_target_pairs={{0,4},{1,5},{2,6},{3,7},{4,0},{5,1},{6,2},{7,3},{8,12},{9,13},{10,... | collective-permute-start | bytes 2457608 | tf_op jit(solution)/shard_map/ppermute | solution.py:311
  43.6 17.2 %collective-permute-start.4 = (f32[136,1024]{1,0:T(8,128)S(1)}, f32[136,1024]{1,0:T(8,128)S(1)}, u32[]{:S(2)}, u32[]{:S(2)}) collective-permute-start(f32[136,1024]{1,0:T(8,128)S(1)} %copy-done.6), channel_id=1, source_target_pairs={{0,12},{1,13},{2,14},{3,15},{4,8},{5,9},{6,10},{7,11},{8,4},{9,5},... | collective-permute-start | bytes 1671176 | tf_op jit(solution)/shard_map/ppermute | solution.py:311
  53.9 19.2 %collective-permute-start.12 = (f32[200,1024]{1,0:T(8,128)S(1)}, f32[200,1024]{1,0:T(8,128)S(1)}, u32[]{:S(2)}, u32[]{:S(2)}) collective-permute-start(f32[200,1024]{1,0:T(8,128)S(1)} %collective-permute-done.refs_0_.refs_1_.refs_2_.refs_3_.refs_12_.refs_16_.refs_29_.refs_8_.refs_20_.refs_24_.refs_37_), channel_id=1, source_target_pairs={{0,2},{1,3},{2,0},{3,1},{4,6},{5,7},{6,4},{7,5},{8,10},{9,11},{10,... | collective-permute-start | bytes 2457608 | tf_op jit(solution)/shard_map/ppermute | solution.py:311
  54.4 19.6 %collective-permute-start.5 = (f32[200,1024]{1,0:T(8,128)S(1)}, f32[200,1024]{1,0:T(8,128)S(1)}, u32[]{:S(2)}, u32[]{:S(2)}) collective-permute-start(f32[200,1024]{1,0:T(8,128)S(1)} %get-tuple-element.123.refs_0_.refs_2_.refs_4_.refs_6_.refs_8_.refs_10_.refs_14_.refs_21_.refs_18_.refs_22_.refs_29_), channel_id=1, source_target_pairs={{0,1},{1,0},{2,3},{3,2},{4,5},{5,4},{6,7},{7,6},{8,9},{9,8},{10,11... | collective-permute-start | bytes 2457608 | tf_op jit(solution)/shard_map/ppermute | solution.py:311
  60.3 14.2 %collective-permute-start.6 = (f32[200,1024]{1,0:T(8,128)S(1)}, f32[200,1024]{1,0:T(8,128)S(1)}, u32[]{:S(2)}, u32[]{:S(2)}) collective-permute-start(f32[200,1024]{1,0:T(8,128)S(1)} %collective-permute-done.1.refs_1_.refs_3_.refs_5_.refs_7_.refs_9_.refs_11_.refs_15_.refs_25_.refs_19_.refs_23_.refs_33_), channel_id=1, source_target_pairs={{0,1},{1,0},{2,3},{3,2},{4,5},{5,4},{6,7},{7,6},{8,9},{9,8},{10,11... | collective-permute-start | bytes 2457608 | tf_op jit(solution)/shard_map/ppermute | solution.py:311
  60.9 13.7 %collective-permute-start.9 = (f32[200,1024]{1,0:T(8,128)S(1)}, f32[200,1024]{1,0:T(8,128)S(1)}, u32[]{:S(2)}, u32[]{:S(2)}) collective-permute-start(f32[200,1024]{1,0:T(8,128)S(1)} %collective-permute-done.2.refs_4_.refs_12_.refs_22_.refs_30_), channel_id=1, source_target_pairs={{0,1},{1,0},{2,3},{3,2},{4,5},{5,4},{6,7},{7,6},{8,9},{9,8},{10,11... | collective-permute-start | bytes 2457608 | tf_op jit(solution)/shard_map/ppermute | solution.py:311
  73.1 14.5 %collective-permute-start.3 = (f32[64,1024]{1,0:T(8,128)S(1)}, f32[64,1024]{1,0:T(8,128)S(1)}, u32[]{:S(2)}, u32[]{:S(2)}) collective-permute-start(f32[64,1024]{1,0:T(8,128)S(1)} %get-tuple-element.106), channel_id=1, source_target_pairs={{0,12},{1,13},{2,14},{3,15},{4,8},{5,9},{6,10},{7,11},{8,4},{9,5},... | collective-permute-start | bytes 786440 | tf_op jit(solution)/shard_map/ppermute | solution.py:311
  74.0 17.5 %collective-permute-start.15 = (f32[136,1024]{1,0:T(8,128)S(1)}, f32[136,1024]{1,0:T(8,128)S(1)}, u32[]{:S(2)}, u32[]{:S(2)}) collective-permute-start(f32[136,1024]{1,0:T(8,128)S(1)} %collective-permute-done.4.refs_0_.refs_1_.refs_2_.refs_13_.refs_17_.refs_33_.refs_9_.refs_21_.refs_25_.refs_41_), channel_id=1, source_target_pairs={{0,2},{1,3},{2,0},{3,1},{4,6},{5,7},{6,4},{7,5},{8,10},{9,11},{10,... | collective-permute-start | bytes 1671176 | tf_op jit(solution)/shard_map/ppermute | solution.py:311
  83.5 12.8 %collective-permute-start.14 = (f32[136,1024]{1,0:T(8,128)S(1)}, f32[136,1024]{1,0:T(8,128)S(1)}, u32[]{:S(2)}, u32[]{:S(2)}) collective-permute-start(f32[136,1024]{1,0:T(8,128)S(1)} %collective-permute-done.4.refs_0_.refs_1_.refs_2_.refs_13_.refs_17_.refs_33_.refs_9_.refs_21_.refs_25_.refs_41_), channel_id=1, source_target_pairs={{0,1},{1,0},{2,3},{3,2},{4,5},{5,4},{6,7},{7,6},{8,9},{9,8},{10,11... | collective-permute-start | bytes 1671176 | tf_op jit(solution)/shard_map/ppermute | solution.py:311
  100.8 24.9 %collective-permute-start.24 = (f32[256,1024]{1,0:T(8,128)S(1)}, f32[256,1024]{1,0:T(8,128)S(1)}, u32[]{:S(2)}, u32[]{:S(2)}) collective-permute-start(f32[256,1024]{1,0:T(8,128)S(1)} %get-tuple-element.149.refs_0_.refs_4_.refs_8_.refs_9_.refs_12_.refs_17_), channel_id=1, source_target_pairs={{0,2},{1,3},{2,0},{3,1},{4,6},{5,7},{6,4},{7,5},{8,10},{9,11},{10,... | collective-permute-start | bytes 3145736 | tf_op jit(solution)/shard_map/ppermute | solution.py:311
  111.7 12.6 %collective-permute-start.22 = (f32[8,128]{1,0:T(8,128)S(1)}, f32[8,128]{1,0:T(8,128)S(1)}, u32[]{:S(2)}, u32[]{:S(2)}) collective-permute-start(f32[8,128]{1,0:T(8,128)S(1)} %fold_own.1.refs_0_), channel_id=1, source_target_pairs={{0,12},{1,13},{2,14},{3,15},{4,8},{5,9},{6,10},{7,11},{8,4},{9,5},... | collective-permute-start | bytes 12296 | tf_op jit(solution)/shard_map/ppermute | solution.py:311
  112.5 11.8 %collective-permute-start.21 = (f32[8,128]{1,0:T(8,128)S(1)}, f32[8,128]{1,0:T(8,128)S(1)}, u32[]{:S(2)}, u32[]{:S(2)}) collective-permute-start(f32[8,128]{1,0:T(8,128)S(1)} %fold_own.1.refs_0_), channel_id=1, source_target_pairs={{0,8},{1,9},{2,10},{3,11},{4,12},{5,13},{6,14},{7,15},{8,0},{9,1},... | collective-permute-start | bytes 12296 | tf_op jit(solution)/shard_map/ppermute | solution.py:311
  128.8 21.5 %collective-permute-start.34 = (f32[256,1024]{1,0:T(8,128)S(1)}, f32[256,1024]{1,0:T(8,128)S(1)}, u32[]{:S(2)}, u32[]{:S(2)}) collective-permute-start(f32[256,1024]{1,0:T(8,128)S(1)} %get-tuple-element.159.refs_1_.refs_0_.refs_4_.refs_16_), channel_id=1, source_target_pairs={{0,1},{1,0},{2,3},{3,2},{4,5},{5,4},{6,7},{7,6},{8,9},{9,8},{10,11... | collective-permute-start | bytes 3145736 | tf_op jit(solution)/shard_map/ppermute | solution.py:311
  130.4 24.0 %collective-permute-start.25 = (f32[256,1024]{1,0:T(8,128)S(1)}, f32[256,1024]{1,0:T(8,128)S(1)}, u32[]{:S(2)}, u32[]{:S(2)}) collective-permute-start(f32[256,1024]{1,0:T(8,128)S(1)} %get-tuple-element.159.refs_1_.refs_0_.refs_4_.refs_16_), channel_id=1, source_target_pairs={{0,2},{1,3},{2,0},{3,1},{4,6},{5,7},{6,4},{7,5},{8,10},{9,11},{10,... | collective-permute-start | bytes 3145736 | tf_op jit(solution)/shard_map/ppermute | solution.py:311
  138.2 16.3 %collective-permute-start.31 = (f32[64,1024]{1,0:T(8,128)S(1)}, f32[64,1024]{1,0:T(8,128)S(1)}, u32[]{:S(2)}, u32[]{:S(2)}) collective-permute-start(f32[64,1024]{1,0:T(8,128)S(1)} %get-tuple-element.153), channel_id=1, source_target_pairs={{0,4},{1,5},{2,6},{3,7},{4,0},{5,1},{6,2},{7,3},{8,12},{9,13},{10,... | collective-permute-start | bytes 786440 | tf_op jit(solution)/shard_map/ppermute | solution.py:311
  141.6 12.8 %collective-permute-start.32 = (f32[32,1024]{1,0:T(8,128)S(1)}, f32[32,1024]{1,0:T(8,128)S(1)}, u32[]{:S(2)}, u32[]{:S(2)}) collective-permute-start(f32[32,1024]{1,0:T(8,128)S(1)} %get-tuple-element.154), channel_id=1, source_target_pairs={{0,8},{1,9},{2,10},{3,11},{4,12},{5,13},{6,14},{7,15},{8,0},{9,1},... | collective-permute-start | bytes 393224 | tf_op jit(solution)/shard_map/ppermute | solution.py:311
  142.1 12.3 %collective-permute-start.33 = (f32[32,1024]{1,0:T(8,128)S(1)}, f32[32,1024]{1,0:T(8,128)S(1)}, u32[]{:S(2)}, u32[]{:S(2)}) collective-permute-start(f32[32,1024]{1,0:T(8,128)S(1)} %get-tuple-element.156), channel_id=1, source_target_pairs={{0,12},{1,13},{2,14},{3,15},{4,8},{5,9},{6,10},{7,11},{8,4},{9,5},... | collective-permute-start | bytes 393224 | tf_op jit(solution)/shard_map/ppermute | solution.py:311
  154.4 13.2 %collective-permute-start.36 = (f32[256,1024]{1,0:T(8,128)S(1)}, f32[256,1024]{1,0:T(8,128)S(1)}, u32[]{:S(2)}, u32[]{:S(2)}) collective-permute-start(f32[256,1024]{1,0:T(8,128)S(1)} %collective-permute-done.25.refs_2_.refs_6_), channel_id=1, source_target_pairs={{0,1},{1,0},{2,3},{3,2},{4,5},{5,4},{6,7},{7,6},{8,9},{9,8},{10,11... | collective-permute-start | bytes 3145736 | tf_op jit(solution)/shard_map/ppermute | solution.py:311
  154.5 20.3 %collective-permute-start.37 = (f32[32,1024]{1,0:T(8,128)S(1)}, f32[32,1024]{1,0:T(8,128)S(1)}, u32[]{:S(2)}, u32[]{:S(2)}) collective-permute-start(f32[32,1024]{1,0:T(8,128)S(1)} %get-tuple-element.155), channel_id=1, source_target_pairs={{0,8},{1,9},{2,10},{3,11},{4,12},{5,13},{6,14},{7,15},{8,0},{9,1},... | collective-permute-start | bytes 393224 | tf_op jit(solution)/shard_map/ppermute | solution.py:311
  158.4 16.4 %collective-permute-start.38 = (f32[32,1024]{1,0:T(8,128)S(1)}, f32[32,1024]{1,0:T(8,128)S(1)}, u32[]{:S(2)}, u32[]{:S(2)}) collective-permute-start(f32[32,1024]{1,0:T(8,128)S(1)} %get-tuple-element.157), channel_id=1, source_target_pairs={{0,12},{1,13},{2,14},{3,15},{4,8},{5,9},{6,10},{7,11},{8,4},{9,5},... | collective-permute-start | bytes 393224 | tf_op jit(solution)/shard_map/ppermute | solution.py:311
  159.4 24.9 %collective-permute-start.35 = (f32[256,1024]{1,0:T(8,128)S(1)}, f32[256,1024]{1,0:T(8,128)S(1)}, u32[]{:S(2)}, u32[]{:S(2)}) collective-permute-start(f32[256,1024]{1,0:T(8,128)S(1)} %get-tuple-element.161.refs_0_.refs_4_.refs_16_), channel_id=1, source_target_pairs={{0,2},{1,3},{2,0},{3,1},{4,6},{5,7},{6,4},{7,5},{8,10},{9,11},{10,... | collective-permute-start | bytes 3145736 | tf_op jit(solution)/shard_map/ppermute | solution.py:311
  174.8 14.7 %collective-permute-start.39 = (f32[64,1024]{1,0:T(8,128)S(1)}, f32[64,1024]{1,0:T(8,128)S(1)}, u32[]{:S(2)}, u32[]{:S(2)}) collective-permute-start(f32[64,1024]{1,0:T(8,128)S(1)} %get-tuple-element.172), channel_id=1, source_target_pairs={{0,4},{1,5},{2,6},{3,7},{4,0},{5,1},{6,2},{7,3},{8,12},{9,13},{10,... | collective-permute-start | bytes 786440 | tf_op jit(solution)/shard_map/ppermute | solution.py:311
  175.4 12.1 %collective-permute-start.40 = (f32[32,1024]{1,0:T(8,128)S(1)}, f32[32,1024]{1,0:T(8,128)S(1)}, u32[]{:S(2)}, u32[]{:S(2)}) collective-permute-start(f32[32,1024]{1,0:T(8,128)S(1)} %get-tuple-element.173), channel_id=1, source_target_pairs={{0,8},{1,9},{2,10},{3,11},{4,12},{5,13},{6,14},{7,15},{8,0},{9,1},... | collective-permute-start | bytes 393224 | tf_op jit(solution)/shard_map/ppermute | solution.py:311
  177.3 12.2 %collective-permute-start.41 = (f32[32,1024]{1,0:T(8,128)S(1)}, f32[32,1024]{1,0:T(8,128)S(1)}, u32[]{:S(2)}, u32[]{:S(2)}) collective-permute-start(f32[32,1024]{1,0:T(8,128)S(1)} %get-tuple-element.174), channel_id=1, source_target_pairs={{0,12},{1,13},{2,14},{3,15},{4,8},{5,9},{6,10},{7,11},{8,4},{9,5},... | collective-permute-start | bytes 393224 | tf_op jit(solution)/shard_map/ppermute | solution.py:311
  178.3 13.4 %collective-permute-start.23 = (f32[256,1024]{1,0:T(8,128)S(1)}, f32[256,1024]{1,0:T(8,128)S(1)}, u32[]{:S(2)}, u32[]{:S(2)}) collective-permute-start(f32[256,1024]{1,0:T(8,128)S(1)} %get-tuple-element.161.refs_0_.refs_4_.refs_16_), channel_id=1, source_target_pairs={{0,1},{1,0},{2,3},{3,2},{4,5},{5,4},{6,7},{7,6},{8,9},{9,8},{10,11... | collective-permute-start | bytes 3145736 | tf_op jit(solution)/shard_map/ppermute | solution.py:311
  190.8 13.3 %collective-permute-start.44 = (f32[32,1024]{1,0:T(8,128)S(1)}, f32[32,1024]{1,0:T(8,128)S(1)}, u32[]{:S(2)}, u32[]{:S(2)}) collective-permute-start(f32[32,1024]{1,0:T(8,128)S(1)} %get-tuple-element.186), channel_id=1, source_target_pairs={{0,12},{1,13},{2,14},{3,15},{4,8},{5,9},{6,10},{7,11},{8,4},{9,5},... | collective-permute-start | bytes 393224 | tf_op jit(solution)/shard_map/ppermute | solution.py:311
  204.1 20.5 %collective-permute-start.46 = (f32[64,1024]{1,0:T(8,128)S(1)}, f32[64,1024]{1,0:T(8,128)S(1)}, u32[]{:S(2)}, u32[]{:S(2)}) collective-permute-start(f32[64,1024]{1,0:T(8,128)S(1)} %get-tuple-element.189), channel_id=1, source_target_pairs={{0,8},{1,9},{2,10},{3,11},{4,12},{5,13},{6,14},{7,15},{8,0},{9,1},... | collective-permute-start | bytes 786440 | tf_op jit(solution)/shard_map/ppermute | solution.py:311
  206.6 23.5 %collective-permute-start.47 = (f32[64,1024]{1,0:T(8,128)S(1)}, f32[64,1024]{1,0:T(8,128)S(1)}, u32[]{:S(2)}, u32[]{:S(2)}) collective-permute-start(f32[64,1024]{1,0:T(8,128)S(1)} %get-tuple-element.190), channel_id=1, source_target_pairs={{0,12},{1,13},{2,14},{3,15},{4,8},{5,9},{6,10},{7,11},{8,4},{9,5},... | collective-permute-start | bytes 786440 | tf_op jit(solution)/shard_map/ppermute | solution.py:311
  (23 other events, 167.2 us)
